TPU v7x, 32 devices: a whole 2x2x4 slice. The times are simulated.
32 devices in a mesh: ex: 4 (over x, core), ey: 8 (over z, y).
Axes of the slice: x: 2, y: 2, z: 4, core: 2. Of those that a mesh axis runs over, the one named last changes fastest.
Arguments:
- source: float32 [8, 8, 8, 4, 1024], P(None, None, None, 'ex', 'ey'), may hold values from -4 to 4
- point_base: int32 [3, 32], P(None, ('ex', 'ey')), may hold values from 0 to 62, as said below
- point_offset: float32 [3, 32], P(None, ('ex', 'ey')), may hold values from -0.5 to 0.5
- point_force: float32 [3, 32], P(None, ('ex', 'ey')), may hold values from -4 to 4
Outputs:
- pressure: float32 [8, 8, 8, 4, 1024], P(None, None, None, 'ex', 'ey')
- forces: float32 [3, 8, 8, 8, 4, 1024], P(None, None, None, None, 'ex', 'ey')
Inputs may be any that keep to these rules, and one draw needn't show every extreme that they name: `point_base`: row 0 is the turbine's element index along the first dimension, the same for all points of a turbine; the first turbine has 0 and the last 2. Rows 1 and 2 lie within 6 of their turbine's hub, between 0 and 14, resp. 0 and 62; the first point sits at 14 in row 1 and 62 in row 2.
All inputs are finite; a program needn't handle non-finite values.
Results may differ from a plain program's by a relative error of at most 0.00027.
Values sent between devices are 32-bit elements; how exact they have to be, the bound alone decides.
No kernel may reach another device: no remote copies, remote signals or barrier semaphores. Data moves between devices by JAX's collectives and lax.ppermute only.
A program may use at most 128 MiB of HBM per device.

v0:
```python
import math

import jax
import jax.numpy as jnp
import numpy as np
from jax import lax
from jax.sharding import PartitionSpec as P

EZ = 64
CG_STEPS = 4
CYCLES = 2


GLL_POINTS = np.array(
    [
        -1.0,
        -0.8717401485096066,
        -0.5917001814331423,
        -0.2092992179024789,
        0.2092992179024789,
        0.5917001814331423,
        0.8717401485096066,
        1.0,
    ]
)
WIDTH_EPS = 0.35
GAUSS_NORM = 1.0 / (math.pi**1.5 * WIDTH_EPS**3)
CHEB_LOW = 1.5
CHEB_HIGH = 12.0
HIGHEST = lax.Precision.HIGHEST


def padded(cells, sides, width):
    for axis, dim in sides:
        count = lax.axis_size(axis)
        ends = count - 1
        head = lax.slice_in_dim(cells, 0, width, axis=dim)
        tail = lax.slice_in_dim(cells, cells.shape[dim] - width, cells.shape[dim], axis=dim)
        cells = jnp.concatenate(
            [
                lax.ppermute(tail, axis, [(i, (i + 1) % count) for i in range(ends)]),
                cells,
                lax.ppermute(head, axis, [((i + 1) % count, i) for i in range(ends)]),
            ],
            axis=dim,
        )
    return cells


def build_tables():
    points = GLL_POINTS
    degree = len(points) - 1
    previous = points * 0.0 + 1.0
    current = points.copy()
    for k in range(1, degree):
        following = ((2 * k + 1) * points * current - k * previous) / (k + 1)
        previous = current
        current = following
    derivative = np.zeros((degree + 1, degree + 1))
    for i in range(degree + 1):
        for j in range(degree + 1):
            if i != j:
                derivative[i, j] = current[i] / (current[j] * (points[i] - points[j]))
    derivative[0, 0] = -degree * (degree + 1) / 4.0
    derivative[degree, degree] = degree * (degree + 1) / 4.0
    weights = 2.0 / (degree * (degree + 1) * current**2)
    interp = np.stack([(1.0 - points) / 2.0, (1.0 + points) / 2.0], axis=1)
    stiff_one = derivative.T @ (weights[:, None] * derivative)
    stiff_two = interp.T @ stiff_one @ interp
    mass_two = interp.T @ (weights[:, None] * interp)
    coarse_matrix = 0.5 * (
        np.kron(np.kron(stiff_two, mass_two), mass_two)
        + np.kron(np.kron(mass_two, stiff_two), mass_two)
        + np.kron(np.kron(mass_two, mass_two), stiff_two)
    )
    stiff_diag = (weights[:, None] * derivative**2).sum(axis=0)
    return (
        jnp.asarray(derivative, jnp.float32),
        jnp.asarray(weights, jnp.float32),
        jnp.asarray(interp, jnp.float32),
        jnp.asarray(coarse_matrix, jnp.float32),
        jnp.asarray(stiff_diag, jnp.float32),
    )


def edge_flags(size_n, first, elem_count, total):
    node_index = jnp.arange(size_n, dtype=jnp.int32)[:, None]
    elem_index = first + jnp.arange(elem_count, dtype=jnp.int32)[None, :]
    outer = (node_index == 0) & (elem_index == 0) | (node_index == size_n - 1) & (
        elem_index == total - 1
    )
    interior = jnp.where(outer, jnp.float32(0.0), jnp.float32(1.0))
    owner_flag = jnp.where((node_index == 0) & (elem_index > 0), jnp.float32(0.0), jnp.float32(1.0))
    return (interior, owner_flag)


def tensor_flags(flag_x, flag_y, flag_z):
    combined = (
        flag_x[:, None, None, :, None, None]
        * flag_y[None, :, None, None, :, None]
        * flag_z[None, None, :, None, None, :]
    )
    dims_all = combined.shape
    return combined.reshape(
        dims_all[0], dims_all[1], dims_all[2], dims_all[3], dims_all[4] * dims_all[5]
    )


def assemble_side(grid_vals, node_dim, elem_dim, fetcher):
    last_node = grid_vals.shape[node_dim] - 1
    elem_count = grid_vals.shape[elem_dim]
    lower_face = lax.index_in_dim(grid_vals, 0, node_dim, keepdims=False)
    upper_face = lax.index_in_dim(grid_vals, last_node, node_dim, keepdims=False)
    paired = jnp.stack([lower_face, upper_face], 0)
    if fetcher is None:
        widths = [(0, 0)] * paired.ndim
        widths[elem_dim] = (1, 1)
        extended = jnp.pad(paired, widths)
    else:
        extended = fetcher(paired)
    from_below = lax.slice_in_dim(extended[1], 0, elem_count, axis=elem_dim - 1)
    from_above = lax.slice_in_dim(extended[0], 2, elem_count + 2, axis=elem_dim - 1)
    middle = lax.slice_in_dim(grid_vals, 1, last_node, axis=node_dim)
    return jnp.concatenate(
        [
            jnp.expand_dims(lower_face + from_below, node_dim),
            middle,
            jnp.expand_dims(upper_face + from_above, node_dim),
        ],
        node_dim,
    )


def assemble(grid_vals, slab_width, fetch_x, fetch_y):
    dims_all = grid_vals.shape
    blocks = grid_vals.reshape(
        dims_all[0], dims_all[1], dims_all[2], dims_all[3], dims_all[4] // slab_width, slab_width
    )
    blocks = assemble_side(blocks, 0, 3, fetch_x)
    blocks = assemble_side(blocks, 1, 4, fetch_y)
    blocks = assemble_side(blocks, 2, 5, None)
    return blocks.reshape(dims_all)


def faces_fine_x(paired):
    return padded(paired, (("ex", 3),), 1)


def faces_fine_y(paired):
    return padded(paired, (("ey", 4),), 1)


def faces_vertex_x(paired):
    return padded(paired, (("ex", 3),), 1)


def faces_vertex_y(paired):
    return padded(paired, (("ey", 4),), 1)


def curv_spread(value):
    return lax.psum(value, ("ex", "ey"))


def norm_spread(value):
    return lax.psum(value, ("ex", "ey"))


def stiffness(grid_vals, derivative, half_weights):
    grad_x = jnp.einsum("ai,ijklm->ajklm", derivative, grid_vals, precision=HIGHEST)
    grad_y = jnp.einsum("aj,ijklm->iaklm", derivative, grid_vals, precision=HIGHEST)
    grad_z = jnp.einsum("ak,ijklm->ijalm", derivative, grid_vals, precision=HIGHEST)
    return (
        jnp.einsum("ai,ajklm->ijklm", derivative, half_weights * grad_x, precision=HIGHEST)
        + jnp.einsum("aj,iaklm->ijklm", derivative, half_weights * grad_y, precision=HIGHEST)
        + jnp.einsum("ak,ijalm->ijklm", derivative, half_weights * grad_z, precision=HIGHEST)
    )


def weak_divergence(forces, derivative, tensor_weights):
    return 0.25 * (
        jnp.einsum("ai,ajklm->ijklm", derivative, tensor_weights * forces[0], precision=HIGHEST)
        + jnp.einsum("aj,iaklm->ijklm", derivative, tensor_weights * forces[1], precision=HIGHEST)
        + jnp.einsum("ak,ijalm->ijklm", derivative, tensor_weights * forces[2], precision=HIGHEST)
    )


def restrict(grid_vals, interp):
    return jnp.einsum("ia,jb,kc,ijklm->abclm", interp, interp, interp, grid_vals, precision=HIGHEST)


def prolong(vertex_vals, interp):
    return jnp.einsum(
        "ia,jb,kc,abclm->ijklm", interp, interp, interp, vertex_vals, precision=HIGHEST
    )


def coarse_apply(vertex_vals, coarse_matrix):
    dims_all = vertex_vals.shape
    flattened = vertex_vals.reshape(8, dims_all[3] * dims_all[4])
    return jnp.dot(coarse_matrix, flattened, precision=HIGHEST).reshape(dims_all)


def gauss_factor(position, base_elem, first, elem_count):
    points = jnp.asarray(GLL_POINTS, jnp.float32)
    elem_index = first + jnp.arange(elem_count, dtype=jnp.int32)
    coords = elem_index.astype(jnp.float32)[None, :] + 0.5 * (1.0 + points)[:, None]
    distance = coords[None, :, :] - position[:, None, None]
    node_index = jnp.arange(8, dtype=jnp.int32)[None, :, None]
    elem_grid = elem_index[None, None, :]
    base_grid = base_elem[:, None, None]
    inside = (
        (elem_grid == base_grid)
        | (elem_grid == base_grid + 1)
        | (elem_grid == base_grid - 1) & (node_index == 7)
        | (elem_grid == base_grid + 2) & (node_index == 0)
    )
    return jnp.where(
        inside, jnp.exp(-(distance * distance) / (WIDTH_EPS * WIDTH_EPS)), jnp.float32(0.0)
    )


def spread_forces(base_elem, offset, force, first_x, count_x, first_y, count_y, depth):
    position = base_elem.astype(jnp.float32) + 1.0 + offset
    factor_x = gauss_factor(position[0], base_elem[0], first_x, count_x)
    factor_y = gauss_factor(position[1], base_elem[1], first_y, count_y)
    factor_z = gauss_factor(position[2], base_elem[2], 0, depth)
    spread = jnp.einsum(
        "cp,pie,pjf,pkg->cijkefg",
        GAUSS_NORM * force,
        factor_x,
        factor_y,
        factor_z,
        precision=HIGHEST,
    )
    return spread.reshape(3, 8, 8, 8, count_x, count_y * depth)


def chebyshev_pass(solution, residual, operate, inverse_diag, need_residual):
    theta_mid = 0.5 * (CHEB_HIGH + CHEB_LOW)
    delta_half = 0.5 * (CHEB_HIGH - CHEB_LOW)
    rho_first = delta_half / theta_mid
    rho_second = 1.0 / (2.0 * theta_mid / delta_half - rho_first)
    update = inverse_diag * residual / theta_mid
    solution = solution + update
    residual = residual - operate(update)
    update = (
        rho_second * rho_first * update + 2.0 * rho_second / delta_half * inverse_diag * residual
    )
    solution = solution + update
    if need_residual:
        residual = residual - operate(update)
    return (solution, residual)


def coarse_cg_classic(right_side, operate, owner_flag, reduce_curv, reduce_norm):
    solution = jnp.zeros_like(right_side)
    residual = right_side
    direction = right_side
    norm_now = reduce_norm(jnp.sum(owner_flag * residual * residual))
    for step in range(CG_STEPS):
        image = operate(direction)
        alpha = norm_now / reduce_curv(jnp.sum(owner_flag * direction * image))
        solution = solution + alpha * direction
        residual = residual - alpha * image
        norm_next = reduce_norm(jnp.sum(owner_flag * residual * residual))
        direction = residual + norm_next / norm_now * direction
        norm_now = norm_next
    return solution


def vcycle(solution, right_side, operate, inverse_diag, own_fine, mask_fine, interp, solve_coarse):
    residual = right_side - operate(solution)
    solution, residual = chebyshev_pass(solution, residual, operate, inverse_diag, True)
    correction = solve_coarse(restrict(own_fine * residual, interp))
    solution = solution + mask_fine * prolong(correction, interp)
    residual = right_side - operate(solution)
    solution, residual = chebyshev_pass(solution, residual, operate, inverse_diag, False)
    return solution


def shards(source, point_base, point_offset, point_force):
    derivative, weights, interp, coarse_matrix, stiff_diag = build_tables()
    tensor_weights = (weights[:, None, None] * weights[None, :, None] * weights[None, None, :])[
        :, :, :, None, None
    ]
    half_weights = 0.5 * tensor_weights
    tiles_x = source.shape[3]
    width_yz = source.shape[4]
    tiles_y = width_yz // EZ
    index_x = lax.axis_index("ex")
    index_y = lax.axis_index("ey")
    total_x = tiles_x * lax.axis_size("ex")
    total_y = tiles_y * lax.axis_size("ey")
    first_x = index_x * tiles_x
    first_y = index_y * tiles_y
    kept_x, own_x = edge_flags(8, first_x, tiles_x, total_x)
    kept_y, own_y = edge_flags(8, first_y, tiles_y, total_y)
    kept_z, own_z = edge_flags(8, 0, EZ, EZ)
    mask_fine = tensor_flags(kept_x, kept_y, kept_z)
    own_fine = tensor_flags(own_x, own_y, own_z)
    packed = jnp.concatenate([point_base.astype(jnp.float32), point_offset, point_force], 0)
    piece = lax.all_gather(packed, ("ex", "ey"), axis=1, tiled=True)
    forces = spread_forces(
        piece[0:3].astype(jnp.int32), piece[3:6], piece[6:9], first_x, tiles_x, first_y, tiles_y, EZ
    )
    right_side = mask_fine * assemble(
        source + weak_divergence(forces, derivative, tensor_weights), EZ, faces_fine_x, faces_fine_y
    )
    diag_local = 0.5 * (
        stiff_diag[:, None, None] * weights[None, :, None] * weights[None, None, :]
        + weights[:, None, None] * stiff_diag[None, :, None] * weights[None, None, :]
        + weights[:, None, None] * weights[None, :, None] * stiff_diag[None, None, :]
    )
    diagonal = assemble(
        jnp.broadcast_to(diag_local[:, :, :, None, None], source.shape),
        EZ,
        faces_fine_x,
        faces_fine_y,
    )
    inverse_diag = mask_fine / diagonal

    def operate(grid_vals):
        return mask_fine * assemble(
            stiffness(grid_vals, derivative, half_weights), EZ, faces_fine_x, faces_fine_y
        )

    vkept_x, vown_x = edge_flags(2, first_x, tiles_x, total_x)
    vkept_y, vown_y = edge_flags(2, first_y, tiles_y, total_y)
    vkept_z, vown_z = edge_flags(2, 0, EZ, EZ)
    mask_vertex = tensor_flags(vkept_x, vkept_y, vkept_z)
    own_vertex = tensor_flags(vown_x, vown_y, vown_z)

    def operate_coarse(vertex_vals):
        return mask_vertex * assemble(
            coarse_apply(vertex_vals, coarse_matrix), EZ, faces_vertex_x, faces_vertex_y
        )

    def solve_coarse(local_load):
        assembled = mask_vertex * assemble(local_load, EZ, faces_vertex_x, faces_vertex_y)
        return coarse_cg_classic(assembled, operate_coarse, own_vertex, curv_spread, norm_spread)

    solution = jnp.zeros_like(source)
    for cycle in range(CYCLES):
        solution = vcycle(
            solution, right_side, operate, inverse_diag, own_fine, mask_fine, interp, solve_coarse
        )
    return (solution, forces)


def solution(mesh):
    in_specs = (
        P(None, None, None, "ex", "ey"),
        P(None, ("ex", "ey")),
        P(None, ("ex", "ey")),
        P(None, ("ex", "ey")),
    )
    out_specs = (P(None, None, None, "ex", "ey"), P(None, None, None, None, "ex", "ey"))
    return jax.shard_map(shards, mesh=mesh, in_specs=in_specs, out_specs=out_specs, check_vma=False)
```

profile of v0, /device:TPU:0, one launch (start us, length us, event | category | flops | bytes accessed | tf_op | source)
XLA Modules:
  0.0 1305.4 jit_solution(5034322435665233329)
XLA Ops:
  15.0 5.1 collective-permute-start.8
  20.2 67.4 %all-gather = f32[32,1,9]{2,1,0:T(1,128)S(1)} all-gather(f32[1,1,9]{2,1,0:T(1,128)S(1)} %maximum_bitcast_fusion), channel_id=1, replica_groups=mesh['ex'=4,'ey'=8] {'ex','ey'}, dimensions={0}, use_global_device_ids=true | all-gather | bytes 1188 | tf_op jit(solution)/shard_map/all_gather | solution.py:303
  116.0 4.5 collective-permute-start.2
  123.6 4.5 collective-permute-start.6
  131.0 4.4 collective-permute-done.7
  169.7 4.5 collective-permute-start.14
  275.6 40.1 %all-reduce.23 = (f32[]{:T(128)}, f32[]{:T(128)}) all-reduce(f32[]{:T(128)} %get-tuple-element.41, f32[]{:T(128)} %get-tuple-element.40), channel_id=1, replica_groups=mesh['ex'=4,'ey'=8] {'ex','ey'}, use_global_device_ids=true, to_apply=%region_1.2 | all-reduce | flops 2 | bytes 16 | tf_op jit(solution)/shard_map/psum | solution.py:166
  317.6 42.3 %psum.114 = f32[]{:T(128)} all-reduce(f32[]{:T(128)} %get-tuple-element.52), channel_id=1, replica_groups=mesh['ex'=4,'ey'=8] {'ex','ey'}, use_global_device_ids=true, to_apply=%region_5.6 | all-reduce | flops 1 | bytes 8 | tf_op jit(solution)/shard_map/psum | solution.py:166
  379.7 40.8 %psum.115 = f32[]{:T(128)} all-reduce(f32[]{:T(128)} %fusion.373), channel_id=1, replica_groups=mesh['ex'=4,'ey'=8] {'ex','ey'}, use_global_device_ids=true, to_apply=%region_7.8 | all-reduce | flops 1 | bytes 8 | tf_op jit(solution)/shard_map/psum | solution.py:162
  422.3 39.8 %psum.116 = f32[]{:T(128)} all-reduce(f32[]{:T(128)} %get-tuple-element.50), channel_id=1, replica_groups=mesh['ex'=4,'ey'=8] {'ex','ey'}, use_global_device_ids=true, to_apply=%region_9.10 | all-reduce | flops 1 | bytes 8 | tf_op jit(solution)/shard_map/psum | solution.py:166
  475.4 4.4 collective-permute-start.34
  486.4 40.8 %psum.117 = f32[]{:T(128)} all-reduce(f32[]{:T(128)} %get-tuple-element.393), channel_id=1, replica_groups=mesh['ex'=4,'ey'=8] {'ex','ey'}, use_global_device_ids=true, to_apply=%region_11.12 | all-reduce | flops 1 | bytes 8 | tf_op jit(solution)/shard_map/psum | solution.py:162
  529.2 39.4 %psum.118 = f32[]{:T(128)} all-reduce(f32[]{:T(128)} %fusion.381), channel_id=1, replica_groups=mesh['ex'=4,'ey'=8] {'ex','ey'}, use_global_device_ids=true, to_apply=%region_13.14 | all-reduce | flops 1 | bytes 8 | tf_op jit(solution)/shard_map/psum | solution.py:166
  582.6 5.0 collective-permute-start.38
  612.9 41.7 %psum.119 = f32[]{:T(128)} all-reduce(f32[]{:T(128)} %fusion.385), channel_id=1, replica_groups=mesh['ex'=4,'ey'=8] {'ex','ey'}, use_global_device_ids=true, to_apply=%region_15.16 | all-reduce | flops 1 | bytes 8 | tf_op jit(solution)/shard_map/psum | solution.py:162
  675.1 4.6 collective-permute-done.43
  720.7 6.2 collective-permute-start.48
  750.7 4.8 collective-permute-start.52
  789.5 5.1 collective-permute-start.56
  807.2 4.4 collective-permute-done.59
  856.7 43.7 %all-reduce.22 = (f32[]{:T(128)}, f32[]{:T(128)}) all-reduce(f32[]{:T(128)} %get-tuple-element.39, f32[]{:T(128)} %get-tuple-element.38), channel_id=1, replica_groups=mesh['ex'=4,'ey'=8] {'ex','ey'}, use_global_device_ids=true, to_apply=%region_17.18 | all-reduce | flops 2 | bytes 16 | tf_op jit(solution)/shard_map/psum | solution.py:166
  902.3 41.1 %psum.122 = f32[]{:T(128)} all-reduce(f32[]{:T(128)} %get-tuple-element.48), channel_id=1, replica_groups=mesh['ex'=4,'ey'=8] {'ex','ey'}, use_global_device_ids=true, to_apply=%region_21.22 | all-reduce | flops 1 | bytes 8 | tf_op jit(solution)/shard_map/psum | solution.py:166
  950.3 4.4 collective-permute-start.70
  968.1 41.1 %psum.123 = f32[]{:T(128)} all-reduce(f32[]{:T(128)} %fusion.371), channel_id=1, replica_groups=mesh['ex'=4,'ey'=8] {'ex','ey'}, use_global_device_ids=true, to_apply=%region_23.24 | all-reduce | flops 1 | bytes 8 | tf_op jit(solution)/shard_map/psum | solution.py:162
  1012.4 40.8 %psum.124 = f32[]{:T(128)} all-reduce(f32[]{:T(128)} %get-tuple-element.46), channel_id=1, replica_groups=mesh['ex'=4,'ey'=8] {'ex','ey'}, use_global_device_ids=true, to_apply=%region_25.26 | all-reduce | flops 1 | bytes 8 | tf_op jit(solution)/shard_map/psum | solution.py:166
  1072.2 4.4 collective-permute-start.74
  1090.6 39.3 %psum.125 = f32[]{:T(128)} all-reduce(f32[]{:T(128)} %get-tuple-element.379), channel_id=1, replica_groups=mesh['ex'=4,'ey'=8] {'ex','ey'}, use_global_device_ids=true, to_apply=%region_27.28 | all-reduce | flops 1 | bytes 8 | tf_op jit(solution)/shard_map/psum | solution.py:162
  1132.6 39.9 %psum.126 = f32[]{:T(128)} all-reduce(f32[]{:T(128)} %fusion.378), channel_id=1, replica_groups=mesh['ex'=4,'ey'=8] {'ex','ey'}, use_global_device_ids=true, to_apply=%region_29.30 | all-reduce | flops 1 | bytes 8 | tf_op jit(solution)/shard_map/psum | solution.py:166
  1190.7 5.0 collective-permute-start.78
  1211.8 40.9 %psum.127 = f32[]{:T(128)} all-reduce(f32[]{:T(128)} %fusion.384), channel_id=1, replica_groups=mesh['ex'=4,'ey'=8] {'ex','ey'}, use_global_device_ids=true, to_apply=%region_31.32 | all-reduce | flops 1 | bytes 8 | tf_op jit(solution)/shard_map/psum | solution.py:162
  1267.9 4.4 collective-permute-start.82
  1274.5 4.6 collective-permute-done.83
  (1302 shorter events, 561.2 us)
Async XLA Ops:
  4.0 102.6 %collective-permute-start.1 = (f32[2,8,8,1,2,64]{5,4,2,1,3,0:T(2,128)}, f32[2,8,8,1,2,64]{5,4,2,1,3,0:T(2,128)}, u32[]{:S(2)}, u32[]{:S(2)}) collective-permute-start(f32[2,8,8,1,2,64]{5,4,2,1,3,0:T(2,128)} %pad_maximum_fusion.28), channel_id=1, source_target_pairs={{8,0},{16,8},{24,16},{9,1},{17,9},{25,17},{10,2},{18,10},{26,18},{... | collective-permute-start | bytes 196616 | tf_op jit(solution)/shard_map/ppermute | solution.py:43
  5.3 104.4 %collective-permute-start = (f32[2,8,8,1,2,64]{5,4,2,1,3,0:T(2,128)}, f32[2,8,8,1,2,64]{5,4,2,1,3,0:T(2,128)}, u32[]{:S(2)}, u32[]{:S(2)}) collective-permute-start(f32[2,8,8,1,2,64]{5,4,2,1,3,0:T(2,128)} %pad_maximum_fusion.28), channel_id=1, source_target_pairs={{0,8},{8,16},{16,24},{1,9},{9,17},{17,25},{2,10},{10,18},{18,26},{... | collective-permute-start | bytes 196616 | tf_op jit(solution)/shard_map/ppermute | solution.py:41
  13.7 97.2 %collective-permute-start.9 = (f32[2,8,8,1,2,64]{5,4,2,1,3,0:T(2,128)}, f32[2,8,8,1,2,64]{5,4,2,1,3,0:T(2,128)}, u32[]{:S(2)}, u32[]{:S(2)}) collective-permute-start(f32[2,8,8,1,2,64]{5,4,2,1,3,0:T(2,128)} %constant_dynamic-update-slice_fusion.2), channel_id=1, source_target_pairs={{8,0},{16,8},{24,16},{9,1},{17,9},{25,17},{10,2},{18,10},{26,18},{... | collective-permute-start | bytes 196616 | tf_op jit(solution)/shard_map/ppermute | solution.py:43
  15.0 95.9 %collective-permute-start.8 = (f32[2,8,8,1,2,64]{5,4,2,1,3,0:T(2,128)}, f32[2,8,8,1,2,64]{5,4,2,1,3,0:T(2,128)}, u32[]{:S(2)}, u32[]{:S(2)}) collective-permute-start(f32[2,8,8,1,2,64]{5,4,2,1,3,0:T(2,128)} %constant_dynamic-update-slice_fusion.2), channel_id=1, source_target_pairs={{0,8},{8,16},{16,24},{1,9},{9,17},{17,25},{2,10},{10,18},{18,26},{... | collective-permute-start | bytes 196616 | tf_op jit(solution)/shard_map/ppermute | solution.py:41
  101.5 19.1 %collective-permute-start.5 = (f32[2,8,8,1,2,64]{5,4,2,1,3,0:T(2,128)}, f32[2,8,8,1,2,64]{5,4,2,1,3,0:T(2,128)}, u32[]{:S(2)}, u32[]{:S(2)}) collective-permute-start(f32[2,8,8,1,2,64]{5,4,2,1,3,0:T(2,128)} %constant_dynamic-update-slice_fusion), channel_id=1, source_target_pairs={{8,0},{16,8},{24,16},{9,1},{17,9},{25,17},{10,2},{18,10},{26,18},{... | collective-permute-start | bytes 196616 | tf_op jit(solution)/shard_map/ppermute | solution.py:43
  106.6 15.5 %collective-permute-start.4 = (f32[2,8,8,1,2,64]{5,4,2,1,3,0:T(2,128)}, f32[2,8,8,1,2,64]{5,4,2,1,3,0:T(2,128)S(1)}, u32[]{:S(2)}, u32[]{:S(2)}) collective-permute-start(f32[2,8,8,1,2,64]{5,4,2,1,3,0:T(2,128)} %constant_dynamic-update-slice_fusion), channel_id=1, source_target_pairs={{0,8},{8,16},{16,24},{1,9},{9,17},{17,25},{2,10},{10,18},{18,26},{... | collective-permute-start | bytes 196616 | tf_op jit(solution)/shard_map/ppermute | solution.py:41
  112.5 15.7 %collective-permute-start.10 = (f32[2,8,8,1,1,64]{5,4,2,1,3,0:T(1,128)S(1)}, f32[2,8,8,1,1,64]{5,4,2,1,3,0:T(1,128)S(1)}, u32[]{:S(2)}, u32[]{:S(2)}) collective-permute-start(f32[2,8,8,1,1,64]{5,4,2,1,3,0:T(1,128)S(1)} %get-tuple-element.245), channel_id=1, source_target_pairs={{0,1},{1,2},{2,3},{3,4},{4,5},{5,6},{6,7},{8,9},{9,10},{10,11},{11... | collective-permute-start | bytes 98312 | tf_op jit(solution)/shard_map/ppermute | solution.py:41
  113.8 15.7 %collective-permute-start.11 = (f32[2,8,8,1,1,64]{5,4,2,1,3,0:T(1,128)S(1)}, f32[2,8,8,1,1,64]{5,4,2,1,3,0:T(1,128)S(1)}, u32[]{:S(2)}, u32[]{:S(2)}) collective-permute-start(f32[2,8,8,1,1,64]{5,4,2,1,3,0:T(1,128)S(1)} %get-tuple-element.246), channel_id=1, source_target_pairs={{1,0},{2,1},{3,2},{4,3},{5,4},{6,5},{7,6},{9,8},{10,9},{11,10},{12... | collective-permute-start | bytes 98312 | tf_op jit(solution)/shard_map/ppermute | solution.py:43
  116.0 14.2 %collective-permute-start.2 = (f32[2,8,8,1,1,64]{5,4,2,1,3,0:T(1,128)S(1)}, f32[2,8,8,1,1,64]{5,4,2,1,3,0:T(1,128)S(1)}, u32[]{:S(2)}, u32[]{:S(2)}) collective-permute-start(f32[2,8,8,1,1,64]{5,4,2,1,3,0:T(1,128)S(1)} %get-tuple-element.237), channel_id=1, source_target_pairs={{0,1},{1,2},{2,3},{3,4},{4,5},{5,6},{6,7},{8,9},{9,10},{10,11},{11... | collective-permute-start | bytes 98312 | tf_op jit(solution)/shard_map/ppermute | solution.py:41
  120.6 9.6 collective-permute-start.3
  123.6 7.4 collective-permute-start.6
  128.2 7.2 collective-permute-start.7
  157.1 10.9 collective-permute-start.13
  158.3 9.7 collective-permute-start.12
  169.7 6.9 collective-permute-start.14
  198.7 11.6 collective-permute-start.17
  200.0 10.3 collective-permute-start.16
  213.2 8.1 collective-permute-start.18
  582.6 27.9 %collective-permute-start.38 = (f32[2,2,2,1,1,64]{5,4,2,1,3,0:T(1,128)}, f32[2,2,2,1,1,64]{5,4,2,1,3,0:T(1,128)}, u32[]{:S(2)}, u32[]{:S(2)}) collective-permute-start(f32[2,2,2,1,1,64]{5,4,2,1,3,0:T(1,128)} %get-tuple-element.336), channel_id=1, source_target_pairs={{0,1},{1,2},{2,3},{3,4},{4,5},{5,6},{6,7},{8,9},{9,10},{10,11},{11... | collective-permute-start | bytes 6152 | tf_op jit(solution)/shard_map/ppermute | solution.py:41
  587.6 22.9 %collective-permute-start.39 = (f32[2,2,2,1,1,64]{5,4,2,1,3,0:T(1,128)}, f32[2,2,2,1,1,64]{5,4,2,1,3,0:T(1,128)}, u32[]{:S(2)}, u32[]{:S(2)}) collective-permute-start(f32[2,2,2,1,1,64]{5,4,2,1,3,0:T(1,128)} %get-tuple-element.337), channel_id=1, source_target_pairs={{1,0},{2,1},{3,2},{4,3},{5,4},{6,5},{7,6},{9,8},{10,9},{11,10},{12... | collective-permute-start | bytes 6152 | tf_op jit(solution)/shard_map/ppermute | solution.py:43
  694.6 8.8 collective-permute-start.46
  719.4 8.7 collective-permute-start.49
  720.7 7.4 collective-permute-start.48
  749.4 11.0 collective-permute-start.53
  750.7 9.7 collective-permute-start.52
  788.2 12.3 collective-permute-start.57
  789.5 11.1 collective-permute-start.56
  1062.4 7.6 collective-permute-start.73
  1179.8 6.9 collective-permute-start.77
  1190.7 18.0 %collective-permute-start.78 = (f32[2,2,2,1,1,64]{5,4,2,1,3,0:T(1,128)}, f32[2,2,2,1,1,64]{5,4,2,1,3,0:T(1,128)}, u32[]{:S(2)}, u32[]{:S(2)}) collective-permute-start(f32[2,2,2,1,1,64]{5,4,2,1,3,0:T(1,128)} %get-tuple-element.296), channel_id=1, source_target_pairs={{0,1},{1,2},{2,3},{3,4},{4,5},{5,6},{6,7},{8,9},{9,10},{10,11},{11... | collective-permute-start | bytes 6152 | tf_op jit(solution)/shard_map/ppermute | solution.py:41
  1195.7 13.0 collective-permute-start.79
  1291.0 8.8 collective-permute-start.86
  (199 other events, 3829.5 us)
where the time goes:
time: 1330 us; the launch traced here: 1310 us
  blocking collectives  639 us (48%)
  starting transfers between devices  228 us (17%)
  local copies, waits for them, and re-layouts  201 us (15%)
  other arithmetic  98.8 us (7%)
  waiting for transfers between devices  72.5 us (5%)
  matrix products  41.1 us (3%)
  between operations  24.6 us (2%)
    psum x8, blocking collectives, norm_spread(): return lax.psum(value, ('ex', 'ey'))  327 us
    psum x6, blocking collectives, curv_spread(): return lax.psum(value, ('ex', 'ey'))  245 us
    ppermute x44, starting transfers between devices, padded(): lax.ppermute(tail, axis, [(i, (i + 1) % count) for i in range(ends)])  170 us
    concatenate x142, local copies, waits for them, and re-layouts, assemble_side(): jnp.concatenate([jnp.expand_dims(lower_face + from_below, node_dim), midd...  84.2 us
    all_gather x1, blocking collectives, shards(): piece = lax.all_gather(packed, ('ex', 'ey'), axis=1, tiled=True)  67.4 us
    ppermute x44, waiting for transfers between devices, padded(): lax.ppermute(head, axis, [((i + 1) % count, i) for i in range(ends)])  67 us
    ppermute x44, starting transfers between devices, padded(): lax.ppermute(head, axis, [((i + 1) % count, i) for i in range(ends)])  58.3 us
  transfers between devices with their start and end apart: 88, of which 28 were waited for; matrix products, arithmetic and copies ran while one was open for 9% of the time, Pallas kernels for 0%

commit v1 on v0

v1 whole, which is shorter than its diff:
```python
import functools
import math

import jax
import jax.numpy as jnp
import numpy as np
from jax import lax
from jax.experimental import pallas as pl
from jax.experimental.pallas import tpu as pltpu
from jax.sharding import PartitionSpec as P

EZ = 64
CG_STEPS = 4
CYCLES = 2
N = 8
GLL_POINTS = np.array(
    [
        -1.0,
        -0.8717401485096066,
        -0.5917001814331423,
        -0.2092992179024789,
        0.2092992179024789,
        0.5917001814331423,
        0.8717401485096066,
        1.0,
    ]
)
WIDTH_EPS = 0.35
GAUSS_NORM = 1.0 / (math.pi**1.5 * WIDTH_EPS**3)
CHEB_LOW = 1.5
CHEB_HIGH = 12.0
THETA = 0.5 * (CHEB_HIGH + CHEB_LOW)
DELTA = 0.5 * (CHEB_HIGH - CHEB_LOW)
RHO_FIRST = DELTA / THETA
RHO_SECOND = 1.0 / (2.0 * THETA / DELTA - RHO_FIRST)
HIGHEST = lax.Precision.HIGHEST
F32 = jnp.float32
BF16 = jnp.bfloat16
PAD = 128
FACE = N * N


def build_tables():
    points = GLL_POINTS
    degree = len(points) - 1
    previous = points * 0.0 + 1.0
    current = points.copy()
    for k in range(1, degree):
        following = ((2 * k + 1) * points * current - k * previous) / (k + 1)
        previous = current
        current = following
    derivative = np.zeros((degree + 1, degree + 1))
    for i in range(degree + 1):
        for j in range(degree + 1):
            if i != j:
                derivative[i, j] = current[i] / (current[j] * (points[i] - points[j]))
    derivative[0, 0] = -degree * (degree + 1) / 4.0
    derivative[degree, degree] = degree * (degree + 1) / 4.0
    weights = 2.0 / (degree * (degree + 1) * current**2)
    interp = np.stack([(1.0 - points) / 2.0, (1.0 + points) / 2.0], axis=1)
    stiff_one = derivative.T @ (weights[:, None] * derivative)
    return derivative, weights, interp, stiff_one


def kron3(a, b, c):
    return np.kron(np.kron(a, b), c)


class Layout:
    def __init__(self, mesh_x, mesh_y, tiles_x, tiles_y):
        self.mesh_x, self.mesh_y = mesh_x, mesh_y
        self.num_x, self.num_y = tiles_x * mesh_x, tiles_y * mesh_y
        self.tiles_y = tiles_y
        self.joint = EZ % (2 * mesh_x * mesh_y) == 0
        self.axis = ("ex", "ey") if self.joint else "ey"
        self.slabs = mesh_x * mesh_y if self.joint else mesh_y
        self.depth = EZ // self.slabs
        self.width = self.num_x * self.num_y * self.depth
        self.step_y = self.depth
        self.step_x = self.depth * self.num_y
        self.order = self._order()
        self.slab_of = np.argsort(self.order)

    def _order(self):
        snake = []
        if self.joint and self.mesh_x % 2 == 0 and self.mesh_y % 2 == 0:
            cols = [(x, y) for x in range(self.mesh_x // 2) for y in ((0, 1) if x % 2 == 0 else (1, 0))]
            high = self.mesh_y // 2
            for n, (x, y) in enumerate(cols):
                for z in range(high) if n % 2 == 0 else range(high - 1, -1, -1):
                    for core in range(2):
                        snake.append((x * 2 + core) * self.mesh_y + z * 2 + y)
        elif not self.joint and self.mesh_y % 8 == 0:
            for n in range(self.mesh_y // 8):
                row = list(range(8 * n, 8 * n + 8))
                snake += row if n % 2 == 0 else row[::-1]
        else:
            snake = list(range(self.slabs))
        return np.array(snake)

    def swaps(self, first):
        pairs = []
        for s in range(first, self.slabs - 1, 2):
            a, b = int(self.order[s]), int(self.order[s + 1])
            pairs += [(a, b), (b, a)]
        return pairs

    def pack_matrices(self):
        rows = self.slabs * self.tiles_y * self.depth
        lanes = self.tiles_y * EZ
        out = np.zeros((3, rows, lanes))
        for d in range(self.slabs):
            slab = int(self.slab_of[d])
            for e2 in range(self.tiles_y):
                for e3 in range(self.depth):
                    row = (d * self.tiles_y + e2) * self.depth + e3
                    z = slab * self.depth + e3
                    out[0, row, e2 * EZ + z] = 1
                    if e3 == 0 and z > 0:
                        out[1, row, e2 * EZ + z - 1] = 1
                    if e3 == self.depth - 1 and z < EZ - 1:
                        out[2, row, e2 * EZ + z + 1] = 1
        return out


def split(x):
    high = x.astype(BF16)
    return high, (x - high.astype(F32)).astype(BF16)


def times3(high, low, x):
    xh, xl = split(x)
    dot = functools.partial(jnp.dot, preferred_element_type=F32)
    return dot(high, xh) + dot(high, xl) + dot(low, xh)


def dot_exact(a, b, dims):
    return lax.dot_general(a, b, (dims, ((), ())), precision=HIGHEST, preferred_element_type=F32)


def roll(x, shift, axis):
    size = x.shape[axis]
    return pltpu.roll(x, shift % size, axis)


def lane_parts(lay, shape):
    lane = lax.broadcasted_iota(jnp.int32, shape, len(shape) - 1)
    part_z = lane & (lay.depth - 1)
    part_y = lax.shift_right_logical(lane, int(math.log2(lay.step_y))) & (lay.num_y - 1)
    part_x = lax.shift_right_logical(lane, int(math.log2(lay.step_x)))
    return part_x, part_y, part_z


def get_rows(ref, k):
    if ref.shape[1] == 128:
        return ref[pl.ds(k, FACE, stride=N), :]
    return jnp.concatenate([ref[pl.ds(n * N + k, 1), :] for n in range(FACE)], 0)


def set_rows(ref, k, value):
    if ref.shape[1] == 128:
        ref[pl.ds(k, FACE, stride=N), :] = value
    else:
        for n in range(FACE):
            ref[pl.ds(n * N + k, 1), :] = value[n : n + 1]


def assemble(lay, g_ref, s_ref, halo):
    _, _, part_z = lane_parts(lay, halo.shape)
    s_ref[...] = g_ref[...]
    low = get_rows(g_ref, 0)
    high = get_rows(g_ref, N - 1)
    set_rows(s_ref, 0, low + jnp.where(part_z == 0, halo, roll(high, 1, 1)))
    set_rows(s_ref, N - 1, high + jnp.where(part_z == lay.depth - 1, halo, roll(low, -1, 1)))
    last = N - 1
    for j in range(N):
        a, b = pl.ds(j * N, N), pl.ds((last * N + j) * N, N)
        low, high = s_ref[a, :], s_ref[b, :]
        s_ref[a, :] = low + roll(high, lay.step_x, 1)
        s_ref[b, :] = high + roll(low, -lay.step_x, 1)
    for i in range(N):
        a, b = pl.ds(i * N * N, N), pl.ds((i * N + last) * N, N)
        low, high = s_ref[a, :], s_ref[b, :]
        s_ref[a, :] = low + roll(high, lay.step_y, 1)
        s_ref[b, :] = high + roll(low, -lay.step_y, 1)


def store_faces(lay, g_ref, face_ref):
    low = get_rows(g_ref, 0)
    high = get_rows(g_ref, N - 1)
    _, _, part_z = lane_parts(lay, low.shape)
    face_ref[...] = jnp.where(part_z == 0, low, high)


def halo_of(lay, slab_ref, core_ref, chip_ref):
    odd = (slab_ref[0] & 1) == 1
    core, chip = core_ref[...], chip_ref[...]
    below = jnp.where(odd, core, chip)
    above = jnp.where(odd, chip, core)
    _, _, part_z = lane_parts(lay, core.shape)
    return jnp.where(part_z == 0, roll(below, 1 - lay.depth, 1), roll(above, lay.depth - 1, 1))


def pack_kernel(lay, source_ref, perm_ref, points_ref, out_ref):
    nt = ((1,), (1,))
    body = dot_exact(perm_ref[0], source_ref[...], nt)
    below = dot_exact(perm_ref[1], get_rows(source_ref, N - 1), nt)
    above = dot_exact(perm_ref[2], get_rows(source_ref, 0), nt)
    block = lay.tiles_y * lay.depth
    tail = jnp.concatenate([below + above, jnp.broadcast_to(points_ref[...], below.shape)], 1)
    for d in range(lay.slabs):
        part = slice(d * block, (d + 1) * block)
        out_ref[d, :, : N**3] = body[part]
        out_ref[d, :, N**3 :] = tail[part]


def gauss(elem, base, position, half_nodes):
    node = lax.broadcasted_iota(jnp.int32, elem.shape, 0)
    elem = elem.astype(F32)
    away = elem + half_nodes - position
    inside = (
        (elem == base)
        | (elem == base + 1.0)
        | ((elem == base - 1.0) & (node == N - 1))
        | ((elem == base + 2.0) & (node == 0))
    )
    return jnp.where(inside, jnp.exp(-(away * away) / (WIDTH_EPS * WIDTH_EPS)), 0.0)


def right_side(lay, num_points, slab_ref, points_ref, nodes_ref, dcols_ref, g_ref, halo_ref):
    shape = (N, lay.width)
    part_x, part_y, part_z = lane_parts(lay, shape)
    first_z = slab_ref[0] * lay.depth
    elem_z = first_z + part_z
    elem_halo = jnp.where(part_z == 0, first_z - 1, first_z + lay.depth)

    def weighted(elem, base, position):
        plain = nodes_ref[1] * gauss(elem, base, position, nodes_ref[0])
        deriv = dcols_ref[0] * plain[0:1]
        for a in range(1, N):
            deriv = deriv + dcols_ref[a] * plain[a : a + 1]
        return plain, deriv

    def one(p, _):
        base = [points_ref[p, d] for d in range(3)]
        position = [points_ref[p, d] + 1.0 + points_ref[p, 3 + d] for d in range(3)]
        force = [points_ref[p, 6 + d] * (0.25 * GAUSS_NORM) for d in range(3)]
        first = first_z.astype(F32)

        @pl.when((base[2] + 2.0 >= first - 1.0) & (base[2] - 1.0 <= first + lay.depth))
        def _():
            x0, x1 = weighted(part_x, base[0], position[0])
            y0, y1 = weighted(part_y, base[1], position[1])
            z0, z1 = weighted(elem_z, base[2], position[2])
            h0, h1 = weighted(elem_halo, base[2], position[2])
            pick = part_z[0:1] == 0
            h0 = jnp.where(pick, h0[N - 1 : N], h0[0:1])
            h1 = jnp.where(pick, h1[N - 1 : N], h1[0:1])
            x1 = force[0] * x1
            fz1 = force[2] * z1
            fz0 = force[1] * z0
            for j in range(N):
                first_part = y0[j : j + 1] * z0
                other_part = y1[j : j + 1] * fz0 + y0[j : j + 1] * fz1
                for i in range(N):
                    rows = pl.ds((i * N + j) * N, N)
                    g_ref[rows, :] += x1[i : i + 1] * first_part + x0[i : i + 1] * other_part
            first_part = y0 * h0
            other_part = y1 * (force[1] * h0) + y0 * (force[2] * h1)
            for i in range(N):
                rows = pl.ds(i * N, N)
                halo_ref[rows, :] += x1[i : i + 1] * first_part + x0[i : i + 1] * other_part

        return 0

    lax.fori_loop(0, num_points, one, 0)


def inverse_diagonal(lay, slab_ref, factor_ref, dinv_ref):
    shape = (N, lay.width)
    part_x, part_y, part_z = lane_parts(lay, shape)
    part_z = slab_ref[0] * lay.depth + part_z
    node = lax.broadcasted_iota(jnp.int32, shape, 0)

    def share(low, high):
        return (
            jnp.where(low, 0.0, 0.5),
            jnp.where(high, 0.0, 0.5),
        )

    low_z, high_z = share(part_z == 0, part_z == EZ - 1)
    along_z = jnp.where(node == 0, low_z, jnp.where(node == N - 1, high_z, 1.0))
    along_x = dict(zip((0, N - 1), share(part_x == 0, part_x == lay.num_x - 1)))
    along_y = dict(zip((0, N - 1), share(part_y == 0, part_y == lay.num_y - 1)))
    for i in range(N):
        for j in range(N):
            rows = pl.ds((i * N + j) * N, N)
            value = factor_ref[rows, :] * along_z
            if i in along_x:
                value = value * along_x[i]
            if j in along_y:
                value = value * along_y[j]
            dinv_ref[rows, :] = value


def first_kernel(
    lay,
    num_points,
    slab_ref,
    points_ref,
    recv_ref,
    nodes_ref,
    dcols_ref,
    factor_ref,
    high_ref,
    low_ref,
    g_ref,
    x_ref,
    dinv_ref,
    face_ref,
    s_ref,
    halo_ref,
    flat_ref,
):
    count, block = recv_ref.shape[0], recv_ref.shape[1]
    for d in range(count):
        flat_ref[pl.ds(d * block, block), :] = recv_ref[d]
    g_ref[...] = flat_ref[:, : N**3].T
    halo_ref[...] = flat_ref[:, N**3 :].T[:FACE]
    inverse_diagonal(lay, slab_ref, factor_ref, dinv_ref)
    right_side(lay, num_points, slab_ref, points_ref, nodes_ref, dcols_ref, g_ref, halo_ref)
    assemble(lay, g_ref, s_ref, halo_ref[...])
    update = (1.0 / THETA) * dinv_ref[...] * s_ref[...]
    x_ref[...] = update
    g_ref[...] = g_ref[...] - times3(high_ref[...], low_ref[...], update)
    store_faces(lay, g_ref, face_ref)


def step_kernel(
    lay,
    coef_old,
    coef_new,
    kind,
    slab_ref,
    core_ref,
    chip_ref,
    g_ref,
    x_ref,
    *refs,
):
    refs = list(refs)
    u_ref = refs.pop(0) if coef_old else None
    dinv_ref = refs.pop(0)
    if kind != "last":
        high_ref, low_ref = refs.pop(0), refs.pop(0)
    if kind == "restrict":
        interp_ref = refs.pop(0)
    if kind == "last":
        out_ref, s_ref = refs
    elif kind == "restrict":
        g_out, x_out, send_ref, s_ref = refs
    else:
        g_out, x_out, u_out, face_ref, s_ref = refs
    assemble(lay, g_ref, s_ref, halo_of(lay, slab_ref, core_ref, chip_ref))
    update = coef_new * dinv_ref[...] * s_ref[...]
    if coef_old:
        update = update + coef_old * u_ref[...]
    if kind == "last":
        total = (x_ref[...] + update).T
        count, block = out_ref.shape[0], out_ref.shape[1]
        for d in range(count):
            out_ref[d] = total[d * block : (d + 1) * block]
        return
    x_out[...] = x_ref[...] + update
    g_out[...] = g_ref[...] - times3(high_ref[...], low_ref[...], update)
    if kind == "restrict":
        inner = jnp.where(dinv_ref[...] != 0.0, g_out[...], 0.0)
        load = dot_exact(interp_ref[...], inner, ((0,), (0,)))
        rows = [load[n : n + 1] for n in range(N)]
        rows = [rows[n] + roll(rows[4 + n], lay.step_x, 1) for n in range(4)]
        rows = [rows[n] + roll(rows[2 + n], lay.step_y, 1) for n in range(2)]
        for d in range(send_ref.shape[0]):
            send_ref[d, 0:1] = rows[0]
            send_ref[d, 1:2] = rows[1]
    else:
        u_out[...] = update
        store_faces(lay, g_out, face_ref)


def coarse_kernel(
    lay,
    mass,
    stiff,
    slab_ref,
    loads_ref,
    g_ref,
    x_ref,
    interp_ref,
    image_ref,
    g_out,
    x_out,
    face_ref,
    first_ref,
    second_ref,
):
    for s in range(lay.slabs):
        d = int(lay.order[s])
        first_ref[pl.ds(s, 1), :] = loads_ref[d, 0:1]
        second_ref[pl.ds(s, 1), :] = loads_ref[d, 1:2]
    shape = (lay.slabs, lay.width)
    part_x, part_y, part_z = lane_parts(lay, shape)
    row = lax.broadcasted_iota(jnp.int32, shape, 0)
    keep = ((part_x > 0) & (part_y > 0) & ((part_z > 0) | (row > 0))).astype(F32)
    bottom, top = part_z == 0, part_z == lay.depth - 1

    def below(v):
        return jnp.where(bottom, roll(roll(v, 1, 0), 1 - lay.depth, 1), roll(v, 1, 1))

    def above(v):
        return jnp.where(top, roll(roll(v, -1, 0), lay.depth - 1, 1), roll(v, -1, 1))

    def neighbours(v, step):
        return roll(v, step, 1) + roll(v, -step, 1)

    def mix(pair, v, around):
        return (2.0 * pair[0]) * v + pair[1] * around

    def operate(v):
        around = below(v) + above(v)
        mass_z, stiff_z = mix(mass, v, around), mix(stiff, v, around)
        around = neighbours(mass_z, lay.step_y)
        both = mix(mass, mass_z, around)
        rest = mix(stiff, mass_z, around) + mix(mass, stiff_z, neighbours(stiff_z, lay.step_y))
        out = mix(stiff, both, neighbours(both, lay.step_x)) + mix(
            mass, rest, neighbours(rest, lay.step_x)
        )
        return (0.5 * keep) * out

    def inner(a, b):
        return jnp.sum(jnp.sum(a * b, axis=1, keepdims=True), axis=0, keepdims=True)

    residual = keep * (first_ref[...] + below(second_ref[...]))
    direction = residual
    total = jnp.zeros(shape, F32)
    norm = inner(residual, residual)
    for step in range(CG_STEPS):
        image = operate(direction)
        alpha = norm / inner(direction, image)
        total = total + alpha * direction
        if step + 1 < CG_STEPS:
            residual = residual - alpha * image
            following = inner(residual, residual)
            direction = residual + (following / norm) * direction
            norm = following
    first_ref[...] = total
    second_ref[...] = above(total)
    mine = pl.ds(slab_ref[0], 1)
    rows = [first_ref[mine, :], second_ref[mine, :]]
    rows = rows + [roll(r, -lay.step_y, 1) for r in rows]
    rows = rows + [roll(r, -lay.step_x, 1) for r in rows]
    corner = lax.broadcasted_iota(jnp.int32, (N, lay.width), 0)
    local = jnp.broadcast_to(rows[0], (N, lay.width))
    for n in range(1, N):
        local = jnp.where(corner == n, rows[n], local)
    plain = ((1,), (0,))
    x_out[...] = x_ref[...] + dot_exact(interp_ref[...], local, plain)
    g_out[...] = g_ref[...] - dot_exact(image_ref[...], local, plain)
    store_faces(lay, g_out, face_ref)


def unpack_kernel(recv_ref, perm_ref, out_ref, flat_ref):
    count, block = recv_ref.shape[0], recv_ref.shape[1]
    for d in range(count):
        flat_ref[pl.ds(d * block, block), :] = recv_ref[d]
    out_ref[...] = dot_exact(flat_ref[...], perm_ref[0], ((0,), (0,)))


def forces_kernel(tiles_y, num_points, place_ref, points_ref, nodes_ref, out_ref):
    width = tiles_y * EZ
    shape = (N, width)
    lane = lax.broadcasted_iota(jnp.int32, shape, 1)
    first_x, first_y = place_ref[0], place_ref[1]
    elem_x = jnp.broadcast_to(first_x, shape)
    elem_y = first_y + lax.shift_right_logical(lane, int(math.log2(EZ)))
    elem_z = lane & (EZ - 1)
    out_ref[...] = jnp.zeros(out_ref.shape, F32)

    def one(p, _):
        base = [points_ref[p, d] for d in range(3)]
        position = [points_ref[p, d] + 1.0 + points_ref[p, 3 + d] for d in range(3)]
        force = [points_ref[p, 6 + d] * GAUSS_NORM for d in range(3)]
        low_x, low_y = first_x.astype(F32), first_y.astype(F32)

        @pl.when(
            (base[0] + 2.0 >= low_x)
            & (base[0] - 1.0 <= low_x)
            & (base[1] + 2.0 >= low_y)
            & (base[1] - 1.0 <= low_y + (tiles_y - 1))
        )
        def _():
            x = gauss(elem_x, base[0], position[0], nodes_ref[0])
            y = gauss(elem_y, base[1], position[1], nodes_ref[0])
            z = gauss(elem_z, base[2], position[2], nodes_ref[0])
            for j in range(N):
                plane = y[j : j + 1] * z
                for i in range(N):
                    value = x[i : i + 1] * plane
                    rows = pl.ds((i * N + j) * N, N)
                    for c in range(3):
                        out_ref[c, rows, :] += force[c] * value

        return 0

    lax.fori_loop(0, num_points, one, 0)


def call(kernel, outs, inputs, scratch=(), smem=0):
    specs = [
        pl.BlockSpec(memory_space=pltpu.SMEM if n < smem else pltpu.VMEM) for n in range(len(inputs))
    ]
    shapes = [jax.ShapeDtypeStruct(s, F32) for s in outs]
    result = pl.pallas_call(
        kernel,
        out_shape=shapes,
        in_specs=specs,
        out_specs=[pl.BlockSpec(memory_space=pltpu.VMEM)] * len(shapes),
        scratch_shapes=[pltpu.VMEM(s, F32) for s in scratch],
        compiler_params=pltpu.CompilerParams(vmem_limit_bytes=40 * 1024 * 1024),
    )(*inputs)
    return result


def shards(source, point_base, point_offset, point_force):
    tiles_x, tiles_y = source.shape[3], source.shape[4] // EZ
    lay = Layout(lax.axis_size("ex"), lax.axis_size("ey"), tiles_x, tiles_y)
    devices = lay.mesh_x * lay.mesh_y
    derivative, weights, interp, stiff_one = build_tables()
    width, fields = lay.width, (N**3, lay.width)

    diag_w = np.diag(weights)
    full = 0.5 * (
        kron3(stiff_one, diag_w, diag_w)
        + kron3(diag_w, stiff_one, diag_w)
        + kron3(diag_w, diag_w, stiff_one)
    )
    full_high = full.astype(BF16)
    full_low = (full - full_high.astype(np.float64)).astype(BF16)
    interp3 = kron3(interp, interp, interp)
    image3 = full @ interp3
    ratio = (weights[:, None] * derivative**2).sum(axis=0) / weights
    diag = 0.5 * (ratio[:, None, None] + ratio[None, :, None] + ratio[None, None, :])
    diag = diag * weights[:, None, None] * weights[None, :, None] * weights[None, None, :]
    factor = np.broadcast_to(1.0 / diag.reshape(N**3, 1), fields)
    nodes = np.stack([0.5 * (1.0 + GLL_POINTS), weights])
    nodes_wide = np.broadcast_to(nodes[:, :, None], (2, N, width))
    nodes_local = np.broadcast_to(nodes[:, :, None], (2, N, tiles_y * EZ))
    dcols = np.broadcast_to(derivative[:, :, None], (N, N, width))
    mass = interp.T @ diag_w @ interp
    stiff = interp.T @ stiff_one @ interp
    perms = jnp.asarray(lay.pack_matrices(), F32)
    high, low = jnp.asarray(full_high), jnp.asarray(full_low)
    interp3, image3 = jnp.asarray(interp3, F32), jnp.asarray(image3, F32)
    factor, nodes_wide, nodes_local, dcols = (
        jnp.asarray(t, F32) for t in (factor, nodes_wide, nodes_local, dcols)
    )

    slab = jnp.asarray(lay.slab_of, jnp.int32)[lax.axis_index(lay.axis)].reshape(1)
    place = jnp.stack([lax.axis_index("ex") * tiles_x, lax.axis_index("ey") * tiles_y]).astype(
        jnp.int32
    )

    local_points = point_base.shape[1]
    packed = jnp.concatenate([point_base.astype(F32), point_offset, point_force], 0)
    packed = packed.T.reshape(1, local_points * 9)
    packed = jnp.pad(packed, ((0, 0), (0, PAD - FACE - packed.shape[1])))
    block = lay.tiles_y * lay.depth
    (send,) = call(
        functools.partial(pack_kernel, lay),
        [(lay.slabs, block, N**3 + PAD)],
        [source.reshape(N**3, tiles_y * EZ), perms, packed],
    )
    recv = lax.all_to_all(send, lay.axis, 0, 0)
    if not lay.joint:
        recv = lax.all_gather(recv, "ex", axis=0, tiled=True)
    points = recv[:, 0, N**3 + FACE : N**3 + FACE + 9 * local_points]
    points = points.reshape(devices * local_points, 9)
    num_points = devices * local_points

    (forces,) = call(
        functools.partial(forces_kernel, tiles_y, num_points),
        [(3, N**3, tiles_y * EZ)],
        [place, points, nodes_local],
        smem=2,
    )

    def swap(face):
        return (
            lax.ppermute(face, lay.axis, lay.swaps(0)),
            lax.ppermute(face, lay.axis, lay.swaps(1)),
        )

    face_shape = (FACE, width)
    g, x, dinv, face = call(
        functools.partial(first_kernel, lay, num_points),
        [fields, fields, fields, face_shape],
        [slab, points, recv, nodes_wide, dcols, factor, high, low],
        [fields, face_shape, (width, N**3 + PAD)],
        smem=2,
    )
    u = x
    first = (0.0, 1.0 / THETA)
    second = (RHO_SECOND * RHO_FIRST, 2.0 * RHO_SECOND / DELTA)

    def step(coefs, kind, face, g, x, u):
        inputs = [slab, *swap(face), g, x]
        if coefs[0]:
            inputs.append(u)
        inputs.append(dinv)
        if kind != "last":
            inputs += [high, low]
        if kind == "restrict":
            inputs.append(interp3)
            outs = [fields, fields, (lay.slabs, 2, width)]
        elif kind == "last":
            outs = [(lay.mesh_x * lay.mesh_y, block, N**3)]
        else:
            outs = [fields, fields, fields, face_shape]
        return call(
            functools.partial(step_kernel, lay, *coefs, kind), outs, inputs, [fields], smem=1
        )

    for cycle in range(CYCLES):
        if cycle > 0:
            g, x, u, face = step(first, "plain", face, g, x, u)
        g, x, loads = step(second, "restrict", face, g, x, u)
        loads = lax.all_to_all(loads, lay.axis, 0, 0)
        g, x, face = call(
            functools.partial(coarse_kernel, lay, (mass[0, 0], mass[0, 1]), (stiff[0, 0], stiff[0, 1])),
            [fields, fields, face_shape],
            [slab, loads, g, x, interp3, image3],
            [(lay.slabs, width)] * 2,
            smem=1,
        )
        g, x, u, face = step(first, "plain", face, g, x, u)
        if cycle + 1 < CYCLES:
            g, x, u, face = step(second, "plain", face, g, x, u)
    (out,) = step(second, "last", face, g, x, u)
    if not lay.joint:
        out = lax.dynamic_slice_in_dim(out, lax.axis_index("ex") * lay.mesh_y, lay.mesh_y, 0)
    out = lax.all_to_all(out, lay.axis, 0, 0)
    (pressure,) = call(
        unpack_kernel,
        [(N**3, tiles_y * EZ)],
        [out, perms],
        [(lay.slabs * block, N**3)],
    )
    return (
        pressure.reshape(source.shape),
        forces.reshape((3, *source.shape)),
    )


def solution(mesh):
    in_specs = (
        P(None, None, None, "ex", "ey"),
        P(None, ("ex", "ey")),
        P(None, ("ex", "ey")),
        P(None, ("ex", "ey")),
    )
    out_specs = (P(None, None, None, "ex", "ey"), P(None, None, None, None, "ex", "ey"))
    return jax.shard_map(shards, mesh=mesh, in_specs=in_specs, out_specs=out_specs, check_vma=False)
```

time: 1330 us -> 113 us (0.08); the launches traced: 1310 us -> 113 us
  blocking collectives: 639 us -> 20.9 us
  local copies, waits for them, and re-layouts: 201 us -> 2.66 us
  starting transfers between devices: 228 us -> 35.7 us
  other arithmetic: 98.8 us -> 0.82 us
  waiting for transfers between devices: 72.5 us -> 25.2 us
  matrix products: 41.1 us -> 0 us
  Pallas kernels: 0 us -> 26.6 us
  between operations: 24.6 us -> 0.86 us
    psum x14 -> x0, blocking collectives: 572 us -> none  [the longest x8 327 us: norm_spread(): return lax.psum(value, ('ex', 'ey'))]
    ppermute x88 -> x14, starting transfers between devices: 228 us -> 25.6 us  [the longest x7 20.9 us: swap(): lax.ppermute(face, lay.axis, lay.swaps(0))]
    concatenate x142 -> x0, local copies, waits for them, and re-layouts: 84.2 us -> none  [assemble_side(): jnp.concatenate([jnp.expand_dims(lower_face + from_below, node_dim), midd...]
    all_gather x1 -> x0, blocking collectives: 67.4 us -> none  [shards(): piece = lax.all_gather(packed, ('ex', 'ey'), axis=1, tiled=True)]
    ppermute x88 -> x14, waiting for transfers between devices: 72.5 us -> 6.02 us  [the longest x7 6 us: swap(): lax.ppermute(face, lay.axis, lay.swaps(0))]
    slice x118 -> x1, local copies, waits for them, and re-layouts: 48.9 us -> 0.09 us  [shards(): points = recv[:, 0, N ** 3 + FACE:N ** 3 + FACE + 9 * local_points]]
    dot_general x81 -> x0, matrix products: 41.1 us -> none  [the longest x6 6.07 us: prolong(): jnp.einsum('ia,jb,kc,abclm->ijklm', interp, interp, interp, vertex_vals,...]
    concatenate x80 -> x0, other arithmetic: 34.4 us -> none  [the longest x44 25.8 us: padded(): jnp.concatenate([lax.ppermute(tail, axis, [(i, (i + 1) % count) for i in...]
  transfers between devices with their start and end apart: 88 -> 16, of which waited for: 28 -> 9; matrix products, arithmetic and copies ran while one was open for 9% -> 1% of each run, Pallas kernels for 0% -> 3%
where the time goes in v1:
time: 113 us
  starting transfers between devices  35.7 us (32%)
  Pallas kernels  26.6 us (24%)
  waiting for transfers between devices  25.2 us (22%)
  blocking collectives  20.9 us (18%)
  local copies, waits for them, and re-layouts  2.66 us (2%)
    pallas_call x13, Pallas kernels, call(): pl.pallas_call(kernel, out_shape=shapes, in_specs=specs, out_specs=[pl.Bl...  26.6 us
    ppermute x7, starting transfers between devices, swap(): lax.ppermute(face, lay.axis, lay.swaps(0))  20.9 us
    all_to_all x2, blocking collectives, shards(): loads = lax.all_to_all(loads, lay.axis, 0, 0)  20.9 us
    all_to_all x1, waiting for transfers between devices, shards(): recv = lax.all_to_all(send, lay.axis, 0, 0)  11.5 us
    all_to_all x1, waiting for transfers between devices, shards(): out = lax.all_to_all(out, lay.axis, 0, 0)  7.71 us
    all_to_all x1, starting transfers between devices, shards(): recv = lax.all_to_all(send, lay.axis, 0, 0)  7.3 us
    ppermute x7, waiting for transfers between devices, swap(): lax.ppermute(face, lay.axis, lay.swaps(0))  6 us
    ppermute x7, starting transfers between devices, swap(): lax.ppermute(face, lay.axis, lay.swaps(1))  4.63 us
  transfers between devices with their start and end apart: 16, of which 9 were waited for; matrix products, arithmetic and copies ran while one was open for 1% of the time, Pallas kernels for 3%

profile of v1, /device:TPU:0, one launch (start us, length us, event | category | flops | bytes accessed | tf_op | source)
XLA Modules:
  0.0 112.8 jit_solution(9000351417031851501)
XLA Ops:
  1.4 0.9 copy-done.4
  2.3 0.9 copy-done.7
  3.3 1.2 %shard_map.149 = f32[32,4,640]{2,1,0:T(4,128)} custom-call(f32[512,128]{1,0:T(8,128)S(1)} %bitcast.14, f32[3,128,128]{2,1,0:T(8,128)S(1)} %copy-done.4, f32[1,64]{1,0:T(1,128)S(1)} %pad.4.points_ref), custom_call_target="tpu_custom_call" | custom-call | tf_op jit(solution)/shard_map/pallas_call | solution.py:522
  4.5 7.3 %all-to-all-start = ((f32[32,4,640]{2,1,0:T(4,128)}), f32[32,4,640]{2,1,0:T(4,128)S(1)}, u32[]{:S(2)}, u32[]{:S(2)}) async-start(f32[32,4,640]{2,1,0:T(4,128)} %shard_map.149), calls=%async_computation | async-start | bytes 655360 | tf_op jit(solution)/shard_map/all_to_all | solution.py:582
  12.5 11.5 %all-to-all-done.recv_ref = f32[32,4,640]{2,1,0:T(4,128)S(1)} async-done(((f32[32,4,640]{2,1,0:T(4,128)}), f32[32,4,640]{2,1,0:T(4,128)S(1)}, u32[]{:S(2)}, u32[]{:S(2)}) %all-to-all-start) | async-done | bytes 327712 | tf_op jit(solution)/shard_map/all_to_all | solution.py:582
  24.1 3.1 %shard_map.150 = (f32[512,128]{1,0:T(8,128)S(1)}, f32[512,128]{1,0:T(8,128)S(1)}, f32[512,128]{1,0:T(8,128)S(1)}, f32[64,128]{1,0:T(8,128)S(1)}) custom-call(s32[1]{0:T(128)} %dynamic_slice.3.slab_ref, f32[32,9]{1,0:T(8,128)S(1)} %bitcast.15, f32[32,4,640]{2,1,0:T(4,128)S(1)} %all-to-all-done.recv_ref, f32[2,8,128]{2,1,0:T(8,128)S(1)} %copy-done.8, ...), custom_call_target="tpu_custom_call" | custom-call | tf_op jit(solution)/shard_map/pallas_call | solution.py:522
  27.9 2.2 %collective-permute-start = (f32[64,128]{1,0:T(8,128)S(1)}, f32[64,128]{1,0:T(8,128)S(1)}, u32[]{:S(2)}, u32[]{:S(2)}) collective-permute-start(f32[64,128]{1,0:T(8,128)S(1)} %get-tuple-element.33), channel_id=1, source_target_pairs={{0,8},{8,0},{2,10},{10,2},{4,12},{12,4},{6,14},{14,6},{7,15},{15,7... | collective-permute-start | bytes 98312 | tf_op jit(solution)/shard_map/ppermute | solution.py:598
  30.2 0.9 collective-permute-done.core_ref
  31.0 2.0 %shard_map.151 = (f32[512,128]{1,0:T(8,128)S(1)}, f32[512,128]{1,0:T(8,128)S(1)}, f32[32,2,128]{2,1,0:T(2,128)S(1)}) custom-call(s32[1]{0:T(128)} %dynamic_slice.3.slab_ref, f32[64,128]{1,0:T(8,128)S(1)} %collective-permute-done.core_ref, f32[64,128]{1,0:T(8,128)S(1)} %collective-permute-done.1.chip_ref, f32[512,128]{1,0:T(8,128)S(1)} %get-tuple-element.34.g_ref, ...), custom_call_target="tpu_custom_call" | custom-call | tf_op jit(solution)/shard_map/pallas_call | solution.py:522
  33.0 11.0 %all_to_all.20.loads_ref = f32[32,2,128]{2,1,0:T(2,128)S(1)} all-to-all(f32[32,2,128]{2,1,0:T(2,128)S(1)} %get-tuple-element.37), channel_id=1, replica_groups=mesh['ex'=4,'ey'=8] {'ex','ey'}, dimensions={0} | all-to-all | bytes 65536 | tf_op jit(solution)/shard_map/all_to_all | solution.py:636
  44.1 3.1 %shard_map.152 = (f32[512,128]{1,0:T(8,128)S(1)}, f32[512,128]{1,0:T(8,128)S(1)}, f32[64,128]{1,0:T(8,128)S(1)}) custom-call(s32[1]{0:T(128)} %dynamic_slice.3.slab_ref, f32[32,2,128]{2,1,0:T(2,128)S(1)} %all_to_all.20.loads_ref, f32[512,128]{1,0:T(8,128)S(1)} %get-tuple-element.38.g_ref, f32[512,128]{1,0:T(8,128)S(1)} %get-tuple-element.39.x_ref, ...), custom_call_target="tpu_custom_call" | custom-call | tf_op jit(solution)/shard_map/pallas_call | solution.py:522
  47.9 1.9 %collective-permute-start.2 = (f32[64,128]{1,0:T(8,128)S(1)}, f32[64,128]{1,0:T(8,128)S(1)}, u32[]{:S(2)}, u32[]{:S(2)}) collective-permute-start(f32[64,128]{1,0:T(8,128)S(1)} %get-tuple-element.40), channel_id=1, source_target_pairs={{0,8},{8,0},{2,10},{10,2},{4,12},{12,4},{6,14},{14,6},{7,15},{15,7... | collective-permute-start | bytes 98312 | tf_op jit(solution)/shard_map/ppermute | solution.py:598
  49.8 0.9 collective-permute-done.2.core_ref
  50.6 1.5 %shard_map.153 = (f32[512,128]{1,0:T(8,128)S(1)}, f32[512,128]{1,0:T(8,128)S(1)}, f32[512,128]{1,0:T(8,128)S(1)}, f32[64,128]{1,0:T(8,128)S(1)}) custom-call(s32[1]{0:T(128)} %dynamic_slice.3.slab_ref, f32[64,128]{1,0:T(8,128)S(1)} %collective-permute-done.2.core_ref, f32[64,128]{1,0:T(8,128)S(1)} %collective-permute-done.3.chip_ref, ...), custom_call_target="tpu_custom_call" | custom-call | tf_op jit(solution)/shard_map/pallas_call | solution.py:522
  52.8 3.7 %collective-permute-start.4 = (f32[64,128]{1,0:T(8,128)S(1)}, f32[64,128]{1,0:T(8,128)S(1)}, u32[]{:S(2)}, u32[]{:S(2)}) collective-permute-start(f32[64,128]{1,0:T(8,128)S(1)} %get-tuple-element.43), channel_id=1, source_target_pairs={{0,8},{8,0},{2,10},{10,2},{4,12},{12,4},{6,14},{14,6},{7,15},{15,7... | collective-permute-start | bytes 98312 | tf_op jit(solution)/shard_map/ppermute | solution.py:598
  56.5 0.9 collective-permute-done.4.core_ref
  57.4 2.0 %shard_map.154 = (f32[512,128]{1,0:T(8,128)S(1)}, f32[512,128]{1,0:T(8,128)S(1)}, f32[512,128]{1,0:T(8,128)}, f32[64,128]{1,0:T(8,128)S(1)}) custom-call(s32[1]{0:T(128)} %dynamic_slice.3.slab_ref, f32[64,128]{1,0:T(8,128)S(1)} %collective-permute-done.4.core_ref, f32[64,128]{1,0:T(8,128)S(1)} %collective-permute-done.5.chip_ref, ...), custom_call_target="tpu_custom_call" | custom-call | tf_op jit(solution)/shard_map/pallas_call | solution.py:522
  60.0 3.7 %collective-permute-start.6 = (f32[64,128]{1,0:T(8,128)S(1)}, f32[64,128]{1,0:T(8,128)S(1)}, u32[]{:S(2)}, u32[]{:S(2)}) collective-permute-start(f32[64,128]{1,0:T(8,128)S(1)} %get-tuple-element.47), channel_id=1, source_target_pairs={{0,8},{8,0},{2,10},{10,2},{4,12},{12,4},{6,14},{14,6},{7,15},{15,7... | collective-permute-start | bytes 98312 | tf_op jit(solution)/shard_map/ppermute | solution.py:598
  63.7 0.9 collective-permute-done.6.core_ref
  64.6 1.5 %shard_map.155 = (f32[512,128]{1,0:T(8,128)S(1)}, f32[512,128]{1,0:T(8,128)S(1)}, f32[512,128]{1,0:T(8,128)S(1)}, f32[64,128]{1,0:T(8,128)S(1)}) custom-call(s32[1]{0:T(128)} %dynamic_slice.3.slab_ref, f32[64,128]{1,0:T(8,128)S(1)} %collective-permute-done.6.core_ref, f32[64,128]{1,0:T(8,128)S(1)} %collective-permute-done.7.chip_ref, ...), custom_call_target="tpu_custom_call" | custom-call | tf_op jit(solution)/shard_map/pallas_call | solution.py:522
  66.7 3.7 %collective-permute-start.8 = (f32[64,128]{1,0:T(8,128)S(1)}, f32[64,128]{1,0:T(8,128)S(1)}, u32[]{:S(2)}, u32[]{:S(2)}) collective-permute-start(f32[64,128]{1,0:T(8,128)S(1)} %get-tuple-element.50), channel_id=1, source_target_pairs={{0,8},{8,0},{2,10},{10,2},{4,12},{12,4},{6,14},{14,6},{7,15},{15,7... | collective-permute-start | bytes 98312 | tf_op jit(solution)/shard_map/ppermute | solution.py:598
  71.3 1.9 %shard_map.156 = (f32[512,128]{1,0:T(8,128)S(1)}, f32[512,128]{1,0:T(8,128)S(1)}, f32[32,2,128]{2,1,0:T(2,128)S(1)}) custom-call(s32[1]{0:T(128)} %dynamic_slice.3.slab_ref, f32[64,128]{1,0:T(8,128)S(1)} %collective-permute-done.8.core_ref, f32[64,128]{1,0:T(8,128)S(1)} %collective-permute-done.9.chip_ref, f32[512,128]{1,0:T(8,128)S(1)} %get-tuple-element.51.g_ref, ...), custom_call_target="tpu_custom_call" | custom-call | tf_op jit(solution)/shard_map/pallas_call | solution.py:522
  73.3 9.9 %all_to_all.21.loads_ref = f32[32,2,128]{2,1,0:T(2,128)S(1)} all-to-all(f32[32,2,128]{2,1,0:T(2,128)S(1)} %get-tuple-element.54), channel_id=1, replica_groups=mesh['ex'=4,'ey'=8] {'ex','ey'}, dimensions={0} | all-to-all | bytes 65536 | tf_op jit(solution)/shard_map/all_to_all | solution.py:636
  83.1 3.1 %shard_map.157 = (f32[512,128]{1,0:T(8,128)S(1)}, f32[512,128]{1,0:T(8,128)S(1)}, f32[64,128]{1,0:T(8,128)S(1)}) custom-call(s32[1]{0:T(128)} %dynamic_slice.3.slab_ref, f32[32,2,128]{2,1,0:T(2,128)S(1)} %all_to_all.21.loads_ref, f32[512,128]{1,0:T(8,128)S(1)} %get-tuple-element.55.g_ref, f32[512,128]{1,0:T(8,128)S(1)} %get-tuple-element.56.x_ref, ...), custom_call_target="tpu_custom_call" | custom-call | tf_op jit(solution)/shard_map/pallas_call | solution.py:522
  86.9 1.9 %collective-permute-start.10 = (f32[64,128]{1,0:T(8,128)S(1)}, f32[64,128]{1,0:T(8,128)S(1)}, u32[]{:S(2)}, u32[]{:S(2)}) collective-permute-start(f32[64,128]{1,0:T(8,128)S(1)} %get-tuple-element.57), channel_id=1, source_target_pairs={{0,8},{8,0},{2,10},{10,2},{4,12},{12,4},{6,14},{14,6},{7,15},{15,7... | collective-permute-start | bytes 98312 | tf_op jit(solution)/shard_map/ppermute | solution.py:598
  89.7 1.5 %shard_map.158 = (f32[512,128]{1,0:T(8,128)S(1)}, f32[512,128]{1,0:T(8,128)S(1)}, f32[512,128]{1,0:T(8,128)S(1)}, f32[64,128]{1,0:T(8,128)S(1)}) custom-call(s32[1]{0:T(128)} %dynamic_slice.3.slab_ref, f32[64,128]{1,0:T(8,128)S(1)} %collective-permute-done.10.core_ref, f32[64,128]{1,0:T(8,128)S(1)} %collective-permute-done.11.chip_ref, ...), custom_call_target="tpu_custom_call" | custom-call | tf_op jit(solution)/shard_map/pallas_call | solution.py:522
  91.8 3.7 %collective-permute-start.12 = (f32[64,128]{1,0:T(8,128)S(1)}, f32[64,128]{1,0:T(8,128)S(1)}, u32[]{:S(2)}, u32[]{:S(2)}) collective-permute-start(f32[64,128]{1,0:T(8,128)S(1)} %get-tuple-element.60), channel_id=1, source_target_pairs={{0,8},{8,0},{2,10},{10,2},{4,12},{12,4},{6,14},{14,6},{7,15},{15,7... | collective-permute-start | bytes 98312 | tf_op jit(solution)/shard_map/ppermute | solution.py:598
  96.4 1.7 %shard_map.159 = f32[32,4,512]{2,1,0:T(4,128)} custom-call(s32[1]{0:T(128)} %dynamic_slice.3.slab_ref, f32[64,128]{1,0:T(8,128)S(1)} %collective-permute-done.12.core_ref, f32[64,128]{1,0:T(8,128)S(1)} %collective-permute-done.13.chip_ref, f32[512,128]{1,0:T(8,128)S(1)} %get-tuple-element.61.g_ref, f32[512,128]{1,0:T(8,128)S(1)} %get-tuple-element.62.x_ref, ...), custom_call_target="tpu_custom_call" | custom-call | tf_op jit(solution)/shard_map/pallas_call | solution.py:522
  98.1 2.9 %all-to-all-start.3 = ((f32[32,4,512]{2,1,0:T(4,128)}), f32[32,4,512]{2,1,0:T(4,128)S(1)}, u32[]{:S(2)}, u32[]{:S(2)}) async-start(f32[32,4,512]{2,1,0:T(4,128)} %shard_map.159), calls=%async_computation.3 | async-start | bytes 524288 | tf_op jit(solution)/shard_map/all_to_all | solution.py:650
  101.1 2.9 %shard_map.161 = f32[3,512,128]{2,1,0:T(8,128)} custom-call(s32[2]{0:T(128)S(1)} %pad_add_fusion.place_ref, f32[32,9]{1,0:T(8,128)S(1)} %bitcast.16, f32[2,8,128]{2,1,0:T(8,128)S(1)} %copy-done.8), custom_call_target="tpu_custom_call" | custom-call | tf_op jit(solution)/shard_map/pallas_call | solution.py:522
  103.9 7.7 %all-to-all-done.3.recv_ref = f32[32,4,512]{2,1,0:T(4,128)S(1)} async-done(((f32[32,4,512]{2,1,0:T(4,128)}), f32[32,4,512]{2,1,0:T(4,128)S(1)}, u32[]{:S(2)}, u32[]{:S(2)}) %all-to-all-start.3) | async-done | bytes 262176 | tf_op jit(solution)/shard_map/all_to_all | solution.py:650
  111.6 1.1 %shard_map.160 = f32[512,128]{1,0:T(8,128)} custom-call(f32[32,4,512]{2,1,0:T(4,128)S(1)} %all-to-all-done.3.recv_ref, f32[3,128,128]{2,1,0:T(8,128)S(1)} %copy-done.5), custom_call_target="tpu_custom_call" | custom-call | tf_op jit(solution)/shard_map/pallas_call | solution.py:522
  (47 shorter events, 8.8 us)
Async XLA Ops:
  0.6 0.7 copy-start.10
  0.6 0.7 copy-start.11
  1.4 0.9 copy-start.4
  2.3 0.9 copy-start.7
  3.3 20.8 %copy-start.1 = (bf16[512,512]{1,0:T(8,128)(2,1)S(1)}, bf16[512,512]{1,0:T(8,128)(2,1)}, u32[]{:S(2)}) copy-start(bf16[512,512]{1,0:T(8,128)(2,1)} %constant.37.clone.high_ref.refs_2_.refs_1_) | copy-start | bytes 1572868
  3.3 20.8 %copy-start.6 = (f32[512,128]{1,0:T(8,128)S(1)}, f32[512,128]{1,0:T(8,128)}, u32[]{:S(2)}) copy-start(f32[512,128]{1,0:T(8,128)} %constant.41.clone.factor_ref) | copy-start | bytes 786436
  4.5 7.3 %copy-start.12 = (s32[32]{0:T(128)S(1)}, s32[32]{0:T(128)}, u32[]{:S(2)}) copy-start(s32[32]{0:T(128)} %constant.44.clone) | copy-start | bytes 388
  4.5 19.6 %copy-start = (bf16[512,512]{1,0:T(8,128)(2,1)S(1)}, bf16[512,512]{1,0:T(8,128)(2,1)}, u32[]{:S(2)}) copy-start(bf16[512,512]{1,0:T(8,128)(2,1)} %constant.38.clone.low_ref.refs_3_.refs_2_) | copy-start | bytes 1572868
  4.5 19.4 %all-to-all-start = ((f32[32,4,640]{2,1,0:T(4,128)}), f32[32,4,640]{2,1,0:T(4,128)S(1)}, u32[]{:S(2)}, u32[]{:S(2)}) async-start(f32[32,4,640]{2,1,0:T(4,128)} %shard_map.149), calls=%async_computation | async-start | bytes 655360 | tf_op jit(solution)/shard_map/all_to_all | solution.py:582
  11.8 12.3 %copy-start.9 = (f32[8,8,128]{2,1,0:T(8,128)S(1)}, f32[8,8,128]{2,1,0:T(8,128)}, u32[]{:S(2)}) copy-start(f32[8,8,128]{2,1,0:T(8,128)} %constant.43.clone.dcols_ref) | copy-start | bytes 98308
  12.5 11.6 %copy-start.8 = (f32[2,8,128]{2,1,0:T(8,128)S(1)}, f32[2,8,128]{2,1,0:T(8,128)}, u32[]{:S(2)}) copy-start(f32[2,8,128]{2,1,0:T(8,128)} %constant.42.clone.nodes_ref) | copy-start | bytes 24580
  24.1 6.9 %copy-start.2 = (f32[512,8]{1,0:T(8,128)S(1)}, f32[512,8]{1,0:T(8,128)}, u32[]{:S(2)}) copy-start(f32[512,8]{1,0:T(8,128)} %constant.39.clone.refs_4_.interp_ref) | copy-start | bytes 49156
  27.2 2.9 %collective-permute-start.1 = (f32[64,128]{1,0:T(8,128)S(1)}, f32[64,128]{1,0:T(8,128)S(1)}, u32[]{:S(2)}, u32[]{:S(2)}) collective-permute-start(f32[64,128]{1,0:T(8,128)S(1)} %get-tuple-element.33), channel_id=1, source_target_pairs={{8,2},{2,8},{10,4},{4,10},{12,6},{6,12},{14,7},{7,14},{15,5},{5,15... | collective-permute-start | bytes 98312 | tf_op jit(solution)/shard_map/ppermute | solution.py:599
  27.9 3.1 %collective-permute-start = (f32[64,128]{1,0:T(8,128)S(1)}, f32[64,128]{1,0:T(8,128)S(1)}, u32[]{:S(2)}, u32[]{:S(2)}) collective-permute-start(f32[64,128]{1,0:T(8,128)S(1)} %get-tuple-element.33), channel_id=1, source_target_pairs={{0,8},{8,0},{2,10},{10,2},{4,12},{12,4},{6,14},{14,6},{7,15},{15,7... | collective-permute-start | bytes 98312 | tf_op jit(solution)/shard_map/ppermute | solution.py:598
  31.0 13.0 %copy-start.3 = (f32[512,8]{1,0:T(8,128)S(1)}, f32[512,8]{1,0:T(8,128)}, u32[]{:S(2)}) copy-start(f32[512,8]{1,0:T(8,128)} %constant.40.clone.image_ref) | copy-start | bytes 49156
  47.2 2.6 %collective-permute-start.3 = (f32[64,128]{1,0:T(8,128)S(1)}, f32[64,128]{1,0:T(8,128)S(1)}, u32[]{:S(2)}, u32[]{:S(2)}) collective-permute-start(f32[64,128]{1,0:T(8,128)S(1)} %get-tuple-element.40), channel_id=1, source_target_pairs={{8,2},{2,8},{10,4},{4,10},{12,6},{6,12},{14,7},{7,14},{15,5},{5,15... | collective-permute-start | bytes 98312 | tf_op jit(solution)/shard_map/ppermute | solution.py:599
  47.9 2.8 %collective-permute-start.2 = (f32[64,128]{1,0:T(8,128)S(1)}, f32[64,128]{1,0:T(8,128)S(1)}, u32[]{:S(2)}, u32[]{:S(2)}) collective-permute-start(f32[64,128]{1,0:T(8,128)S(1)} %get-tuple-element.40), channel_id=1, source_target_pairs={{0,8},{8,0},{2,10},{10,2},{4,12},{12,4},{6,14},{14,6},{7,15},{15,7... | collective-permute-start | bytes 98312 | tf_op jit(solution)/shard_map/ppermute | solution.py:598
  52.1 4.4 %collective-permute-start.5 = (f32[64,128]{1,0:T(8,128)S(1)}, f32[64,128]{1,0:T(8,128)S(1)}, u32[]{:S(2)}, u32[]{:S(2)}) collective-permute-start(f32[64,128]{1,0:T(8,128)S(1)} %get-tuple-element.43), channel_id=1, source_target_pairs={{8,2},{2,8},{10,4},{4,10},{12,6},{6,12},{14,7},{7,14},{15,5},{5,15... | collective-permute-start | bytes 98312 | tf_op jit(solution)/shard_map/ppermute | solution.py:599
  52.8 4.6 %collective-permute-start.4 = (f32[64,128]{1,0:T(8,128)S(1)}, f32[64,128]{1,0:T(8,128)S(1)}, u32[]{:S(2)}, u32[]{:S(2)}) collective-permute-start(f32[64,128]{1,0:T(8,128)S(1)} %get-tuple-element.43), channel_id=1, source_target_pairs={{0,8},{8,0},{2,10},{10,2},{4,12},{12,4},{6,14},{14,6},{7,15},{15,7... | collective-permute-start | bytes 98312 | tf_op jit(solution)/shard_map/ppermute | solution.py:598
  59.4 4.4 %collective-permute-start.7 = (f32[64,128]{1,0:T(8,128)S(1)}, f32[64,128]{1,0:T(8,128)S(1)}, u32[]{:S(2)}, u32[]{:S(2)}) collective-permute-start(f32[64,128]{1,0:T(8,128)S(1)} %get-tuple-element.47), channel_id=1, source_target_pairs={{8,2},{2,8},{10,4},{4,10},{12,6},{6,12},{14,7},{7,14},{15,5},{5,15... | collective-permute-start | bytes 98312 | tf_op jit(solution)/shard_map/ppermute | solution.py:599
  60.0 4.6 %collective-permute-start.6 = (f32[64,128]{1,0:T(8,128)S(1)}, f32[64,128]{1,0:T(8,128)S(1)}, u32[]{:S(2)}, u32[]{:S(2)}) collective-permute-start(f32[64,128]{1,0:T(8,128)S(1)} %get-tuple-element.47), channel_id=1, source_target_pairs={{0,8},{8,0},{2,10},{10,2},{4,12},{12,4},{6,14},{14,6},{7,15},{15,7... | collective-permute-start | bytes 98312 | tf_op jit(solution)/shard_map/ppermute | solution.py:598
  66.1 4.4 %collective-permute-start.9 = (f32[64,128]{1,0:T(8,128)S(1)}, f32[64,128]{1,0:T(8,128)S(1)}, u32[]{:S(2)}, u32[]{:S(2)}) collective-permute-start(f32[64,128]{1,0:T(8,128)S(1)} %get-tuple-element.50), channel_id=1, source_target_pairs={{8,2},{2,8},{10,4},{4,10},{12,6},{6,12},{14,7},{7,14},{15,5},{5,15... | collective-permute-start | bytes 98312 | tf_op jit(solution)/shard_map/ppermute | solution.py:599
  66.7 4.6 %collective-permute-start.8 = (f32[64,128]{1,0:T(8,128)S(1)}, f32[64,128]{1,0:T(8,128)S(1)}, u32[]{:S(2)}, u32[]{:S(2)}) collective-permute-start(f32[64,128]{1,0:T(8,128)S(1)} %get-tuple-element.50), channel_id=1, source_target_pairs={{0,8},{8,0},{2,10},{10,2},{4,12},{12,4},{6,14},{14,6},{7,15},{15,7... | collective-permute-start | bytes 98312 | tf_op jit(solution)/shard_map/ppermute | solution.py:598
  86.2 2.6 %collective-permute-start.11 = (f32[64,128]{1,0:T(8,128)S(1)}, f32[64,128]{1,0:T(8,128)S(1)}, u32[]{:S(2)}, u32[]{:S(2)}) collective-permute-start(f32[64,128]{1,0:T(8,128)S(1)} %get-tuple-element.57), channel_id=1, source_target_pairs={{8,2},{2,8},{10,4},{4,10},{12,6},{6,12},{14,7},{7,14},{15,5},{5,15... | collective-permute-start | bytes 98312 | tf_op jit(solution)/shard_map/ppermute | solution.py:599
  86.9 2.8 %collective-permute-start.10 = (f32[64,128]{1,0:T(8,128)S(1)}, f32[64,128]{1,0:T(8,128)S(1)}, u32[]{:S(2)}, u32[]{:S(2)}) collective-permute-start(f32[64,128]{1,0:T(8,128)S(1)} %get-tuple-element.57), channel_id=1, source_target_pairs={{0,8},{8,0},{2,10},{10,2},{4,12},{12,4},{6,14},{14,6},{7,15},{15,7... | collective-permute-start | bytes 98312 | tf_op jit(solution)/shard_map/ppermute | solution.py:598
  91.2 4.4 %collective-permute-start.13 = (f32[64,128]{1,0:T(8,128)S(1)}, f32[64,128]{1,0:T(8,128)S(1)}, u32[]{:S(2)}, u32[]{:S(2)}) collective-permute-start(f32[64,128]{1,0:T(8,128)S(1)} %get-tuple-element.60), channel_id=1, source_target_pairs={{8,2},{2,8},{10,4},{4,10},{12,6},{6,12},{14,7},{7,14},{15,5},{5,15... | collective-permute-start | bytes 98312 | tf_op jit(solution)/shard_map/ppermute | solution.py:599
  91.8 4.6 %collective-permute-start.12 = (f32[64,128]{1,0:T(8,128)S(1)}, f32[64,128]{1,0:T(8,128)S(1)}, u32[]{:S(2)}, u32[]{:S(2)}) collective-permute-start(f32[64,128]{1,0:T(8,128)S(1)} %get-tuple-element.60), channel_id=1, source_target_pairs={{0,8},{8,0},{2,10},{10,2},{4,12},{12,4},{6,14},{14,6},{7,15},{15,7... | collective-permute-start | bytes 98312 | tf_op jit(solution)/shard_map/ppermute | solution.py:598
  98.1 13.5 %all-to-all-start.3 = ((f32[32,4,512]{2,1,0:T(4,128)}), f32[32,4,512]{2,1,0:T(4,128)S(1)}, u32[]{:S(2)}, u32[]{:S(2)}) async-start(f32[32,4,512]{2,1,0:T(4,128)} %shard_map.159), calls=%async_computation.3 | async-start | bytes 524288 | tf_op jit(solution)/shard_map/all_to_all | solution.py:650
  101.1 10.6 %copy-start.5 = (f32[3,128,128]{2,1,0:T(8,128)S(1)}, f32[3,128,128]{2,1,0:T(8,128)}, u32[]{:S(2)}) copy-start(f32[3,128,128]{2,1,0:T(8,128)} %constant.36.clone.perm_ref) | copy-start | bytes 589828

commit v2 on v1

--- a/solution.py
+++ b/solution.py
@@ -36,7 +36,6 @@
 HIGHEST = lax.Precision.HIGHEST
 F32 = jnp.float32
 BF16 = jnp.bfloat16
-PAD = 128
 FACE = N * N
 
 
@@ -66,6 +65,10 @@
     return np.kron(np.kron(a, b), c)
 
 
+def log2(n):
+    return int(n).bit_length() - 1
+
+
 class Layout:
     def __init__(self, mesh_x, mesh_y, tiles_x, tiles_y):
         self.mesh_x, self.mesh_y = mesh_x, mesh_y
@@ -75,52 +78,41 @@
         self.axis = ("ex", "ey") if self.joint else "ey"
         self.slabs = mesh_x * mesh_y if self.joint else mesh_y
         self.depth = EZ // self.slabs
+        assert self.depth == 2 and tiles_x == 1
         self.width = self.num_x * self.num_y * self.depth
         self.step_y = self.depth
         self.step_x = self.depth * self.num_y
-        self.order = self._order()
-        self.slab_of = np.argsort(self.order)
-
-    def _order(self):
-        snake = []
+        self.block = tiles_y * self.depth
+        slab_of = [self.slab_at(d) for d in range(self.slabs)]
+        self.order = [slab_of.index(s) for s in range(self.slabs)]
+
+    def slab_at(self, d):
         if self.joint and self.mesh_x % 2 == 0 and self.mesh_y % 2 == 0:
-            cols = [(x, y) for x in range(self.mesh_x // 2) for y in ((0, 1) if x % 2 == 0 else (1, 0))]
             high = self.mesh_y // 2
-            for n, (x, y) in enumerate(cols):
-                for z in range(high) if n % 2 == 0 else range(high - 1, -1, -1):
-                    for core in range(2):
-                        snake.append((x * 2 + core) * self.mesh_y + z * 2 + y)
-        elif not self.joint and self.mesh_y % 8 == 0:
-            for n in range(self.mesh_y // 8):
-                row = list(range(8 * n, 8 * n + 8))
-                snake += row if n % 2 == 0 else row[::-1]
-        else:
-            snake = list(range(self.slabs))
-        return np.array(snake)
+            y = d & 1
+            z = (d >> 1) & (high - 1)
+            core = (d >> log2(self.mesh_y)) & 1
+            x = d >> (log2(self.mesh_y) + 1)
+            turn = y ^ (x & 1)
+            return ((x * 2 + turn) * high + (z ^ (turn * (high - 1)))) * 2 + core
+        if not self.joint and self.mesh_y % 8 == 0:
+            return d ^ (((d >> 3) & 1) * 7)
+        return d
 
     def swaps(self, first):
         pairs = []
         for s in range(first, self.slabs - 1, 2):
-            a, b = int(self.order[s]), int(self.order[s + 1])
+            a, b = self.order[s], self.order[s + 1]
             pairs += [(a, b), (b, a)]
         return pairs
 
-    def pack_matrices(self):
-        rows = self.slabs * self.tiles_y * self.depth
-        lanes = self.tiles_y * EZ
-        out = np.zeros((3, rows, lanes))
-        for d in range(self.slabs):
-            slab = int(self.slab_of[d])
-            for e2 in range(self.tiles_y):
-                for e3 in range(self.depth):
-                    row = (d * self.tiles_y + e2) * self.depth + e3
-                    z = slab * self.depth + e3
-                    out[0, row, e2 * EZ + z] = 1
-                    if e3 == 0 and z > 0:
-                        out[1, row, e2 * EZ + z - 1] = 1
-                    if e3 == self.depth - 1 and z < EZ - 1:
-                        out[2, row, e2 * EZ + z + 1] = 1
-        return out
+    def permutation(self):
+        shape = (self.slabs * self.block, self.tiles_y * EZ)
+        row = lax.broadcasted_iota(jnp.int32, shape, 0)
+        lane = lax.broadcasted_iota(jnp.int32, shape, 1)
+        slab = self.slab_at(row >> log2(self.block))
+        e2 = (row >> 1) & (self.tiles_y - 1)
+        return (lane == e2 * EZ + slab * self.depth + (row & 1)).astype(F32)
 
 
 def split(x):
@@ -146,8 +138,8 @@
 def lane_parts(lay, shape):
     lane = lax.broadcasted_iota(jnp.int32, shape, len(shape) - 1)
     part_z = lane & (lay.depth - 1)
-    part_y = lax.shift_right_logical(lane, int(math.log2(lay.step_y))) & (lay.num_y - 1)
-    part_x = lax.shift_right_logical(lane, int(math.log2(lay.step_x)))
+    part_y = lax.shift_right_logical(lane, log2(lay.step_y)) & (lay.num_y - 1)
+    part_x = lax.shift_right_logical(lane, log2(lay.step_x))
     return part_x, part_y, part_z
 
 
@@ -165,13 +157,7 @@
             ref[pl.ds(n * N + k, 1), :] = value[n : n + 1]
 
 
-def assemble(lay, g_ref, s_ref, halo):
-    _, _, part_z = lane_parts(lay, halo.shape)
-    s_ref[...] = g_ref[...]
-    low = get_rows(g_ref, 0)
-    high = get_rows(g_ref, N - 1)
-    set_rows(s_ref, 0, low + jnp.where(part_z == 0, halo, roll(high, 1, 1)))
-    set_rows(s_ref, N - 1, high + jnp.where(part_z == lay.depth - 1, halo, roll(low, -1, 1)))
+def assemble_xy(lay, s_ref):
     last = N - 1
     for j in range(N):
         a, b = pl.ds(j * N, N), pl.ds((last * N + j) * N, N)
@@ -185,6 +171,16 @@
         s_ref[b, :] = high + roll(low, -lay.step_y, 1)
 
 
+def assemble(lay, g_ref, s_ref, halo):
+    _, _, part_z = lane_parts(lay, halo.shape)
+    s_ref[...] = g_ref[...]
+    low = get_rows(g_ref, 0)
+    high = get_rows(g_ref, N - 1)
+    set_rows(s_ref, 0, low + jnp.where(part_z == 0, halo, roll(high, 1, 1)))
+    set_rows(s_ref, N - 1, high + jnp.where(part_z == lay.depth - 1, halo, roll(low, -1, 1)))
+    assemble_xy(lay, s_ref)
+
+
 def store_faces(lay, g_ref, face_ref):
     low = get_rows(g_ref, 0)
     high = get_rows(g_ref, N - 1)
@@ -201,17 +197,67 @@
     return jnp.where(part_z == 0, roll(below, 1 - lay.depth, 1), roll(above, lay.depth - 1, 1))
 
 
-def pack_kernel(lay, source_ref, perm_ref, points_ref, out_ref):
-    nt = ((1,), (1,))
-    body = dot_exact(perm_ref[0], source_ref[...], nt)
-    below = dot_exact(perm_ref[1], get_rows(source_ref, N - 1), nt)
-    above = dot_exact(perm_ref[2], get_rows(source_ref, 0), nt)
-    block = lay.tiles_y * lay.depth
-    tail = jnp.concatenate([below + above, jnp.broadcast_to(points_ref[...], below.shape)], 1)
+def assemble_both(lay, g_ref, h_ref, s_ref, sh_ref):
+    low, high = get_rows(g_ref, 0), get_rows(g_ref, N - 1)
+    out_low, out_high = get_rows(h_ref, 0), get_rows(h_ref, N - 1)
+    _, _, part_z = lane_parts(lay, low.shape)
+    bottom = part_z == 0
+    s_ref[...] = g_ref[...]
+    sh_ref[...] = h_ref[...]
+    set_rows(s_ref, 0, low + jnp.where(bottom, out_high, roll(high, 1, 1)))
+    set_rows(s_ref, N - 1, high + jnp.where(bottom, roll(low, -1, 1), out_low))
+    set_rows(sh_ref, N - 1, out_high + jnp.where(bottom, low, 0.0))
+    set_rows(sh_ref, 0, out_low + jnp.where(bottom, 0.0, high))
+    assemble_xy(lay, s_ref)
+    assemble_xy(lay, sh_ref)
+
+
+def send_layers(lay, slab_ref, g_ref, s_ref, core_ref, chip_ref):
+    low, high = get_rows(g_ref, 0), get_rows(g_ref, N - 1)
+    _, _, part_z = lane_parts(lay, low.shape)
+    s_ref[...] = g_ref[...]
+    set_rows(s_ref, N - 1, jnp.where(part_z == 0, high + roll(low, -1, 1), high))
+    set_rows(s_ref, 0, jnp.where(part_z == 0, low, low + roll(high, 1, 1)))
+    half = N**3 // 2
+    a, b = s_ref[:half, :], s_ref[half:, :]
+    _, _, part_z = lane_parts(lay, a.shape)
+    bottom = part_z == 0
+    first = jnp.where(bottom, a, roll(b, 1, 1))
+    second = jnp.where(bottom, roll(a, -1, 1), b)
+    odd = (slab_ref[0] & 1) == 1
+    core_ref[...] = jnp.where(odd, first, second)
+    chip_ref[...] = jnp.where(odd, second, first)
+
+
+def receive_layers(lay, slab_ref, core_ref, chip_ref, h_ref):
+    odd = (slab_ref[0] & 1) == 1
+    core, chip = core_ref[...], chip_ref[...]
+    below, above = jnp.where(odd, core, chip), jnp.where(odd, chip, core)
+    _, _, part_z = lane_parts(lay, core.shape)
+    bottom = part_z == 0
+    half = N**3 // 2
+    h_ref[:half, :] = jnp.where(bottom, below, roll(above, 1, 1))
+    h_ref[half:, :] = jnp.where(bottom, roll(below, -1, 1), above)
+
+
+def pack_kernel(lay, base_ref, offset_ref, force_ref, source_ref, out_ref, s_ref):
+    s_ref[...] = source_ref[...]
+    mean = 0.5 * (get_rows(source_ref, N - 1) + roll(get_rows(source_ref, 0), -1, 1))
+    set_rows(s_ref, N - 1, mean)
+    set_rows(s_ref, 0, roll(mean, 1, 1))
+    body = dot_exact(lay.permutation(), s_ref[...], ((1,), (1,)))
+    shape = (lay.block, N**3)
+    lane = lax.broadcasted_iota(jnp.int32, shape, 1)
+    points = jnp.zeros(shape, F32)
+    for p in range(base_ref.shape[1]):
+        values = [base_ref[d, p].astype(F32) for d in range(3)]
+        values += [ref[d, p] for ref in (offset_ref, force_ref) for d in range(3)]
+        for n, value in enumerate(values):
+            points = jnp.where(lane == (p * 9 + n) * N, value, points)
+    row = lax.broadcasted_iota(jnp.int32, shape, 0)
+    used = (row == 1) & ((lane & (N - 1)) == 0)
     for d in range(lay.slabs):
-        part = slice(d * block, (d + 1) * block)
-        out_ref[d, :, : N**3] = body[part]
-        out_ref[d, :, N**3 :] = tail[part]
+        out_ref[d] = jnp.where(used, points, body[d * lay.block : (d + 1) * lay.block])
 
 
 def gauss(elem, base, position, half_nodes):
@@ -276,10 +322,11 @@
     lax.fori_loop(0, num_points, one, 0)
 
 
-def inverse_diagonal(lay, slab_ref, factor_ref, dinv_ref):
+def inverse_diagonal(lay, slab_ref, factor_ref, dinv_ref, outer):
     shape = (N, lay.width)
     part_x, part_y, part_z = lane_parts(lay, shape)
-    part_z = slab_ref[0] * lay.depth + part_z
+    first = slab_ref[0] * lay.depth
+    part_z = jnp.where(part_z == 0, first - 1, first + lay.depth) if outer else first + part_z
     node = lax.broadcasted_iota(jnp.int32, shape, 0)
 
     def share(low, high):
@@ -290,6 +337,8 @@
 
     low_z, high_z = share(part_z == 0, part_z == EZ - 1)
     along_z = jnp.where(node == 0, low_z, jnp.where(node == N - 1, high_z, 1.0))
+    if outer:
+        along_z = jnp.where((part_z < 0) | (part_z >= EZ), 0.0, along_z)
     along_x = dict(zip((0, N - 1), share(part_x == 0, part_x == lay.num_x - 1)))
     along_y = dict(zip((0, N - 1), share(part_y == 0, part_y == lay.num_y - 1)))
     for i in range(N):
@@ -303,6 +352,11 @@
             dinv_ref[rows, :] = value
 
 
+def diagonal_kernel(lay, slab_ref, factor_ref, dinv_ref, outer_ref):
+    inverse_diagonal(lay, slab_ref, factor_ref, dinv_ref, False)
+    inverse_diagonal(lay, slab_ref, factor_ref, outer_ref, True)
+
+
 def first_kernel(
     lay,
     num_points,
@@ -311,12 +365,11 @@
     recv_ref,
     nodes_ref,
     dcols_ref,
-    factor_ref,
+    dinv_ref,
     high_ref,
     low_ref,
     g_ref,
     x_ref,
-    dinv_ref,
     face_ref,
     s_ref,
     halo_ref,
@@ -325,9 +378,11 @@
     count, block = recv_ref.shape[0], recv_ref.shape[1]
     for d in range(count):
         flat_ref[pl.ds(d * block, block), :] = recv_ref[d]
-    g_ref[...] = flat_ref[:, : N**3].T
-    halo_ref[...] = flat_ref[:, N**3 :].T[:FACE]
-    inverse_diagonal(lay, slab_ref, factor_ref, dinv_ref)
+    g_ref[...] = flat_ref[...].T
+    low, high = get_rows(g_ref, 0), get_rows(g_ref, N - 1)
+    _, _, part_z = lane_parts(lay, low.shape)
+    set_rows(g_ref, 0, jnp.where(part_z == 0, low, roll(high, 1, 1)))
+    halo_ref[...] = jnp.where(part_z == 0, low, high)
     right_side(lay, num_points, slab_ref, points_ref, nodes_ref, dcols_ref, g_ref, halo_ref)
     assemble(lay, g_ref, s_ref, halo_ref[...])
     update = (1.0 / THETA) * dinv_ref[...] * s_ref[...]
@@ -336,88 +391,63 @@
     store_faces(lay, g_ref, face_ref)
 
 
-def step_kernel(
+def restriction(lay, g_ref, dinv_ref, interp_ref, send_ref):
+    inner = jnp.where(dinv_ref[...] != 0.0, g_ref[...], 0.0)
+    load = dot_exact(interp_ref[...], inner, ((0,), (0,)))
+    rows = [load[n : n + 1] for n in range(N)]
+    rows = [rows[n] + roll(rows[4 + n], lay.step_x, 1) for n in range(4)]
+    rows = [rows[n] + roll(rows[2 + n], lay.step_y, 1) for n in range(2)]
+    for d in range(send_ref.shape[0]):
+        send_ref[d, 0:1] = rows[0]
+        send_ref[d, 1:2] = rows[1]
+
+
+OLD = RHO_SECOND * RHO_FIRST
+NEW = 2.0 * RHO_SECOND / DELTA
+
+
+def second_kernel(
     lay,
-    coef_old,
-    coef_new,
-    kind,
     slab_ref,
     core_ref,
     chip_ref,
     g_ref,
     x_ref,
-    *refs,
+    dinv_ref,
+    high_ref,
+    low_ref,
+    interp_ref,
+    g_out,
+    x_out,
+    send_ref,
+    core_out,
+    chip_out,
+    s_ref,
 ):
-    refs = list(refs)
-    u_ref = refs.pop(0) if coef_old else None
-    dinv_ref = refs.pop(0)
-    if kind != "last":
-        high_ref, low_ref = refs.pop(0), refs.pop(0)
-    if kind == "restrict":
-        interp_ref = refs.pop(0)
-    if kind == "last":
-        out_ref, s_ref = refs
-    elif kind == "restrict":
-        g_out, x_out, send_ref, s_ref = refs
-    else:
-        g_out, x_out, u_out, face_ref, s_ref = refs
     assemble(lay, g_ref, s_ref, halo_of(lay, slab_ref, core_ref, chip_ref))
-    update = coef_new * dinv_ref[...] * s_ref[...]
-    if coef_old:
-        update = update + coef_old * u_ref[...]
-    if kind == "last":
-        total = (x_ref[...] + update).T
-        count, block = out_ref.shape[0], out_ref.shape[1]
-        for d in range(count):
-            out_ref[d] = total[d * block : (d + 1) * block]
-        return
+    update = OLD * x_ref[...] + NEW * dinv_ref[...] * s_ref[...]
     x_out[...] = x_ref[...] + update
     g_out[...] = g_ref[...] - times3(high_ref[...], low_ref[...], update)
-    if kind == "restrict":
-        inner = jnp.where(dinv_ref[...] != 0.0, g_out[...], 0.0)
-        load = dot_exact(interp_ref[...], inner, ((0,), (0,)))
-        rows = [load[n : n + 1] for n in range(N)]
-        rows = [rows[n] + roll(rows[4 + n], lay.step_x, 1) for n in range(4)]
-        rows = [rows[n] + roll(rows[2 + n], lay.step_y, 1) for n in range(2)]
-        for d in range(send_ref.shape[0]):
-            send_ref[d, 0:1] = rows[0]
-            send_ref[d, 1:2] = rows[1]
-    else:
-        u_out[...] = update
-        store_faces(lay, g_out, face_ref)
-
-
-def coarse_kernel(
-    lay,
-    mass,
-    stiff,
-    slab_ref,
-    loads_ref,
-    g_ref,
-    x_ref,
-    interp_ref,
-    image_ref,
-    g_out,
-    x_out,
-    face_ref,
-    first_ref,
-    second_ref,
-):
+    restriction(lay, g_out, dinv_ref, interp_ref, send_ref)
+    send_layers(lay, slab_ref, g_out, s_ref, core_out, chip_out)
+
+
+def solve_coarse(lay, mass, stiff, loads_ref, first_ref, second_ref):
     for s in range(lay.slabs):
-        d = int(lay.order[s])
+        d = lay.order[s]
         first_ref[pl.ds(s, 1), :] = loads_ref[d, 0:1]
         second_ref[pl.ds(s, 1), :] = loads_ref[d, 1:2]
     shape = (lay.slabs, lay.width)
     part_x, part_y, part_z = lane_parts(lay, shape)
     row = lax.broadcasted_iota(jnp.int32, shape, 0)
     keep = ((part_x > 0) & (part_y > 0) & ((part_z > 0) | (row > 0))).astype(F32)
-    bottom, top = part_z == 0, part_z == lay.depth - 1
+    bottom = part_z == 0
 
     def below(v):
-        return jnp.where(bottom, roll(roll(v, 1, 0), 1 - lay.depth, 1), roll(v, 1, 1))
+        return jnp.where(bottom, roll(roll(v, 1, 0), -1, 1), roll(v, 1, 1))
 
     def above(v):
-        return jnp.where(top, roll(roll(v, -1, 0), lay.depth - 1, 1), roll(v, -1, 1))
+        return jnp.where(bottom, roll(v, -1, 1), roll(roll(v, -1, 0), 1, 1))
 
     def neighbours(v, step):
         return roll(v, step, 1) + roll(v, -step, 1)
@@ -439,7 +469,8 @@
     def inner(a, b):
         return jnp.sum(jnp.sum(a * b, axis=1, keepdims=True), axis=0, keepdims=True)
 
-    residual = keep * (first_ref[...] + below(second_ref[...]))
+    here = pl.ds(0, lay.slabs)
+    residual = keep * (first_ref[here, :] + below(second_ref[here, :]))
     direction = residual
     total = jnp.zeros(shape, F32)
     norm = inner(residual, residual)
@@ -452,27 +483,101 @@
             following = inner(residual, residual)
             direction = residual + (following / norm) * direction
             norm = following
-    first_ref[...] = total
-    second_ref[...] = above(total)
-    mine = pl.ds(slab_ref[0], 1)
-    rows = [first_ref[mine, :], second_ref[mine, :]]
+    here = pl.ds(N, lay.slabs)
+    for ref, value in ((first_ref, total), (second_ref, above(total))):
+        ref[...] = jnp.zeros(ref.shape, F32)
+        ref[here, :] = value
+
+
+def corners(lay, low, high):
+    rows = [low, high]
     rows = rows + [roll(r, -lay.step_y, 1) for r in rows]
     rows = rows + [roll(r, -lay.step_x, 1) for r in rows]
     corner = lax.broadcasted_iota(jnp.int32, (N, lay.width), 0)
     local = jnp.broadcast_to(rows[0], (N, lay.width))
     for n in range(1, N):
         local = jnp.where(corner == n, rows[n], local)
+    return local
+
+
+def prolong_coarse(lay, slab_ref, first_ref, second_ref, interp_ref, image_ref, edge_ref, g_ref, h_ref, x_ref):
+    mine = slab_ref[0] + N
+    _, _, part_z = lane_parts(lay, (1, lay.width))
+    bottom = part_z == 0
+    own, outer, far = [], [], []
+    for ref in (first_ref, second_ref):
+        before, here, after = (ref[pl.ds(mine + shift, 1), :] for shift in (-1, 0, 1))
+        own.append(here)
+        outer.append(jnp.where(bottom, roll(before, -1, 1), roll(after, 1, 1)))
+        far.append(jnp.where(bottom, before, after))
     plain = ((1,), (0,))
-    x_out[...] = x_ref[...] + dot_exact(interp_ref[...], local, plain)
-    g_out[...] = g_ref[...] - dot_exact(image_ref[...], local, plain)
-    store_faces(lay, g_out, face_ref)
-
-
-def unpack_kernel(recv_ref, perm_ref, out_ref, flat_ref):
+    local = corners(lay, *own)
+    x_ref[...] += dot_exact(interp_ref[...], local, plain)
+    g_ref[...] -= dot_exact(image_ref[...], local, plain)
+    h_ref[...] -= dot_exact(image_ref[...], corners(lay, *outer), plain)
+    edge = dot_exact(edge_ref[...], corners(lay, *far), plain)
+    low, high = get_rows(h_ref, 0), get_rows(h_ref, N - 1)
+    set_rows(h_ref, 0, low - jnp.where(bottom, edge[FACE:], 0.0))
+    set_rows(h_ref, N - 1, high - jnp.where(bottom, 0.0, edge[:FACE]))
+
+
+def pair_kernel(lay, coarse, kind, slab_ref, core_ref, chip_ref, g_ref, x_ref, dinv_ref, outer_ref, *refs):
+    refs = list(refs)
+    high_ref, low_ref, edge_high_ref, edge_low_ref = (refs.pop(0) for _ in range(4))
+    if coarse:
+        loads_ref, image_ref, image_edge_ref = (refs.pop(0) for _ in range(3))
+    if coarse or kind == "restrict":
+        interp_ref = refs.pop(0)
+    if kind == "last":
+        out_ref = refs.pop(0)
+    else:
+        g_out, x_out = refs.pop(0), refs.pop(0)
+        if kind == "restrict":
+            send_ref = refs.pop(0)
+        core_out, chip_out = refs.pop(0), refs.pop(0)
+    s_ref, sh_ref, h_ref = (refs.pop(0) for _ in range(3))
+    if kind == "last":
+        g_out, x_out = refs.pop(0), refs.pop(0)
+
+    g_out[...] = g_ref[...]
+    x_out[...] = x_ref[...]
+    receive_layers(lay, slab_ref, core_ref, chip_ref, h_ref)
+    if coarse:
+        first_ref, second_ref = refs
+        solve_coarse(lay, *coarse, loads_ref, first_ref, second_ref)
+        prolong_coarse(
+            lay, slab_ref, first_ref, second_ref, interp_ref, image_ref, image_edge_ref, g_out, h_ref, x_out
+        )
+    assemble_both(lay, g_out, h_ref, s_ref, sh_ref)
+    update = (1.0 / THETA) * dinv_ref[...] * s_ref[...]
+    outer = (1.0 / THETA) * outer_ref[...] * sh_ref[...]
+    high, low = high_ref[...], low_ref[...]
+    edge = times3(edge_high_ref[...], edge_low_ref[...], outer)
+    _, _, part_z = lane_parts(lay, (FACE, lay.width))
+    near = jnp.where(
+        part_z == 0, get_rows(h_ref, N - 1) - edge[FACE:], get_rows(h_ref, 0) - edge[:FACE]
+    )
+    g_out[...] -= times3(high, low, update)
+    assemble(lay, g_out, s_ref, near)
+    following = OLD * update + NEW * dinv_ref[...] * s_ref[...]
+    if kind == "last":
+        total = (x_out[...] + (update + following)).T
+        count, block = out_ref.shape[0], out_ref.shape[1]
+        for d in range(count):
+            out_ref[d] = total[d * block : (d + 1) * block]
+        return
+    x_out[...] += update + following
+    g_out[...] -= times3(high, low, following)
+    if kind == "restrict":
+        restriction(lay, g_out, dinv_ref, interp_ref, send_ref)
+    send_layers(lay, slab_ref, g_out, s_ref, core_out, chip_out)
+
+
+def unpack_kernel(lay, recv_ref, out_ref, flat_ref):
     count, block = recv_ref.shape[0], recv_ref.shape[1]
     for d in range(count):
         flat_ref[pl.ds(d * block, block), :] = recv_ref[d]
-    out_ref[...] = dot_exact(flat_ref[...], perm_ref[0], ((0,), (0,)))
+    out_ref[...] = dot_exact(flat_ref[...], lay.permutation(), ((0,), (0,)))
 
 
 def forces_kernel(tiles_y, num_points, place_ref, points_ref, nodes_ref, out_ref):
@@ -481,7 +586,7 @@
     lane = lax.broadcasted_iota(jnp.int32, shape, 1)
     first_x, first_y = place_ref[0], place_ref[1]
     elem_x = jnp.broadcast_to(first_x, shape)
-    elem_y = first_y + lax.shift_right_logical(lane, int(math.log2(EZ)))
+    elem_y = first_y + lax.shift_right_logical(lane, log2(EZ))
     elem_z = lane & (EZ - 1)
     out_ref[...] = jnp.zeros(out_ref.shape, F32)
 
@@ -557,34 +662,38 @@
     dcols = np.broadcast_to(derivative[:, :, None], (N, N, width))
     mass = interp.T @ diag_w @ interp
     stiff = interp.T @ stiff_one @ interp
-    perms = jnp.asarray(lay.pack_matrices(), F32)
+    edge_rows = np.concatenate([np.arange(FACE) * N, np.arange(FACE) * N + N - 1])
     high, low = jnp.asarray(full_high), jnp.asarray(full_low)
+    edge_high, edge_low = jnp.asarray(full_high[edge_rows]), jnp.asarray(full_low[edge_rows])
+    image_edge = jnp.asarray(image3[edge_rows], F32)
     interp3, image3 = jnp.asarray(interp3, F32), jnp.asarray(image3, F32)
     factor, nodes_wide, nodes_local, dcols = (
         jnp.asarray(t, F32) for t in (factor, nodes_wide, nodes_local, dcols)
     )
 
-    slab = jnp.asarray(lay.slab_of, jnp.int32)[lax.axis_index(lay.axis)].reshape(1)
+    slab = lay.slab_at(lax.axis_index(lay.axis).astype(jnp.int32)).reshape(1)
     place = jnp.stack([lax.axis_index("ex") * tiles_x, lax.axis_index("ey") * tiles_y]).astype(
         jnp.int32
     )
 
     local_points = point_base.shape[1]
-    packed = jnp.concatenate([point_base.astype(F32), point_offset, point_force], 0)
-    packed = packed.T.reshape(1, local_points * 9)
-    packed = jnp.pad(packed, ((0, 0), (0, PAD - FACE - packed.shape[1])))
-    block = lay.tiles_y * lay.depth
+    block = lay.block
     (send,) = call(
         functools.partial(pack_kernel, lay),
-        [(lay.slabs, block, N**3 + PAD)],
-        [source.reshape(N**3, tiles_y * EZ), perms, packed],
+        [(lay.slabs, block, N**3)],
+        [point_base, point_offset, point_force, source.reshape(N**3, tiles_y * EZ)],
+        [(N**3, tiles_y * EZ)],
+        smem=3,
     )
     recv = lax.all_to_all(send, lay.axis, 0, 0)
     if not lay.joint:
         recv = lax.all_gather(recv, "ex", axis=0, tiled=True)
-    points = recv[:, 0, N**3 + FACE : N**3 + FACE + 9 * local_points]
-    points = points.reshape(devices * local_points, 9)
+    points = recv[:, 1, : 9 * N * local_points : N]
     num_points = devices * local_points
+    points = points.reshape(num_points, 9)
+    dinv, outer = call(
+        functools.partial(diagonal_kernel, lay), [fields, fields], [slab, factor], smem=1
+    )
 
     (forces,) = call(
         functools.partial(forces_kernel, tiles_y, num_points),
@@ -593,65 +702,68 @@
         smem=2,
     )
 
-    def swap(face):
+    def swap(core, chip):
         return (
-            lax.ppermute(face, lay.axis, lay.swaps(0)),
-            lax.ppermute(face, lay.axis, lay.swaps(1)),
+            lax.ppermute(core, lay.axis, lay.swaps(0)),
+            lax.ppermute(chip, lay.axis, lay.swaps(1)),
         )
 
+    def gather(loads):
+        return lax.all_to_all(loads, lay.axis, 0, 0)
+
     face_shape = (FACE, width)
-    g, x, dinv, face = call(
+    layer = (N**3 // 2, width)
+    loads_shape = (lay.slabs, 2, width)
+    g, x, face = call(
         functools.partial(first_kernel, lay, num_points),
-        [fields, fields, fields, face_shape],
-        [slab, points, recv, nodes_wide, dcols, factor, high, low],
-        [fields, face_shape, (width, N**3 + PAD)],
+        [fields, fields, face_shape],
+        [slab, points, recv, nodes_wide, dcols, dinv, high, low],
+        [fields, face_shape, (width, N**3)],
         smem=2,
     )
-    u = x
-    first = (0.0, 1.0 / THETA)
-    second = (RHO_SECOND * RHO_FIRST, 2.0 * RHO_SECOND / DELTA)
-
-    def step(coefs, kind, face, g, x, u):
-        inputs = [slab, *swap(face), g, x]
-        if coefs[0]:
-            inputs.append(u)
-        inputs.append(dinv)
-        if kind != "last":
-            inputs += [high, low]
-        if kind == "restrict":
-            inputs.append(interp3)
-            outs = [fields, fields, (lay.slabs, 2, width)]
-        elif kind == "last":
+    g, x, loads, core, chip = call(
+        functools.partial(second_kernel, lay),
+        [fields, fields, loads_shape, layer, layer],
+        [slab, *swap(face, face), g, x, dinv, high, low, interp3],
+        [fields],
+        smem=1,
+    )
+    coarse = ((mass[0, 0], mass[0, 1]), (stiff[0, 0], stiff[0, 1]))
+    stiffness = [high, low, edge_high, edge_low]
+
+    for cycle in range(CYCLES):
+        core, chip = swap(core, chip)
+        last = cycle + 1 == CYCLES
+        outs = [fields, fields, layer, layer]
+        scratch = [fields, fields, fields]
+        if last:
             outs = [(lay.mesh_x * lay.mesh_y, block, N**3)]
-        else:
-            outs = [fields, fields, fields, face_shape]
-        return call(
-            functools.partial(step_kernel, lay, *coefs, kind), outs, inputs, [fields], smem=1
-        )
-
-    for cycle in range(CYCLES):
-        if cycle > 0:
-            g, x, u, face = step(first, "plain", face, g, x, u)
-        g, x, loads = step(second, "restrict", face, g, x, u)
-        loads = lax.all_to_all(loads, lay.axis, 0, 0)
-        g, x, face = call(
-            functools.partial(coarse_kernel, lay, (mass[0, 0], mass[0, 1]), (stiff[0, 0], stiff[0, 1])),
-            [fields, fields, face_shape],
-            [slab, loads, g, x, interp3, image3],
-            [(lay.slabs, width)] * 2,
+            scratch += [fields, fields]
+        outs = call(
+            functools.partial(pair_kernel, lay, coarse, "last" if last else "plain"),
+            outs,
+            [slab, core, chip, g, x, dinv, outer, *stiffness, gather(loads), image3, image_edge, interp3],
+            scratch + [(lay.slabs + 2 * N, width)] * 2,
             smem=1,
         )
-        g, x, u, face = step(first, "plain", face, g, x, u)
-        if cycle + 1 < CYCLES:
-            g, x, u, face = step(second, "plain", face, g, x, u)
-    (out,) = step(second, "last", face, g, x, u)
+        if last:
+            break
+        g, x, core, chip = outs
+        g, x, loads, core, chip = call(
+            functools.partial(pair_kernel, lay, None, "restrict"),
+            [fields, fields, loads_shape, layer, layer],
+            [slab, *swap(core, chip), g, x, dinv, outer, *stiffness, interp3],
+            [fields, fields, fields],
+            smem=1,
+        )
+    (out,) = outs
     if not lay.joint:
         out = lax.dynamic_slice_in_dim(out, lax.axis_index("ex") * lay.mesh_y, lay.mesh_y, 0)
     out = lax.all_to_all(out, lay.axis, 0, 0)
     (pressure,) = call(
-        unpack_kernel,
+        functools.partial(unpack_kernel, lay),
         [(N**3, tiles_y * EZ)],
-        [out, perms],
+        [out],
         [(lay.slabs * block, N**3)],
     )
     return (

time: 113 us -> 92.5 us (0.82)
  starting transfers between devices: 35.7 us -> 21.7 us
  waiting for transfers between devices: 25.2 us -> 19.7 us
  Pallas kernels: 26.6 us -> 23.6 us
  blocking collectives: 20.9 us -> 22.9 us
    ppermute x14 -> x8, starting transfers between devices: 25.6 us -> 11.9 us  [the longest x4 9.23 us: swap(): lax.ppermute(core, lay.axis, lay.swaps(0))]
    ppermute x14 -> x8, waiting for transfers between devices: 6.02 us -> 1.44 us  [the longest x4 1.43 us: swap(): lax.ppermute(core, lay.axis, lay.swaps(0))]
    pallas_call x13 -> x9, Pallas kernels: 26.6 us -> 23.6 us  [call(): pl.pallas_call(kernel, out_shape=shapes, in_specs=specs, out_specs=[pl.Bl...]
    all_to_all x2, blocking collectives: 20.9 us -> 22.9 us  [gather(): return lax.all_to_all(loads, lay.axis, 0, 0)]
    unnamed x26 -> x29, local copies, waits for them, and re-layouts: 1.93 us -> 2.89 us
  transfers between devices with their start and end apart: 16 -> 10, of which waited for: 9 -> 4; matrix products, arithmetic and copies ran while one was open for 1% -> 0% of each run, Pallas kernels for 3% -> 3%
where the time goes in v2:
time: 92.5 us; the launch traced here: 92 us
  Pallas kernels  23.6 us (26%)
  blocking collectives  22.9 us (25%)
  starting transfers between devices  21.7 us (23%)
  waiting for transfers between devices  19.7 us (21%)
  local copies, waits for them, and re-layouts  3.15 us (3%)
    pallas_call x9, Pallas kernels, call(): pl.pallas_call(kernel, out_shape=shapes, in_specs=specs, out_specs=[pl.Bl...  23.6 us
    all_to_all x2, blocking collectives, gather(): return lax.all_to_all(loads, lay.axis, 0, 0)  22.9 us
    all_to_all x1, waiting for transfers between devices, shards(): recv = lax.all_to_all(send, lay.axis, 0, 0)  10.5 us
    ppermute x4, starting transfers between devices, swap(): lax.ppermute(core, lay.axis, lay.swaps(0))  9.23 us
    all_to_all x1, waiting for transfers between devices, shards(): out = lax.all_to_all(out, lay.axis, 0, 0)  7.71 us
    all_to_all x1, starting transfers between devices, shards(): recv = lax.all_to_all(send, lay.axis, 0, 0)  7.29 us
    unnamed x29, local copies, waits for them, and re-layouts  2.89 us
    ppermute x4, starting transfers between devices, swap(): lax.ppermute(chip, lay.axis, lay.swaps(1))  2.63 us
  transfers between devices with their start and end apart: 10, of which 4 were waited for; matrix products, arithmetic and copies ran while one was open for 0% of the time, Pallas kernels for 3%

profile of v2, /device:TPU:0, one launch (start us, length us, event | category | flops | bytes accessed | tf_op | source)
XLA Modules:
  0.0 92.0 jit_solution(12771003268388939045)
XLA Ops:
  0.6 0.7 copy.24.base_ref
  1.4 0.1 copy.25.offset_ref
  1.5 0.6 copy-done.12
  2.0 0.1 copy.26.force_ref
  2.1 0.9 %copy-done.7 = f32[8,8,8,1,128]{4,3,2,1,0:T(1,128)S(1)} copy-done((f32[8,8,8,1,128]{4,3,2,1,0:T(1,128)S(1)}, f32[8,8,8,1,128]{4,3,2,1,0:T(1,128)}, u32[]{:S(2)}) %copy-start.7) | copy-done | bytes 262168
  3.1 1.9 %shard_map.158 = f32[32,4,512]{2,1,0:T(4,128)} custom-call(s32[3,1]{1,0:T(4,128)S(1)} %copy.24.base_ref, f32[3,1]{1,0:T(4,128)S(1)} %copy.25.offset_ref, f32[3,1]{1,0:T(4,128)S(1)} %copy.26.force_ref, f32[512,128]{1,0:T(8,128)S(1)} %bitcast.13), custom_call_target="tpu_custom_call" | custom-call | tf_op jit(solution)/shard_map/pallas_call | solution.py:627
  5.0 7.3 %all-to-all-start = ((f32[32,4,512]{2,1,0:T(4,128)}), f32[32,4,512]{2,1,0:T(4,128)S(1)}, u32[]{:S(2)}, u32[]{:S(2)}) async-start(f32[32,4,512]{2,1,0:T(4,128)} %shard_map.158), calls=%async_computation | async-start | bytes 524288 | tf_op jit(solution)/shard_map/all_to_all | solution.py:688
  12.4 10.5 %all-to-all-done.recv_ref = f32[32,4,512]{2,1,0:T(4,128)S(1)} async-done(((f32[32,4,512]{2,1,0:T(4,128)}), f32[32,4,512]{2,1,0:T(4,128)S(1)}, u32[]{:S(2)}, u32[]{:S(2)}) %all-to-all-start) | async-done | bytes 262176 | tf_op jit(solution)/shard_map/all_to_all | solution.py:688
  22.9 0.3 slice.3
  23.2 0.4 copy-done.9
  23.6 2.5 %shard_map.160 = (f32[512,128]{1,0:T(8,128)S(1)}, f32[512,128]{1,0:T(8,128)S(1)}, f32[64,128]{1,0:T(8,128)S(1)}) custom-call(s32[1]{0:T(128)} %bitcast.slab_ref, f32[32,9]{1,0:T(8,128)S(1)} %bitcast.14, f32[32,4,512]{2,1,0:T(4,128)S(1)} %all-to-all-done.recv_ref, f32[2,8,128]{2,1,0:T(8,128)S(1)} %copy-done.9, f32[8,8,128]{2,1,0:T(8,128)S(1)} %copy-done.10, ...), custom_call_target="tpu_custom_call" | custom-call | tf_op jit(solution)/shard_map/pallas_call | solution.py:627
  26.1 0.7 collective-permute-start.1
  26.8 2.4 %collective-permute-start = (f32[64,128]{1,0:T(8,128)S(1)}, f32[64,128]{1,0:T(8,128)S(1)}, u32[]{:S(2)}, u32[]{:S(2)}) collective-permute-start(f32[64,128]{1,0:T(8,128)S(1)} %get-tuple-element.22), channel_id=1, source_target_pairs={{0,8},{8,0},{2,10},{10,2},{4,12},{12,4},{6,14},{14,6},{7,15},{15,7... | collective-permute-start | bytes 98312 | tf_op jit(solution)/shard_map/ppermute | solution.py:707
  29.2 0.9 collective-permute-done.core_ref
  30.1 1.4 %shard_map.161 = (f32[512,128]{1,0:T(8,128)S(1)}, f32[512,128]{1,0:T(8,128)S(1)}, f32[32,2,128]{2,1,0:T(2,128)S(1)}, f32[256,128]{1,0:T(8,128)S(1)}, f32[256,128]{1,0:T(8,128)S(1)}) custom-call(s32[1]{0:T(128)} %bitcast.slab_ref, f32[64,128]{1,0:T(8,128)S(1)} %collective-permute-done.core_ref, f32[64,128]{1,0:T(8,128)S(1)} %collective-permute-done.1.chip_ref, ...), custom_call_target="tpu_custom_call" | custom-call | tf_op jit(solution)/shard_map/pallas_call | solution.py:627
  31.4 1.2 %collective-permute-start.2 = (f32[256,128]{1,0:T(8,128)S(1)}, f32[256,128]{1,0:T(8,128)S(1)}, u32[]{:S(2)}, u32[]{:S(2)}) collective-permute-start(f32[256,128]{1,0:T(8,128)S(1)} %get-tuple-element.25), channel_id=1, source_target_pairs={{0,8},{8,0},{2,10},{10,2},{4,12},{12,4},{6,14},{14,6},{7,15},{15,7... | collective-permute-start | bytes 393224 | tf_op jit(solution)/shard_map/ppermute | solution.py:707
  32.6 0.7 collective-permute-start.3
  33.3 12.4 %all_to_all.20.refs_4_ = f32[32,2,128]{2,1,0:T(2,128)S(1)} all-to-all(f32[32,2,128]{2,1,0:T(2,128)S(1)} %get-tuple-element.30), channel_id=1, replica_groups=mesh['ex'=4,'ey'=8] {'ex','ey'}, dimensions={0} | all-to-all | bytes 65536 | tf_op jit(solution)/shard_map/all_to_all | solution.py:712
  45.7 5.7 %shard_map.162 = (f32[512,128]{1,0:T(8,128)S(1)}, f32[512,128]{1,0:T(8,128)S(1)}, f32[256,128]{1,0:T(8,128)S(1)}, f32[256,128]{1,0:T(8,128)S(1)}) custom-call(s32[1]{0:T(128)} %bitcast.slab_ref, f32[256,128]{1,0:T(8,128)S(1)} %collective-permute-done.2.core_ref, f32[256,128]{1,0:T(8,128)S(1)} %collective-permute-done.3.chip_ref, ...), custom_call_target="tpu_custom_call" | custom-call | tf_op jit(solution)/shard_map/pallas_call | solution.py:627
  51.3 0.2 collective-permute-start.4
  51.5 0.7 collective-permute-start.5
  52.2 0.6 collective-permute-done.4.core_ref
  52.8 2.9 %shard_map.163 = (f32[512,128]{1,0:T(8,128)S(1)}, f32[512,128]{1,0:T(8,128)S(1)}, f32[32,2,128]{2,1,0:T(2,128)S(1)}, f32[256,128]{1,0:T(8,128)S(1)}, f32[256,128]{1,0:T(8,128)S(1)}) custom-call(s32[1]{0:T(128)} %bitcast.slab_ref, f32[256,128]{1,0:T(8,128)S(1)} %collective-permute-done.4.core_ref, f32[256,128]{1,0:T(8,128)S(1)} %collective-permute-done.5.chip_ref, ...), custom_call_target="tpu_custom_call" | custom-call | tf_op jit(solution)/shard_map/pallas_call | solution.py:627
  55.7 5.5 %collective-permute-start.6 = (f32[256,128]{1,0:T(8,128)S(1)}, f32[256,128]{1,0:T(8,128)S(1)}, u32[]{:S(2)}, u32[]{:S(2)}) collective-permute-start(f32[256,128]{1,0:T(8,128)S(1)} %get-tuple-element.35), channel_id=1, source_target_pairs={{0,8},{8,0},{2,10},{10,2},{4,12},{12,4},{6,14},{14,6},{7,15},{15,7... | collective-permute-start | bytes 393224 | tf_op jit(solution)/shard_map/ppermute | solution.py:707
  61.2 0.7 collective-permute-start.7
  61.9 10.5 %all_to_all.21.refs_4_ = f32[32,2,128]{2,1,0:T(2,128)S(1)} all-to-all(f32[32,2,128]{2,1,0:T(2,128)S(1)} %get-tuple-element.39), channel_id=1, replica_groups=mesh['ex'=4,'ey'=8] {'ex','ey'}, dimensions={0} | all-to-all | bytes 65536 | tf_op jit(solution)/shard_map/all_to_all | solution.py:712
  72.4 5.2 %shard_map.164 = f32[32,4,512]{2,1,0:T(4,128)} custom-call(s32[1]{0:T(128)} %bitcast.slab_ref, f32[256,128]{1,0:T(8,128)S(1)} %collective-permute-done.6.core_ref, f32[256,128]{1,0:T(8,128)S(1)} %collective-permute-done.7.chip_ref, f32[512,128]{1,0:T(8,128)S(1)} %get-tuple-element.37.g_ref, f32[512,128]{1,0:T(8,128)S(1)} %get-tuple-element.38.x_ref, ...), custom_call_target="tpu_custom_call" | custom-call | tf_op jit(solution)/shard_map/pallas_call | solution.py:627
  77.6 2.6 %all-to-all-start.3 = ((f32[32,4,512]{2,1,0:T(4,128)}), f32[32,4,512]{2,1,0:T(4,128)S(1)}, u32[]{:S(2)}, u32[]{:S(2)}) async-start(f32[32,4,512]{2,1,0:T(4,128)} %shard_map.164), calls=%async_computation.3 | async-start | bytes 524288 | tf_op jit(solution)/shard_map/all_to_all | solution.py:762
  80.2 0.1 pad_add_fusion.place_ref
  80.2 2.9 %shard_map.166 = f32[3,512,128]{2,1,0:T(8,128)} custom-call(s32[2]{0:T(128)S(1)} %pad_add_fusion.place_ref, f32[32,9]{1,0:T(8,128)S(1)} %bitcast.15, f32[2,8,128]{2,1,0:T(8,128)S(1)} %copy-done.9), custom_call_target="tpu_custom_call" | custom-call | tf_op jit(solution)/shard_map/pallas_call | solution.py:627
  83.1 7.7 %all-to-all-done.3.recv_ref = f32[32,4,512]{2,1,0:T(4,128)S(1)} async-done(((f32[32,4,512]{2,1,0:T(4,128)}), f32[32,4,512]{2,1,0:T(4,128)S(1)}, u32[]{:S(2)}, u32[]{:S(2)}) %all-to-all-start.3) | async-done | bytes 262176 | tf_op jit(solution)/shard_map/all_to_all | solution.py:762
  90.8 1.1 %shard_map.165 = f32[512,128]{1,0:T(8,128)} custom-call(f32[32,4,512]{2,1,0:T(4,128)S(1)} %all-to-all-done.3.recv_ref), custom_call_target="tpu_custom_call" | custom-call | tf_op jit(solution)/shard_map/pallas_call | solution.py:627
  (30 shorter events, 0.1 us)
Async XLA Ops:
  0.6 0.8 copy-start.11
  1.4 0.7 copy-start.12
  2.1 0.9 %copy-start.7 = (f32[8,8,8,1,128]{4,3,2,1,0:T(1,128)S(1)}, f32[8,8,8,1,128]{4,3,2,1,0:T(1,128)}, u32[]{:S(2)}) copy-start(f32[8,8,8,1,128]{4,3,2,1,0:T(1,128)} %param.15) | copy-start | bytes 786436
  3.1 9.2 %copy-start.8 = (f32[512,128]{1,0:T(8,128)S(1)}, f32[512,128]{1,0:T(8,128)}, u32[]{:S(2)}) copy-start(f32[512,128]{1,0:T(8,128)} %constant.45.clone.factor_ref) | copy-start | bytes 786436
  3.1 20.1 %copy-start.1 = (bf16[512,512]{1,0:T(8,128)(2,1)S(1)}, bf16[512,512]{1,0:T(8,128)(2,1)}, u32[]{:S(2)}) copy-start(bf16[512,512]{1,0:T(8,128)(2,1)} %constant.38.clone.high_ref.refs_0_) | copy-start | bytes 1572868
  5.0 18.2 %copy-start = (bf16[512,512]{1,0:T(8,128)(2,1)S(1)}, bf16[512,512]{1,0:T(8,128)(2,1)}, u32[]{:S(2)}) copy-start(bf16[512,512]{1,0:T(8,128)(2,1)} %constant.39.clone.low_ref.refs_1_) | copy-start | bytes 1572868
  5.0 17.9 %all-to-all-start = ((f32[32,4,512]{2,1,0:T(4,128)}), f32[32,4,512]{2,1,0:T(4,128)S(1)}, u32[]{:S(2)}, u32[]{:S(2)}) async-start(f32[32,4,512]{2,1,0:T(4,128)} %shard_map.158), calls=%async_computation | async-start | bytes 524288 | tf_op jit(solution)/shard_map/all_to_all | solution.py:688
  12.3 10.9 %copy-start.10 = (f32[8,8,128]{2,1,0:T(8,128)S(1)}, f32[8,8,128]{2,1,0:T(8,128)}, u32[]{:S(2)}) copy-start(f32[8,8,128]{2,1,0:T(8,128)} %constant.47.clone.dcols_ref) | copy-start | bytes 98308
  22.9 0.7 copy-start.9
  23.6 6.4 %copy-start.2 = (f32[512,8]{1,0:T(8,128)S(1)}, f32[512,8]{1,0:T(8,128)}, u32[]{:S(2)}) copy-start(f32[512,8]{1,0:T(8,128)} %constant.43.clone.interp_ref.refs_7_.refs_4_) | copy-start | bytes 49156
  26.1 3.1 %collective-permute-start.1 = (f32[64,128]{1,0:T(8,128)S(1)}, f32[64,128]{1,0:T(8,128)S(1)}, u32[]{:S(2)}, u32[]{:S(2)}) collective-permute-start(f32[64,128]{1,0:T(8,128)S(1)} %get-tuple-element.22), channel_id=1, source_target_pairs={{8,2},{2,8},{10,4},{4,10},{12,6},{6,12},{14,7},{7,14},{15,5},{5,15... | collective-permute-start | bytes 98312 | tf_op jit(solution)/shard_map/ppermute | solution.py:708
  26.8 3.2 %collective-permute-start = (f32[64,128]{1,0:T(8,128)S(1)}, f32[64,128]{1,0:T(8,128)S(1)}, u32[]{:S(2)}, u32[]{:S(2)}) collective-permute-start(f32[64,128]{1,0:T(8,128)S(1)} %get-tuple-element.22), channel_id=1, source_target_pairs={{0,8},{8,0},{2,10},{10,2},{4,12},{12,4},{6,14},{14,6},{7,15},{15,7... | collective-permute-start | bytes 98312 | tf_op jit(solution)/shard_map/ppermute | solution.py:707
  30.0 15.6 %copy-start.3 = (bf16[128,512]{1,0:T(8,128)(2,1)S(1)}, bf16[128,512]{1,0:T(8,128)(2,1)}, u32[]{:S(2)}) copy-start(bf16[128,512]{1,0:T(8,128)(2,1)} %constant.41.clone.refs_3_) | copy-start | bytes 393220
  30.0 15.6 %copy-start.4 = (bf16[128,512]{1,0:T(8,128)(2,1)S(1)}, bf16[128,512]{1,0:T(8,128)(2,1)}, u32[]{:S(2)}) copy-start(bf16[128,512]{1,0:T(8,128)(2,1)} %constant.40.clone.refs_2_) | copy-start | bytes 393220
  30.0 15.6 %copy-start.5 = (f32[512,8]{1,0:T(8,128)S(1)}, f32[512,8]{1,0:T(8,128)}, u32[]{:S(2)}) copy-start(f32[512,8]{1,0:T(8,128)} %constant.44.clone.refs_5_) | copy-start | bytes 49156
  31.4 14.2 %copy-start.6 = (f32[128,8]{1,0:T(8,128)S(1)}, f32[128,8]{1,0:T(8,128)}, u32[]{:S(2)}) copy-start(f32[128,8]{1,0:T(8,128)} %constant.42.clone.refs_6_) | copy-start | bytes 12292
  31.4 14.2 %collective-permute-start.2 = (f32[256,128]{1,0:T(8,128)S(1)}, f32[256,128]{1,0:T(8,128)S(1)}, u32[]{:S(2)}, u32[]{:S(2)}) collective-permute-start(f32[256,128]{1,0:T(8,128)S(1)} %get-tuple-element.25), channel_id=1, source_target_pairs={{0,8},{8,0},{2,10},{10,2},{4,12},{12,4},{6,14},{14,6},{7,15},{15,7... | collective-permute-start | bytes 393224 | tf_op jit(solution)/shard_map/ppermute | solution.py:707
  32.6 13.0 %collective-permute-start.3 = (f32[256,128]{1,0:T(8,128)S(1)}, f32[256,128]{1,0:T(8,128)S(1)}, u32[]{:S(2)}, u32[]{:S(2)}) collective-permute-start(f32[256,128]{1,0:T(8,128)S(1)} %get-tuple-element.26), channel_id=1, source_target_pairs={{8,2},{2,8},{10,4},{4,10},{12,6},{6,12},{14,7},{7,14},{15,5},{5,15... | collective-permute-start | bytes 393224 | tf_op jit(solution)/shard_map/ppermute | solution.py:708
  51.3 1.4 %collective-permute-start.4 = (f32[256,128]{1,0:T(8,128)S(1)}, f32[256,128]{1,0:T(8,128)S(1)}, u32[]{:S(2)}, u32[]{:S(2)}) collective-permute-start(f32[256,128]{1,0:T(8,128)S(1)} %get-tuple-element.31), channel_id=1, source_target_pairs={{0,8},{8,0},{2,10},{10,2},{4,12},{12,4},{6,14},{14,6},{7,15},{15,7... | collective-permute-start | bytes 393224 | tf_op jit(solution)/shard_map/ppermute | solution.py:707
  51.5 1.2 %collective-permute-start.5 = (f32[256,128]{1,0:T(8,128)S(1)}, f32[256,128]{1,0:T(8,128)S(1)}, u32[]{:S(2)}, u32[]{:S(2)}) collective-permute-start(f32[256,128]{1,0:T(8,128)S(1)} %get-tuple-element.32), channel_id=1, source_target_pairs={{8,2},{2,8},{10,4},{4,10},{12,6},{6,12},{14,7},{7,14},{15,5},{5,15... | collective-permute-start | bytes 393224 | tf_op jit(solution)/shard_map/ppermute | solution.py:708
  55.7 16.7 %collective-permute-start.6 = (f32[256,128]{1,0:T(8,128)S(1)}, f32[256,128]{1,0:T(8,128)S(1)}, u32[]{:S(2)}, u32[]{:S(2)}) collective-permute-start(f32[256,128]{1,0:T(8,128)S(1)} %get-tuple-element.35), channel_id=1, source_target_pairs={{0,8},{8,0},{2,10},{10,2},{4,12},{12,4},{6,14},{14,6},{7,15},{15,7... | collective-permute-start | bytes 393224 | tf_op jit(solution)/shard_map/ppermute | solution.py:707
  61.2 11.2 %collective-permute-start.7 = (f32[256,128]{1,0:T(8,128)S(1)}, f32[256,128]{1,0:T(8,128)S(1)}, u32[]{:S(2)}, u32[]{:S(2)}) collective-permute-start(f32[256,128]{1,0:T(8,128)S(1)} %get-tuple-element.36), channel_id=1, source_target_pairs={{8,2},{2,8},{10,4},{4,10},{12,6},{6,12},{14,7},{7,14},{15,5},{5,15... | collective-permute-start | bytes 393224 | tf_op jit(solution)/shard_map/ppermute | solution.py:708
  77.6 13.2 %all-to-all-start.3 = ((f32[32,4,512]{2,1,0:T(4,128)}), f32[32,4,512]{2,1,0:T(4,128)S(1)}, u32[]{:S(2)}, u32[]{:S(2)}) async-start(f32[32,4,512]{2,1,0:T(4,128)} %shard_map.164), calls=%async_computation.3 | async-start | bytes 524288 | tf_op jit(solution)/shard_map/all_to_all | solution.py:762

commit v3 on v2

--- a/solution.py
+++ b/solution.py
@@ -33,7 +33,6 @@
 DELTA = 0.5 * (CHEB_HIGH - CHEB_LOW)
 RHO_FIRST = DELTA / THETA
 RHO_SECOND = 1.0 / (2.0 * THETA / DELTA - RHO_FIRST)
-HIGHEST = lax.Precision.HIGHEST
 F32 = jnp.float32
 BF16 = jnp.bfloat16
 FACE = N * N
@@ -101,18 +100,10 @@
 
     def swaps(self, first):
         pairs = []
-        for s in range(first, self.slabs - 1, 2):
-            a, b = self.order[s], self.order[s + 1]
+        for s in range(first, self.slabs, 2):
+            a, b = self.order[s], self.order[(s + 1) % self.slabs]
             pairs += [(a, b), (b, a)]
         return pairs
-
-    def permutation(self):
-        shape = (self.slabs * self.block, self.tiles_y * EZ)
-        row = lax.broadcasted_iota(jnp.int32, shape, 0)
-        lane = lax.broadcasted_iota(jnp.int32, shape, 1)
-        slab = self.slab_at(row >> log2(self.block))
-        e2 = (row >> 1) & (self.tiles_y - 1)
-        return (lane == e2 * EZ + slab * self.depth + (row & 1)).astype(F32)
 
 
 def split(x):
@@ -126,8 +117,20 @@
     return dot(high, xh) + dot(high, xl) + dot(low, xh)
 
 
-def dot_exact(a, b, dims):
-    return lax.dot_general(a, b, (dims, ((), ())), precision=HIGHEST, preferred_element_type=F32)
+def split_table(x):
+    high = x.astype(BF16)
+    return high, (x - high.astype(np.float64)).astype(BF16)
+
+
+def stacked_table(x):
+    high, low = split_table(x)
+    return np.concatenate([high, high, low, low], 1)
+
+
+def stacked(x):
+    high = x.astype(BF16).astype(F32)
+    low = x - high
+    return jnp.concatenate([high, low, high, low], 0).astype(BF16)
 
 
 def roll(x, shift, axis):
@@ -240,24 +243,50 @@
     h_ref[half:, :] = jnp.where(bottom, roll(below, -1, 1), above)
 
 
-def pack_kernel(lay, base_ref, offset_ref, force_ref, source_ref, out_ref, s_ref):
-    s_ref[...] = source_ref[...]
-    mean = 0.5 * (get_rows(source_ref, N - 1) + roll(get_rows(source_ref, 0), -1, 1))
-    set_rows(s_ref, N - 1, mean)
-    set_rows(s_ref, 0, roll(mean, 1, 1))
-    body = dot_exact(lay.permutation(), s_ref[...], ((1,), (1,)))
-    shape = (lay.block, N**3)
+def pack_kernel(
+    lay,
+    base_ref,
+    offset_ref,
+    force_ref,
+    source_ref,
+    out_ref,
+    base_buf,
+    offset_buf,
+    force_buf,
+    field_ref,
+    flat_ref,
+    sems,
+):
+    pairs = (
+        (source_ref, field_ref),
+        (base_ref, base_buf),
+        (offset_ref, offset_buf),
+        (force_ref, force_buf),
+    )
+    copies = [pltpu.make_async_copy(a, b, sems.at[n]) for n, (a, b) in enumerate(pairs)]
+    for copy in copies:
+        copy.start()
+    for copy in copies:
+        copy.wait()
+    mean = 0.5 * (get_rows(field_ref, N - 1) + roll(get_rows(field_ref, 0), -1, 1))
+    set_rows(field_ref, N - 1, mean)
+    set_rows(field_ref, 0, roll(mean, 1, 1))
+    flat_ref[...] = field_ref[...].T
+    shape = (1, N**3)
     lane = lax.broadcasted_iota(jnp.int32, shape, 1)
     points = jnp.zeros(shape, F32)
-    for p in range(base_ref.shape[1]):
-        values = [base_ref[d, p].astype(F32) for d in range(3)]
-        values += [ref[d, p] for ref in (offset_ref, force_ref) for d in range(3)]
-        for n, value in enumerate(values):
-            points = jnp.where(lane == (p * 9 + n) * N, value, points)
-    row = lax.broadcasted_iota(jnp.int32, shape, 0)
-    used = (row == 1) & ((lane & (N - 1)) == 0)
+    for p in range(base_buf.shape[0]):
+        for c, ref in enumerate((base_buf, offset_buf, force_buf)):
+            for d in range(3):
+                value = ref[p : p + 1, d : d + 1].astype(F32)
+                points = jnp.where(lane == (p * 9 + c * 3 + d) * N, value, points)
+    used = (lane & (N - 1)) == 0
     for d in range(lay.slabs):
-        out_ref[d] = jnp.where(used, points, body[d * lay.block : (d + 1) * lay.block])
+        first = lay.slab_at(d) * lay.depth
+        for e2 in range(lay.tiles_y):
+            rows = flat_ref[pl.ds(e2 * EZ + first, lay.depth), :]
+            out_ref[d, pl.ds(e2 * lay.depth, lay.depth), :] = rows
+        out_ref[d, 1:2, :] = jnp.where(used, points, out_ref[d, 1:2, :])
 
 
 def gauss(elem, base, position, half_nodes):
@@ -393,7 +422,11 @@
 
 def restriction(lay, g_ref, dinv_ref, interp_ref, send_ref):
     inner = jnp.where(dinv_ref[...] != 0.0, g_ref[...], 0.0)
-    load = dot_exact(interp_ref[...], inner, ((0,), (0,)))
+    high, low = split(inner)
+    both = jnp.dot(
+        interp_ref[...], jnp.concatenate([high, low], 1), preferred_element_type=F32
+    )
+    load = both[:N, : lay.width] + both[:N, lay.width :] + both[N:, : lay.width]
     rows = [load[n : n + 1] for n in range(N)]
     rows = [rows[n] + roll(rows[4 + n], lay.step_x, 1) for n in range(4)]
     rows = [rows[n] + roll(rows[2 + n], lay.step_y, 1) for n in range(2)]
@@ -510,12 +543,12 @@
         own.append(here)
         outer.append(jnp.where(bottom, roll(before, -1, 1), roll(after, 1, 1)))
         far.append(jnp.where(bottom, before, after))
-    plain = ((1,), (0,))
-    local = corners(lay, *own)
-    x_ref[...] += dot_exact(interp_ref[...], local, plain)
-    g_ref[...] -= dot_exact(image_ref[...], local, plain)
-    h_ref[...] -= dot_exact(image_ref[...], corners(lay, *outer), plain)
-    edge = dot_exact(edge_ref[...], corners(lay, *far), plain)
+    local = stacked(corners(lay, *own))
+    dot = functools.partial(jnp.dot, preferred_element_type=F32)
+    x_ref[...] += dot(interp_ref[...], local)
+    g_ref[...] -= dot(image_ref[...], local)
+    h_ref[...] -= dot(image_ref[...], stacked(corners(lay, *outer)))
+    edge = dot(edge_ref[...], stacked(corners(lay, *far)))
     low, high = get_rows(h_ref, 0), get_rows(h_ref, N - 1)
     set_rows(h_ref, 0, low - jnp.where(bottom, edge[FACE:], 0.0))
     set_rows(h_ref, N - 1, high - jnp.where(bottom, 0.0, edge[:FACE]))
@@ -574,10 +607,12 @@
 
 
 def unpack_kernel(lay, recv_ref, out_ref, flat_ref):
-    count, block = recv_ref.shape[0], recv_ref.shape[1]
-    for d in range(count):
-        flat_ref[pl.ds(d * block, block), :] = recv_ref[d]
-    out_ref[...] = dot_exact(flat_ref[...], lay.permutation(), ((0,), (0,)))
+    for d in range(lay.slabs):
+        first = lay.slab_at(d) * lay.depth
+        for e2 in range(lay.tiles_y):
+            rows = recv_ref[d, pl.ds(e2 * lay.depth, lay.depth), :]
+            flat_ref[pl.ds(e2 * EZ + first, lay.depth), :] = rows
+    out_ref[...] = flat_ref[...].T
 
 
 def forces_kernel(tiles_y, num_points, place_ref, points_ref, nodes_ref, out_ref):
@@ -619,17 +654,16 @@
     lax.fori_loop(0, num_points, one, 0)
 
 
-def call(kernel, outs, inputs, scratch=(), smem=0):
-    specs = [
-        pl.BlockSpec(memory_space=pltpu.SMEM if n < smem else pltpu.VMEM) for n in range(len(inputs))
-    ]
+def call(kernel, outs, inputs, scratch=(), smem=0, spaces=None):
+    spaces = spaces or [pltpu.SMEM] * smem + [pltpu.VMEM] * (len(inputs) - smem)
+    specs = [pl.BlockSpec(memory_space=space) for space in spaces]
     shapes = [jax.ShapeDtypeStruct(s, F32) for s in outs]
     result = pl.pallas_call(
         kernel,
         out_shape=shapes,
         in_specs=specs,
         out_specs=[pl.BlockSpec(memory_space=pltpu.VMEM)] * len(shapes),
-        scratch_shapes=[pltpu.VMEM(s, F32) for s in scratch],
+        scratch_shapes=[pltpu.VMEM(s, F32) if isinstance(s, tuple) else s for s in scratch],
         compiler_params=pltpu.CompilerParams(vmem_limit_bytes=40 * 1024 * 1024),
     )(*inputs)
     return result
@@ -648,8 +682,7 @@
         + kron3(diag_w, stiff_one, diag_w)
         + kron3(diag_w, diag_w, stiff_one)
     )
-    full_high = full.astype(BF16)
-    full_low = (full - full_high.astype(np.float64)).astype(BF16)
+    full_high, full_low = split_table(full)
     interp3 = kron3(interp, interp, interp)
     image3 = full @ interp3
     ratio = (weights[:, None] * derivative**2).sum(axis=0) / weights
@@ -665,8 +698,10 @@
     edge_rows = np.concatenate([np.arange(FACE) * N, np.arange(FACE) * N + N - 1])
     high, low = jnp.asarray(full_high), jnp.asarray(full_low)
     edge_high, edge_low = jnp.asarray(full_high[edge_rows]), jnp.asarray(full_low[edge_rows])
-    image_edge = jnp.asarray(image3[edge_rows], F32)
-    interp3, image3 = jnp.asarray(interp3, F32), jnp.asarray(image3, F32)
+    restrict3 = jnp.asarray(np.concatenate(split_table(interp3.T), 0))
+    prolong3, image3, image_edge = (
+        jnp.asarray(stacked_table(t)) for t in (interp3, image3, image3[edge_rows])
+    )
     factor, nodes_wide, nodes_local, dcols = (
         jnp.asarray(t, F32) for t in (factor, nodes_wide, nodes_local, dcols)
     )
@@ -681,9 +716,16 @@
     (send,) = call(
         functools.partial(pack_kernel, lay),
         [(lay.slabs, block, N**3)],
-        [point_base, point_offset, point_force, source.reshape(N**3, tiles_y * EZ)],
-        [(N**3, tiles_y * EZ)],
-        smem=3,
+        [point_base.T, point_offset.T, point_force.T, source.reshape(N**3, tiles_y * EZ)],
+        [
+            pltpu.VMEM((local_points, 3), jnp.int32),
+            (local_points, 3),
+            (local_points, 3),
+            (N**3, tiles_y * EZ),
+            (tiles_y * EZ, N**3),
+            pltpu.SemaphoreType.DMA((4,)),
+        ],
+        spaces=[pl.ANY] * 4,
     )
     recv = lax.all_to_all(send, lay.axis, 0, 0)
     if not lay.joint:
@@ -724,7 +766,7 @@
     g, x, loads, core, chip = call(
         functools.partial(second_kernel, lay),
         [fields, fields, loads_shape, layer, layer],
-        [slab, *swap(face, face), g, x, dinv, high, low, interp3],
+        [slab, *swap(face, face), g, x, dinv, high, low, restrict3],
         [fields],
         smem=1,
     )
@@ -742,7 +784,7 @@
         outs = call(
             functools.partial(pair_kernel, lay, coarse, "last" if last else "plain"),
             outs,
-            [slab, core, chip, g, x, dinv, outer, *stiffness, gather(loads), image3, image_edge, interp3],
+            [slab, core, chip, g, x, dinv, outer, *stiffness, gather(loads), image3, image_edge, prolong3],
             scratch + [(lay.slabs + 2 * N, width)] * 2,
             smem=1,
         )
@@ -752,7 +794,7 @@
         g, x, loads, core, chip = call(
             functools.partial(pair_kernel, lay, None, "restrict"),
             [fields, fields, loads_shape, layer, layer],
-            [slab, *swap(core, chip), g, x, dinv, outer, *stiffness, interp3],
+            [slab, *swap(core, chip), g, x, dinv, outer, *stiffness, restrict3],
             [fields, fields, fields],
             smem=1,
         )

time: 92.5 us -> 81.4 us (0.88)
  starting transfers between devices: 21.7 us -> 13.9 us
  waiting for transfers between devices: 19.7 us -> 24.4 us
  blocking collectives: 22.9 us -> 18.8 us
  Pallas kernels: 23.6 us -> 20.6 us
    ppermute x4, starting transfers between devices: 9.23 us -> 1.38 us  [swap(): lax.ppermute(core, lay.axis, lay.swaps(0))]
    ppermute x4, waiting for transfers between devices: 0.01 us -> 5.19 us  [swap(): lax.ppermute(chip, lay.axis, lay.swaps(1))]
    all_to_all x2, blocking collectives: 22.9 us -> 18.8 us  [gather(): return lax.all_to_all(loads, lay.axis, 0, 0)]
    pallas_call x9, Pallas kernels: 23.6 us -> 20.6 us  [call(): pl.pallas_call(kernel, out_shape=shapes, in_specs=specs, out_specs=[pl.Bl...]
    unnamed x29 -> x30, local copies, waits for them, and re-layouts: 2.89 us -> 2.07 us
  transfers between devices with their start and end apart: 10 -> 10, of which waited for: 4 -> 5; matrix products, arithmetic and copies ran while one was open for 0% -> 0% of each run, Pallas kernels for 3% -> 3%
where the time goes in v3:
time: 81.4 us; the launch traced here: 80.9 us
  waiting for transfers between devices  24.4 us (30%)
  Pallas kernels  20.6 us (25%)
  blocking collectives  18.8 us (23%)
  starting transfers between devices  13.9 us (17%)
  local copies, waits for them, and re-layouts  2.32 us (3%)
  between operations  0.87 us (1%)
    pallas_call x9, Pallas kernels, call(): pl.pallas_call(kernel, out_shape=shapes, in_specs=specs, out_specs=[pl.Bl...  20.6 us
    all_to_all x2, blocking collectives, gather(): return lax.all_to_all(loads, lay.axis, 0, 0)  18.8 us
    all_to_all x1, waiting for transfers between devices, shards(): recv = lax.all_to_all(send, lay.axis, 0, 0)  10.5 us
    all_to_all x1, waiting for transfers between devices, shards(): out = lax.all_to_all(out, lay.axis, 0, 0)  8.08 us
    all_to_all x1, starting transfers between devices, shards(): recv = lax.all_to_all(send, lay.axis, 0, 0)  7.3 us
    ppermute x4, waiting for transfers between devices, swap(): lax.ppermute(chip, lay.axis, lay.swaps(1))  5.19 us
    ppermute x4, starting transfers between devices, swap(): lax.ppermute(chip, lay.axis, lay.swaps(1))  2.61 us
    all_to_all x1, starting transfers between devices, shards(): out = lax.all_to_all(out, lay.axis, 0, 0)  2.59 us
  transfers between devices with their start and end apart: 10, of which 5 were waited for; matrix products, arithmetic and copies ran while one was open for 0% of the time, Pallas kernels for 3%

profile of v3, /device:TPU:0, one launch (start us, length us, event | category | flops | bytes accessed | tf_op | source)
XLA Modules:
  0.0 80.9 jit_solution(1432289423267425815)
XLA Ops:
  0.7 0.6 copy-done.12
  1.3 0.0 copy-done.13
  1.3 0.9 %copy-done.6 = f32[8,8,8,1,128]{4,3,2,1,0:T(1,128)S(1)} copy-done((f32[8,8,8,1,128]{4,3,2,1,0:T(1,128)S(1)}, f32[8,8,8,1,128]{4,3,2,1,0:T(1,128)}, u32[]{:S(2)}) %copy-start.6) | copy-done | bytes 262168
  2.3 1.1 %shard_map.167 = f32[32,4,512]{2,1,0:T(4,128)} custom-call(s32[1,3]{1,0:T(1,128)S(1)} %bitcast.19, f32[1,3]{1,0:T(1,128)S(1)} %bitcast.20, f32[1,3]{1,0:T(1,128)S(1)} %bitcast.21, f32[512,128]{1,0:T(8,128)S(1)} %bitcast.16), custom_call_target="tpu_custom_call" | custom-call | tf_op jit(solution)/shard_map/pallas_call | solution.py:661
  3.4 7.3 %all-to-all-start = ((f32[32,4,512]{2,1,0:T(4,128)}), f32[32,4,512]{2,1,0:T(4,128)S(1)}, u32[]{:S(2)}, u32[]{:S(2)}) async-start(f32[32,4,512]{2,1,0:T(4,128)} %shard_map.167), calls=%async_computation | async-start | bytes 524288 | tf_op jit(solution)/shard_map/all_to_all | solution.py:730
  10.8 0.1 shard_map.168
  10.8 10.5 %all-to-all-done.recv_ref = f32[32,4,512]{2,1,0:T(4,128)S(1)} async-done(((f32[32,4,512]{2,1,0:T(4,128)}), f32[32,4,512]{2,1,0:T(4,128)S(1)}, u32[]{:S(2)}, u32[]{:S(2)}) %all-to-all-start) | async-done | bytes 262176 | tf_op jit(solution)/shard_map/all_to_all | solution.py:730
  21.4 0.3 slice.3
  21.7 0.4 copy-done.10
  22.1 2.6 %shard_map.169 = (f32[512,128]{1,0:T(8,128)S(1)}, f32[512,128]{1,0:T(8,128)S(1)}, f32[64,128]{1,0:T(8,128)S(1)}) custom-call(s32[1]{0:T(128)} %bitcast.slab_ref, f32[32,9]{1,0:T(8,128)S(1)} %bitcast.17, f32[32,4,512]{2,1,0:T(4,128)S(1)} %all-to-all-done.recv_ref, f32[2,8,128]{2,1,0:T(8,128)S(1)} %copy-done.10, f32[8,8,128]{2,1,0:T(8,128)S(1)} %copy-done.11, ...), custom_call_target="tpu_custom_call" | custom-call | tf_op jit(solution)/shard_map/pallas_call | solution.py:661
  24.7 0.8 %collective-permute-start.1 = (f32[64,128]{1,0:T(8,128)S(1)}, f32[64,128]{1,0:T(8,128)S(1)}, u32[]{:S(2)}, u32[]{:S(2)}) collective-permute-start(f32[64,128]{1,0:T(8,128)S(1)} %get-tuple-element.22), channel_id=1, source_target_pairs={{8,2},{2,8},{10,4},{4,10},{12,6},{6,12},{14,7},{7,14},{15,5},{5,15... | collective-permute-start | bytes 98312 | tf_op jit(solution)/shard_map/ppermute | solution.py:750
  25.5 0.6 collective-permute-start
  26.1 2.0 %collective-permute-done.1.chip_ref = f32[64,128]{1,0:T(8,128)S(1)} collective-permute-done((f32[64,128]{1,0:T(8,128)S(1)}, f32[64,128]{1,0:T(8,128)S(1)}, u32[]{:S(2)}, u32[]{:S(2)}) %collective-permute-start.1) | collective-permute-done | bytes 32800 | tf_op jit(solution)/shard_map/ppermute | solution.py:750
  28.1 1.2 %shard_map.170 = (f32[512,128]{1,0:T(8,128)S(1)}, f32[512,128]{1,0:T(8,128)S(1)}, f32[32,2,128]{2,1,0:T(2,128)S(1)}, f32[256,128]{1,0:T(8,128)S(1)}, f32[256,128]{1,0:T(8,128)S(1)}) custom-call(s32[1]{0:T(128)} %bitcast.slab_ref, f32[64,128]{1,0:T(8,128)S(1)} %collective-permute-done.core_ref, f32[64,128]{1,0:T(8,128)S(1)} %collective-permute-done.1.chip_ref, ...), custom_call_target="tpu_custom_call" | custom-call | tf_op jit(solution)/shard_map/pallas_call | solution.py:661
  29.4 0.2 collective-permute-start.2
  29.5 0.8 %collective-permute-start.3 = (f32[256,128]{1,0:T(8,128)S(1)}, f32[256,128]{1,0:T(8,128)S(1)}, u32[]{:S(2)}, u32[]{:S(2)}) collective-permute-start(f32[256,128]{1,0:T(8,128)S(1)} %get-tuple-element.26), channel_id=1, source_target_pairs={{8,2},{2,8},{10,4},{4,10},{12,6},{6,12},{14,7},{7,14},{15,5},{5,15... | collective-permute-start | bytes 393224 | tf_op jit(solution)/shard_map/ppermute | solution.py:750
  30.4 9.8 %all_to_all.20.refs_4_ = f32[32,2,128]{2,1,0:T(2,128)S(1)} all-to-all(f32[32,2,128]{2,1,0:T(2,128)S(1)} %get-tuple-element.30), channel_id=1, replica_groups=mesh['ex'=4,'ey'=8] {'ex','ey'}, dimensions={0} | all-to-all | bytes 65536 | tf_op jit(solution)/shard_map/all_to_all | solution.py:754
  40.2 4.9 %shard_map.171 = (f32[512,128]{1,0:T(8,128)S(1)}, f32[512,128]{1,0:T(8,128)S(1)}, f32[256,128]{1,0:T(8,128)S(1)}, f32[256,128]{1,0:T(8,128)S(1)}) custom-call(s32[1]{0:T(128)} %bitcast.slab_ref, f32[256,128]{1,0:T(8,128)S(1)} %collective-permute-done.2.core_ref, f32[256,128]{1,0:T(8,128)S(1)} %collective-permute-done.3.chip_ref, ...), custom_call_target="tpu_custom_call" | custom-call | tf_op jit(solution)/shard_map/pallas_call | solution.py:661
  45.2 0.2 collective-permute-start.4
  45.4 0.6 collective-permute-start.5
  46.0 0.6 collective-permute-done.4.core_ref
  46.6 3.2 %collective-permute-done.5.chip_ref = f32[256,128]{1,0:T(8,128)S(1)} collective-permute-done((f32[256,128]{1,0:T(8,128)S(1)}, f32[256,128]{1,0:T(8,128)S(1)}, u32[]{:S(2)}, u32[]{:S(2)}) %collective-permute-start.5) | collective-permute-done | bytes 131104 | tf_op jit(solution)/shard_map/ppermute | solution.py:750
  49.8 2.9 %shard_map.172 = (f32[512,128]{1,0:T(8,128)S(1)}, f32[512,128]{1,0:T(8,128)S(1)}, f32[32,2,128]{2,1,0:T(2,128)S(1)}, f32[256,128]{1,0:T(8,128)S(1)}, f32[256,128]{1,0:T(8,128)S(1)}) custom-call(s32[1]{0:T(128)} %bitcast.slab_ref, f32[256,128]{1,0:T(8,128)S(1)} %collective-permute-done.4.core_ref, f32[256,128]{1,0:T(8,128)S(1)} %collective-permute-done.5.chip_ref, ...), custom_call_target="tpu_custom_call" | custom-call | tf_op jit(solution)/shard_map/pallas_call | solution.py:661
  52.7 0.5 collective-permute-start.6
  53.1 0.3 collective-permute-start.7
  53.5 8.9 %all_to_all.21.refs_4_ = f32[32,2,128]{2,1,0:T(2,128)S(1)} all-to-all(f32[32,2,128]{2,1,0:T(2,128)S(1)} %get-tuple-element.39), channel_id=1, replica_groups=mesh['ex'=4,'ey'=8] {'ex','ey'}, dimensions={0} | all-to-all | bytes 65536 | tf_op jit(solution)/shard_map/all_to_all | solution.py:754
  62.4 4.4 %shard_map.173 = f32[32,4,512]{2,1,0:T(4,128)} custom-call(s32[1]{0:T(128)} %bitcast.slab_ref, f32[256,128]{1,0:T(8,128)S(1)} %collective-permute-done.6.core_ref, f32[256,128]{1,0:T(8,128)S(1)} %collective-permute-done.7.chip_ref, f32[512,128]{1,0:T(8,128)S(1)} %get-tuple-element.37.g_ref, f32[512,128]{1,0:T(8,128)S(1)} %get-tuple-element.38.x_ref, ...), custom_call_target="tpu_custom_call" | custom-call | tf_op jit(solution)/shard_map/pallas_call | solution.py:661
  66.8 2.6 %all-to-all-start.3 = ((f32[32,4,512]{2,1,0:T(4,128)}), f32[32,4,512]{2,1,0:T(4,128)S(1)}, u32[]{:S(2)}, u32[]{:S(2)}) async-start(f32[32,4,512]{2,1,0:T(4,128)} %shard_map.173), calls=%async_computation.3 | async-start | bytes 524288 | tf_op jit(solution)/shard_map/all_to_all | solution.py:804
  69.4 0.1 pad_add_fusion.place_ref
  69.5 2.5 %shard_map.175 = f32[3,512,128]{2,1,0:T(8,128)} custom-call(s32[2]{0:T(128)S(1)} %pad_add_fusion.place_ref, f32[32,9]{1,0:T(8,128)S(1)} %bitcast.18, f32[2,8,128]{2,1,0:T(8,128)S(1)} %copy-done.10), custom_call_target="tpu_custom_call" | custom-call | tf_op jit(solution)/shard_map/pallas_call | solution.py:661
  71.9 8.1 %all-to-all-done.3.recv_ref = f32[32,4,512]{2,1,0:T(4,128)S(1)} async-done(((f32[32,4,512]{2,1,0:T(4,128)}), f32[32,4,512]{2,1,0:T(4,128)S(1)}, u32[]{:S(2)}, u32[]{:S(2)}) %all-to-all-start.3) | async-done | bytes 262176 | tf_op jit(solution)/shard_map/all_to_all | solution.py:804
  80.0 0.9 %shard_map.174 = f32[512,128]{1,0:T(8,128)} custom-call(f32[32,4,512]{2,1,0:T(4,128)S(1)} %all-to-all-done.3.recv_ref), custom_call_target="tpu_custom_call" | custom-call | tf_op jit(solution)/shard_map/pallas_call | solution.py:661
  (31 shorter events, 0.1 us)
Async XLA Ops:
  0.6 0.7 copy-start.12
  0.6 0.7 copy-start.13
  0.7 0.7 copy-start.14
  1.3 0.9 %copy-start.6 = (f32[8,8,8,1,128]{4,3,2,1,0:T(1,128)S(1)}, f32[8,8,8,1,128]{4,3,2,1,0:T(1,128)}, u32[]{:S(2)}) copy-start(f32[8,8,8,1,128]{4,3,2,1,0:T(1,128)} %param.16) | copy-start | bytes 786436
  2.3 8.5 %copy-start.7 = (f32[512,128]{1,0:T(8,128)S(1)}, f32[512,128]{1,0:T(8,128)}, u32[]{:S(2)}) copy-start(f32[512,128]{1,0:T(8,128)} %constant.48.clone.factor_ref) | copy-start | bytes 786436
  2.3 19.4 %copy-start.1 = (bf16[512,512]{1,0:T(8,128)(2,1)S(1)}, bf16[512,512]{1,0:T(8,128)(2,1)}, u32[]{:S(2)}) copy-start(bf16[512,512]{1,0:T(8,128)(2,1)} %constant.40.clone.high_ref.refs_0_) | copy-start | bytes 1572868
  3.4 18.2 %copy-start = (bf16[512,512]{1,0:T(8,128)(2,1)S(1)}, bf16[512,512]{1,0:T(8,128)(2,1)}, u32[]{:S(2)}) copy-start(bf16[512,512]{1,0:T(8,128)(2,1)} %constant.41.clone.low_ref.refs_1_) | copy-start | bytes 1572868
  3.4 18.0 %all-to-all-start = ((f32[32,4,512]{2,1,0:T(4,128)}), f32[32,4,512]{2,1,0:T(4,128)S(1)}, u32[]{:S(2)}, u32[]{:S(2)}) async-start(f32[32,4,512]{2,1,0:T(4,128)} %shard_map.167), calls=%async_computation | async-start | bytes 524288 | tf_op jit(solution)/shard_map/all_to_all | solution.py:730
  10.8 10.9 %copy-start.11 = (f32[8,8,128]{2,1,0:T(8,128)S(1)}, f32[8,8,128]{2,1,0:T(8,128)}, u32[]{:S(2)}) copy-start(f32[8,8,128]{2,1,0:T(8,128)} %constant.50.clone.dcols_ref) | copy-start | bytes 98308
  21.4 0.7 copy-start.10
  22.1 6.0 %copy-start.9 = (bf16[16,512]{1,0:T(8,128)(2,1)S(1)}, bf16[16,512]{1,0:T(8,128)(2,1)}, u32[]{:S(2)}) copy-start(bf16[16,512]{1,0:T(8,128)(2,1)} %constant.44.clone.interp_ref.refs_4_) | copy-start | bytes 49156
  24.7 3.4 %collective-permute-start.1 = (f32[64,128]{1,0:T(8,128)S(1)}, f32[64,128]{1,0:T(8,128)S(1)}, u32[]{:S(2)}, u32[]{:S(2)}) collective-permute-start(f32[64,128]{1,0:T(8,128)S(1)} %get-tuple-element.22), channel_id=1, source_target_pairs={{8,2},{2,8},{10,4},{4,10},{12,6},{6,12},{14,7},{7,14},{15,5},{5,15... | collective-permute-start | bytes 98312 | tf_op jit(solution)/shard_map/ppermute | solution.py:750
  25.5 2.6 %collective-permute-start = (f32[64,128]{1,0:T(8,128)S(1)}, f32[64,128]{1,0:T(8,128)S(1)}, u32[]{:S(2)}, u32[]{:S(2)}) collective-permute-start(f32[64,128]{1,0:T(8,128)S(1)} %get-tuple-element.22), channel_id=1, source_target_pairs={{0,8},{8,0},{2,10},{10,2},{4,12},{12,4},{6,14},{14,6},{7,15},{15,7... | collective-permute-start | bytes 98312 | tf_op jit(solution)/shard_map/ppermute | solution.py:749
  28.1 12.1 %copy-start.2 = (bf16[128,512]{1,0:T(8,128)(2,1)S(1)}, bf16[128,512]{1,0:T(8,128)(2,1)}, u32[]{:S(2)}) copy-start(bf16[128,512]{1,0:T(8,128)(2,1)} %constant.43.clone.refs_3_) | copy-start | bytes 393220
  28.1 12.1 %copy-start.3 = (bf16[128,512]{1,0:T(8,128)(2,1)S(1)}, bf16[128,512]{1,0:T(8,128)(2,1)}, u32[]{:S(2)}) copy-start(bf16[128,512]{1,0:T(8,128)(2,1)} %constant.42.clone.refs_2_) | copy-start | bytes 393220
  28.1 12.1 %copy-start.4 = (bf16[512,32]{1,0:T(8,128)(2,1)S(1)}, bf16[512,32]{1,0:T(8,128)(2,1)}, u32[]{:S(2)}) copy-start(bf16[512,32]{1,0:T(8,128)(2,1)} %constant.46.clone.refs_5_) | copy-start | bytes 98308
  28.1 12.1 %copy-start.5 = (bf16[512,32]{1,0:T(8,128)(2,1)S(1)}, bf16[512,32]{1,0:T(8,128)(2,1)}, u32[]{:S(2)}) copy-start(bf16[512,32]{1,0:T(8,128)(2,1)} %constant.45.clone.refs_7_) | copy-start | bytes 98308
  29.4 10.8 %collective-permute-start.2 = (f32[256,128]{1,0:T(8,128)S(1)}, f32[256,128]{1,0:T(8,128)S(1)}, u32[]{:S(2)}, u32[]{:S(2)}) collective-permute-start(f32[256,128]{1,0:T(8,128)S(1)} %get-tuple-element.25), channel_id=1, source_target_pairs={{0,8},{8,0},{2,10},{10,2},{4,12},{12,4},{6,14},{14,6},{7,15},{15,7... | collective-permute-start | bytes 393224 | tf_op jit(solution)/shard_map/ppermute | solution.py:749
  29.5 10.7 %collective-permute-start.3 = (f32[256,128]{1,0:T(8,128)S(1)}, f32[256,128]{1,0:T(8,128)S(1)}, u32[]{:S(2)}, u32[]{:S(2)}) collective-permute-start(f32[256,128]{1,0:T(8,128)S(1)} %get-tuple-element.26), channel_id=1, source_target_pairs={{8,2},{2,8},{10,4},{4,10},{12,6},{6,12},{14,7},{7,14},{15,5},{5,15... | collective-permute-start | bytes 393224 | tf_op jit(solution)/shard_map/ppermute | solution.py:750
  30.4 9.9 %copy-start.8 = (bf16[128,32]{1,0:T(8,128)(2,1)S(1)}, bf16[128,32]{1,0:T(8,128)(2,1)}, u32[]{:S(2)}) copy-start(bf16[128,32]{1,0:T(8,128)(2,1)} %constant.47.clone.refs_6_) | copy-start | bytes 24580
  45.2 1.4 %collective-permute-start.4 = (f32[256,128]{1,0:T(8,128)S(1)}, f32[256,128]{1,0:T(8,128)S(1)}, u32[]{:S(2)}, u32[]{:S(2)}) collective-permute-start(f32[256,128]{1,0:T(8,128)S(1)} %get-tuple-element.31), channel_id=1, source_target_pairs={{0,8},{8,0},{2,10},{10,2},{4,12},{12,4},{6,14},{14,6},{7,15},{15,7... | collective-permute-start | bytes 393224 | tf_op jit(solution)/shard_map/ppermute | solution.py:749
  45.4 4.4 %collective-permute-start.5 = (f32[256,128]{1,0:T(8,128)S(1)}, f32[256,128]{1,0:T(8,128)S(1)}, u32[]{:S(2)}, u32[]{:S(2)}) collective-permute-start(f32[256,128]{1,0:T(8,128)S(1)} %get-tuple-element.32), channel_id=1, source_target_pairs={{8,2},{2,8},{10,4},{4,10},{12,6},{6,12},{14,7},{7,14},{15,5},{5,15... | collective-permute-start | bytes 393224 | tf_op jit(solution)/shard_map/ppermute | solution.py:750
  52.7 9.7 %collective-permute-start.6 = (f32[256,128]{1,0:T(8,128)S(1)}, f32[256,128]{1,0:T(8,128)S(1)}, u32[]{:S(2)}, u32[]{:S(2)}) collective-permute-start(f32[256,128]{1,0:T(8,128)S(1)} %get-tuple-element.35), channel_id=1, source_target_pairs={{0,8},{8,0},{2,10},{10,2},{4,12},{12,4},{6,14},{14,6},{7,15},{15,7... | collective-permute-start | bytes 393224 | tf_op jit(solution)/shard_map/ppermute | solution.py:749
  53.1 9.3 %collective-permute-start.7 = (f32[256,128]{1,0:T(8,128)S(1)}, f32[256,128]{1,0:T(8,128)S(1)}, u32[]{:S(2)}, u32[]{:S(2)}) collective-permute-start(f32[256,128]{1,0:T(8,128)S(1)} %get-tuple-element.36), channel_id=1, source_target_pairs={{8,2},{2,8},{10,4},{4,10},{12,6},{6,12},{14,7},{7,14},{15,5},{5,15... | collective-permute-start | bytes 393224 | tf_op jit(solution)/shard_map/ppermute | solution.py:750
  66.8 13.2 %all-to-all-start.3 = ((f32[32,4,512]{2,1,0:T(4,128)}), f32[32,4,512]{2,1,0:T(4,128)S(1)}, u32[]{:S(2)}, u32[]{:S(2)}) async-start(f32[32,4,512]{2,1,0:T(4,128)} %shard_map.173), calls=%async_computation.3 | async-start | bytes 524288 | tf_op jit(solution)/shard_map/all_to_all | solution.py:804

commit v4 on v3

--- a/solution.py
+++ b/solution.py
@@ -133,6 +133,32 @@
     return jnp.concatenate([high, low, high, low], 0).astype(BF16)
 
 
+def subtract_stiffness(lay, one, u_ref, g_ref, high_ref, low_ref, along_ref):
+    matrix, weights = one
+    dot = functools.partial(jnp.dot, preferred_element_type=F32)
+    half = N // 2
+    for first in (0, half):
+        scaled = [
+            float(weights[i]) * u_ref[pl.ds(i * FACE, FACE), :] for i in range(first, first + half)
+        ]
+        xh, xl = split(jnp.concatenate(scaled, 0))
+        both = dot(high_ref[...], jnp.concatenate([xh, xl], 1))
+        rows = pl.ds(first * FACE, half * FACE)
+        g_ref[rows, :] -= both[:, : lay.width] + both[:, lay.width :] + dot(low_ref[...], xh)
+    even = 0.5 * (matrix[:half, :half] + matrix[:half, :half - 1 : -1])
+    odd = 0.5 * (matrix[:half, :half] - matrix[:half, :half - 1 : -1])
+    for j in range(N):
+        values = [u_ref[pl.ds((i * N + j) * N, N), :] for i in range(N)]
+        sums = [values[i] + values[N - 1 - i] for i in range(half)]
+        gaps = [values[i] - values[N - 1 - i] for i in range(half)]
+        along = along_ref[pl.ds(j * N, N), :]
+        for i in range(half):
+            a = sum(float(even[i, q]) * sums[q] for q in range(half))
+            b = sum(float(odd[i, q]) * gaps[q] for q in range(half))
+            g_ref[pl.ds((i * N + j) * N, N), :] -= along * (a + b)
+            g_ref[pl.ds(((N - 1 - i) * N + j) * N, N), :] -= along * (a - b)
+
+
 def roll(x, shift, axis):
     size = x.shape[axis]
     return pltpu.roll(x, shift % size, axis)
@@ -289,6 +315,14 @@
         out_ref[d, 1:2, :] = jnp.where(used, points, out_ref[d, 1:2, :])
 
 
+def column(values, shape):
+    node = lax.broadcasted_iota(jnp.int32, shape, 0)
+    out = jnp.full(shape, float(values[0]), F32)
+    for n in range(1, N):
+        out = jnp.where(node == n, float(values[n]), out)
+    return out
+
+
 def gauss(elem, base, position, half_nodes):
     node = lax.broadcasted_iota(jnp.int32, elem.shape, 0)
     elem = elem.astype(F32)
@@ -302,24 +336,42 @@
     return jnp.where(inside, jnp.exp(-(away * away) / (WIDTH_EPS * WIDTH_EPS)), 0.0)
 
 
-def right_side(lay, num_points, slab_ref, points_ref, nodes_ref, dcols_ref, g_ref, halo_ref):
+def point_values(points_ref, row, place, scale):
+    base, offset, force = (
+        [points_ref[row, (place * 9 + c * 3 + d) * N] for d in range(3)] for c in range(3)
+    )
+    return base, [b + 1.0 + o for b, o in zip(base, offset)], [scale * f for f in force]
+
+
+def for_points(points_ref, local_points, visit):
+    def row_of(row, _):
+        for place in range(local_points):
+            visit(row, place)
+        return 0
+
+    lax.fori_loop(0, points_ref.shape[0], row_of, 0)
+
+
+def right_side(lay, local_points, one, slab_ref, points_ref, g_ref, halo_ref):
+    derivative, weights = one
     shape = (N, lay.width)
     part_x, part_y, part_z = lane_parts(lay, shape)
     first_z = slab_ref[0] * lay.depth
     elem_z = first_z + part_z
     elem_halo = jnp.where(part_z == 0, first_z - 1, first_z + lay.depth)
+    half_nodes = column(0.5 * (1.0 + GLL_POINTS), shape)
+    weight = column(weights, shape)
+    columns = [column(derivative[a], shape) for a in range(N)]
 
     def weighted(elem, base, position):
-        plain = nodes_ref[1] * gauss(elem, base, position, nodes_ref[0])
-        deriv = dcols_ref[0] * plain[0:1]
-        for a in range(1, N):
-            deriv = deriv + dcols_ref[a] * plain[a : a + 1]
-        return plain, deriv
-
-    def one(p, _):
-        base = [points_ref[p, d] for d in range(3)]
-        position = [points_ref[p, d] + 1.0 + points_ref[p, 3 + d] for d in range(3)]
-        force = [points_ref[p, 6 + d] * (0.25 * GAUSS_NORM) for d in range(3)]
+        plain = weight * gauss(elem, base, position, half_nodes)
+        terms = [columns[a] * plain[a : a + 1] for a in range(N)]
+        while len(terms) > 1:
+            terms = [a + b for a, b in zip(terms[::2], terms[1::2])]
+        return plain, terms[0]
+
+    def visit(p, place):
+        base, position, force = point_values(points_ref, p, place, 0.25 * GAUSS_NORM)
         first = first_z.astype(F32)
 
         @pl.when((base[2] + 2.0 >= first - 1.0) & (base[2] - 1.0 <= first + lay.depth))
@@ -346,9 +398,7 @@
                 rows = pl.ds(i * N, N)
                 halo_ref[rows, :] += x1[i : i + 1] * first_part + x0[i : i + 1] * other_part
 
-        return 0
-
-    lax.fori_loop(0, num_points, one, 0)
+    for_points(points_ref, local_points, visit)
 
 
 def inverse_diagonal(lay, slab_ref, factor_ref, dinv_ref, outer):
@@ -388,23 +438,30 @@
 
 def first_kernel(
     lay,
-    num_points,
+    local_points,
+    derivative,
+    one,
     slab_ref,
-    points_ref,
     recv_ref,
-    nodes_ref,
-    dcols_ref,
     dinv_ref,
     high_ref,
     low_ref,
+    along_ref,
     g_ref,
     x_ref,
     face_ref,
+    points_ref,
     s_ref,
     halo_ref,
     flat_ref,
+    table_ref,
+    sem,
 ):
     count, block = recv_ref.shape[0], recv_ref.shape[1]
+    for d in range(count):
+        points_ref[pl.ds(d, 1), :] = recv_ref[d, 1:2, : points_ref.shape[1]]
+    copy = pltpu.make_async_copy(points_ref, table_ref, sem)
+    copy.start()
     for d in range(count):
         flat_ref[pl.ds(d * block, block), :] = recv_ref[d]
     g_ref[...] = flat_ref[...].T
@@ -412,11 +469,11 @@
     _, _, part_z = lane_parts(lay, low.shape)
     set_rows(g_ref, 0, jnp.where(part_z == 0, low, roll(high, 1, 1)))
     halo_ref[...] = jnp.where(part_z == 0, low, high)
-    right_side(lay, num_points, slab_ref, points_ref, nodes_ref, dcols_ref, g_ref, halo_ref)
+    copy.wait()
+    right_side(lay, local_points, (derivative, one[1]), slab_ref, table_ref, g_ref, halo_ref)
     assemble(lay, g_ref, s_ref, halo_ref[...])
-    update = (1.0 / THETA) * dinv_ref[...] * s_ref[...]
-    x_ref[...] = update
-    g_ref[...] = g_ref[...] - times3(high_ref[...], low_ref[...], update)
+    x_ref[...] = (1.0 / THETA) * dinv_ref[...] * s_ref[...]
+    subtract_stiffness(lay, one, x_ref, g_ref, high_ref, low_ref, along_ref)
     store_faces(lay, g_ref, face_ref)
 
 
@@ -441,6 +498,7 @@
 
 def second_kernel(
     lay,
+    one,
     slab_ref,
     core_ref,
     chip_ref,
@@ -449,6 +507,7 @@
     dinv_ref,
     high_ref,
     low_ref,
+    along_ref,
     interp_ref,
     g_out,
     x_out,
@@ -456,11 +515,14 @@
     core_out,
     chip_out,
     s_ref,
+    u_ref,
 ):
     assemble(lay, g_ref, s_ref, halo_of(lay, slab_ref, core_ref, chip_ref))
     update = OLD * x_ref[...] + NEW * dinv_ref[...] * s_ref[...]
+    u_ref[...] = update
     x_out[...] = x_ref[...] + update
-    g_out[...] = g_ref[...] - times3(high_ref[...], low_ref[...], update)
+    g_out[...] = g_ref[...]
+    subtract_stiffness(lay, one, u_ref, g_out, high_ref, low_ref, along_ref)
     restriction(lay, g_out, dinv_ref, interp_ref, send_ref)
     send_layers(lay, slab_ref, g_out, s_ref, core_out, chip_out)
 
@@ -479,6 +541,9 @@
     def below(v):
         return jnp.where(bottom, roll(roll(v, 1, 0), -1, 1), roll(v, 1, 1))
 
+    def around_z(v):
+        return jnp.where(bottom, roll(v + roll(v, 1, 0), -1, 1), roll(v + roll(v, -1, 0), 1, 1))
+
     def above(v):
         return jnp.where(bottom, roll(v, -1, 1), roll(roll(v, -1, 0), 1, 1))
 
@@ -489,7 +554,7 @@
         return (2.0 * pair[0]) * v + pair[1] * around
 
     def operate(v):
-        around = below(v) + above(v)
+        around = around_z(v)
         mass_z, stiff_z = mix(mass, v, around), mix(stiff, v, around)
         around = neighbours(mass_z, lay.step_y)
         both = mix(mass, mass_z, around)
@@ -504,18 +569,28 @@
 
     here = pl.ds(0, lay.slabs)
     residual = keep * (first_ref[here, :] + below(second_ref[here, :]))
-    direction = residual
+    image = operate(residual)
     total = jnp.zeros(shape, F32)
-    norm = inner(residual, residual)
     for step in range(CG_STEPS):
-        image = operate(direction)
-        alpha = norm / inner(direction, image)
+        last = step + 1 == CG_STEPS
+        norm, curv = inner(residual, residual), inner(image, residual)
+        if not last:
+            second = operate(image)
+        if step == 0:
+            alpha = norm / curv
+            direction, moved = residual, image
+            if not last:
+                moved_image = second
+        else:
+            beta = norm / norm_old
+            alpha = norm / (curv - beta * norm / alpha)
+            direction = residual + beta * direction
+            if not last:
+                moved, moved_image = image + beta * moved, second + beta * moved_image
+        norm_old = norm
         total = total + alpha * direction
-        if step + 1 < CG_STEPS:
-            residual = residual - alpha * image
-            following = inner(residual, residual)
-            direction = residual + (following / norm) * direction
-            norm = following
+        if not last:
+            residual, image = residual - alpha * moved, image - alpha * moved_image
     here = pl.ds(N, lay.slabs)
     for ref, value in ((first_ref, total), (second_ref, above(total))):
         ref[...] = jnp.zeros(ref.shape, F32)
@@ -554,9 +629,9 @@
     set_rows(h_ref, N - 1, high - jnp.where(bottom, 0.0, edge[:FACE]))
 
 
-def pair_kernel(lay, coarse, kind, slab_ref, core_ref, chip_ref, g_ref, x_ref, dinv_ref, outer_ref, *refs):
+def pair_kernel(lay, one, coarse, kind, slab_ref, core_ref, chip_ref, g_ref, x_ref, dinv_ref, outer_ref, *refs):
     refs = list(refs)
-    high_ref, low_ref, edge_high_ref, edge_low_ref = (refs.pop(0) for _ in range(4))
+    high_ref, low_ref, along_ref, edge_high_ref, edge_low_ref = (refs.pop(0) for _ in range(5))
     if coarse:
         loads_ref, image_ref, image_edge_ref = (refs.pop(0) for _ in range(3))
     if coarse or kind == "restrict":
@@ -568,7 +643,7 @@
         if kind == "restrict":
             send_ref = refs.pop(0)
         core_out, chip_out = refs.pop(0), refs.pop(0)
-    s_ref, sh_ref, h_ref = (refs.pop(0) for _ in range(3))
+    s_ref, sh_ref, h_ref, u_ref = (refs.pop(0) for _ in range(4))
     if kind == "last":
         g_out, x_out = refs.pop(0), refs.pop(0)
 
@@ -583,15 +658,16 @@
         )
     assemble_both(lay, g_out, h_ref, s_ref, sh_ref)
     update = (1.0 / THETA) * dinv_ref[...] * s_ref[...]
+    u_ref[...] = update
     outer = (1.0 / THETA) * outer_ref[...] * sh_ref[...]
-    high, low = high_ref[...], low_ref[...]
     edge = times3(edge_high_ref[...], edge_low_ref[...], outer)
     _, _, part_z = lane_parts(lay, (FACE, lay.width))
     near = jnp.where(
         part_z == 0, get_rows(h_ref, N - 1) - edge[FACE:], get_rows(h_ref, 0) - edge[:FACE]
     )
-    g_out[...] -= times3(high, low, update)
+    subtract_stiffness(lay, one, u_ref, g_out, high_ref, low_ref, along_ref)
     assemble(lay, g_out, s_ref, near)
+    update = u_ref[...]
     following = OLD * update + NEW * dinv_ref[...] * s_ref[...]
     if kind == "last":
         total = (x_out[...] + (update + following)).T
@@ -600,7 +676,8 @@
             out_ref[d] = total[d * block : (d + 1) * block]
         return
     x_out[...] += update + following
-    g_out[...] -= times3(high, low, following)
+    u_ref[...] = following
+    subtract_stiffness(lay, one, u_ref, g_out, high_ref, low_ref, along_ref)
     if kind == "restrict":
         restriction(lay, g_out, dinv_ref, interp_ref, send_ref)
     send_layers(lay, slab_ref, g_out, s_ref, core_out, chip_out)
@@ -615,20 +692,18 @@
     out_ref[...] = flat_ref[...].T
 
 
-def forces_kernel(tiles_y, num_points, place_ref, points_ref, nodes_ref, out_ref):
-    width = tiles_y * EZ
-    shape = (N, width)
+def forces_kernel(tiles_y, local_points, place_ref, points_ref, out_ref):
+    shape = (N, tiles_y * EZ)
     lane = lax.broadcasted_iota(jnp.int32, shape, 1)
     first_x, first_y = place_ref[0], place_ref[1]
     elem_x = jnp.broadcast_to(first_x, shape)
     elem_y = first_y + lax.shift_right_logical(lane, log2(EZ))
     elem_z = lane & (EZ - 1)
+    half_nodes = column(0.5 * (1.0 + GLL_POINTS), shape)
     out_ref[...] = jnp.zeros(out_ref.shape, F32)
 
-    def one(p, _):
-        base = [points_ref[p, d] for d in range(3)]
-        position = [points_ref[p, d] + 1.0 + points_ref[p, 3 + d] for d in range(3)]
-        force = [points_ref[p, 6 + d] * GAUSS_NORM for d in range(3)]
+    def visit(p, place):
+        base, position, force = point_values(points_ref, p, place, GAUSS_NORM)
         low_x, low_y = first_x.astype(F32), first_y.astype(F32)
 
         @pl.when(
@@ -638,9 +713,9 @@
             & (base[1] - 1.0 <= low_y + (tiles_y - 1))
         )
         def _():
-            x = gauss(elem_x, base[0], position[0], nodes_ref[0])
-            y = gauss(elem_y, base[1], position[1], nodes_ref[0])
-            z = gauss(elem_z, base[2], position[2], nodes_ref[0])
+            x = gauss(elem_x, base[0], position[0], half_nodes)
+            y = gauss(elem_y, base[1], position[1], half_nodes)
+            z = gauss(elem_z, base[2], position[2], half_nodes)
             for j in range(N):
                 plane = y[j : j + 1] * z
                 for i in range(N):
@@ -649,9 +724,7 @@
                     for c in range(3):
                         out_ref[c, rows, :] += force[c] * value
 
-        return 0
-
-    lax.fori_loop(0, num_points, one, 0)
+    for_points(points_ref, local_points, visit)
 
 
 def call(kernel, outs, inputs, scratch=(), smem=0, spaces=None):
@@ -682,29 +755,26 @@
         + kron3(diag_w, stiff_one, diag_w)
         + kron3(diag_w, diag_w, stiff_one)
     )
-    full_high, full_low = split_table(full)
+    edge_rows = np.concatenate([np.arange(FACE) * N, np.arange(FACE) * N + N - 1])
+    plane = 0.5 * (np.kron(stiff_one, diag_w) + np.kron(diag_w, stiff_one))
+    high, low = (jnp.asarray(t) for t in split_table(np.kron(np.eye(N // 2), plane)))
+    along = np.broadcast_to(0.5 * np.kron(weights, weights)[:, None], (FACE, width))
+    along = jnp.asarray(along, F32)
+    edge_high, edge_low = (jnp.asarray(t) for t in split_table(full[edge_rows]))
+    one = (stiff_one, weights)
     interp3 = kron3(interp, interp, interp)
     image3 = full @ interp3
     ratio = (weights[:, None] * derivative**2).sum(axis=0) / weights
     diag = 0.5 * (ratio[:, None, None] + ratio[None, :, None] + ratio[None, None, :])
     diag = diag * weights[:, None, None] * weights[None, :, None] * weights[None, None, :]
     factor = np.broadcast_to(1.0 / diag.reshape(N**3, 1), fields)
-    nodes = np.stack([0.5 * (1.0 + GLL_POINTS), weights])
-    nodes_wide = np.broadcast_to(nodes[:, :, None], (2, N, width))
-    nodes_local = np.broadcast_to(nodes[:, :, None], (2, N, tiles_y * EZ))
-    dcols = np.broadcast_to(derivative[:, :, None], (N, N, width))
     mass = interp.T @ diag_w @ interp
     stiff = interp.T @ stiff_one @ interp
-    edge_rows = np.concatenate([np.arange(FACE) * N, np.arange(FACE) * N + N - 1])
-    high, low = jnp.asarray(full_high), jnp.asarray(full_low)
-    edge_high, edge_low = jnp.asarray(full_high[edge_rows]), jnp.asarray(full_low[edge_rows])
     restrict3 = jnp.asarray(np.concatenate(split_table(interp3.T), 0))
     prolong3, image3, image_edge = (
         jnp.asarray(stacked_table(t)) for t in (interp3, image3, image3[edge_rows])
     )
-    factor, nodes_wide, nodes_local, dcols = (
-        jnp.asarray(t, F32) for t in (factor, nodes_wide, nodes_local, dcols)
-    )
+    factor = jnp.asarray(factor, F32)
 
     slab = lay.slab_at(lax.axis_index(lay.axis).astype(jnp.int32)).reshape(1)
     place = jnp.stack([lax.axis_index("ex") * tiles_x, lax.axis_index("ey") * tiles_y]).astype(
@@ -725,23 +795,13 @@
             (tiles_y * EZ, N**3),
             pltpu.SemaphoreType.DMA((4,)),
         ],
-        spaces=[pl.ANY] * 4,
+        spaces=[pltpu.HBM] * 4,
     )
     recv = lax.all_to_all(send, lay.axis, 0, 0)
     if not lay.joint:
         recv = lax.all_gather(recv, "ex", axis=0, tiled=True)
-    points = recv[:, 1, : 9 * N * local_points : N]
-    num_points = devices * local_points
-    points = points.reshape(num_points, 9)
     dinv, outer = call(
         functools.partial(diagonal_kernel, lay), [fields, fields], [slab, factor], smem=1
-    )
-
-    (forces,) = call(
-        functools.partial(forces_kernel, tiles_y, num_points),
-        [(3, N**3, tiles_y * EZ)],
-        [place, points, nodes_local],
-        smem=2,
     )
 
     def swap(core, chip):
@@ -756,33 +816,40 @@
     face_shape = (FACE, width)
     layer = (N**3 // 2, width)
     loads_shape = (lay.slabs, 2, width)
-    g, x, face = call(
-        functools.partial(first_kernel, lay, num_points),
-        [fields, fields, face_shape],
-        [slab, points, recv, nodes_wide, dcols, dinv, high, low],
-        [fields, face_shape, (width, N**3)],
+    table = (devices, -(-9 * N * local_points // 128) * 128)
+    g, x, face, points = call(
+        functools.partial(first_kernel, lay, local_points, derivative, one),
+        [fields, fields, face_shape, table],
+        [slab, recv, dinv, high, low, along],
+        [fields, face_shape, (width, N**3), pltpu.SMEM(table, F32), pltpu.SemaphoreType.DMA],
+        smem=1,
+    )
+    (forces,) = call(
+        functools.partial(forces_kernel, tiles_y, local_points),
+        [(3, N**3, tiles_y * EZ)],
+        [place, points],
         smem=2,
     )
     g, x, loads, core, chip = call(
-        functools.partial(second_kernel, lay),
+        functools.partial(second_kernel, lay, one),
         [fields, fields, loads_shape, layer, layer],
-        [slab, *swap(face, face), g, x, dinv, high, low, restrict3],
-        [fields],
+        [slab, *swap(face, face), g, x, dinv, high, low, along, restrict3],
+        [fields, fields],
         smem=1,
     )
     coarse = ((mass[0, 0], mass[0, 1]), (stiff[0, 0], stiff[0, 1]))
-    stiffness = [high, low, edge_high, edge_low]
+    stiffness = [high, low, along, edge_high, edge_low]
 
     for cycle in range(CYCLES):
         core, chip = swap(core, chip)
         last = cycle + 1 == CYCLES
         outs = [fields, fields, layer, layer]
-        scratch = [fields, fields, fields]
+        scratch = [fields] * 4
         if last:
             outs = [(lay.mesh_x * lay.mesh_y, block, N**3)]
             scratch += [fields, fields]
         outs = call(
-            functools.partial(pair_kernel, lay, coarse, "last" if last else "plain"),
+            functools.partial(pair_kernel, lay, one, coarse, "last" if last else "plain"),
             outs,
             [slab, core, chip, g, x, dinv, outer, *stiffness, gather(loads), image3, image_edge, prolong3],
             scratch + [(lay.slabs + 2 * N, width)] * 2,
@@ -792,10 +859,10 @@
             break
         g, x, core, chip = outs
         g, x, loads, core, chip = call(
-            functools.partial(pair_kernel, lay, None, "restrict"),
+            functools.partial(pair_kernel, lay, one, None, "restrict"),
             [fields, fields, loads_shape, layer, layer],
             [slab, *swap(core, chip), g, x, dinv, outer, *stiffness, restrict3],
-            [fields, fields, fields],
+            [fields] * 4,
             smem=1,
         )
     (out,) = outs

time: 81.4 us -> 76.6 us (0.941)
  Pallas kernels: 20.6 us -> 17.2 us
    pallas_call x9, Pallas kernels: 20.6 us -> 17.2 us  [call(): pl.pallas_call(kernel, out_shape=shapes, in_specs=specs, out_specs=[pl.Bl...]
    unnamed x30 -> x28, local copies, waits for them, and re-layouts: 2.07 us -> 1.67 us
  transfers between devices with their start and end apart: 10 -> 10, of which waited for: 5 -> 5; matrix products, arithmetic and copies ran while one was open for 0% -> 0% of each run, Pallas kernels for 3% -> 4%
where the time goes in v4:
time: 76.6 us; the launch traced here: 76.4 us
  waiting for transfers between devices  24 us (31%)
  blocking collectives  19 us (25%)
  Pallas kernels  17.2 us (22%)
  starting transfers between devices  13.6 us (18%)
  local copies, waits for them, and re-layouts  1.67 us (2%)
  between operations  0.87 us (1%)
    all_to_all x2, blocking collectives, gather(): return lax.all_to_all(loads, lay.axis, 0, 0)  19 us
    pallas_call x9, Pallas kernels, call(): pl.pallas_call(kernel, out_shape=shapes, in_specs=specs, out_specs=[pl.Bl...  17.2 us
    all_to_all x1, waiting for transfers between devices, shards(): recv = lax.all_to_all(send, lay.axis, 0, 0)  10.5 us
    all_to_all x1, waiting for transfers between devices, shards(): out = lax.all_to_all(out, lay.axis, 0, 0)  7.69 us
    all_to_all x1, starting transfers between devices, shards(): recv = lax.all_to_all(send, lay.axis, 0, 0)  7.3 us
    ppermute x4, waiting for transfers between devices, swap(): lax.ppermute(chip, lay.axis, lay.swaps(1))  5.19 us
    all_to_all x1, starting transfers between devices, shards(): out = lax.all_to_all(out, lay.axis, 0, 0)  2.59 us
    ppermute x4, starting transfers between devices, swap(): lax.ppermute(chip, lay.axis, lay.swaps(1))  2.17 us
  transfers between devices with their start and end apart: 10, of which 5 were waited for; matrix products, arithmetic and copies ran while one was open for 0% of the time, Pallas kernels for 4%

profile of v4, /device:TPU:0, one launch (start us, length us, event | category | flops | bytes accessed | tf_op | source)
XLA Modules:
  0.0 76.4 jit_solution(8501498750982238030)
XLA Ops:
  0.7 0.6 copy-done.11
  1.3 0.0 copy-done.12
  1.3 0.0 copy-done.13
  1.3 0.9 %copy-done.7 = f32[8,8,8,1,128]{4,3,2,1,0:T(1,128)S(1)} copy-done((f32[8,8,8,1,128]{4,3,2,1,0:T(1,128)S(1)}, f32[8,8,8,1,128]{4,3,2,1,0:T(1,128)}, u32[]{:S(2)}) %copy-start.7) | copy-done | bytes 262168
  2.3 1.1 %shard_map.149 = f32[32,4,512]{2,1,0:T(4,128)} custom-call(s32[1,3]{1,0:T(1,128)S(1)} %bitcast.14, f32[1,3]{1,0:T(1,128)S(1)} %bitcast.15, f32[1,3]{1,0:T(1,128)S(1)} %bitcast.16, f32[512,128]{1,0:T(8,128)S(1)} %bitcast.13), custom_call_target="tpu_custom_call" | custom-call | tf_op jit(solution)/shard_map/pallas_call | solution.py:734
  3.4 0.0 copy-start.8
  3.4 7.3 %all-to-all-start = ((f32[32,4,512]{2,1,0:T(4,128)}), f32[32,4,512]{2,1,0:T(4,128)S(1)}, u32[]{:S(2)}, u32[]{:S(2)}) async-start(f32[32,4,512]{2,1,0:T(4,128)} %shard_map.149), calls=%async_computation | async-start | bytes 524288 | tf_op jit(solution)/shard_map/all_to_all | solution.py:800
  10.8 0.1 shard_map.150
  10.9 10.5 %all-to-all-done.recv_ref = f32[32,4,512]{2,1,0:T(4,128)S(1)} async-done(((f32[32,4,512]{2,1,0:T(4,128)}), f32[32,4,512]{2,1,0:T(4,128)S(1)}, u32[]{:S(2)}, u32[]{:S(2)}) %all-to-all-start) | async-done | bytes 262176 | tf_op jit(solution)/shard_map/all_to_all | solution.py:800
  21.4 2.4 %shard_map.151 = (f32[512,128]{1,0:T(8,128)S(1)}, f32[512,128]{1,0:T(8,128)S(1)}, f32[64,128]{1,0:T(8,128)S(1)}, f32[32,128]{1,0:T(8,128)S(1)}) custom-call(s32[1]{0:T(128)} %bitcast.slab_ref, f32[32,4,512]{2,1,0:T(4,128)S(1)} %all-to-all-done.recv_ref, f32[512,128]{1,0:T(8,128)S(1)} %get-tuple-element.22.dinv_ref, bf16[256,256]{1,0:T(8,128)(2,1)S(1)} %copy-done.1, ...), custom_call_target="tpu_custom_call" | custom-call | tf_op jit(solution)/shard_map/pallas_call | solution.py:734
  23.8 0.6 collective-permute-start.1
  24.5 0.8 collective-permute-start
  25.2 2.0 %collective-permute-done.1.chip_ref = f32[64,128]{1,0:T(8,128)S(1)} collective-permute-done((f32[64,128]{1,0:T(8,128)S(1)}, f32[64,128]{1,0:T(8,128)S(1)}, u32[]{:S(2)}, u32[]{:S(2)}) %collective-permute-start.1) | collective-permute-done | bytes 32800 | tf_op jit(solution)/shard_map/ppermute | solution.py:810
  27.3 0.9 %shard_map.152 = (f32[512,128]{1,0:T(8,128)S(1)}, f32[512,128]{1,0:T(8,128)S(1)}, f32[32,2,128]{2,1,0:T(2,128)S(1)}, f32[256,128]{1,0:T(8,128)S(1)}, f32[256,128]{1,0:T(8,128)S(1)}) custom-call(s32[1]{0:T(128)} %bitcast.slab_ref, f32[64,128]{1,0:T(8,128)S(1)} %collective-permute-done.core_ref, f32[64,128]{1,0:T(8,128)S(1)} %collective-permute-done.1.chip_ref, ...), custom_call_target="tpu_custom_call" | custom-call | tf_op jit(solution)/shard_map/pallas_call | solution.py:734
  28.2 0.2 collective-permute-start.2
  28.4 0.6 collective-permute-start.3
  29.0 10.0 %all_to_all.20.refs_5_ = f32[32,2,128]{2,1,0:T(2,128)S(1)} all-to-all(f32[32,2,128]{2,1,0:T(2,128)S(1)} %get-tuple-element.31), channel_id=1, replica_groups=mesh['ex'=4,'ey'=8] {'ex','ey'}, dimensions={0} | all-to-all | bytes 65536 | tf_op jit(solution)/shard_map/all_to_all | solution.py:814
  39.1 3.4 %shard_map.153 = (f32[512,128]{1,0:T(8,128)S(1)}, f32[512,128]{1,0:T(8,128)S(1)}, f32[256,128]{1,0:T(8,128)S(1)}, f32[256,128]{1,0:T(8,128)S(1)}) custom-call(s32[1]{0:T(128)} %bitcast.slab_ref, f32[256,128]{1,0:T(8,128)S(1)} %collective-permute-done.2.core_ref, f32[256,128]{1,0:T(8,128)S(1)} %collective-permute-done.3.chip_ref, ...), custom_call_target="tpu_custom_call" | custom-call | tf_op jit(solution)/shard_map/pallas_call | solution.py:734
  42.5 0.2 collective-permute-start.4
  42.7 0.6 collective-permute-start.5
  43.3 0.6 collective-permute-done.4.core_ref
  44.0 3.2 %collective-permute-done.5.chip_ref = f32[256,128]{1,0:T(8,128)S(1)} collective-permute-done((f32[256,128]{1,0:T(8,128)S(1)}, f32[256,128]{1,0:T(8,128)S(1)}, u32[]{:S(2)}, u32[]{:S(2)}) %collective-permute-start.5) | collective-permute-done | bytes 131104 | tf_op jit(solution)/shard_map/ppermute | solution.py:810
  47.1 1.7 %shard_map.154 = (f32[512,128]{1,0:T(8,128)S(1)}, f32[512,128]{1,0:T(8,128)S(1)}, f32[32,2,128]{2,1,0:T(2,128)S(1)}, f32[256,128]{1,0:T(8,128)S(1)}, f32[256,128]{1,0:T(8,128)S(1)}) custom-call(s32[1]{0:T(128)} %bitcast.slab_ref, f32[256,128]{1,0:T(8,128)S(1)} %collective-permute-done.4.core_ref, f32[256,128]{1,0:T(8,128)S(1)} %collective-permute-done.5.chip_ref, ...), custom_call_target="tpu_custom_call" | custom-call | tf_op jit(solution)/shard_map/pallas_call | solution.py:734
  48.8 0.5 collective-permute-start.6
  49.3 0.3 collective-permute-start.7
  49.6 8.9 %all_to_all.21.refs_5_ = f32[32,2,128]{2,1,0:T(2,128)S(1)} all-to-all(f32[32,2,128]{2,1,0:T(2,128)S(1)} %get-tuple-element.40), channel_id=1, replica_groups=mesh['ex'=4,'ey'=8] {'ex','ey'}, dimensions={0} | all-to-all | bytes 65536 | tf_op jit(solution)/shard_map/all_to_all | solution.py:814
  58.6 3.7 %shard_map.155 = f32[32,4,512]{2,1,0:T(4,128)} custom-call(s32[1]{0:T(128)} %bitcast.slab_ref, f32[256,128]{1,0:T(8,128)S(1)} %collective-permute-done.6.core_ref, f32[256,128]{1,0:T(8,128)S(1)} %collective-permute-done.7.chip_ref, f32[512,128]{1,0:T(8,128)S(1)} %get-tuple-element.38.g_ref, f32[512,128]{1,0:T(8,128)S(1)} %get-tuple-element.39.x_ref, ...), custom_call_target="tpu_custom_call" | custom-call | tf_op jit(solution)/shard_map/pallas_call | solution.py:734
  62.3 2.6 %all-to-all-start.3 = ((f32[32,4,512]{2,1,0:T(4,128)}), f32[32,4,512]{2,1,0:T(4,128)S(1)}, u32[]{:S(2)}, u32[]{:S(2)}) async-start(f32[32,4,512]{2,1,0:T(4,128)} %shard_map.155), calls=%async_computation.3 | async-start | bytes 524288 | tf_op jit(solution)/shard_map/all_to_all | solution.py:871
  64.9 0.1 pad_add_fusion.place_ref
  65.0 2.9 %shard_map.157 = f32[3,512,128]{2,1,0:T(8,128)} custom-call(s32[2]{0:T(128)S(1)} %pad_add_fusion.place_ref, f32[32,128]{1,0:T(8,128)S(1)} %get-tuple-element.41.points_ref), custom_call_target="tpu_custom_call" | custom-call | tf_op jit(solution)/shard_map/pallas_call | solution.py:734
  67.8 7.7 %all-to-all-done.3.recv_ref = f32[32,4,512]{2,1,0:T(4,128)S(1)} async-done(((f32[32,4,512]{2,1,0:T(4,128)}), f32[32,4,512]{2,1,0:T(4,128)S(1)}, u32[]{:S(2)}, u32[]{:S(2)}) %all-to-all-start.3) | async-done | bytes 262176 | tf_op jit(solution)/shard_map/all_to_all | solution.py:871
  75.5 0.9 %shard_map.156 = f32[512,128]{1,0:T(8,128)} custom-call(f32[32,4,512]{2,1,0:T(4,128)S(1)} %all-to-all-done.3.recv_ref), custom_call_target="tpu_custom_call" | custom-call | tf_op jit(solution)/shard_map/pallas_call | solution.py:734
  (28 shorter events, 0.1 us)
Async XLA Ops:
  0.6 0.7 copy-start.11
  0.6 0.7 copy-start.12
  0.7 0.7 copy-start.13
  1.3 0.9 %copy-start.7 = (f32[8,8,8,1,128]{4,3,2,1,0:T(1,128)S(1)}, f32[8,8,8,1,128]{4,3,2,1,0:T(1,128)}, u32[]{:S(2)}) copy-start(f32[8,8,8,1,128]{4,3,2,1,0:T(1,128)} %param.14) | copy-start | bytes 786436
  3.4 7.4 %copy-start.8 = (f32[512,128]{1,0:T(8,128)S(1)}, f32[512,128]{1,0:T(8,128)}, u32[]{:S(2)}) copy-start(f32[512,128]{1,0:T(8,128)} %constant.47.clone.factor_ref) | copy-start | bytes 786436
  3.4 18.0 %all-to-all-start = ((f32[32,4,512]{2,1,0:T(4,128)}), f32[32,4,512]{2,1,0:T(4,128)S(1)}, u32[]{:S(2)}, u32[]{:S(2)}) async-start(f32[32,4,512]{2,1,0:T(4,128)} %shard_map.149), calls=%async_computation | async-start | bytes 524288 | tf_op jit(solution)/shard_map/all_to_all | solution.py:800
  10.8 10.6 %copy-start.4 = (f32[64,128]{1,0:T(8,128)S(1)}, f32[64,128]{1,0:T(8,128)}, u32[]{:S(2)}) copy-start(f32[64,128]{1,0:T(8,128)} %constant.40.clone.along_ref.refs_2_) | copy-start | bytes 98308
  10.8 10.6 %copy-start = (bf16[256,256]{1,0:T(8,128)(2,1)S(1)}, bf16[256,256]{1,0:T(8,128)(2,1)}, u32[]{:S(2)}) copy-start(bf16[256,256]{1,0:T(8,128)(2,1)} %constant.39.clone.low_ref.refs_1_) | copy-start | bytes 393220
  10.8 10.6 %copy-start.1 = (bf16[256,256]{1,0:T(8,128)(2,1)S(1)}, bf16[256,256]{1,0:T(8,128)(2,1)}, u32[]{:S(2)}) copy-start(bf16[256,256]{1,0:T(8,128)(2,1)} %constant.38.clone.high_ref.refs_0_) | copy-start | bytes 393220
  21.4 5.8 %copy-start.10 = (bf16[16,512]{1,0:T(8,128)(2,1)S(1)}, bf16[16,512]{1,0:T(8,128)(2,1)}, u32[]{:S(2)}) copy-start(bf16[16,512]{1,0:T(8,128)(2,1)} %constant.43.clone.interp_ref.refs_5_) | copy-start | bytes 49156
  23.8 3.4 %collective-permute-start.1 = (f32[64,128]{1,0:T(8,128)S(1)}, f32[64,128]{1,0:T(8,128)S(1)}, u32[]{:S(2)}, u32[]{:S(2)}) collective-permute-start(f32[64,128]{1,0:T(8,128)S(1)} %get-tuple-element.23), channel_id=1, source_target_pairs={{8,2},{2,8},{10,4},{4,10},{12,6},{6,12},{14,7},{7,14},{15,5},{5,15... | collective-permute-start | bytes 98312 | tf_op jit(solution)/shard_map/ppermute | solution.py:810
  24.5 2.8 %collective-permute-start = (f32[64,128]{1,0:T(8,128)S(1)}, f32[64,128]{1,0:T(8,128)S(1)}, u32[]{:S(2)}, u32[]{:S(2)}) collective-permute-start(f32[64,128]{1,0:T(8,128)S(1)} %get-tuple-element.23), channel_id=1, source_target_pairs={{0,8},{8,0},{2,10},{10,2},{4,12},{12,4},{6,14},{14,6},{7,15},{15,7... | collective-permute-start | bytes 98312 | tf_op jit(solution)/shard_map/ppermute | solution.py:809
  27.3 11.8 %copy-start.2 = (bf16[128,512]{1,0:T(8,128)(2,1)S(1)}, bf16[128,512]{1,0:T(8,128)(2,1)}, u32[]{:S(2)}) copy-start(bf16[128,512]{1,0:T(8,128)(2,1)} %constant.42.clone.refs_4_) | copy-start | bytes 393220
  27.3 11.8 %copy-start.3 = (bf16[128,512]{1,0:T(8,128)(2,1)S(1)}, bf16[128,512]{1,0:T(8,128)(2,1)}, u32[]{:S(2)}) copy-start(bf16[128,512]{1,0:T(8,128)(2,1)} %constant.41.clone.refs_3_) | copy-start | bytes 393220
  27.3 11.8 %copy-start.5 = (bf16[512,32]{1,0:T(8,128)(2,1)S(1)}, bf16[512,32]{1,0:T(8,128)(2,1)}, u32[]{:S(2)}) copy-start(bf16[512,32]{1,0:T(8,128)(2,1)} %constant.45.clone.refs_6_) | copy-start | bytes 98308
  27.3 11.8 %copy-start.6 = (bf16[512,32]{1,0:T(8,128)(2,1)S(1)}, bf16[512,32]{1,0:T(8,128)(2,1)}, u32[]{:S(2)}) copy-start(bf16[512,32]{1,0:T(8,128)(2,1)} %constant.44.clone.refs_8_) | copy-start | bytes 98308
  28.2 10.8 %collective-permute-start.2 = (f32[256,128]{1,0:T(8,128)S(1)}, f32[256,128]{1,0:T(8,128)S(1)}, u32[]{:S(2)}, u32[]{:S(2)}) collective-permute-start(f32[256,128]{1,0:T(8,128)S(1)} %get-tuple-element.26), channel_id=1, source_target_pairs={{0,8},{8,0},{2,10},{10,2},{4,12},{12,4},{6,14},{14,6},{7,15},{15,7... | collective-permute-start | bytes 393224 | tf_op jit(solution)/shard_map/ppermute | solution.py:809
  28.4 10.7 %collective-permute-start.3 = (f32[256,128]{1,0:T(8,128)S(1)}, f32[256,128]{1,0:T(8,128)S(1)}, u32[]{:S(2)}, u32[]{:S(2)}) collective-permute-start(f32[256,128]{1,0:T(8,128)S(1)} %get-tuple-element.27), channel_id=1, source_target_pairs={{8,2},{2,8},{10,4},{4,10},{12,6},{6,12},{14,7},{7,14},{15,5},{5,15... | collective-permute-start | bytes 393224 | tf_op jit(solution)/shard_map/ppermute | solution.py:810
  29.0 10.1 %copy-start.9 = (bf16[128,32]{1,0:T(8,128)(2,1)S(1)}, bf16[128,32]{1,0:T(8,128)(2,1)}, u32[]{:S(2)}) copy-start(bf16[128,32]{1,0:T(8,128)(2,1)} %constant.46.clone.refs_7_) | copy-start | bytes 24580
  42.5 1.4 %collective-permute-start.4 = (f32[256,128]{1,0:T(8,128)S(1)}, f32[256,128]{1,0:T(8,128)S(1)}, u32[]{:S(2)}, u32[]{:S(2)}) collective-permute-start(f32[256,128]{1,0:T(8,128)S(1)} %get-tuple-element.32), channel_id=1, source_target_pairs={{0,8},{8,0},{2,10},{10,2},{4,12},{12,4},{6,14},{14,6},{7,15},{15,7... | collective-permute-start | bytes 393224 | tf_op jit(solution)/shard_map/ppermute | solution.py:809
  42.7 4.4 %collective-permute-start.5 = (f32[256,128]{1,0:T(8,128)S(1)}, f32[256,128]{1,0:T(8,128)S(1)}, u32[]{:S(2)}, u32[]{:S(2)}) collective-permute-start(f32[256,128]{1,0:T(8,128)S(1)} %get-tuple-element.33), channel_id=1, source_target_pairs={{8,2},{2,8},{10,4},{4,10},{12,6},{6,12},{14,7},{7,14},{15,5},{5,15... | collective-permute-start | bytes 393224 | tf_op jit(solution)/shard_map/ppermute | solution.py:810
  48.8 9.7 %collective-permute-start.6 = (f32[256,128]{1,0:T(8,128)S(1)}, f32[256,128]{1,0:T(8,128)S(1)}, u32[]{:S(2)}, u32[]{:S(2)}) collective-permute-start(f32[256,128]{1,0:T(8,128)S(1)} %get-tuple-element.36), channel_id=1, source_target_pairs={{0,8},{8,0},{2,10},{10,2},{4,12},{12,4},{6,14},{14,6},{7,15},{15,7... | collective-permute-start | bytes 393224 | tf_op jit(solution)/shard_map/ppermute | solution.py:809
  49.3 9.3 %collective-permute-start.7 = (f32[256,128]{1,0:T(8,128)S(1)}, f32[256,128]{1,0:T(8,128)S(1)}, u32[]{:S(2)}, u32[]{:S(2)}) collective-permute-start(f32[256,128]{1,0:T(8,128)S(1)} %get-tuple-element.37), channel_id=1, source_target_pairs={{8,2},{2,8},{10,4},{4,10},{12,6},{6,12},{14,7},{7,14},{15,5},{5,15... | collective-permute-start | bytes 393224 | tf_op jit(solution)/shard_map/ppermute | solution.py:810
  62.3 13.2 %all-to-all-start.3 = ((f32[32,4,512]{2,1,0:T(4,128)}), f32[32,4,512]{2,1,0:T(4,128)S(1)}, u32[]{:S(2)}, u32[]{:S(2)}) async-start(f32[32,4,512]{2,1,0:T(4,128)} %shard_map.155), calls=%async_computation.3 | async-start | bytes 524288 | tf_op jit(solution)/shard_map/all_to_all | solution.py:871

commit v5 on v4

--- a/solution.py
+++ b/solution.py
@@ -98,6 +98,10 @@
             return d ^ (((d >> 3) & 1) * 7)
         return d
 
+    def slab(self):
+        d = lax.axis_index("ey")
+        return self.slab_at(lax.axis_index("ex") * self.mesh_y + d if self.joint else d)
+
     def swaps(self, first):
         pairs = []
         for s in range(first, self.slabs, 2):
@@ -217,8 +221,8 @@
     face_ref[...] = jnp.where(part_z == 0, low, high)
 
 
-def halo_of(lay, slab_ref, core_ref, chip_ref):
-    odd = (slab_ref[0] & 1) == 1
+def halo_of(lay, core_ref, chip_ref):
+    odd = (lay.slab() & 1) == 1
     core, chip = core_ref[...], chip_ref[...]
     below = jnp.where(odd, core, chip)
     above = jnp.where(odd, chip, core)
@@ -241,7 +245,7 @@
     assemble_xy(lay, sh_ref)
 
 
-def send_layers(lay, slab_ref, g_ref, s_ref, core_ref, chip_ref):
+def send_layers(lay, g_ref, s_ref, core_ref, chip_ref):
     low, high = get_rows(g_ref, 0), get_rows(g_ref, N - 1)
     _, _, part_z = lane_parts(lay, low.shape)
     s_ref[...] = g_ref[...]
@@ -253,13 +257,13 @@
     bottom = part_z == 0
     first = jnp.where(bottom, a, roll(b, 1, 1))
     second = jnp.where(bottom, roll(a, -1, 1), b)
-    odd = (slab_ref[0] & 1) == 1
+    odd = (lay.slab() & 1) == 1
     core_ref[...] = jnp.where(odd, first, second)
     chip_ref[...] = jnp.where(odd, second, first)
 
 
-def receive_layers(lay, slab_ref, core_ref, chip_ref, h_ref):
-    odd = (slab_ref[0] & 1) == 1
+def receive_layers(lay, core_ref, chip_ref, h_ref):
+    odd = (lay.slab() & 1) == 1
     core, chip = core_ref[...], chip_ref[...]
     below, above = jnp.where(odd, core, chip), jnp.where(odd, chip, core)
     _, _, part_z = lane_parts(lay, core.shape)
@@ -352,11 +356,11 @@
     lax.fori_loop(0, points_ref.shape[0], row_of, 0)
 
 
-def right_side(lay, local_points, one, slab_ref, points_ref, g_ref, halo_ref):
+def right_side(lay, local_points, one, points_ref, g_ref, halo_ref):
     derivative, weights = one
     shape = (N, lay.width)
     part_x, part_y, part_z = lane_parts(lay, shape)
-    first_z = slab_ref[0] * lay.depth
+    first_z = lay.slab() * lay.depth
     elem_z = first_z + part_z
     elem_halo = jnp.where(part_z == 0, first_z - 1, first_z + lay.depth)
     half_nodes = column(0.5 * (1.0 + GLL_POINTS), shape)
@@ -401,10 +405,10 @@
     for_points(points_ref, local_points, visit)
 
 
-def inverse_diagonal(lay, slab_ref, factor_ref, dinv_ref, outer):
+def inverse_diagonal(lay, factor, dinv_ref, outer):
     shape = (N, lay.width)
     part_x, part_y, part_z = lane_parts(lay, shape)
-    first = slab_ref[0] * lay.depth
+    first = lay.slab() * lay.depth
     part_z = jnp.where(part_z == 0, first - 1, first + lay.depth) if outer else first + part_z
     node = lax.broadcasted_iota(jnp.int32, shape, 0)
 
@@ -420,10 +424,14 @@
         along_z = jnp.where((part_z < 0) | (part_z >= EZ), 0.0, along_z)
     along_x = dict(zip((0, N - 1), share(part_x == 0, part_x == lay.num_x - 1)))
     along_y = dict(zip((0, N - 1), share(part_y == 0, part_y == lay.num_y - 1)))
+    tables = {}
+    for i in range(N // 2):
+        for j in range(i + 1):
+            tables[i, j] = tables[j, i] = column(factor[i, j], shape) * along_z
     for i in range(N):
         for j in range(N):
             rows = pl.ds((i * N + j) * N, N)
-            value = factor_ref[rows, :] * along_z
+            value = tables[min(i, N - 1 - i), min(j, N - 1 - j)]
             if i in along_x:
                 value = value * along_x[i]
             if j in along_y:
@@ -431,24 +439,20 @@
             dinv_ref[rows, :] = value
 
 
-def diagonal_kernel(lay, slab_ref, factor_ref, dinv_ref, outer_ref):
-    inverse_diagonal(lay, slab_ref, factor_ref, dinv_ref, False)
-    inverse_diagonal(lay, slab_ref, factor_ref, outer_ref, True)
-
-
 def first_kernel(
     lay,
     local_points,
     derivative,
     one,
-    slab_ref,
+    factor,
     recv_ref,
-    dinv_ref,
     high_ref,
     low_ref,
     along_ref,
     g_ref,
     x_ref,
+    dinv_ref,
+    outer_ref,
     face_ref,
     points_ref,
     s_ref,
@@ -469,8 +473,10 @@
     _, _, part_z = lane_parts(lay, low.shape)
     set_rows(g_ref, 0, jnp.where(part_z == 0, low, roll(high, 1, 1)))
     halo_ref[...] = jnp.where(part_z == 0, low, high)
+    inverse_diagonal(lay, factor, dinv_ref, False)
+    inverse_diagonal(lay, factor, outer_ref, True)
     copy.wait()
-    right_side(lay, local_points, (derivative, one[1]), slab_ref, table_ref, g_ref, halo_ref)
+    right_side(lay, local_points, (derivative, one[1]), table_ref, g_ref, halo_ref)
     assemble(lay, g_ref, s_ref, halo_ref[...])
     x_ref[...] = (1.0 / THETA) * dinv_ref[...] * s_ref[...]
     subtract_stiffness(lay, one, x_ref, g_ref, high_ref, low_ref, along_ref)
@@ -499,7 +505,6 @@
 def second_kernel(
     lay,
     one,
-    slab_ref,
     core_ref,
     chip_ref,
     g_ref,
@@ -517,14 +522,14 @@
     s_ref,
     u_ref,
 ):
-    assemble(lay, g_ref, s_ref, halo_of(lay, slab_ref, core_ref, chip_ref))
+    assemble(lay, g_ref, s_ref, halo_of(lay, core_ref, chip_ref))
     update = OLD * x_ref[...] + NEW * dinv_ref[...] * s_ref[...]
     u_ref[...] = update
     x_out[...] = x_ref[...] + update
     g_out[...] = g_ref[...]
     subtract_stiffness(lay, one, u_ref, g_out, high_ref, low_ref, along_ref)
     restriction(lay, g_out, dinv_ref, interp_ref, send_ref)
-    send_layers(lay, slab_ref, g_out, s_ref, core_out, chip_out)
+    send_layers(lay, g_out, s_ref, core_out, chip_out)
 
 
 def solve_coarse(lay, mass, stiff, loads_ref, first_ref, second_ref):
@@ -608,8 +613,8 @@
     return local
 
 
-def prolong_coarse(lay, slab_ref, first_ref, second_ref, interp_ref, image_ref, edge_ref, g_ref, h_ref, x_ref):
-    mine = slab_ref[0] + N
+def prolong_coarse(lay, first_ref, second_ref, interp_ref, image_ref, edge_ref, g_ref, h_ref, x_ref):
+    mine = lay.slab() + N
     _, _, part_z = lane_parts(lay, (1, lay.width))
     bottom = part_z == 0
     own, outer, far = [], [], []
@@ -629,13 +634,15 @@
     set_rows(h_ref, N - 1, high - jnp.where(bottom, 0.0, edge[:FACE]))
 
 
-def pair_kernel(lay, one, coarse, kind, slab_ref, core_ref, chip_ref, g_ref, x_ref, dinv_ref, outer_ref, *refs):
+def pair_kernel(lay, one, coarse, kind, core_ref, chip_ref, g_ref, x_ref, dinv_ref, outer_ref, *refs):
     refs = list(refs)
     high_ref, low_ref, along_ref, edge_high_ref, edge_low_ref = (refs.pop(0) for _ in range(5))
     if coarse:
         loads_ref, image_ref, image_edge_ref = (refs.pop(0) for _ in range(3))
     if coarse or kind == "restrict":
         interp_ref = refs.pop(0)
+    if kind != "last":
+        extra_ref = refs.pop(0)
     if kind == "last":
         out_ref = refs.pop(0)
     else:
@@ -643,18 +650,21 @@
         if kind == "restrict":
             send_ref = refs.pop(0)
         core_out, chip_out = refs.pop(0), refs.pop(0)
+        if kind == "plain":
+            points_out = refs.pop(0)
+            points_out[...] = extra_ref[...]
     s_ref, sh_ref, h_ref, u_ref = (refs.pop(0) for _ in range(4))
     if kind == "last":
         g_out, x_out = refs.pop(0), refs.pop(0)
 
     g_out[...] = g_ref[...]
     x_out[...] = x_ref[...]
-    receive_layers(lay, slab_ref, core_ref, chip_ref, h_ref)
+    receive_layers(lay, core_ref, chip_ref, h_ref)
     if coarse:
         first_ref, second_ref = refs
         solve_coarse(lay, *coarse, loads_ref, first_ref, second_ref)
         prolong_coarse(
-            lay, slab_ref, first_ref, second_ref, interp_ref, image_ref, image_edge_ref, g_out, h_ref, x_out
+            lay, first_ref, second_ref, interp_ref, image_ref, image_edge_ref, g_out, h_ref, x_out
         )
     assemble_both(lay, g_out, h_ref, s_ref, sh_ref)
     update = (1.0 / THETA) * dinv_ref[...] * s_ref[...]
@@ -680,7 +690,7 @@
     subtract_stiffness(lay, one, u_ref, g_out, high_ref, low_ref, along_ref)
     if kind == "restrict":
         restriction(lay, g_out, dinv_ref, interp_ref, send_ref)
-    send_layers(lay, slab_ref, g_out, s_ref, core_out, chip_out)
+    send_layers(lay, g_out, s_ref, core_out, chip_out)
 
 
 def unpack_kernel(lay, recv_ref, out_ref, flat_ref):
@@ -692,15 +702,16 @@
     out_ref[...] = flat_ref[...].T
 
 
-def forces_kernel(tiles_y, local_points, place_ref, points_ref, out_ref):
+def forces_kernel(tiles_y, local_points, points_ref, out_ref, done_ref):
     shape = (N, tiles_y * EZ)
     lane = lax.broadcasted_iota(jnp.int32, shape, 1)
-    first_x, first_y = place_ref[0], place_ref[1]
+    first_x, first_y = lax.axis_index("ex"), lax.axis_index("ey") * tiles_y
     elem_x = jnp.broadcast_to(first_x, shape)
     elem_y = first_y + lax.shift_right_logical(lane, log2(EZ))
     elem_z = lane & (EZ - 1)
     half_nodes = column(0.5 * (1.0 + GLL_POINTS), shape)
     out_ref[...] = jnp.zeros(out_ref.shape, F32)
+    done_ref[...] = jnp.zeros(done_ref.shape, F32)
 
     def visit(p, place):
         base, position, force = point_values(points_ref, p, place, GAUSS_NORM)
@@ -727,7 +738,7 @@
     for_points(points_ref, local_points, visit)
 
 
-def call(kernel, outs, inputs, scratch=(), smem=0, spaces=None):
+def call(kernel, outs, inputs, scratch=(), smem=0, spaces=None, limit=40):
     spaces = spaces or [pltpu.SMEM] * smem + [pltpu.VMEM] * (len(inputs) - smem)
     specs = [pl.BlockSpec(memory_space=space) for space in spaces]
     shapes = [jax.ShapeDtypeStruct(s, F32) for s in outs]
@@ -737,7 +748,7 @@
         in_specs=specs,
         out_specs=[pl.BlockSpec(memory_space=pltpu.VMEM)] * len(shapes),
         scratch_shapes=[pltpu.VMEM(s, F32) if isinstance(s, tuple) else s for s in scratch],
-        compiler_params=pltpu.CompilerParams(vmem_limit_bytes=40 * 1024 * 1024),
+        compiler_params=pltpu.CompilerParams(vmem_limit_bytes=limit * 1024 * 1024),
     )(*inputs)
     return result
 
@@ -767,18 +778,12 @@
     ratio = (weights[:, None] * derivative**2).sum(axis=0) / weights
     diag = 0.5 * (ratio[:, None, None] + ratio[None, :, None] + ratio[None, None, :])
     diag = diag * weights[:, None, None] * weights[None, :, None] * weights[None, None, :]
-    factor = np.broadcast_to(1.0 / diag.reshape(N**3, 1), fields)
+    factor = 1.0 / diag
     mass = interp.T @ diag_w @ interp
     stiff = interp.T @ stiff_one @ interp
     restrict3 = jnp.asarray(np.concatenate(split_table(interp3.T), 0))
     prolong3, image3, image_edge = (
         jnp.asarray(stacked_table(t)) for t in (interp3, image3, image3[edge_rows])
-    )
-    factor = jnp.asarray(factor, F32)
-
-    slab = lay.slab_at(lax.axis_index(lay.axis).astype(jnp.int32)).reshape(1)
-    place = jnp.stack([lax.axis_index("ex") * tiles_x, lax.axis_index("ey") * tiles_y]).astype(
-        jnp.int32
     )
 
     local_points = point_base.shape[1]
@@ -796,13 +801,11 @@
             pltpu.SemaphoreType.DMA((4,)),
         ],
         spaces=[pltpu.HBM] * 4,
+        limit=60,
     )
     recv = lax.all_to_all(send, lay.axis, 0, 0)
     if not lay.joint:
         recv = lax.all_gather(recv, "ex", axis=0, tiled=True)
-    dinv, outer = call(
-        functools.partial(diagonal_kernel, lay), [fields, fields], [slab, factor], smem=1
-    )
 
     def swap(core, chip):
         return (
@@ -817,25 +820,17 @@
     layer = (N**3 // 2, width)
     loads_shape = (lay.slabs, 2, width)
     table = (devices, -(-9 * N * local_points // 128) * 128)
-    g, x, face, points = call(
-        functools.partial(first_kernel, lay, local_points, derivative, one),
-        [fields, fields, face_shape, table],
-        [slab, recv, dinv, high, low, along],
+    g, x, dinv, outer, face, points = call(
+        functools.partial(first_kernel, lay, local_points, derivative, one, factor),
+        [fields, fields, fields, fields, face_shape, table],
+        [recv, high, low, along],
         [fields, face_shape, (width, N**3), pltpu.SMEM(table, F32), pltpu.SemaphoreType.DMA],
-        smem=1,
-    )
-    (forces,) = call(
-        functools.partial(forces_kernel, tiles_y, local_points),
-        [(3, N**3, tiles_y * EZ)],
-        [place, points],
-        smem=2,
     )
     g, x, loads, core, chip = call(
         functools.partial(second_kernel, lay, one),
         [fields, fields, loads_shape, layer, layer],
-        [slab, *swap(face, face), g, x, dinv, high, low, along, restrict3],
+        [*swap(face, face), g, x, dinv, high, low, along, restrict3],
         [fields, fields],
-        smem=1,
     )
     coarse = ((mass[0, 0], mass[0, 1]), (stiff[0, 0], stiff[0, 1]))
     stiffness = [high, low, along, edge_high, edge_low]
@@ -843,27 +838,33 @@
     for cycle in range(CYCLES):
         core, chip = swap(core, chip)
         last = cycle + 1 == CYCLES
-        outs = [fields, fields, layer, layer]
+        outs = [fields, fields, layer, layer, table]
+        extra = [points]
         scratch = [fields] * 4
         if last:
+            extra = []
             outs = [(lay.mesh_x * lay.mesh_y, block, N**3)]
             scratch += [fields, fields]
         outs = call(
             functools.partial(pair_kernel, lay, one, coarse, "last" if last else "plain"),
             outs,
-            [slab, core, chip, g, x, dinv, outer, *stiffness, gather(loads), image3, image_edge, prolong3],
+            [core, chip, g, x, dinv, outer, *stiffness, gather(loads), image3, image_edge, prolong3, *extra],
             scratch + [(lay.slabs + 2 * N, width)] * 2,
-            smem=1,
         )
         if last:
             break
-        g, x, core, chip = outs
+        g, x, core, chip, points = outs
+        forces, done = call(
+            functools.partial(forces_kernel, tiles_y, local_points),
+            [(3, N**3, tiles_y * EZ), (N, 128)],
+            [points],
+            smem=1,
+        )
         g, x, loads, core, chip = call(
             functools.partial(pair_kernel, lay, one, None, "restrict"),
             [fields, fields, loads_shape, layer, layer],
-            [slab, *swap(core, chip), g, x, dinv, outer, *stiffness, restrict3],
+            [*swap(core, chip), g, x, dinv, outer, *stiffness, restrict3, done],
             [fields] * 4,
-            smem=1,
         )
     (out,) = outs
     if not lay.joint:

time: 76.6 us -> 75.9 us (level)
  blocking collectives: 19 us -> 50.5 us
  waiting for transfers between devices: 24 us -> 3.41 us
  starting transfers between devices: 13.6 us -> 3.95 us
  local copies, waits for them, and re-layouts: 1.67 us -> 0.06 us
    all_to_all x0 -> x2, blocking collectives: none -> 30.3 us  [the longest x1 18 us: shards(): recv = lax.all_to_all(send, lay.axis, 0, 0)]
    all_to_all x2 -> x0, waiting for transfers between devices: 18.2 us -> none  [the longest x1 10.5 us: shards(): recv = lax.all_to_all(send, lay.axis, 0, 0)]
    all_to_all x2 -> x0, starting transfers between devices: 9.89 us -> none  [the longest x1 7.3 us: shards(): recv = lax.all_to_all(send, lay.axis, 0, 0)]
    ppermute x4, waiting for transfers between devices: 5.19 us -> 3.4 us  [swap(): lax.ppermute(chip, lay.axis, lay.swaps(1))]
    unnamed x28 -> x18, local copies, waits for them, and re-layouts: 1.67 us -> 0.06 us
    all_to_all x2, blocking collectives: 19 us -> 20.2 us  [gather(): return lax.all_to_all(loads, lay.axis, 0, 0)]
    ppermute x4, starting transfers between devices: 2.17 us -> 3.14 us  [swap(): lax.ppermute(chip, lay.axis, lay.swaps(1))]
    ppermute x4, starting transfers between devices: 1.58 us -> 0.81 us  [swap(): lax.ppermute(core, lay.axis, lay.swaps(0))]
  transfers between devices with their start and end apart: 10 -> 8, of which waited for: 5 -> 2; matrix products, arithmetic and copies ran while one was open for 0% -> 0% of each run, Pallas kernels for 4% -> 3%
where the time goes in v5:
time: 75.9 us; the launch traced here: 75.6 us
  blocking collectives  50.5 us (67%)
  Pallas kernels  16.8 us (22%)
  starting transfers between devices  3.95 us (5%)
  waiting for transfers between devices  3.41 us (4%)
  between operations  0.79 us (1%)
    all_to_all x2, blocking collectives, gather(): return lax.all_to_all(loads, lay.axis, 0, 0)  20.2 us
    all_to_all x1, blocking collectives, shards(): recv = lax.all_to_all(send, lay.axis, 0, 0)  18 us
    pallas_call x8, Pallas kernels, call(): pl.pallas_call(kernel, out_shape=shapes, in_specs=specs, out_specs=[pl.Bl...  16.8 us
    all_to_all x1, blocking collectives, shards(): out = lax.all_to_all(out, lay.axis, 0, 0)  12.4 us
    ppermute x4, waiting for transfers between devices, swap(): lax.ppermute(chip, lay.axis, lay.swaps(1))  3.4 us
    ppermute x4, starting transfers between devices, swap(): lax.ppermute(chip, lay.axis, lay.swaps(1))  3.14 us
  transfers between devices with their start and end apart: 8, of which 2 were waited for; matrix products, arithmetic and copies ran while one was open for 0% of the time, Pallas kernels for 3%

profile of v5, /device:TPU:0, one launch (start us, length us, event | category | flops | bytes accessed | tf_op | source)
XLA Modules:
  0.0 75.6 jit_solution(14402645741735547727)
XLA Ops:
  0.6 2.1 %shard_map.140 = f32[32,4,512]{2,1,0:T(4,128)} custom-call(s32[1,3]{1,0:T(1,128)} %bitcast.12, f32[1,3]{1,0:T(1,128)} %bitcast.13, f32[1,3]{1,0:T(1,128)} %bitcast.14, f32[512,128]{1,0:T(8,128)} %bitcast.10), custom_call_target="tpu_custom_call" | custom-call | tf_op jit(solution)/shard_map/pallas_call | solution.py:745
  2.7 0.0 copy-start
  2.7 0.0 copy-start.1
  2.7 0.0 copy-start.4
  2.7 18.0 %all_to_all.20.recv_ref = f32[32,4,512]{2,1,0:T(4,128)S(1)} all-to-all(f32[32,4,512]{2,1,0:T(4,128)} %shard_map.140), channel_id=1, replica_groups=mesh['ex'=4,'ey'=8] {'ex','ey'}, dimensions={0} | all-to-all | bytes 524288 | tf_op jit(solution)/shard_map/all_to_all | solution.py:806
  20.7 0.0 copy-start.8
  20.7 2.3 %shard_map.141 = (f32[512,128]{1,0:T(8,128)S(1)}, f32[512,128]{1,0:T(8,128)S(1)}, f32[512,128]{1,0:T(8,128)S(1)}, f32[512,128]{1,0:T(8,128)S(1)}, f32[64,128]{1,0:T(8,128)S(1)}, /*index=5*/f32[32,128]{1,0:T(8,128)S(1)}) custom-call(f32[32,4,512]{2,1,0:T(4,128)S(1)} %all_to_all.20.recv_ref, bf16[256,256]{1,0:T(8,128)(2,1)S(1)} %copy-done.1, ...), custom_call_target="tpu_custom_call" | custom-call | tf_op jit(solution)/shard_map/pallas_call | solution.py:745
  23.0 1.1 %collective-permute-start.1 = (f32[64,128]{1,0:T(8,128)S(1)}, f32[64,128]{1,0:T(8,128)S(1)}, u32[]{:S(2)}, u32[]{:S(2)}) collective-permute-start(f32[64,128]{1,0:T(8,128)S(1)} %get-tuple-element.25), channel_id=1, source_target_pairs={{8,2},{2,8},{10,4},{4,10},{12,6},{6,12},{14,7},{7,14},{15,5},{5,15... | collective-permute-start | bytes 98312 | tf_op jit(solution)/shard_map/ppermute | solution.py:813
  24.1 0.0 collective-permute-start
  24.1 2.3 %collective-permute-done.1.chip_ref = f32[64,128]{1,0:T(8,128)S(1)} collective-permute-done((f32[64,128]{1,0:T(8,128)S(1)}, f32[64,128]{1,0:T(8,128)S(1)}, u32[]{:S(2)}, u32[]{:S(2)}) %collective-permute-start.1) | collective-permute-done | bytes 32800 | tf_op jit(solution)/shard_map/ppermute | solution.py:813
  26.4 0.0 collective-permute-done.core_ref
  26.4 0.0 copy-start.3
  26.4 0.0 copy-start.5
  26.4 0.0 copy-start.6
  26.5 0.9 %shard_map.142 = (f32[512,128]{1,0:T(8,128)S(1)}, f32[512,128]{1,0:T(8,128)S(1)}, f32[32,2,128]{2,1,0:T(2,128)S(1)}, f32[256,128]{1,0:T(8,128)S(1)}, f32[256,128]{1,0:T(8,128)S(1)}) custom-call(f32[64,128]{1,0:T(8,128)S(1)} %collective-permute-done.core_ref, f32[64,128]{1,0:T(8,128)S(1)} %collective-permute-done.1.chip_ref, ...), custom_call_target="tpu_custom_call" | custom-call | tf_op jit(solution)/shard_map/pallas_call | solution.py:745
  27.4 0.1 collective-permute-start.2
  27.5 1.1 %collective-permute-start.3 = (f32[256,128]{1,0:T(8,128)S(1)}, f32[256,128]{1,0:T(8,128)S(1)}, u32[]{:S(2)}, u32[]{:S(2)}) collective-permute-start(f32[256,128]{1,0:T(8,128)S(1)} %get-tuple-element.30), channel_id=1, source_target_pairs={{8,2},{2,8},{10,4},{4,10},{12,6},{6,12},{14,7},{7,14},{15,5},{5,15... | collective-permute-start | bytes 393224 | tf_op jit(solution)/shard_map/ppermute | solution.py:813
  28.6 9.9 %all_to_all.21.refs_5_ = f32[32,2,128]{2,1,0:T(2,128)S(1)} all-to-all(f32[32,2,128]{2,1,0:T(2,128)S(1)} %get-tuple-element.34), channel_id=1, replica_groups=mesh['ex'=4,'ey'=8] {'ex','ey'}, dimensions={0} | all-to-all | bytes 65536 | tf_op jit(solution)/shard_map/all_to_all | solution.py:817
  38.5 0.0 collective-permute-done.2.core_ref
  38.5 0.0 collective-permute-done.3.chip_ref
  38.5 3.4 %shard_map.143 = (f32[512,128]{1,0:T(8,128)S(1)}, f32[512,128]{1,0:T(8,128)S(1)}, f32[256,128]{1,0:T(8,128)S(1)}, f32[256,128]{1,0:T(8,128)S(1)}, f32[32,128]{1,0:T(8,128)S(1)}) custom-call(f32[256,128]{1,0:T(8,128)S(1)} %collective-permute-done.2.core_ref, f32[256,128]{1,0:T(8,128)S(1)} %collective-permute-done.3.chip_ref, ...), custom_call_target="tpu_custom_call" | custom-call | tf_op jit(solution)/shard_map/pallas_call | solution.py:745
  41.9 0.2 collective-permute-start.4
  42.1 0.6 collective-permute-start.5
  42.8 2.6 %shard_map.144 = (f32[3,512,128]{2,1,0:T(8,128)}, f32[8,128]{1,0:T(8,128)S(1)}) custom-call(f32[32,128]{1,0:T(8,128)S(1)} %get-tuple-element.40.points_ref), custom_call_target="tpu_custom_call" | custom-call | tf_op jit(solution)/shard_map/pallas_call | solution.py:745
  45.4 1.1 %collective-permute-done.5.chip_ref = f32[256,128]{1,0:T(8,128)S(1)} collective-permute-done((f32[256,128]{1,0:T(8,128)S(1)}, f32[256,128]{1,0:T(8,128)S(1)}, u32[]{:S(2)}, u32[]{:S(2)}) %collective-permute-start.5) | collective-permute-done | bytes 131104 | tf_op jit(solution)/shard_map/ppermute | solution.py:813
  46.5 1.7 %shard_map.145 = (f32[512,128]{1,0:T(8,128)S(1)}, f32[512,128]{1,0:T(8,128)S(1)}, f32[32,2,128]{2,1,0:T(2,128)S(1)}, f32[256,128]{1,0:T(8,128)S(1)}, f32[256,128]{1,0:T(8,128)S(1)}) custom-call(f32[256,128]{1,0:T(8,128)S(1)} %collective-permute-done.4.core_ref, f32[256,128]{1,0:T(8,128)S(1)} %collective-permute-done.5.chip_ref, ...), custom_call_target="tpu_custom_call" | custom-call | tf_op jit(solution)/shard_map/pallas_call | solution.py:745
  48.2 0.5 collective-permute-start.6
  48.7 0.3 collective-permute-start.7
  49.0 10.3 %all_to_all.22.refs_5_ = f32[32,2,128]{2,1,0:T(2,128)S(1)} all-to-all(f32[32,2,128]{2,1,0:T(2,128)S(1)} %get-tuple-element.46), channel_id=1, replica_groups=mesh['ex'=4,'ey'=8] {'ex','ey'}, dimensions={0} | all-to-all | bytes 65536 | tf_op jit(solution)/shard_map/all_to_all | solution.py:817
  59.4 2.9 %shard_map.146 = f32[32,4,512]{2,1,0:T(4,128)S(1)} custom-call(f32[256,128]{1,0:T(8,128)S(1)} %collective-permute-done.6.core_ref, f32[256,128]{1,0:T(8,128)S(1)} %collective-permute-done.7.chip_ref, f32[512,128]{1,0:T(8,128)S(1)} %get-tuple-element.44.g_ref, f32[512,128]{1,0:T(8,128)S(1)} %get-tuple-element.45.x_ref, ...), custom_call_target="tpu_custom_call" | custom-call | tf_op jit(solution)/shard_map/pallas_call | solution.py:745
  62.3 12.4 %all_to_all.23.recv_ref = f32[32,4,512]{2,1,0:T(4,128)S(1)} all-to-all(f32[32,4,512]{2,1,0:T(4,128)S(1)} %shard_map.146), channel_id=1, replica_groups=mesh['ex'=4,'ey'=8] {'ex','ey'}, dimensions={0} | all-to-all | bytes 524288 | tf_op jit(solution)/shard_map/all_to_all | solution.py:872
  74.7 0.9 %shard_map.147 = f32[512,128]{1,0:T(8,128)} custom-call(f32[32,4,512]{2,1,0:T(4,128)S(1)} %all_to_all.23.recv_ref), custom_call_target="tpu_custom_call" | custom-call | tf_op jit(solution)/shard_map/pallas_call | solution.py:745
  (14 shorter events, 0.0 us)
Async XLA Ops:
  2.7 18.0 %copy-start = (bf16[256,256]{1,0:T(8,128)(2,1)S(1)}, bf16[256,256]{1,0:T(8,128)(2,1)}, u32[]{:S(2)}) copy-start(bf16[256,256]{1,0:T(8,128)(2,1)} %constant.19.clone.low_ref.refs_1_) | copy-start | bytes 393220
  2.7 18.0 %copy-start.1 = (bf16[256,256]{1,0:T(8,128)(2,1)S(1)}, bf16[256,256]{1,0:T(8,128)(2,1)}, u32[]{:S(2)}) copy-start(bf16[256,256]{1,0:T(8,128)(2,1)} %constant.18.clone.high_ref.refs_0_) | copy-start | bytes 393220
  2.7 18.0 %copy-start.4 = (f32[64,128]{1,0:T(8,128)S(1)}, f32[64,128]{1,0:T(8,128)}, u32[]{:S(2)}) copy-start(f32[64,128]{1,0:T(8,128)} %constant.20.clone.along_ref.refs_2_) | copy-start | bytes 98308
  20.7 5.7 %copy-start.8 = (bf16[16,512]{1,0:T(8,128)(2,1)S(1)}, bf16[16,512]{1,0:T(8,128)(2,1)}, u32[]{:S(2)}) copy-start(bf16[16,512]{1,0:T(8,128)(2,1)} %constant.23.clone.interp_ref.refs_5_) | copy-start | bytes 49156
  23.0 3.4 %collective-permute-start.1 = (f32[64,128]{1,0:T(8,128)S(1)}, f32[64,128]{1,0:T(8,128)S(1)}, u32[]{:S(2)}, u32[]{:S(2)}) collective-permute-start(f32[64,128]{1,0:T(8,128)S(1)} %get-tuple-element.25), channel_id=1, source_target_pairs={{8,2},{2,8},{10,4},{4,10},{12,6},{6,12},{14,7},{7,14},{15,5},{5,15... | collective-permute-start | bytes 98312 | tf_op jit(solution)/shard_map/ppermute | solution.py:813
  24.1 2.3 %collective-permute-start = (f32[64,128]{1,0:T(8,128)S(1)}, f32[64,128]{1,0:T(8,128)S(1)}, u32[]{:S(2)}, u32[]{:S(2)}) collective-permute-start(f32[64,128]{1,0:T(8,128)S(1)} %get-tuple-element.25), channel_id=1, source_target_pairs={{0,8},{8,0},{2,10},{10,2},{4,12},{12,4},{6,14},{14,6},{7,15},{15,7... | collective-permute-start | bytes 98312 | tf_op jit(solution)/shard_map/ppermute | solution.py:812
  26.4 12.1 %copy-start.2 = (bf16[128,512]{1,0:T(8,128)(2,1)S(1)}, bf16[128,512]{1,0:T(8,128)(2,1)}, u32[]{:S(2)}) copy-start(bf16[128,512]{1,0:T(8,128)(2,1)} %constant.22.clone.refs_4_) | copy-start | bytes 393220
  26.4 12.1 %copy-start.3 = (bf16[128,512]{1,0:T(8,128)(2,1)S(1)}, bf16[128,512]{1,0:T(8,128)(2,1)}, u32[]{:S(2)}) copy-start(bf16[128,512]{1,0:T(8,128)(2,1)} %constant.21.clone.refs_3_) | copy-start | bytes 393220
  26.4 12.1 %copy-start.5 = (bf16[512,32]{1,0:T(8,128)(2,1)S(1)}, bf16[512,32]{1,0:T(8,128)(2,1)}, u32[]{:S(2)}) copy-start(bf16[512,32]{1,0:T(8,128)(2,1)} %constant.25.clone.refs_6_) | copy-start | bytes 98308
  26.4 12.1 %copy-start.6 = (bf16[512,32]{1,0:T(8,128)(2,1)S(1)}, bf16[512,32]{1,0:T(8,128)(2,1)}, u32[]{:S(2)}) copy-start(bf16[512,32]{1,0:T(8,128)(2,1)} %constant.24.clone.refs_8_) | copy-start | bytes 98308
  27.4 11.1 %collective-permute-start.2 = (f32[256,128]{1,0:T(8,128)S(1)}, f32[256,128]{1,0:T(8,128)S(1)}, u32[]{:S(2)}, u32[]{:S(2)}) collective-permute-start(f32[256,128]{1,0:T(8,128)S(1)} %get-tuple-element.29), channel_id=1, source_target_pairs={{0,8},{8,0},{2,10},{10,2},{4,12},{12,4},{6,14},{14,6},{7,15},{15,7... | collective-permute-start | bytes 393224 | tf_op jit(solution)/shard_map/ppermute | solution.py:812
  27.5 11.0 %collective-permute-start.3 = (f32[256,128]{1,0:T(8,128)S(1)}, f32[256,128]{1,0:T(8,128)S(1)}, u32[]{:S(2)}, u32[]{:S(2)}) collective-permute-start(f32[256,128]{1,0:T(8,128)S(1)} %get-tuple-element.30), channel_id=1, source_target_pairs={{8,2},{2,8},{10,4},{4,10},{12,6},{6,12},{14,7},{7,14},{15,5},{5,15... | collective-permute-start | bytes 393224 | tf_op jit(solution)/shard_map/ppermute | solution.py:813
  28.6 9.9 %copy-start.7 = (bf16[128,32]{1,0:T(8,128)(2,1)S(1)}, bf16[128,32]{1,0:T(8,128)(2,1)}, u32[]{:S(2)}) copy-start(bf16[128,32]{1,0:T(8,128)(2,1)} %constant.26.clone.refs_7_) | copy-start | bytes 24580
  41.9 3.5 %collective-permute-start.4 = (f32[256,128]{1,0:T(8,128)S(1)}, f32[256,128]{1,0:T(8,128)S(1)}, u32[]{:S(2)}, u32[]{:S(2)}) collective-permute-start(f32[256,128]{1,0:T(8,128)S(1)} %get-tuple-element.36), channel_id=1, source_target_pairs={{0,8},{8,0},{2,10},{10,2},{4,12},{12,4},{6,14},{14,6},{7,15},{15,7... | collective-permute-start | bytes 393224 | tf_op jit(solution)/shard_map/ppermute | solution.py:812
  42.1 4.4 %collective-permute-start.5 = (f32[256,128]{1,0:T(8,128)S(1)}, f32[256,128]{1,0:T(8,128)S(1)}, u32[]{:S(2)}, u32[]{:S(2)}) collective-permute-start(f32[256,128]{1,0:T(8,128)S(1)} %get-tuple-element.37), channel_id=1, source_target_pairs={{8,2},{2,8},{10,4},{4,10},{12,6},{6,12},{14,7},{7,14},{15,5},{5,15... | collective-permute-start | bytes 393224 | tf_op jit(solution)/shard_map/ppermute | solution.py:813
  48.2 11.1 %collective-permute-start.6 = (f32[256,128]{1,0:T(8,128)S(1)}, f32[256,128]{1,0:T(8,128)S(1)}, u32[]{:S(2)}, u32[]{:S(2)}) collective-permute-start(f32[256,128]{1,0:T(8,128)S(1)} %get-tuple-element.42), channel_id=1, source_target_pairs={{0,8},{8,0},{2,10},{10,2},{4,12},{12,4},{6,14},{14,6},{7,15},{15,7... | collective-permute-start | bytes 393224 | tf_op jit(solution)/shard_map/ppermute | solution.py:812
  48.7 10.7 %collective-permute-start.7 = (f32[256,128]{1,0:T(8,128)S(1)}, f32[256,128]{1,0:T(8,128)S(1)}, u32[]{:S(2)}, u32[]{:S(2)}) collective-permute-start(f32[256,128]{1,0:T(8,128)S(1)} %get-tuple-element.43), channel_id=1, source_target_pairs={{8,2},{2,8},{10,4},{4,10},{12,6},{6,12},{14,7},{7,14},{15,5},{5,15... | collective-permute-start | bytes 393224 | tf_op jit(solution)/shard_map/ppermute | solution.py:813

commit v6 on v5

--- a/solution.py
+++ b/solution.py
@@ -727,13 +727,30 @@
             x = gauss(elem_x, base[0], position[0], half_nodes)
             y = gauss(elem_y, base[1], position[1], half_nodes)
             z = gauss(elem_z, base[2], position[2], half_nodes)
-            for j in range(N):
-                plane = y[j : j + 1] * z
-                for i in range(N):
-                    value = x[i : i + 1] * plane
-                    rows = pl.ds((i * N + j) * N, N)
-                    for c in range(3):
-                        out_ref[c, rows, :] += force[c] * value
+
+            def add(along_x, along_y):
+                for j in along_y:
+                    plane = y[j : j + 1] * z
+                    for i in along_x:
+                        value = x[i : i + 1] * plane
+                        rows = pl.ds((i * N + j) * N, N)
+                        for c in range(3):
+                            out_ref[c, rows, :] += force[c] * value
+
+            last_y = low_y + (tiles_y - 1)
+            in_x = ((base[0] == low_x) | (base[0] + 1.0 == low_x), range(N))
+            in_y = ((base[1] + 1.0 >= low_y) & (base[1] <= last_y), range(N))
+            for when_x, along_x in (
+                in_x,
+                (base[0] + 2.0 == low_x, (0,)),
+                (base[0] - 1.0 == low_x, (N - 1,)),
+            ):
+                for when_y, along_y in (
+                    in_y,
+                    (base[1] + 2.0 == low_y, (0,)),
+                    (base[1] - 1.0 == last_y, (N - 1,)),
+                ):
+                    pl.when(when_x & when_y)(functools.partial(add, along_x, along_y))
 
     for_points(points_ref, local_points, visit)
 
@@ -791,7 +808,15 @@
     (send,) = call(
         functools.partial(pack_kernel, lay),
         [(lay.slabs, block, N**3)],
-        [point_base.T, point_offset.T, point_force.T, source.reshape(N**3, tiles_y * EZ)],
+        [
+            pltpu.with_memory_space_constraint(t, pltpu.HBM)
+            for t in (
+                point_base.T,
+                point_offset.T,
+                point_force.T,
+                source.reshape(N**3, tiles_y * EZ),
+            )
+        ],
         [
             pltpu.VMEM((local_points, 3), jnp.int32),
             (local_points, 3),
@@ -801,7 +826,6 @@
             pltpu.SemaphoreType.DMA((4,)),
         ],
         spaces=[pltpu.HBM] * 4,
-        limit=60,
     )
     recv = lax.all_to_all(send, lay.axis, 0, 0)
     if not lay.joint:

time: 75.9 us -> 74.6 us (0.983)
    pallas_call x8, Pallas kernels: 16.8 us -> 16.1 us  [call(): pl.pallas_call(kernel, out_shape=shapes, in_specs=specs, out_specs=[pl.Bl...]
where the time goes in v6:
time: 74.6 us; the launch traced here: 74.2 us
  blocking collectives  49.9 us (67%)
  Pallas kernels  16.1 us (22%)
  starting transfers between devices  3.94 us (5%)
  waiting for transfers between devices  3.39 us (5%)
  between operations  0.79 us (1%)
    all_to_all x2, blocking collectives, gather(): return lax.all_to_all(loads, lay.axis, 0, 0)  19.8 us
    all_to_all x1, blocking collectives, shards(): recv = lax.all_to_all(send, lay.axis, 0, 0)  17.8 us
    pallas_call x8, Pallas kernels, call(): pl.pallas_call(kernel, out_shape=shapes, in_specs=specs, out_specs=[pl.Bl...  16.1 us
    all_to_all x1, blocking collectives, shards(): out = lax.all_to_all(out, lay.axis, 0, 0)  12.4 us
    ppermute x4, waiting for transfers between devices, swap(): lax.ppermute(chip, lay.axis, lay.swaps(1))  3.38 us
    ppermute x4, starting transfers between devices, swap(): lax.ppermute(chip, lay.axis, lay.swaps(1))  2.82 us
  transfers between devices with their start and end apart: 8, of which 2 were waited for; matrix products, arithmetic and copies ran while one was open for 0% of the time, Pallas kernels for 3%

profile of v6, /device:TPU:0, one launch (start us, length us, event | category | flops | bytes accessed | tf_op | source)
XLA Modules:
  0.0 74.2 jit_solution(15006198376211357368)
XLA Ops:
  0.6 1.4 %shard_map.140 = f32[32,4,512]{2,1,0:T(4,128)S(1)} custom-call(s32[1,3]{1,0:T(1,128)} %bitcast.12, f32[1,3]{1,0:T(1,128)} %bitcast.13, f32[1,3]{1,0:T(1,128)} %bitcast.14, f32[512,128]{1,0:T(8,128)} %bitcast.10), custom_call_target="tpu_custom_call" | custom-call | tf_op jit(solution)/shard_map/pallas_call | solution.py:762
  2.0 0.0 copy-start
  2.0 0.0 copy-start.1
  2.0 0.0 copy-start.4
  2.0 17.8 %all_to_all.20.recv_ref = f32[32,4,512]{2,1,0:T(4,128)S(1)} all-to-all(f32[32,4,512]{2,1,0:T(4,128)S(1)} %shard_map.140), channel_id=1, replica_groups=mesh['ex'=4,'ey'=8] {'ex','ey'}, dimensions={0} | all-to-all | bytes 524288 | tf_op jit(solution)/shard_map/all_to_all | solution.py:830
  19.8 0.0 copy-start.8
  19.8 2.3 %shard_map.141 = (f32[512,128]{1,0:T(8,128)S(1)}, f32[512,128]{1,0:T(8,128)S(1)}, f32[512,128]{1,0:T(8,128)S(1)}, f32[512,128]{1,0:T(8,128)S(1)}, f32[64,128]{1,0:T(8,128)S(1)}, /*index=5*/f32[32,128]{1,0:T(8,128)S(1)}) custom-call(f32[32,4,512]{2,1,0:T(4,128)S(1)} %all_to_all.20.recv_ref, bf16[256,256]{1,0:T(8,128)(2,1)S(1)} %copy-done.1, ...), custom_call_target="tpu_custom_call" | custom-call | tf_op jit(solution)/shard_map/pallas_call | solution.py:762
  22.1 0.9 %collective-permute-start.1 = (f32[64,128]{1,0:T(8,128)S(1)}, f32[64,128]{1,0:T(8,128)S(1)}, u32[]{:S(2)}, u32[]{:S(2)}) collective-permute-start(f32[64,128]{1,0:T(8,128)S(1)} %get-tuple-element.25), channel_id=1, source_target_pairs={{8,2},{2,8},{10,4},{4,10},{12,6},{6,12},{14,7},{7,14},{15,5},{5,15... | collective-permute-start | bytes 98312 | tf_op jit(solution)/shard_map/ppermute | solution.py:837
  22.9 0.4 collective-permute-start
  23.3 2.2 %collective-permute-done.1.chip_ref = f32[64,128]{1,0:T(8,128)S(1)} collective-permute-done((f32[64,128]{1,0:T(8,128)S(1)}, f32[64,128]{1,0:T(8,128)S(1)}, u32[]{:S(2)}, u32[]{:S(2)}) %collective-permute-start.1) | collective-permute-done | bytes 32800 | tf_op jit(solution)/shard_map/ppermute | solution.py:837
  25.5 0.0 collective-permute-done.core_ref
  25.5 0.0 copy-start.3
  25.5 0.0 copy-start.5
  25.5 0.0 copy-start.6
  25.5 0.9 %shard_map.142 = (f32[512,128]{1,0:T(8,128)S(1)}, f32[512,128]{1,0:T(8,128)S(1)}, f32[32,2,128]{2,1,0:T(2,128)S(1)}, f32[256,128]{1,0:T(8,128)S(1)}, f32[256,128]{1,0:T(8,128)S(1)}) custom-call(f32[64,128]{1,0:T(8,128)S(1)} %collective-permute-done.core_ref, f32[64,128]{1,0:T(8,128)S(1)} %collective-permute-done.1.chip_ref, ...), custom_call_target="tpu_custom_call" | custom-call | tf_op jit(solution)/shard_map/pallas_call | solution.py:762
  26.5 0.1 collective-permute-start.2
  26.6 1.0 %collective-permute-start.3 = (f32[256,128]{1,0:T(8,128)S(1)}, f32[256,128]{1,0:T(8,128)S(1)}, u32[]{:S(2)}, u32[]{:S(2)}) collective-permute-start(f32[256,128]{1,0:T(8,128)S(1)} %get-tuple-element.30), channel_id=1, source_target_pairs={{8,2},{2,8},{10,4},{4,10},{12,6},{6,12},{14,7},{7,14},{15,5},{5,15... | collective-permute-start | bytes 393224 | tf_op jit(solution)/shard_map/ppermute | solution.py:837
  27.6 10.1 %all_to_all.21.refs_5_ = f32[32,2,128]{2,1,0:T(2,128)S(1)} all-to-all(f32[32,2,128]{2,1,0:T(2,128)S(1)} %get-tuple-element.34), channel_id=1, replica_groups=mesh['ex'=4,'ey'=8] {'ex','ey'}, dimensions={0} | all-to-all | bytes 65536 | tf_op jit(solution)/shard_map/all_to_all | solution.py:841
  37.8 3.4 %shard_map.143 = (f32[512,128]{1,0:T(8,128)S(1)}, f32[512,128]{1,0:T(8,128)S(1)}, f32[256,128]{1,0:T(8,128)S(1)}, f32[256,128]{1,0:T(8,128)S(1)}, f32[32,128]{1,0:T(8,128)S(1)}) custom-call(f32[256,128]{1,0:T(8,128)S(1)} %collective-permute-done.2.core_ref, f32[256,128]{1,0:T(8,128)S(1)} %collective-permute-done.3.chip_ref, ...), custom_call_target="tpu_custom_call" | custom-call | tf_op jit(solution)/shard_map/pallas_call | solution.py:762
  41.2 0.2 collective-permute-start.4
  41.4 0.6 collective-permute-start.5
  42.0 2.6 %shard_map.144 = (f32[3,512,128]{2,1,0:T(8,128)}, f32[8,128]{1,0:T(8,128)S(1)}) custom-call(f32[32,128]{1,0:T(8,128)S(1)} %get-tuple-element.40.points_ref), custom_call_target="tpu_custom_call" | custom-call | tf_op jit(solution)/shard_map/pallas_call | solution.py:762
  44.6 1.2 %collective-permute-done.5.chip_ref = f32[256,128]{1,0:T(8,128)S(1)} collective-permute-done((f32[256,128]{1,0:T(8,128)S(1)}, f32[256,128]{1,0:T(8,128)S(1)}, u32[]{:S(2)}, u32[]{:S(2)}) %collective-permute-start.5) | collective-permute-done | bytes 131104 | tf_op jit(solution)/shard_map/ppermute | solution.py:837
  45.8 1.7 %shard_map.145 = (f32[512,128]{1,0:T(8,128)S(1)}, f32[512,128]{1,0:T(8,128)S(1)}, f32[32,2,128]{2,1,0:T(2,128)S(1)}, f32[256,128]{1,0:T(8,128)S(1)}, f32[256,128]{1,0:T(8,128)S(1)}) custom-call(f32[256,128]{1,0:T(8,128)S(1)} %collective-permute-done.4.core_ref, f32[256,128]{1,0:T(8,128)S(1)} %collective-permute-done.5.chip_ref, ...), custom_call_target="tpu_custom_call" | custom-call | tf_op jit(solution)/shard_map/pallas_call | solution.py:762
  47.5 0.5 collective-permute-start.6
  47.9 0.3 collective-permute-start.7
  48.3 9.7 %all_to_all.22.refs_5_ = f32[32,2,128]{2,1,0:T(2,128)S(1)} all-to-all(f32[32,2,128]{2,1,0:T(2,128)S(1)} %get-tuple-element.46), channel_id=1, replica_groups=mesh['ex'=4,'ey'=8] {'ex','ey'}, dimensions={0} | all-to-all | bytes 65536 | tf_op jit(solution)/shard_map/all_to_all | solution.py:841
  58.0 0.0 collective-permute-done.6.core_ref
  58.0 0.0 collective-permute-done.7.chip_ref
  58.0 2.9 %shard_map.146 = f32[32,4,512]{2,1,0:T(4,128)S(1)} custom-call(f32[256,128]{1,0:T(8,128)S(1)} %collective-permute-done.6.core_ref, f32[256,128]{1,0:T(8,128)S(1)} %collective-permute-done.7.chip_ref, f32[512,128]{1,0:T(8,128)S(1)} %get-tuple-element.44.g_ref, f32[512,128]{1,0:T(8,128)S(1)} %get-tuple-element.45.x_ref, ...), custom_call_target="tpu_custom_call" | custom-call | tf_op jit(solution)/shard_map/pallas_call | solution.py:762
  60.9 12.4 %all_to_all.23.recv_ref = f32[32,4,512]{2,1,0:T(4,128)S(1)} all-to-all(f32[32,4,512]{2,1,0:T(4,128)S(1)} %shard_map.146), channel_id=1, replica_groups=mesh['ex'=4,'ey'=8] {'ex','ey'}, dimensions={0} | all-to-all | bytes 524288 | tf_op jit(solution)/shard_map/all_to_all | solution.py:896
  73.3 0.9 %shard_map.147 = f32[512,128]{1,0:T(8,128)} custom-call(f32[32,4,512]{2,1,0:T(4,128)S(1)} %all_to_all.23.recv_ref), custom_call_target="tpu_custom_call" | custom-call | tf_op jit(solution)/shard_map/pallas_call | solution.py:762
  (14 shorter events, 0.0 us)
Async XLA Ops:
  2.0 17.8 %copy-start = (bf16[256,256]{1,0:T(8,128)(2,1)S(1)}, bf16[256,256]{1,0:T(8,128)(2,1)}, u32[]{:S(2)}) copy-start(bf16[256,256]{1,0:T(8,128)(2,1)} %constant.19.clone.low_ref.refs_1_) | copy-start | bytes 393220
  2.0 17.8 %copy-start.1 = (bf16[256,256]{1,0:T(8,128)(2,1)S(1)}, bf16[256,256]{1,0:T(8,128)(2,1)}, u32[]{:S(2)}) copy-start(bf16[256,256]{1,0:T(8,128)(2,1)} %constant.18.clone.high_ref.refs_0_) | copy-start | bytes 393220
  2.0 17.8 %copy-start.4 = (f32[64,128]{1,0:T(8,128)S(1)}, f32[64,128]{1,0:T(8,128)}, u32[]{:S(2)}) copy-start(f32[64,128]{1,0:T(8,128)} %constant.20.clone.along_ref.refs_2_) | copy-start | bytes 98308
  19.8 5.7 %copy-start.8 = (bf16[16,512]{1,0:T(8,128)(2,1)S(1)}, bf16[16,512]{1,0:T(8,128)(2,1)}, u32[]{:S(2)}) copy-start(bf16[16,512]{1,0:T(8,128)(2,1)} %constant.23.clone.interp_ref.refs_5_) | copy-start | bytes 49156
  22.1 3.4 %collective-permute-start.1 = (f32[64,128]{1,0:T(8,128)S(1)}, f32[64,128]{1,0:T(8,128)S(1)}, u32[]{:S(2)}, u32[]{:S(2)}) collective-permute-start(f32[64,128]{1,0:T(8,128)S(1)} %get-tuple-element.25), channel_id=1, source_target_pairs={{8,2},{2,8},{10,4},{4,10},{12,6},{6,12},{14,7},{7,14},{15,5},{5,15... | collective-permute-start | bytes 98312 | tf_op jit(solution)/shard_map/ppermute | solution.py:837
  22.9 2.6 %collective-permute-start = (f32[64,128]{1,0:T(8,128)S(1)}, f32[64,128]{1,0:T(8,128)S(1)}, u32[]{:S(2)}, u32[]{:S(2)}) collective-permute-start(f32[64,128]{1,0:T(8,128)S(1)} %get-tuple-element.25), channel_id=1, source_target_pairs={{0,8},{8,0},{2,10},{10,2},{4,12},{12,4},{6,14},{14,6},{7,15},{15,7... | collective-permute-start | bytes 98312 | tf_op jit(solution)/shard_map/ppermute | solution.py:836
  25.5 12.2 %copy-start.2 = (bf16[128,512]{1,0:T(8,128)(2,1)S(1)}, bf16[128,512]{1,0:T(8,128)(2,1)}, u32[]{:S(2)}) copy-start(bf16[128,512]{1,0:T(8,128)(2,1)} %constant.22.clone.refs_4_) | copy-start | bytes 393220
  25.5 12.2 %copy-start.3 = (bf16[128,512]{1,0:T(8,128)(2,1)S(1)}, bf16[128,512]{1,0:T(8,128)(2,1)}, u32[]{:S(2)}) copy-start(bf16[128,512]{1,0:T(8,128)(2,1)} %constant.21.clone.refs_3_) | copy-start | bytes 393220
  25.5 12.2 %copy-start.5 = (bf16[512,32]{1,0:T(8,128)(2,1)S(1)}, bf16[512,32]{1,0:T(8,128)(2,1)}, u32[]{:S(2)}) copy-start(bf16[512,32]{1,0:T(8,128)(2,1)} %constant.25.clone.refs_6_) | copy-start | bytes 98308
  25.5 12.2 %copy-start.6 = (bf16[512,32]{1,0:T(8,128)(2,1)S(1)}, bf16[512,32]{1,0:T(8,128)(2,1)}, u32[]{:S(2)}) copy-start(bf16[512,32]{1,0:T(8,128)(2,1)} %constant.24.clone.refs_8_) | copy-start | bytes 98308
  26.5 11.2 %collective-permute-start.2 = (f32[256,128]{1,0:T(8,128)S(1)}, f32[256,128]{1,0:T(8,128)S(1)}, u32[]{:S(2)}, u32[]{:S(2)}) collective-permute-start(f32[256,128]{1,0:T(8,128)S(1)} %get-tuple-element.29), channel_id=1, source_target_pairs={{0,8},{8,0},{2,10},{10,2},{4,12},{12,4},{6,14},{14,6},{7,15},{15,7... | collective-permute-start | bytes 393224 | tf_op jit(solution)/shard_map/ppermute | solution.py:836
  26.6 11.1 %collective-permute-start.3 = (f32[256,128]{1,0:T(8,128)S(1)}, f32[256,128]{1,0:T(8,128)S(1)}, u32[]{:S(2)}, u32[]{:S(2)}) collective-permute-start(f32[256,128]{1,0:T(8,128)S(1)} %get-tuple-element.30), channel_id=1, source_target_pairs={{8,2},{2,8},{10,4},{4,10},{12,6},{6,12},{14,7},{7,14},{15,5},{5,15... | collective-permute-start | bytes 393224 | tf_op jit(solution)/shard_map/ppermute | solution.py:837
  27.6 10.2 %copy-start.7 = (bf16[128,32]{1,0:T(8,128)(2,1)S(1)}, bf16[128,32]{1,0:T(8,128)(2,1)}, u32[]{:S(2)}) copy-start(bf16[128,32]{1,0:T(8,128)(2,1)} %constant.26.clone.refs_7_) | copy-start | bytes 24580
  41.2 3.4 %collective-permute-start.4 = (f32[256,128]{1,0:T(8,128)S(1)}, f32[256,128]{1,0:T(8,128)S(1)}, u32[]{:S(2)}, u32[]{:S(2)}) collective-permute-start(f32[256,128]{1,0:T(8,128)S(1)} %get-tuple-element.36), channel_id=1, source_target_pairs={{0,8},{8,0},{2,10},{10,2},{4,12},{12,4},{6,14},{14,6},{7,15},{15,7... | collective-permute-start | bytes 393224 | tf_op jit(solution)/shard_map/ppermute | solution.py:836
  41.4 4.4 %collective-permute-start.5 = (f32[256,128]{1,0:T(8,128)S(1)}, f32[256,128]{1,0:T(8,128)S(1)}, u32[]{:S(2)}, u32[]{:S(2)}) collective-permute-start(f32[256,128]{1,0:T(8,128)S(1)} %get-tuple-element.37), channel_id=1, source_target_pairs={{8,2},{2,8},{10,4},{4,10},{12,6},{6,12},{14,7},{7,14},{15,5},{5,15... | collective-permute-start | bytes 393224 | tf_op jit(solution)/shard_map/ppermute | solution.py:837
  47.5 10.5 %collective-permute-start.6 = (f32[256,128]{1,0:T(8,128)S(1)}, f32[256,128]{1,0:T(8,128)S(1)}, u32[]{:S(2)}, u32[]{:S(2)}) collective-permute-start(f32[256,128]{1,0:T(8,128)S(1)} %get-tuple-element.42), channel_id=1, source_target_pairs={{0,8},{8,0},{2,10},{10,2},{4,12},{12,4},{6,14},{14,6},{7,15},{15,7... | collective-permute-start | bytes 393224 | tf_op jit(solution)/shard_map/ppermute | solution.py:836
  47.9 10.0 %collective-permute-start.7 = (f32[256,128]{1,0:T(8,128)S(1)}, f32[256,128]{1,0:T(8,128)S(1)}, u32[]{:S(2)}, u32[]{:S(2)}) collective-permute-start(f32[256,128]{1,0:T(8,128)S(1)} %get-tuple-element.43), channel_id=1, source_target_pairs={{8,2},{2,8},{10,4},{4,10},{12,6},{6,12},{14,7},{7,14},{15,5},{5,15... | collective-permute-start | bytes 393224 | tf_op jit(solution)/shard_map/ppermute | solution.py:837

commit v7 on v6

--- a/solution.py
+++ b/solution.py
@@ -483,23 +483,103 @@
     store_faces(lay, g_ref, face_ref)
 
 
-def restriction(lay, g_ref, dinv_ref, interp_ref, send_ref):
-    inner = jnp.where(dinv_ref[...] != 0.0, g_ref[...], 0.0)
-    high, low = split(inner)
+def restrict_rows(lay, field, interp_ref):
+    high, low = split(field)
     both = jnp.dot(
         interp_ref[...], jnp.concatenate([high, low], 1), preferred_element_type=F32
     )
     load = both[:N, : lay.width] + both[:N, lay.width :] + both[N:, : lay.width]
     rows = [load[n : n + 1] for n in range(N)]
     rows = [rows[n] + roll(rows[4 + n], lay.step_x, 1) for n in range(4)]
-    rows = [rows[n] + roll(rows[2 + n], lay.step_y, 1) for n in range(2)]
+    return [rows[n] + roll(rows[2 + n], lay.step_y, 1) for n in range(2)]
+
+
+def send_loads(lay, own, outer, far, send_ref, token_ref):
+    _, _, part_z = lane_parts(lay, own[0].shape)
+    bottom = part_z == 0
+    before = jnp.where(bottom, 0.0, roll(outer[0], 1, 1))
+    here = own[0] + jnp.where(bottom, outer[1], roll(own[1], 1, 1))
+    after = jnp.where(bottom, roll(own[1], -1, 1) + roll(outer[0], -1, 1), outer[1])
+    second = jnp.zeros_like(here)
+    if far is not None:
+        before = before + jnp.where(bottom, far[0], roll(far[1], 1, 1))
+        after = after + jnp.where(bottom, 0.0, far[0])
+        second = jnp.where(bottom, roll(far[1], -1, 1), 0.0)
+    rows = jnp.concatenate([before, here, after, second] * 2, 0)
     for d in range(send_ref.shape[0]):
-        send_ref[d, 0:1] = rows[0]
-        send_ref[d, 1:2] = rows[1]
+        send_ref[d] = rows
+    token_ref[...] = jnp.zeros(token_ref.shape, F32)
+
+
+def embed_faces(lay, u_ref, out_ref):
+    low, high = get_rows(u_ref, 0), get_rows(u_ref, N - 1)
+    _, _, part_z = lane_parts(lay, low.shape)
+    out_ref[...] = jnp.zeros(out_ref.shape, F32)
+    set_rows(out_ref, N - 1, jnp.where(part_z == 0, low, 0.0))
+    set_rows(out_ref, 0, jnp.where(part_z == 0, 0.0, high))
 
 
 OLD = RHO_SECOND * RHO_FIRST
 NEW = 2.0 * RHO_SECOND / DELTA
+
+
+def first_response(
+    lay, one, g_ref, x_ref, dinv_ref, high_ref, low_ref, along_ref, interp_ref, send_ref, token_ref, s_ref, u_ref, t_ref
+):
+    tile = (high_ref, low_ref, along_ref)
+    assemble(lay, g_ref, s_ref, jnp.zeros((FACE, lay.width), F32))
+    update = NEW * dinv_ref[...] * s_ref[...]
+    s_ref[...] = update
+    u_ref[...] = OLD * x_ref[...] + update
+    t_ref[...] = g_ref[...]
+    subtract_stiffness(lay, one, u_ref, t_ref, *tile)
+    own = restrict_rows(lay, t_ref[...], interp_ref)
+    embed_faces(lay, s_ref, u_ref)
+    t_ref[...] = jnp.zeros(t_ref.shape, F32)
+    subtract_stiffness(lay, one, u_ref, t_ref, *tile)
+    outer = restrict_rows(lay, t_ref[...], interp_ref)
+    send_loads(lay, own, outer, None, send_ref, token_ref)
+
+
+def pair_response(
+    lay,
+    one,
+    g_ref,
+    dinv_ref,
+    outer_ref,
+    high_ref,
+    low_ref,
+    along_ref,
+    interp_ref,
+    send_ref,
+    token_ref,
+    s_ref,
+    sh_ref,
+    u_ref,
+    v_ref,
+    t_ref,
+    h_ref,
+):
+    tile = (high_ref, low_ref, along_ref)
+    assemble(lay, g_ref, s_ref, jnp.zeros((FACE, lay.width), F32))
+    u_ref[...] = (1.0 / THETA) * dinv_ref[...] * s_ref[...]
+    t_ref[...] = g_ref[...]
+    subtract_stiffness(lay, one, u_ref, t_ref, *tile)
+    embed_faces(lay, u_ref, v_ref)
+    h_ref[...] = jnp.zeros(h_ref.shape, F32)
+    subtract_stiffness(lay, one, v_ref, h_ref, *tile)
+    assemble_both(lay, t_ref, h_ref, s_ref, sh_ref)
+    u_ref[...] = OLD * u_ref[...] + NEW * dinv_ref[...] * s_ref[...]
+    v_ref[...] = OLD * v_ref[...] + NEW * outer_ref[...] * sh_ref[...]
+    subtract_stiffness(lay, one, u_ref, t_ref, *tile)
+    own = restrict_rows(lay, t_ref[...], interp_ref)
+    subtract_stiffness(lay, one, v_ref, h_ref, *tile)
+    outer = restrict_rows(lay, h_ref[...], interp_ref)
+    embed_faces(lay, v_ref, u_ref)
+    t_ref[...] = jnp.zeros(t_ref.shape, F32)
+    subtract_stiffness(lay, one, u_ref, t_ref, *tile)
+    far = restrict_rows(lay, t_ref[...], interp_ref)
+    send_loads(lay, own, outer, far, send_ref, token_ref)
 
 
 def second_kernel(
@@ -513,10 +593,9 @@
     high_ref,
     low_ref,
     along_ref,
-    interp_ref,
+    token_ref,
     g_out,
     x_out,
-    send_ref,
     core_out,
     chip_out,
     s_ref,
@@ -528,23 +607,26 @@
     x_out[...] = x_ref[...] + update
     g_out[...] = g_ref[...]
     subtract_stiffness(lay, one, u_ref, g_out, high_ref, low_ref, along_ref)
-    restriction(lay, g_out, dinv_ref, interp_ref, send_ref)
     send_layers(lay, g_out, s_ref, core_out, chip_out)
 
 
-def solve_coarse(lay, mass, stiff, loads_ref, first_ref, second_ref):
+def solve_coarse(lay, mass, stiff, loads_ref, rows_ref, first_ref, second_ref):
+    count = 4
     for s in range(lay.slabs):
-        d = lay.order[s]
-        first_ref[pl.ds(s, 1), :] = loads_ref[d, 0:1]
-        second_ref[pl.ds(s, 1), :] = loads_ref[d, 1:2]
+        rows_ref[pl.ds(s * count, count), :] = loads_ref[lay.order[s], :count]
+
+    def part(n):
+        if lay.width == 128:
+            return rows_ref[pl.ds(n, lay.slabs, stride=count), :]
+        return jnp.concatenate(
+            [rows_ref[pl.ds(s * count + n, 1), :] for s in range(lay.slabs)], 0
+        )
+
     shape = (lay.slabs, lay.width)
     part_x, part_y, part_z = lane_parts(lay, shape)
     row = lax.broadcasted_iota(jnp.int32, shape, 0)
     keep = ((part_x > 0) & (part_y > 0) & ((part_z > 0) | (row > 0))).astype(F32)
     bottom = part_z == 0
-
-    def below(v):
-        return jnp.where(bottom, roll(roll(v, 1, 0), -1, 1), roll(v, 1, 1))
 
     def around_z(v):
         return jnp.where(bottom, roll(v + roll(v, 1, 0), -1, 1), roll(v + roll(v, -1, 0), 1, 1))
@@ -572,8 +654,7 @@
     def inner(a, b):
         return jnp.sum(jnp.sum(a * b, axis=1, keepdims=True), axis=0, keepdims=True)
 
-    here = pl.ds(0, lay.slabs)
-    residual = keep * (first_ref[here, :] + below(second_ref[here, :]))
+    residual = keep * (part(1) + roll(part(0), -1, 0) + roll(part(2), 1, 0) + roll(part(3), 2, 0))
     image = operate(residual)
     total = jnp.zeros(shape, F32)
     for step in range(CG_STEPS):
@@ -639,20 +720,19 @@
     high_ref, low_ref, along_ref, edge_high_ref, edge_low_ref = (refs.pop(0) for _ in range(5))
     if coarse:
         loads_ref, image_ref, image_edge_ref = (refs.pop(0) for _ in range(3))
-    if coarse or kind == "restrict":
         interp_ref = refs.pop(0)
-    if kind != "last":
-        extra_ref = refs.pop(0)
+    if kind == "inner":
+        token_ref, points_ref = refs.pop(0), refs.pop(0)
+    if kind == "last":
+        token_ref = refs.pop(0)
     if kind == "last":
         out_ref = refs.pop(0)
     else:
         g_out, x_out = refs.pop(0), refs.pop(0)
-        if kind == "restrict":
-            send_ref = refs.pop(0)
         core_out, chip_out = refs.pop(0), refs.pop(0)
-        if kind == "plain":
+        if kind == "inner":
             points_out = refs.pop(0)
-            points_out[...] = extra_ref[...]
+            points_out[...] = points_ref[...]
     s_ref, sh_ref, h_ref, u_ref = (refs.pop(0) for _ in range(4))
     if kind == "last":
         g_out, x_out = refs.pop(0), refs.pop(0)
@@ -661,8 +741,8 @@
     x_out[...] = x_ref[...]
     receive_layers(lay, core_ref, chip_ref, h_ref)
     if coarse:
-        first_ref, second_ref = refs
-        solve_coarse(lay, *coarse, loads_ref, first_ref, second_ref)
+        rows_ref, first_ref, second_ref = refs
+        solve_coarse(lay, *coarse, loads_ref, rows_ref, first_ref, second_ref)
         prolong_coarse(
             lay, first_ref, second_ref, interp_ref, image_ref, image_edge_ref, g_out, h_ref, x_out
         )
@@ -688,8 +768,6 @@
     x_out[...] += update + following
     u_ref[...] = following
     subtract_stiffness(lay, one, u_ref, g_out, high_ref, low_ref, along_ref)
-    if kind == "restrict":
-        restriction(lay, g_out, dinv_ref, interp_ref, send_ref)
     send_layers(lay, g_out, s_ref, core_out, chip_out)
 
 
@@ -842,7 +920,7 @@
 
     face_shape = (FACE, width)
     layer = (N**3 // 2, width)
-    loads_shape = (lay.slabs, 2, width)
+    loads_shape = (lay.slabs, N, width)
     table = (devices, -(-9 * N * local_points // 128) * 128)
     g, x, dinv, outer, face, points = call(
         functools.partial(first_kernel, lay, local_points, derivative, one, factor),
@@ -850,10 +928,18 @@
         [recv, high, low, along],
         [fields, face_shape, (width, N**3), pltpu.SMEM(table, F32), pltpu.SemaphoreType.DMA],
     )
-    g, x, loads, core, chip = call(
+    faces = swap(face, face)
+    loads, token = call(
+        functools.partial(first_response, lay, one),
+        [loads_shape, (N, 128)],
+        [g, x, dinv, high, low, along, restrict3],
+        [fields] * 3,
+    )
+    loads = gather(loads)
+    g, x, core, chip = call(
         functools.partial(second_kernel, lay, one),
-        [fields, fields, loads_shape, layer, layer],
-        [*swap(face, face), g, x, dinv, high, low, along, restrict3],
+        [fields, fields, layer, layer],
+        [*faces, g, x, dinv, high, low, along, token],
         [fields, fields],
     )
     coarse = ((mass[0, 0], mass[0, 1]), (stiff[0, 0], stiff[0, 1]))
@@ -862,33 +948,40 @@
     for cycle in range(CYCLES):
         core, chip = swap(core, chip)
         last = cycle + 1 == CYCLES
-        outs = [fields, fields, layer, layer, table]
-        extra = [points]
+        outs = [fields, fields, layer, layer]
+        extra = [done] if last else []
         scratch = [fields] * 4
         if last:
-            extra = []
             outs = [(lay.mesh_x * lay.mesh_y, block, N**3)]
             scratch += [fields, fields]
         outs = call(
             functools.partial(pair_kernel, lay, one, coarse, "last" if last else "plain"),
             outs,
-            [core, chip, g, x, dinv, outer, *stiffness, gather(loads), image3, image_edge, prolong3, *extra],
-            scratch + [(lay.slabs + 2 * N, width)] * 2,
+            [core, chip, g, x, dinv, outer, *stiffness, loads, image3, image_edge, prolong3, *extra],
+            scratch + [(lay.slabs * 4, width)] + [(lay.slabs + 2 * N, width)] * 2,
         )
         if last:
             break
-        g, x, core, chip, points = outs
+        g, x, core, chip = outs
+        layers = swap(core, chip)
+        loads, token = call(
+            functools.partial(pair_response, lay, one),
+            [loads_shape, (N, 128)],
+            [g, dinv, outer, high, low, along, restrict3],
+            [fields] * 6,
+        )
+        loads = gather(loads)
+        g, x, core, chip, points = call(
+            functools.partial(pair_kernel, lay, one, None, "inner"),
+            [fields, fields, layer, layer, table],
+            [*layers, g, x, dinv, outer, *stiffness, token, points],
+            [fields] * 4,
+        )
         forces, done = call(
             functools.partial(forces_kernel, tiles_y, local_points),
             [(3, N**3, tiles_y * EZ), (N, 128)],
             [points],
             smem=1,
-        )
-        g, x, loads, core, chip = call(
-            functools.partial(pair_kernel, lay, one, None, "restrict"),
-            [fields, fields, loads_shape, layer, layer],
-            [*swap(core, chip), g, x, dinv, outer, *stiffness, restrict3, done],
-            [fields] * 4,
         )
     (out,) = outs
     if not lay.joint:

time: 74.6 us -> 76.5 us (1.025)
  blocking collectives: 49.9 us -> 32.5 us
  starting transfers between devices: 3.94 us -> 16.2 us
  Pallas kernels: 16.1 us -> 20.6 us
  waiting for transfers between devices: 3.39 us -> 6.16 us
    all_to_all x2 -> x0, blocking collectives: 19.8 us -> none  [gather(): return lax.all_to_all(loads, lay.axis, 0, 0)]
    all_to_all x0 -> x2, starting transfers between devices: none -> 7.4 us  [gather(): return lax.all_to_all(loads, lay.axis, 0, 0)]
    pallas_call x8 -> x10, Pallas kernels: 16.1 us -> 20.6 us  [call(): pl.pallas_call(kernel, out_shape=shapes, in_specs=specs, out_specs=[pl.Bl...]
    ppermute x4, starting transfers between devices: 2.82 us -> 5.46 us  [swap(): lax.ppermute(chip, lay.axis, lay.swaps(1))]
    all_to_all x1, blocking collectives: 12.4 us -> 14.7 us  [shards(): out = lax.all_to_all(out, lay.axis, 0, 0)]
    ppermute x4, starting transfers between devices: 1.12 us -> 3.38 us  [swap(): lax.ppermute(core, lay.axis, lay.swaps(0))]
    all_to_all x0 -> x2, waiting for transfers between devices: none -> 1.56 us  [gather(): return lax.all_to_all(loads, lay.axis, 0, 0)]
    ppermute x4, waiting for transfers between devices: 3.38 us -> 4.59 us  [swap(): lax.ppermute(chip, lay.axis, lay.swaps(1))]
  transfers between devices with their start and end apart: 8 -> 10, of which waited for: 2 -> 3; matrix products, arithmetic and copies ran while one was open for 0% -> 0% of each run, Pallas kernels for 3% -> 10%
where the time goes in v7:
time: 76.5 us; the launch traced here: 76.3 us
  blocking collectives  32.5 us (42%)
  Pallas kernels  20.6 us (27%)
  starting transfers between devices  16.2 us (21%)
  waiting for transfers between devices  6.16 us (8%)
  between operations  0.81 us (1%)
    pallas_call x10, Pallas kernels, call(): pl.pallas_call(kernel, out_shape=shapes, in_specs=specs, out_specs=[pl.Bl...  20.6 us
    all_to_all x1, blocking collectives, shards(): recv = lax.all_to_all(send, lay.axis, 0, 0)  17.8 us
    all_to_all x1, blocking collectives, shards(): out = lax.all_to_all(out, lay.axis, 0, 0)  14.7 us
    all_to_all x2, starting transfers between devices, gather(): return lax.all_to_all(loads, lay.axis, 0, 0)  7.4 us
    ppermute x4, starting transfers between devices, swap(): lax.ppermute(chip, lay.axis, lay.swaps(1))  5.46 us
    ppermute x4, waiting for transfers between devices, swap(): lax.ppermute(chip, lay.axis, lay.swaps(1))  4.59 us
    ppermute x4, starting transfers between devices, swap(): lax.ppermute(core, lay.axis, lay.swaps(0))  3.38 us
    all_to_all x2, waiting for transfers between devices, gather(): return lax.all_to_all(loads, lay.axis, 0, 0)  1.56 us
  transfers between devices with their start and end apart: 10, of which 3 were waited for; matrix products, arithmetic and copies ran while one was open for 0% of the time, Pallas kernels for 10%

profile of v7, /device:TPU:0, one launch (start us, length us, event | category | flops | bytes accessed | tf_op | source)
XLA Modules:
  0.0 76.3 jit_solution(3048836838698066878)
XLA Ops:
  0.6 1.4 %shard_map.140 = f32[32,4,512]{2,1,0:T(4,128)S(1)} custom-call(s32[1,3]{1,0:T(1,128)} %bitcast.12, f32[1,3]{1,0:T(1,128)} %bitcast.13, f32[1,3]{1,0:T(1,128)} %bitcast.14, f32[512,128]{1,0:T(8,128)} %bitcast.10), custom_call_target="tpu_custom_call" | custom-call | tf_op jit(solution)/shard_map/pallas_call | solution.py:840
  2.0 0.0 copy-start
  2.0 0.0 copy-start.1
  2.0 0.0 copy-start.2
  2.0 17.8 %all_to_all.20.recv_ref = f32[32,4,512]{2,1,0:T(4,128)S(1)} all-to-all(f32[32,4,512]{2,1,0:T(4,128)S(1)} %shard_map.140), channel_id=1, replica_groups=mesh['ex'=4,'ey'=8] {'ex','ey'}, dimensions={0} | all-to-all | bytes 524288 | tf_op jit(solution)/shard_map/all_to_all | solution.py:908
  19.8 0.0 copy-start.8
  19.8 2.3 %shard_map.141 = (f32[512,128]{1,0:T(8,128)S(1)}, f32[512,128]{1,0:T(8,128)S(1)}, f32[512,128]{1,0:T(8,128)S(1)}, f32[512,128]{1,0:T(8,128)S(1)}, f32[64,128]{1,0:T(8,128)S(1)}, /*index=5*/f32[32,128]{1,0:T(8,128)S(1)}) custom-call(f32[32,4,512]{2,1,0:T(4,128)S(1)} %all_to_all.20.recv_ref, bf16[256,256]{1,0:T(8,128)(2,1)S(1)} %copy-done.1, ...), custom_call_target="tpu_custom_call" | custom-call | tf_op jit(solution)/shard_map/pallas_call | solution.py:840
  22.1 1.9 %shard_map.142 = (f32[32,8,128]{2,1,0:T(8,128)}, f32[8,128]{1,0:T(8,128)S(1)}) custom-call(f32[512,128]{1,0:T(8,128)S(1)} %get-tuple-element.28.g_ref, f32[512,128]{1,0:T(8,128)S(1)} %get-tuple-element.29.x_ref, f32[512,128]{1,0:T(8,128)S(1)} %get-tuple-element.30.dinv_ref, bf16[256,256]{1,0:T(8,128)(2,1)S(1)} %copy-done.1, bf16[256,256]{1,0:T(8,128)(2,1)S(1)} %copy-done, ...), custom_call_target="tpu_custom_call" | custom-call | tf_op jit(solution)/shard_map/pallas_call | solution.py:840
  24.0 3.0 %all-to-all-start.1 = ((f32[32,8,128]{2,1,0:T(8,128)}), f32[32,8,128]{2,1,0:T(8,128)S(1)}, u32[]{:S(2)}, u32[]{:S(2)}) async-start(f32[32,8,128]{2,1,0:T(8,128)} %get-tuple-element.37), calls=%async_computation.1 | async-start | bytes 262144 | tf_op jit(solution)/shard_map/all_to_all | solution.py:919
  27.0 1.6 %collective-permute-start.1 = (f32[64,128]{1,0:T(8,128)S(1)}, f32[64,128]{1,0:T(8,128)S(1)}, u32[]{:S(2)}, u32[]{:S(2)}) collective-permute-start(f32[64,128]{1,0:T(8,128)S(1)} %get-tuple-element.27), channel_id=1, source_target_pairs={{8,2},{2,8},{10,4},{4,10},{12,6},{6,12},{14,7},{7,14},{15,5},{5,15... | collective-permute-start | bytes 98312 | tf_op jit(solution)/shard_map/ppermute | solution.py:915
  28.6 0.4 collective-permute-start
  28.9 1.5 %collective-permute-done.1.chip_ref = f32[64,128]{1,0:T(8,128)S(1)} collective-permute-done((f32[64,128]{1,0:T(8,128)S(1)}, f32[64,128]{1,0:T(8,128)S(1)}, u32[]{:S(2)}, u32[]{:S(2)}) %collective-permute-start.1) | collective-permute-done | bytes 32800 | tf_op jit(solution)/shard_map/ppermute | solution.py:915
  30.4 0.0 copy-start.6
  30.4 0.0 copy-start.7
  30.4 0.8 %shard_map.143 = (f32[512,128]{1,0:T(8,128)S(1)}, f32[512,128]{1,0:T(8,128)S(1)}, f32[256,128]{1,0:T(8,128)S(1)}, f32[256,128]{1,0:T(8,128)S(1)}) custom-call(f32[64,128]{1,0:T(8,128)S(1)} %collective-permute-done.core_ref, f32[64,128]{1,0:T(8,128)S(1)} %collective-permute-done.1.chip_ref, f32[512,128]{1,0:T(8,128)S(1)} %get-tuple-element.28.g_ref, ...), custom_call_target="tpu_custom_call" | custom-call | tf_op jit(solution)/shard_map/pallas_call | solution.py:840
  31.2 1.2 %collective-permute-start.2 = (f32[256,128]{1,0:T(8,128)S(1)}, f32[256,128]{1,0:T(8,128)S(1)}, u32[]{:S(2)}, u32[]{:S(2)}) collective-permute-start(f32[256,128]{1,0:T(8,128)S(1)} %get-tuple-element.32), channel_id=1, source_target_pairs={{0,8},{8,0},{2,10},{10,2},{4,12},{12,4},{6,14},{14,6},{7,15},{15,7... | collective-permute-start | bytes 393224 | tf_op jit(solution)/shard_map/ppermute | solution.py:914
  32.4 1.3 %collective-permute-start.3 = (f32[256,128]{1,0:T(8,128)S(1)}, f32[256,128]{1,0:T(8,128)S(1)}, u32[]{:S(2)}, u32[]{:S(2)}) collective-permute-start(f32[256,128]{1,0:T(8,128)S(1)} %get-tuple-element.33), channel_id=1, source_target_pairs={{8,2},{2,8},{10,4},{4,10},{12,6},{6,12},{14,7},{7,14},{15,5},{5,15... | collective-permute-start | bytes 393224 | tf_op jit(solution)/shard_map/ppermute | solution.py:915
  33.7 0.0 collective-permute-done.2.core_ref
  33.7 3.1 %collective-permute-done.3.chip_ref = f32[256,128]{1,0:T(8,128)S(1)} collective-permute-done((f32[256,128]{1,0:T(8,128)S(1)}, f32[256,128]{1,0:T(8,128)S(1)}, u32[]{:S(2)}, u32[]{:S(2)}) %collective-permute-start.3) | collective-permute-done | bytes 131104 | tf_op jit(solution)/shard_map/ppermute | solution.py:915
  36.8 3.3 %shard_map.144 = (f32[512,128]{1,0:T(8,128)S(1)}, f32[512,128]{1,0:T(8,128)S(1)}, f32[256,128]{1,0:T(8,128)S(1)}, f32[256,128]{1,0:T(8,128)S(1)}) custom-call(f32[256,128]{1,0:T(8,128)S(1)} %collective-permute-done.2.core_ref, f32[256,128]{1,0:T(8,128)S(1)} %collective-permute-done.3.chip_ref, f32[512,128]{1,0:T(8,128)S(1)} %get-tuple-element.34.g_ref, ...), custom_call_target="tpu_custom_call" | custom-call | tf_op jit(solution)/shard_map/pallas_call | solution.py:840
  40.2 1.5 %collective-permute-start.4 = (f32[256,128]{1,0:T(8,128)S(1)}, f32[256,128]{1,0:T(8,128)S(1)}, u32[]{:S(2)}, u32[]{:S(2)}) collective-permute-start(f32[256,128]{1,0:T(8,128)S(1)} %get-tuple-element.38), channel_id=1, source_target_pairs={{0,8},{8,0},{2,10},{10,2},{4,12},{12,4},{6,14},{14,6},{7,15},{15,7... | collective-permute-start | bytes 393224 | tf_op jit(solution)/shard_map/ppermute | solution.py:914
  41.7 1.0 %collective-permute-start.5 = (f32[256,128]{1,0:T(8,128)S(1)}, f32[256,128]{1,0:T(8,128)S(1)}, u32[]{:S(2)}, u32[]{:S(2)}) collective-permute-start(f32[256,128]{1,0:T(8,128)S(1)} %get-tuple-element.39), channel_id=1, source_target_pairs={{8,2},{2,8},{10,4},{4,10},{12,6},{6,12},{14,7},{7,14},{15,5},{5,15... | collective-permute-start | bytes 393224 | tf_op jit(solution)/shard_map/ppermute | solution.py:915
  42.7 2.9 %shard_map.145 = (f32[32,8,128]{2,1,0:T(8,128)}, f32[8,128]{1,0:T(8,128)S(1)}) custom-call(f32[512,128]{1,0:T(8,128)S(1)} %get-tuple-element.40.g_ref, f32[512,128]{1,0:T(8,128)S(1)} %get-tuple-element.30.dinv_ref, f32[512,128]{1,0:T(8,128)S(1)} %get-tuple-element.36.outer_ref, bf16[256,256]{1,0:T(8,128)(2,1)S(1)} %copy-done.1, ...), custom_call_target="tpu_custom_call" | custom-call | tf_op jit(solution)/shard_map/pallas_call | solution.py:840
  45.6 4.4 %all-to-all-start.2 = ((f32[32,8,128]{2,1,0:T(8,128)}), f32[32,8,128]{2,1,0:T(8,128)S(1)}, u32[]{:S(2)}, u32[]{:S(2)}) async-start(f32[32,8,128]{2,1,0:T(8,128)} %get-tuple-element.48), calls=%async_computation.2 | async-start | bytes 262144 | tf_op jit(solution)/shard_map/all_to_all | solution.py:919
  50.0 1.6 %shard_map.146 = (f32[512,128]{1,0:T(8,128)S(1)}, f32[512,128]{1,0:T(8,128)S(1)}, f32[256,128]{1,0:T(8,128)S(1)}, f32[256,128]{1,0:T(8,128)S(1)}, f32[32,128]{1,0:T(8,128)S(1)}) custom-call(f32[256,128]{1,0:T(8,128)S(1)} %collective-permute-done.4.core_ref, f32[256,128]{1,0:T(8,128)S(1)} %collective-permute-done.5.chip_ref, ...), custom_call_target="tpu_custom_call" | custom-call | tf_op jit(solution)/shard_map/pallas_call | solution.py:840
  51.6 0.3 collective-permute-start.6
  52.0 1.6 %collective-permute-start.7 = (f32[256,128]{1,0:T(8,128)S(1)}, f32[256,128]{1,0:T(8,128)S(1)}, u32[]{:S(2)}, u32[]{:S(2)}) collective-permute-start(f32[256,128]{1,0:T(8,128)S(1)} %get-tuple-element.45), channel_id=1, source_target_pairs={{8,2},{2,8},{10,4},{4,10},{12,6},{6,12},{14,7},{7,14},{15,5},{5,15... | collective-permute-start | bytes 393224 | tf_op jit(solution)/shard_map/ppermute | solution.py:915
  53.6 2.7 %shard_map.147 = (f32[3,512,128]{2,1,0:T(8,128)}, f32[8,128]{1,0:T(8,128)S(1)}) custom-call(f32[32,128]{1,0:T(8,128)S(1)} %get-tuple-element.49.points_ref), custom_call_target="tpu_custom_call" | custom-call | tf_op jit(solution)/shard_map/pallas_call | solution.py:840
  56.3 1.6 %all-to-all-done.2.refs_5_ = f32[32,8,128]{2,1,0:T(8,128)S(1)} async-done(((f32[32,8,128]{2,1,0:T(8,128)}), f32[32,8,128]{2,1,0:T(8,128)S(1)}, u32[]{:S(2)}, u32[]{:S(2)}) %all-to-all-start.2) | async-done | bytes 131104 | tf_op jit(solution)/shard_map/all_to_all | solution.py:919
  57.8 2.9 %shard_map.148 = f32[32,4,512]{2,1,0:T(4,128)S(1)} custom-call(f32[256,128]{1,0:T(8,128)S(1)} %collective-permute-done.6.core_ref, f32[256,128]{1,0:T(8,128)S(1)} %collective-permute-done.7.chip_ref, f32[512,128]{1,0:T(8,128)S(1)} %get-tuple-element.46.g_ref, f32[512,128]{1,0:T(8,128)S(1)} %get-tuple-element.47.x_ref, ...), custom_call_target="tpu_custom_call" | custom-call | tf_op jit(solution)/shard_map/pallas_call | solution.py:840
  60.7 14.7 %all_to_all.21.recv_ref = f32[32,4,512]{2,1,0:T(4,128)S(1)} all-to-all(f32[32,4,512]{2,1,0:T(4,128)S(1)} %shard_map.148), channel_id=1, replica_groups=mesh['ex'=4,'ey'=8] {'ex','ey'}, dimensions={0} | all-to-all | bytes 524288 | tf_op jit(solution)/shard_map/all_to_all | solution.py:989
  75.4 0.9 %shard_map.149 = f32[512,128]{1,0:T(8,128)} custom-call(f32[32,4,512]{2,1,0:T(4,128)S(1)} %all_to_all.21.recv_ref), custom_call_target="tpu_custom_call" | custom-call | tf_op jit(solution)/shard_map/pallas_call | solution.py:840
  (18 shorter events, 0.0 us)
Async XLA Ops:
  2.0 17.8 %copy-start = (bf16[256,256]{1,0:T(8,128)(2,1)S(1)}, bf16[256,256]{1,0:T(8,128)(2,1)}, u32[]{:S(2)}) copy-start(bf16[256,256]{1,0:T(8,128)(2,1)} %constant.19.clone.low_ref.refs_1_) | copy-start | bytes 393220
  2.0 17.8 %copy-start.1 = (bf16[256,256]{1,0:T(8,128)(2,1)S(1)}, bf16[256,256]{1,0:T(8,128)(2,1)}, u32[]{:S(2)}) copy-start(bf16[256,256]{1,0:T(8,128)(2,1)} %constant.18.clone.high_ref.refs_0_) | copy-start | bytes 393220
  2.0 17.8 %copy-start.2 = (f32[64,128]{1,0:T(8,128)S(1)}, f32[64,128]{1,0:T(8,128)}, u32[]{:S(2)}) copy-start(f32[64,128]{1,0:T(8,128)} %constant.20.clone.along_ref.refs_2_) | copy-start | bytes 98308
  19.8 2.3 %copy-start.8 = (bf16[16,512]{1,0:T(8,128)(2,1)S(1)}, bf16[16,512]{1,0:T(8,128)(2,1)}, u32[]{:S(2)}) copy-start(bf16[16,512]{1,0:T(8,128)(2,1)} %constant.23.clone.interp_ref) | copy-start | bytes 49156
  24.0 12.8 %all-to-all-start.1 = ((f32[32,8,128]{2,1,0:T(8,128)}), f32[32,8,128]{2,1,0:T(8,128)S(1)}, u32[]{:S(2)}, u32[]{:S(2)}) async-start(f32[32,8,128]{2,1,0:T(8,128)} %get-tuple-element.37), calls=%async_computation.1 | async-start | bytes 262144 | tf_op jit(solution)/shard_map/all_to_all | solution.py:919
  27.0 3.4 %collective-permute-start.1 = (f32[64,128]{1,0:T(8,128)S(1)}, f32[64,128]{1,0:T(8,128)S(1)}, u32[]{:S(2)}, u32[]{:S(2)}) collective-permute-start(f32[64,128]{1,0:T(8,128)S(1)} %get-tuple-element.27), channel_id=1, source_target_pairs={{8,2},{2,8},{10,4},{4,10},{12,6},{6,12},{14,7},{7,14},{15,5},{5,15... | collective-permute-start | bytes 98312 | tf_op jit(solution)/shard_map/ppermute | solution.py:915
  28.6 1.8 %collective-permute-start = (f32[64,128]{1,0:T(8,128)S(1)}, f32[64,128]{1,0:T(8,128)S(1)}, u32[]{:S(2)}, u32[]{:S(2)}) collective-permute-start(f32[64,128]{1,0:T(8,128)S(1)} %get-tuple-element.27), channel_id=1, source_target_pairs={{0,8},{8,0},{2,10},{10,2},{4,12},{12,4},{6,14},{14,6},{7,15},{15,7... | collective-permute-start | bytes 98312 | tf_op jit(solution)/shard_map/ppermute | solution.py:914
  30.4 6.4 %copy-start.3 = (bf16[128,512]{1,0:T(8,128)(2,1)S(1)}, bf16[128,512]{1,0:T(8,128)(2,1)}, u32[]{:S(2)}) copy-start(bf16[128,512]{1,0:T(8,128)(2,1)} %constant.22.clone.refs_4_) | copy-start | bytes 393220
  30.4 6.4 %copy-start.4 = (bf16[128,512]{1,0:T(8,128)(2,1)S(1)}, bf16[128,512]{1,0:T(8,128)(2,1)}, u32[]{:S(2)}) copy-start(bf16[128,512]{1,0:T(8,128)(2,1)} %constant.21.clone.refs_3_) | copy-start | bytes 393220
  30.4 6.4 %copy-start.5 = (bf16[512,32]{1,0:T(8,128)(2,1)S(1)}, bf16[512,32]{1,0:T(8,128)(2,1)}, u32[]{:S(2)}) copy-start(bf16[512,32]{1,0:T(8,128)(2,1)} %constant.25.clone.refs_6_) | copy-start | bytes 98308
  30.4 6.4 %copy-start.6 = (bf16[512,32]{1,0:T(8,128)(2,1)S(1)}, bf16[512,32]{1,0:T(8,128)(2,1)}, u32[]{:S(2)}) copy-start(bf16[512,32]{1,0:T(8,128)(2,1)} %constant.24.clone.refs_8_) | copy-start | bytes 98308
  30.4 6.4 %copy-start.7 = (bf16[128,32]{1,0:T(8,128)(2,1)S(1)}, bf16[128,32]{1,0:T(8,128)(2,1)}, u32[]{:S(2)}) copy-start(bf16[128,32]{1,0:T(8,128)(2,1)} %constant.26.clone.refs_7_) | copy-start | bytes 24580
  31.2 2.4 %collective-permute-start.2 = (f32[256,128]{1,0:T(8,128)S(1)}, f32[256,128]{1,0:T(8,128)S(1)}, u32[]{:S(2)}, u32[]{:S(2)}) collective-permute-start(f32[256,128]{1,0:T(8,128)S(1)} %get-tuple-element.32), channel_id=1, source_target_pairs={{0,8},{8,0},{2,10},{10,2},{4,12},{12,4},{6,14},{14,6},{7,15},{15,7... | collective-permute-start | bytes 393224 | tf_op jit(solution)/shard_map/ppermute | solution.py:914
  32.4 4.4 %collective-permute-start.3 = (f32[256,128]{1,0:T(8,128)S(1)}, f32[256,128]{1,0:T(8,128)S(1)}, u32[]{:S(2)}, u32[]{:S(2)}) collective-permute-start(f32[256,128]{1,0:T(8,128)S(1)} %get-tuple-element.33), channel_id=1, source_target_pairs={{8,2},{2,8},{10,4},{4,10},{12,6},{6,12},{14,7},{7,14},{15,5},{5,15... | collective-permute-start | bytes 393224 | tf_op jit(solution)/shard_map/ppermute | solution.py:915
  40.2 9.8 %collective-permute-start.4 = (f32[256,128]{1,0:T(8,128)S(1)}, f32[256,128]{1,0:T(8,128)S(1)}, u32[]{:S(2)}, u32[]{:S(2)}) collective-permute-start(f32[256,128]{1,0:T(8,128)S(1)} %get-tuple-element.38), channel_id=1, source_target_pairs={{0,8},{8,0},{2,10},{10,2},{4,12},{12,4},{6,14},{14,6},{7,15},{15,7... | collective-permute-start | bytes 393224 | tf_op jit(solution)/shard_map/ppermute | solution.py:914
  41.7 8.3 %collective-permute-start.5 = (f32[256,128]{1,0:T(8,128)S(1)}, f32[256,128]{1,0:T(8,128)S(1)}, u32[]{:S(2)}, u32[]{:S(2)}) collective-permute-start(f32[256,128]{1,0:T(8,128)S(1)} %get-tuple-element.39), channel_id=1, source_target_pairs={{8,2},{2,8},{10,4},{4,10},{12,6},{6,12},{14,7},{7,14},{15,5},{5,15... | collective-permute-start | bytes 393224 | tf_op jit(solution)/shard_map/ppermute | solution.py:915
  45.6 12.2 %all-to-all-start.2 = ((f32[32,8,128]{2,1,0:T(8,128)}), f32[32,8,128]{2,1,0:T(8,128)S(1)}, u32[]{:S(2)}, u32[]{:S(2)}) async-start(f32[32,8,128]{2,1,0:T(8,128)} %get-tuple-element.48), calls=%async_computation.2 | async-start | bytes 262144 | tf_op jit(solution)/shard_map/all_to_all | solution.py:919
  51.6 6.2 %collective-permute-start.6 = (f32[256,128]{1,0:T(8,128)S(1)}, f32[256,128]{1,0:T(8,128)S(1)}, u32[]{:S(2)}, u32[]{:S(2)}) collective-permute-start(f32[256,128]{1,0:T(8,128)S(1)} %get-tuple-element.44), channel_id=1, source_target_pairs={{0,8},{8,0},{2,10},{10,2},{4,12},{12,4},{6,14},{14,6},{7,15},{15,7... | collective-permute-start | bytes 393224 | tf_op jit(solution)/shard_map/ppermute | solution.py:914
  52.0 5.9 %collective-permute-start.7 = (f32[256,128]{1,0:T(8,128)S(1)}, f32[256,128]{1,0:T(8,128)S(1)}, u32[]{:S(2)}, u32[]{:S(2)}) collective-permute-start(f32[256,128]{1,0:T(8,128)S(1)} %get-tuple-element.45), channel_id=1, source_target_pairs={{8,2},{2,8},{10,4},{4,10},{12,6},{6,12},{14,7},{7,14},{15,5},{5,15... | collective-permute-start | bytes 393224 | tf_op jit(solution)/shard_map/ppermute | solution.py:915

commit v8 on v7

--- a/solution.py
+++ b/solution.py
@@ -218,12 +218,13 @@
     low = get_rows(g_ref, 0)
     high = get_rows(g_ref, N - 1)
     _, _, part_z = lane_parts(lay, low.shape)
-    face_ref[...] = jnp.where(part_z == 0, low, high)
+    face_ref[...] = jnp.zeros(face_ref.shape, F32)
+    face_ref[:FACE, :] = jnp.where(part_z == 0, low, high)
 
 
 def halo_of(lay, core_ref, chip_ref):
     odd = (lay.slab() & 1) == 1
-    core, chip = core_ref[...], chip_ref[...]
+    core, chip = core_ref[:FACE, :], chip_ref[:FACE, :]
     below = jnp.where(odd, core, chip)
     above = jnp.where(odd, chip, core)
     _, _, part_z = lane_parts(lay, core.shape)
@@ -483,15 +484,19 @@
     store_faces(lay, g_ref, face_ref)
 
 
-def restrict_rows(lay, field, interp_ref):
-    high, low = split(field)
-    both = jnp.dot(
-        interp_ref[...], jnp.concatenate([high, low], 1), preferred_element_type=F32
-    )
+def vertex_rows(lay, table_ref, values):
+    high, low = split(values)
+    both = jnp.dot(table_ref[...], jnp.concatenate([high, low], 1), preferred_element_type=F32)
     load = both[:N, : lay.width] + both[:N, lay.width :] + both[N:, : lay.width]
     rows = [load[n : n + 1] for n in range(N)]
     rows = [rows[n] + roll(rows[4 + n], lay.step_x, 1) for n in range(4)]
     return [rows[n] + roll(rows[2 + n], lay.step_y, 1) for n in range(2)]
+
+
+def face_values(lay, u_ref):
+    low, high = get_rows(u_ref, 0), get_rows(u_ref, N - 1)
+    _, _, part_z = lane_parts(lay, low.shape)
+    return jnp.where(part_z == 0, low, 0.0), jnp.where(part_z == 0, 0.0, high)
 
 
 def send_loads(lay, own, outer, far, send_ref, token_ref):
@@ -511,33 +516,19 @@
     token_ref[...] = jnp.zeros(token_ref.shape, F32)
 
 
-def embed_faces(lay, u_ref, out_ref):
-    low, high = get_rows(u_ref, 0), get_rows(u_ref, N - 1)
-    _, _, part_z = lane_parts(lay, low.shape)
-    out_ref[...] = jnp.zeros(out_ref.shape, F32)
-    set_rows(out_ref, N - 1, jnp.where(part_z == 0, low, 0.0))
-    set_rows(out_ref, 0, jnp.where(part_z == 0, 0.0, high))
-
-
 OLD = RHO_SECOND * RHO_FIRST
 NEW = 2.0 * RHO_SECOND / DELTA
 
 
 def first_response(
-    lay, one, g_ref, x_ref, dinv_ref, high_ref, low_ref, along_ref, interp_ref, send_ref, token_ref, s_ref, u_ref, t_ref
+    lay, g_ref, x_ref, dinv_ref, loads_ref, near_ref, send_ref, token_ref, s_ref
 ):
-    tile = (high_ref, low_ref, along_ref)
     assemble(lay, g_ref, s_ref, jnp.zeros((FACE, lay.width), F32))
     update = NEW * dinv_ref[...] * s_ref[...]
     s_ref[...] = update
-    u_ref[...] = OLD * x_ref[...] + update
-    t_ref[...] = g_ref[...]
-    subtract_stiffness(lay, one, u_ref, t_ref, *tile)
-    own = restrict_rows(lay, t_ref[...], interp_ref)
-    embed_faces(lay, s_ref, u_ref)
-    t_ref[...] = jnp.zeros(t_ref.shape, F32)
-    subtract_stiffness(lay, one, u_ref, t_ref, *tile)
-    outer = restrict_rows(lay, t_ref[...], interp_ref)
+    total = OLD * x_ref[...] + update
+    own = vertex_rows(lay, loads_ref, jnp.concatenate([g_ref[...], total], 0))
+    outer = vertex_rows(lay, near_ref, jnp.concatenate(face_values(lay, s_ref), 0))
     send_loads(lay, own, outer, None, send_ref, token_ref)
 
 
@@ -550,7 +541,8 @@
     high_ref,
     low_ref,
     along_ref,
-    interp_ref,
+    loads_ref,
+    near_ref,
     send_ref,
     token_ref,
     s_ref,
@@ -565,20 +557,18 @@
     u_ref[...] = (1.0 / THETA) * dinv_ref[...] * s_ref[...]
     t_ref[...] = g_ref[...]
     subtract_stiffness(lay, one, u_ref, t_ref, *tile)
-    embed_faces(lay, u_ref, v_ref)
+    low, high = face_values(lay, u_ref)
+    v_ref[...] = jnp.zeros(v_ref.shape, F32)
+    set_rows(v_ref, N - 1, low)
+    set_rows(v_ref, 0, high)
     h_ref[...] = jnp.zeros(h_ref.shape, F32)
     subtract_stiffness(lay, one, v_ref, h_ref, *tile)
     assemble_both(lay, t_ref, h_ref, s_ref, sh_ref)
-    u_ref[...] = OLD * u_ref[...] + NEW * dinv_ref[...] * s_ref[...]
+    update = OLD * u_ref[...] + NEW * dinv_ref[...] * s_ref[...]
+    own = vertex_rows(lay, loads_ref, jnp.concatenate([t_ref[...], update], 0))
     v_ref[...] = OLD * v_ref[...] + NEW * outer_ref[...] * sh_ref[...]
-    subtract_stiffness(lay, one, u_ref, t_ref, *tile)
-    own = restrict_rows(lay, t_ref[...], interp_ref)
-    subtract_stiffness(lay, one, v_ref, h_ref, *tile)
-    outer = restrict_rows(lay, h_ref[...], interp_ref)
-    embed_faces(lay, v_ref, u_ref)
-    t_ref[...] = jnp.zeros(t_ref.shape, F32)
-    subtract_stiffness(lay, one, u_ref, t_ref, *tile)
-    far = restrict_rows(lay, t_ref[...], interp_ref)
+    outer = vertex_rows(lay, loads_ref, jnp.concatenate([h_ref[...], v_ref[...]], 0))
+    far = vertex_rows(lay, near_ref, jnp.concatenate(face_values(lay, v_ref), 0))
     send_loads(lay, own, outer, far, send_ref, token_ref)
 
 
@@ -876,7 +866,14 @@
     factor = 1.0 / diag
     mass = interp.T @ diag_w @ interp
     stiff = interp.T @ stiff_one @ interp
-    restrict3 = jnp.asarray(np.concatenate(split_table(interp3.T), 0))
+    moved = -interp3.T @ full
+    loads_table, near_table = (
+        jnp.asarray(np.concatenate(split_table(t), 0))
+        for t in (
+            np.concatenate([interp3.T, moved], 1),
+            np.concatenate([moved[:, edge_rows[FACE:]], moved[:, edge_rows[:FACE]]], 1),
+        )
+    )
     prolong3, image3, image_edge = (
         jnp.asarray(stacked_table(t)) for t in (interp3, image3, image3[edge_rows])
     )
@@ -924,16 +921,16 @@
     table = (devices, -(-9 * N * local_points // 128) * 128)
     g, x, dinv, outer, face, points = call(
         functools.partial(first_kernel, lay, local_points, derivative, one, factor),
-        [fields, fields, fields, fields, face_shape, table],
+        [fields, fields, fields, fields, (256, width), table],
         [recv, high, low, along],
         [fields, face_shape, (width, N**3), pltpu.SMEM(table, F32), pltpu.SemaphoreType.DMA],
     )
     faces = swap(face, face)
     loads, token = call(
-        functools.partial(first_response, lay, one),
+        functools.partial(first_response, lay),
         [loads_shape, (N, 128)],
-        [g, x, dinv, high, low, along, restrict3],
-        [fields] * 3,
+        [g, x, dinv, loads_table, near_table],
+        [fields],
     )
     loads = gather(loads)
     g, x, core, chip = call(
@@ -967,7 +964,7 @@
         loads, token = call(
             functools.partial(pair_response, lay, one),
             [loads_shape, (N, 128)],
-            [g, dinv, outer, high, low, along, restrict3],
+            [g, dinv, outer, high, low, along, loads_table, near_table],
             [fields] * 6,
         )
         loads = gather(loads)

time: 76.5 us -> 72.3 us (0.945)
  starting transfers between devices: 16.2 us -> 12.5 us
  Pallas kernels: 20.6 us -> 19.4 us
    all_to_all x2, waiting for transfers between devices: 1.56 us -> 6.35 us  [gather(): return lax.all_to_all(loads, lay.axis, 0, 0)]
    ppermute x4, waiting for transfers between devices: 4.59 us -> 0.01 us  [swap(): lax.ppermute(chip, lay.axis, lay.swaps(1))]
    ppermute x4, starting transfers between devices: 3.38 us -> 1.32 us  [swap(): lax.ppermute(core, lay.axis, lay.swaps(0))]
    all_to_all x2, starting transfers between devices: 7.4 us -> 5.95 us  [gather(): return lax.all_to_all(loads, lay.axis, 0, 0)]
    pallas_call x10, Pallas kernels: 20.6 us -> 19.4 us  [call(): pl.pallas_call(kernel, out_shape=shapes, in_specs=specs, out_specs=[pl.Bl...]
  transfers between devices with their start and end apart: 10 -> 10, of which waited for: 3 -> 2; matrix products, arithmetic and copies ran while one was open for 0% -> 0% of each run, Pallas kernels for 10% -> 12%
where the time goes in v8:
time: 72.3 us; the launch traced here: 71.6 us
  blocking collectives  32.5 us (45%)
  Pallas kernels  19.4 us (27%)
  starting transfers between devices  12.5 us (17%)
  waiting for transfers between devices  6.37 us (9%)
  between operations  0.85 us (1%)
    pallas_call x10, Pallas kernels, call(): pl.pallas_call(kernel, out_shape=shapes, in_specs=specs, out_specs=[pl.Bl...  19.4 us
    all_to_all x1, blocking collectives, shards(): recv = lax.all_to_all(send, lay.axis, 0, 0)  17.8 us
    all_to_all x1, blocking collectives, shards(): out = lax.all_to_all(out, lay.axis, 0, 0)  14.7 us
    all_to_all x2, waiting for transfers between devices, gather(): return lax.all_to_all(loads, lay.axis, 0, 0)  6.35 us
    all_to_all x2, starting transfers between devices, gather(): return lax.all_to_all(loads, lay.axis, 0, 0)  5.95 us
    ppermute x4, starting transfers between devices, swap(): lax.ppermute(chip, lay.axis, lay.swaps(1))  5.19 us
  transfers between devices with their start and end apart: 10, of which 2 were waited for; matrix products, arithmetic and copies ran while one was open for 0% of the time, Pallas kernels for 12%

profile of v8, /device:TPU:0, one launch (start us, length us, event | category | flops | bytes accessed | tf_op | source)
XLA Modules:
  0.0 71.6 jit_solution(5621593462038494555)
XLA Ops:
  0.6 1.4 %shard_map.149 = f32[32,4,512]{2,1,0:T(4,128)S(1)} custom-call(s32[1,3]{1,0:T(1,128)} %bitcast.12, f32[1,3]{1,0:T(1,128)} %bitcast.13, f32[1,3]{1,0:T(1,128)} %bitcast.14, f32[512,128]{1,0:T(8,128)} %bitcast.10), custom_call_target="tpu_custom_call" | custom-call | tf_op jit(solution)/shard_map/pallas_call | solution.py:830
  2.0 0.0 copy-start
  2.0 0.0 copy-start.1
  2.0 17.8 %all_to_all.20.recv_ref = f32[32,4,512]{2,1,0:T(4,128)S(1)} all-to-all(f32[32,4,512]{2,1,0:T(4,128)S(1)} %shard_map.149), channel_id=1, replica_groups=mesh['ex'=4,'ey'=8] {'ex','ey'}, dimensions={0} | all-to-all | bytes 524288 | tf_op jit(solution)/shard_map/all_to_all | solution.py:905
  19.8 0.0 copy-start.8
  19.8 2.4 %shard_map.150 = (f32[512,128]{1,0:T(8,128)S(1)}, f32[512,128]{1,0:T(8,128)S(1)}, f32[512,128]{1,0:T(8,128)S(1)}, f32[512,128]{1,0:T(8,128)S(1)}, f32[256,128]{1,0:T(8,128)S(1)}, /*index=5*/f32[32,128]{1,0:T(8,128)S(1)}) custom-call(f32[32,4,512]{2,1,0:T(4,128)S(1)} %all_to_all.20.recv_ref, bf16[256,256]{1,0:T(8,128)(2,1)S(1)} %copy-done.1, ...), custom_call_target="tpu_custom_call" | custom-call | tf_op jit(solution)/shard_map/pallas_call | solution.py:830
  22.2 0.0 copy-start.9
  22.2 0.9 %collective-permute-start.1 = (f32[256,128]{1,0:T(8,128)S(1)}, f32[256,128]{1,0:T(8,128)S(1)}, u32[]{:S(2)}, u32[]{:S(2)}) collective-permute-start(f32[256,128]{1,0:T(8,128)S(1)} %get-tuple-element.27), channel_id=1, source_target_pairs={{8,2},{2,8},{10,4},{4,10},{12,6},{6,12},{14,7},{7,14},{15,5},{5,15... | collective-permute-start | bytes 393224 | tf_op jit(solution)/shard_map/ppermute | solution.py:912
  23.1 0.5 collective-permute-start
  23.6 1.3 %shard_map.151 = (f32[32,8,128]{2,1,0:T(8,128)}, f32[8,128]{1,0:T(8,128)S(1)}) custom-call(f32[512,128]{1,0:T(8,128)S(1)} %get-tuple-element.28.g_ref, f32[512,128]{1,0:T(8,128)S(1)} %get-tuple-element.29.x_ref, f32[512,128]{1,0:T(8,128)S(1)} %get-tuple-element.30.dinv_ref, bf16[16,1024]{1,0:T(8,128)(2,1)S(1)} %copy-done.8, bf16[16,128]{1,0:T(8,128)(2,1)S(1)} %copy-done.9), custom_call_target="tpu_custom_call" | custom-call | tf_op jit(solution)/shard_map/pallas_call | solution.py:830
  24.9 2.6 %all-to-all-start.1 = ((f32[32,8,128]{2,1,0:T(8,128)}), f32[32,8,128]{2,1,0:T(8,128)S(1)}, u32[]{:S(2)}, u32[]{:S(2)}) async-start(f32[32,8,128]{2,1,0:T(8,128)} %get-tuple-element.37), calls=%async_computation.1 | async-start | bytes 262144 | tf_op jit(solution)/shard_map/all_to_all | solution.py:916
  27.5 0.0 copy-start.3
  27.5 0.0 copy-start.4
  27.5 0.0 copy-start.5
  27.6 0.0 copy-start.6
  27.6 0.8 %shard_map.152 = (f32[512,128]{1,0:T(8,128)S(1)}, f32[512,128]{1,0:T(8,128)S(1)}, f32[256,128]{1,0:T(8,128)S(1)}, f32[256,128]{1,0:T(8,128)S(1)}) custom-call(f32[256,128]{1,0:T(8,128)S(1)} %collective-permute-done.core_ref, f32[256,128]{1,0:T(8,128)S(1)} %collective-permute-done.1.chip_ref, f32[512,128]{1,0:T(8,128)S(1)} %get-tuple-element.28.g_ref, ...), custom_call_target="tpu_custom_call" | custom-call | tf_op jit(solution)/shard_map/pallas_call | solution.py:830
  28.4 0.3 collective-permute-start.2
  28.7 1.6 %collective-permute-start.3 = (f32[256,128]{1,0:T(8,128)S(1)}, f32[256,128]{1,0:T(8,128)S(1)}, u32[]{:S(2)}, u32[]{:S(2)}) collective-permute-start(f32[256,128]{1,0:T(8,128)S(1)} %get-tuple-element.33), channel_id=1, source_target_pairs={{8,2},{2,8},{10,4},{4,10},{12,6},{6,12},{14,7},{7,14},{15,5},{5,15... | collective-permute-start | bytes 393224 | tf_op jit(solution)/shard_map/ppermute | solution.py:912
  30.3 4.9 %all-to-all-done.1.refs_5_ = f32[32,8,128]{2,1,0:T(8,128)S(1)} async-done(((f32[32,8,128]{2,1,0:T(8,128)}), f32[32,8,128]{2,1,0:T(8,128)S(1)}, u32[]{:S(2)}, u32[]{:S(2)}) %all-to-all-start.1) | async-done | bytes 131104 | tf_op jit(solution)/shard_map/all_to_all | solution.py:916
  35.3 3.3 %shard_map.153 = (f32[512,128]{1,0:T(8,128)S(1)}, f32[512,128]{1,0:T(8,128)S(1)}, f32[256,128]{1,0:T(8,128)S(1)}, f32[256,128]{1,0:T(8,128)S(1)}) custom-call(f32[256,128]{1,0:T(8,128)S(1)} %collective-permute-done.2.core_ref, f32[256,128]{1,0:T(8,128)S(1)} %collective-permute-done.3.chip_ref, f32[512,128]{1,0:T(8,128)S(1)} %get-tuple-element.34.g_ref, ...), custom_call_target="tpu_custom_call" | custom-call | tf_op jit(solution)/shard_map/pallas_call | solution.py:830
  38.6 0.2 collective-permute-start.4
  38.8 1.1 %collective-permute-start.5 = (f32[256,128]{1,0:T(8,128)S(1)}, f32[256,128]{1,0:T(8,128)S(1)}, u32[]{:S(2)}, u32[]{:S(2)}) collective-permute-start(f32[256,128]{1,0:T(8,128)S(1)} %get-tuple-element.39), channel_id=1, source_target_pairs={{8,2},{2,8},{10,4},{4,10},{12,6},{6,12},{14,7},{7,14},{15,5},{5,15... | collective-permute-start | bytes 393224 | tf_op jit(solution)/shard_map/ppermute | solution.py:912
  39.9 2.1 %shard_map.154 = (f32[32,8,128]{2,1,0:T(8,128)}, f32[8,128]{1,0:T(8,128)S(1)}) custom-call(f32[512,128]{1,0:T(8,128)S(1)} %get-tuple-element.40.g_ref, f32[512,128]{1,0:T(8,128)S(1)} %get-tuple-element.30.dinv_ref, f32[512,128]{1,0:T(8,128)S(1)} %get-tuple-element.36.outer_ref, bf16[256,256]{1,0:T(8,128)(2,1)S(1)} %copy-done.1, ...), custom_call_target="tpu_custom_call" | custom-call | tf_op jit(solution)/shard_map/pallas_call | solution.py:830
  42.0 3.3 %all-to-all-start.2 = ((f32[32,8,128]{2,1,0:T(8,128)}), f32[32,8,128]{2,1,0:T(8,128)S(1)}, u32[]{:S(2)}, u32[]{:S(2)}) async-start(f32[32,8,128]{2,1,0:T(8,128)} %get-tuple-element.48), calls=%async_computation.2 | async-start | bytes 262144 | tf_op jit(solution)/shard_map/all_to_all | solution.py:916
  45.3 1.6 %shard_map.155 = (f32[512,128]{1,0:T(8,128)S(1)}, f32[512,128]{1,0:T(8,128)S(1)}, f32[256,128]{1,0:T(8,128)S(1)}, f32[256,128]{1,0:T(8,128)S(1)}, f32[32,128]{1,0:T(8,128)S(1)}) custom-call(f32[256,128]{1,0:T(8,128)S(1)} %collective-permute-done.4.core_ref, f32[256,128]{1,0:T(8,128)S(1)} %collective-permute-done.5.chip_ref, ...), custom_call_target="tpu_custom_call" | custom-call | tf_op jit(solution)/shard_map/pallas_call | solution.py:830
  46.9 0.3 collective-permute-start.6
  47.3 1.6 %collective-permute-start.7 = (f32[256,128]{1,0:T(8,128)S(1)}, f32[256,128]{1,0:T(8,128)S(1)}, u32[]{:S(2)}, u32[]{:S(2)}) collective-permute-start(f32[256,128]{1,0:T(8,128)S(1)} %get-tuple-element.45), channel_id=1, source_target_pairs={{8,2},{2,8},{10,4},{4,10},{12,6},{6,12},{14,7},{7,14},{15,5},{5,15... | collective-permute-start | bytes 393224 | tf_op jit(solution)/shard_map/ppermute | solution.py:912
  48.9 2.8 %shard_map.156 = (f32[3,512,128]{2,1,0:T(8,128)}, f32[8,128]{1,0:T(8,128)S(1)}) custom-call(f32[32,128]{1,0:T(8,128)S(1)} %get-tuple-element.49.points_ref), custom_call_target="tpu_custom_call" | custom-call | tf_op jit(solution)/shard_map/pallas_call | solution.py:830
  51.7 1.4 %all-to-all-done.2.refs_5_ = f32[32,8,128]{2,1,0:T(8,128)S(1)} async-done(((f32[32,8,128]{2,1,0:T(8,128)}), f32[32,8,128]{2,1,0:T(8,128)S(1)}, u32[]{:S(2)}, u32[]{:S(2)}) %all-to-all-start.2) | async-done | bytes 131104 | tf_op jit(solution)/shard_map/all_to_all | solution.py:916
  53.1 2.9 %shard_map.157 = f32[32,4,512]{2,1,0:T(4,128)S(1)} custom-call(f32[256,128]{1,0:T(8,128)S(1)} %collective-permute-done.6.core_ref, f32[256,128]{1,0:T(8,128)S(1)} %collective-permute-done.7.chip_ref, f32[512,128]{1,0:T(8,128)S(1)} %get-tuple-element.46.g_ref, f32[512,128]{1,0:T(8,128)S(1)} %get-tuple-element.47.x_ref, ...), custom_call_target="tpu_custom_call" | custom-call | tf_op jit(solution)/shard_map/pallas_call | solution.py:830
  56.0 14.7 %all_to_all.21.recv_ref = f32[32,4,512]{2,1,0:T(4,128)S(1)} all-to-all(f32[32,4,512]{2,1,0:T(4,128)S(1)} %shard_map.157), channel_id=1, replica_groups=mesh['ex'=4,'ey'=8] {'ex','ey'}, dimensions={0} | all-to-all | bytes 524288 | tf_op jit(solution)/shard_map/all_to_all | solution.py:986
  70.8 0.9 %shard_map.158 = f32[512,128]{1,0:T(8,128)} custom-call(f32[32,4,512]{2,1,0:T(4,128)S(1)} %all_to_all.21.recv_ref), custom_call_target="tpu_custom_call" | custom-call | tf_op jit(solution)/shard_map/pallas_call | solution.py:830
  (20 shorter events, 0.1 us)
Async XLA Ops:
  2.0 17.8 %copy-start = (bf16[256,256]{1,0:T(8,128)(2,1)S(1)}, bf16[256,256]{1,0:T(8,128)(2,1)}, u32[]{:S(2)}) copy-start(bf16[256,256]{1,0:T(8,128)(2,1)} %constant.21.clone.low_ref.refs_1_) | copy-start | bytes 393220
  2.0 17.8 %copy-start.1 = (bf16[256,256]{1,0:T(8,128)(2,1)S(1)}, bf16[256,256]{1,0:T(8,128)(2,1)}, u32[]{:S(2)}) copy-start(bf16[256,256]{1,0:T(8,128)(2,1)} %constant.20.clone.high_ref.refs_0_) | copy-start | bytes 393220
  2.0 17.8 %copy-start.2 = (f32[64,128]{1,0:T(8,128)S(1)}, f32[64,128]{1,0:T(8,128)}, u32[]{:S(2)}) copy-start(f32[64,128]{1,0:T(8,128)} %constant.22.clone.along_ref.refs_2_) | copy-start | bytes 98308
  19.8 3.8 %copy-start.8 = (bf16[16,1024]{1,0:T(8,128)(2,1)S(1)}, bf16[16,1024]{1,0:T(8,128)(2,1)}, u32[]{:S(2)}) copy-start(bf16[16,1024]{1,0:T(8,128)(2,1)} %constant.25.clone.loads_ref) | copy-start | bytes 98308
  22.2 1.4 %copy-start.9 = (bf16[16,128]{1,0:T(8,128)(2,1)S(1)}, bf16[16,128]{1,0:T(8,128)(2,1)}, u32[]{:S(2)}) copy-start(bf16[16,128]{1,0:T(8,128)(2,1)} %constant.26.clone.near_ref) | copy-start | bytes 12292
  22.2 5.3 %collective-permute-start.1 = (f32[256,128]{1,0:T(8,128)S(1)}, f32[256,128]{1,0:T(8,128)S(1)}, u32[]{:S(2)}, u32[]{:S(2)}) collective-permute-start(f32[256,128]{1,0:T(8,128)S(1)} %get-tuple-element.27), channel_id=1, source_target_pairs={{8,2},{2,8},{10,4},{4,10},{12,6},{6,12},{14,7},{7,14},{15,5},{5,15... | collective-permute-start | bytes 393224 | tf_op jit(solution)/shard_map/ppermute | solution.py:912
  23.1 4.5 %collective-permute-start = (f32[256,128]{1,0:T(8,128)S(1)}, f32[256,128]{1,0:T(8,128)S(1)}, u32[]{:S(2)}, u32[]{:S(2)}) collective-permute-start(f32[256,128]{1,0:T(8,128)S(1)} %get-tuple-element.27), channel_id=1, source_target_pairs={{0,8},{8,0},{2,10},{10,2},{4,12},{12,4},{6,14},{14,6},{7,15},{15,7... | collective-permute-start | bytes 393224 | tf_op jit(solution)/shard_map/ppermute | solution.py:911
  24.9 10.4 %all-to-all-start.1 = ((f32[32,8,128]{2,1,0:T(8,128)}), f32[32,8,128]{2,1,0:T(8,128)S(1)}, u32[]{:S(2)}, u32[]{:S(2)}) async-start(f32[32,8,128]{2,1,0:T(8,128)} %get-tuple-element.37), calls=%async_computation.1 | async-start | bytes 262144 | tf_op jit(solution)/shard_map/all_to_all | solution.py:916
  27.5 7.7 %copy-start.3 = (bf16[128,512]{1,0:T(8,128)(2,1)S(1)}, bf16[128,512]{1,0:T(8,128)(2,1)}, u32[]{:S(2)}) copy-start(bf16[128,512]{1,0:T(8,128)(2,1)} %constant.24.clone.refs_4_) | copy-start | bytes 393220
  27.5 7.7 %copy-start.4 = (bf16[128,512]{1,0:T(8,128)(2,1)S(1)}, bf16[128,512]{1,0:T(8,128)(2,1)}, u32[]{:S(2)}) copy-start(bf16[128,512]{1,0:T(8,128)(2,1)} %constant.23.clone.refs_3_) | copy-start | bytes 393220
  27.5 7.7 %copy-start.5 = (bf16[512,32]{1,0:T(8,128)(2,1)S(1)}, bf16[512,32]{1,0:T(8,128)(2,1)}, u32[]{:S(2)}) copy-start(bf16[512,32]{1,0:T(8,128)(2,1)} %constant.28.clone.refs_6_) | copy-start | bytes 98308
  27.6 7.7 %copy-start.6 = (bf16[512,32]{1,0:T(8,128)(2,1)S(1)}, bf16[512,32]{1,0:T(8,128)(2,1)}, u32[]{:S(2)}) copy-start(bf16[512,32]{1,0:T(8,128)(2,1)} %constant.27.clone.refs_8_) | copy-start | bytes 98308
  27.6 7.7 %copy-start.7 = (bf16[128,32]{1,0:T(8,128)(2,1)S(1)}, bf16[128,32]{1,0:T(8,128)(2,1)}, u32[]{:S(2)}) copy-start(bf16[128,32]{1,0:T(8,128)(2,1)} %constant.29.clone.refs_7_) | copy-start | bytes 24580
  28.4 6.9 %collective-permute-start.2 = (f32[256,128]{1,0:T(8,128)S(1)}, f32[256,128]{1,0:T(8,128)S(1)}, u32[]{:S(2)}, u32[]{:S(2)}) collective-permute-start(f32[256,128]{1,0:T(8,128)S(1)} %get-tuple-element.32), channel_id=1, source_target_pairs={{0,8},{8,0},{2,10},{10,2},{4,12},{12,4},{6,14},{14,6},{7,15},{15,7... | collective-permute-start | bytes 393224 | tf_op jit(solution)/shard_map/ppermute | solution.py:911
  28.7 6.5 %collective-permute-start.3 = (f32[256,128]{1,0:T(8,128)S(1)}, f32[256,128]{1,0:T(8,128)S(1)}, u32[]{:S(2)}, u32[]{:S(2)}) collective-permute-start(f32[256,128]{1,0:T(8,128)S(1)} %get-tuple-element.33), channel_id=1, source_target_pairs={{8,2},{2,8},{10,4},{4,10},{12,6},{6,12},{14,7},{7,14},{15,5},{5,15... | collective-permute-start | bytes 393224 | tf_op jit(solution)/shard_map/ppermute | solution.py:912
  38.6 6.7 %collective-permute-start.4 = (f32[256,128]{1,0:T(8,128)S(1)}, f32[256,128]{1,0:T(8,128)S(1)}, u32[]{:S(2)}, u32[]{:S(2)}) collective-permute-start(f32[256,128]{1,0:T(8,128)S(1)} %get-tuple-element.38), channel_id=1, source_target_pairs={{0,8},{8,0},{2,10},{10,2},{4,12},{12,4},{6,14},{14,6},{7,15},{15,7... | collective-permute-start | bytes 393224 | tf_op jit(solution)/shard_map/ppermute | solution.py:911
  38.8 6.5 %collective-permute-start.5 = (f32[256,128]{1,0:T(8,128)S(1)}, f32[256,128]{1,0:T(8,128)S(1)}, u32[]{:S(2)}, u32[]{:S(2)}) collective-permute-start(f32[256,128]{1,0:T(8,128)S(1)} %get-tuple-element.39), channel_id=1, source_target_pairs={{8,2},{2,8},{10,4},{4,10},{12,6},{6,12},{14,7},{7,14},{15,5},{5,15... | collective-permute-start | bytes 393224 | tf_op jit(solution)/shard_map/ppermute | solution.py:912
  42.0 11.1 %all-to-all-start.2 = ((f32[32,8,128]{2,1,0:T(8,128)}), f32[32,8,128]{2,1,0:T(8,128)S(1)}, u32[]{:S(2)}, u32[]{:S(2)}) async-start(f32[32,8,128]{2,1,0:T(8,128)} %get-tuple-element.48), calls=%async_computation.2 | async-start | bytes 262144 | tf_op jit(solution)/shard_map/all_to_all | solution.py:916
  46.9 6.2 %collective-permute-start.6 = (f32[256,128]{1,0:T(8,128)S(1)}, f32[256,128]{1,0:T(8,128)S(1)}, u32[]{:S(2)}, u32[]{:S(2)}) collective-permute-start(f32[256,128]{1,0:T(8,128)S(1)} %get-tuple-element.44), channel_id=1, source_target_pairs={{0,8},{8,0},{2,10},{10,2},{4,12},{12,4},{6,14},{14,6},{7,15},{15,7... | collective-permute-start | bytes 393224 | tf_op jit(solution)/shard_map/ppermute | solution.py:911
  47.3 5.9 %collective-permute-start.7 = (f32[256,128]{1,0:T(8,128)S(1)}, f32[256,128]{1,0:T(8,128)S(1)}, u32[]{:S(2)}, u32[]{:S(2)}) collective-permute-start(f32[256,128]{1,0:T(8,128)S(1)} %get-tuple-element.45), channel_id=1, source_target_pairs={{8,2},{2,8},{10,4},{4,10},{12,6},{6,12},{14,7},{7,14},{15,5},{5,15... | collective-permute-start | bytes 393224 | tf_op jit(solution)/shard_map/ppermute | solution.py:912

commit v9 on v8

--- a/solution.py
+++ b/solution.py
@@ -770,57 +770,60 @@
     out_ref[...] = flat_ref[...].T
 
 
+def gauss_at(elem, node, base, position):
+    half_nodes = jnp.full(node.shape, 0.5 * (1.0 + GLL_POINTS[0]), F32)
+    for n in range(1, N):
+        half_nodes = jnp.where(node == n, 0.5 * (1.0 + GLL_POINTS[n]), half_nodes)
+    elem = elem.astype(F32)
+    away = elem + half_nodes - position
+    inside = (
+        (elem == base)
+        | (elem == base + 1.0)
+        | ((elem == base - 1.0) & (node == N - 1))
+        | ((elem == base + 2.0) & (node == 0))
+    )
+    return jnp.where(inside, jnp.exp(-(away * away) / (WIDTH_EPS * WIDTH_EPS)), 0.0)
+
+
 def forces_kernel(tiles_y, local_points, points_ref, out_ref, done_ref):
-    shape = (N, tiles_y * EZ)
-    lane = lax.broadcasted_iota(jnp.int32, shape, 1)
+    done_ref[...] = jnp.zeros(done_ref.shape, F32)
+    count = points_ref.shape[0]
     first_x, first_y = lax.axis_index("ex"), lax.axis_index("ey") * tiles_y
-    elem_x = jnp.broadcast_to(first_x, shape)
-    elem_y = first_y + lax.shift_right_logical(lane, log2(EZ))
-    elem_z = lane & (EZ - 1)
-    half_nodes = column(0.5 * (1.0 + GLL_POINTS), shape)
-    out_ref[...] = jnp.zeros(out_ref.shape, F32)
-    done_ref[...] = jnp.zeros(done_ref.shape, F32)
-
-    def visit(p, place):
-        base, position, force = point_values(points_ref, p, place, GAUSS_NORM)
-        low_x, low_y = first_x.astype(F32), first_y.astype(F32)
-
-        @pl.when(
-            (base[0] + 2.0 >= low_x)
-            & (base[0] - 1.0 <= low_x)
-            & (base[1] + 2.0 >= low_y)
-            & (base[1] - 1.0 <= low_y + (tiles_y - 1))
+    lane = lax.broadcasted_iota(jnp.int32, (count, 3 * FACE), 1)
+    node_x, node_y, part = (lane >> 3) & (N - 1), lane & (N - 1), lane >> 6
+    lane_z = lax.broadcasted_iota(jnp.int32, (count, tiles_y * EZ), 1)
+    planes, columns = [], []
+    for place in range(local_points):
+
+        def value(n):
+            at = (place * 9 + n) * N
+            return points_ref[:, at : at + 1]
+
+        base = [value(d) for d in range(3)]
+        position = [value(d) + 1.0 + value(3 + d) for d in range(3)]
+        force = jnp.where(part == 0, value(6), jnp.where(part == 1, value(7), value(8)))
+        x = gauss_at(jnp.broadcast_to(first_x, lane.shape), node_x, base[0], position[0])
+        scaled = GAUSS_NORM * force * x
+        for e2 in range(tiles_y):
+            y = gauss_at(jnp.broadcast_to(first_y + e2, lane.shape), node_y, base[1], position[1])
+            planes.append(scaled * y)
+            columns.append((e2, base[2], position[2]))
+    high, low = split(jnp.concatenate(planes, 0))
+    plane = jnp.concatenate([high, high, low], 0)
+    elem_z, row_z = lane_z & (EZ - 1), lane_z >> log2(EZ)
+    for k in range(N):
+        node = jnp.full(lane_z.shape, k, jnp.int32)
+        along = [
+            jnp.where(row_z == e2, gauss_at(elem_z, node, base, position), 0.0)
+            for e2, base, position in columns
+        ]
+        high, low = split(jnp.concatenate(along, 0))
+        out_ref[pl.ds(k, 3 * FACE, stride=N), :] = lax.dot_general(
+            plane,
+            jnp.concatenate([high, low, high], 0),
+            (((0,), (0,)), ((), ())),
+            preferred_element_type=F32,
         )
-        def _():
-            x = gauss(elem_x, base[0], position[0], half_nodes)
-            y = gauss(elem_y, base[1], position[1], half_nodes)
-            z = gauss(elem_z, base[2], position[2], half_nodes)
-
-            def add(along_x, along_y):
-                for j in along_y:
-                    plane = y[j : j + 1] * z
-                    for i in along_x:
-                        value = x[i : i + 1] * plane
-                        rows = pl.ds((i * N + j) * N, N)
-                        for c in range(3):
-                            out_ref[c, rows, :] += force[c] * value
-
-            last_y = low_y + (tiles_y - 1)
-            in_x = ((base[0] == low_x) | (base[0] + 1.0 == low_x), range(N))
-            in_y = ((base[1] + 1.0 >= low_y) & (base[1] <= last_y), range(N))
-            for when_x, along_x in (
-                in_x,
-                (base[0] + 2.0 == low_x, (0,)),
-                (base[0] - 1.0 == low_x, (N - 1,)),
-            ):
-                for when_y, along_y in (
-                    in_y,
-                    (base[1] + 2.0 == low_y, (0,)),
-                    (base[1] - 1.0 == last_y, (N - 1,)),
-                ):
-                    pl.when(when_x & when_y)(functools.partial(add, along_x, along_y))
-
-    for_points(points_ref, local_points, visit)
 
 
 def call(kernel, outs, inputs, scratch=(), smem=0, spaces=None, limit=40):
@@ -976,9 +979,8 @@
         )
         forces, done = call(
             functools.partial(forces_kernel, tiles_y, local_points),
-            [(3, N**3, tiles_y * EZ), (N, 128)],
+            [(3 * N**3, tiles_y * EZ), (N, 128)],
             [points],
-            smem=1,
         )
     (out,) = outs
     if not lay.joint:

time: 72.3 us -> 72.1 us (level)
  Pallas kernels: 19.4 us -> 18 us
  waiting for transfers between devices: 6.37 us -> 7.68 us
    pallas_call x10, Pallas kernels: 19.4 us -> 18 us  [call(): pl.pallas_call(kernel, out_shape=shapes, in_specs=specs, out_specs=[pl.Bl...]
    all_to_all x2, waiting for transfers between devices: 6.35 us -> 7.66 us  [gather(): return lax.all_to_all(loads, lay.axis, 0, 0)]
  transfers between devices with their start and end apart: 10 -> 10, of which waited for: 2 -> 2; matrix products, arithmetic and copies ran while one was open for 0% -> 0% of each run, Pallas kernels for 12% -> 10%
where the time goes in v9:
time: 72.1 us; the launch traced here: 71.6 us
  blocking collectives  32.5 us (45%)
  Pallas kernels  18 us (25%)
  starting transfers between devices  12.5 us (17%)
  waiting for transfers between devices  7.68 us (11%)
  between operations  0.85 us (1%)
    pallas_call x10, Pallas kernels, call(): pl.pallas_call(kernel, out_shape=shapes, in_specs=specs, out_specs=[pl.Bl...  18 us
    all_to_all x1, blocking collectives, shards(): recv = lax.all_to_all(send, lay.axis, 0, 0)  17.8 us
    all_to_all x1, blocking collectives, shards(): out = lax.all_to_all(out, lay.axis, 0, 0)  14.7 us
    all_to_all x2, waiting for transfers between devices, gather(): return lax.all_to_all(loads, lay.axis, 0, 0)  7.66 us
    all_to_all x2, starting transfers between devices, gather(): return lax.all_to_all(loads, lay.axis, 0, 0)  5.95 us
    ppermute x4, starting transfers between devices, swap(): lax.ppermute(chip, lay.axis, lay.swaps(1))  5.29 us
  transfers between devices with their start and end apart: 10, of which 2 were waited for; matrix products, arithmetic and copies ran while one was open for 0% of the time, Pallas kernels for 10%

profile of v9, /device:TPU:0, one launch (start us, length us, event | category | flops | bytes accessed | tf_op | source)
XLA Modules:
  0.0 71.6 jit_solution(5410122731893932345)
XLA Ops:
  0.6 1.4 %shard_map.149 = f32[32,4,512]{2,1,0:T(4,128)S(1)} custom-call(s32[1,3]{1,0:T(1,128)} %bitcast.12, f32[1,3]{1,0:T(1,128)} %bitcast.13, f32[1,3]{1,0:T(1,128)} %bitcast.14, f32[512,128]{1,0:T(8,128)} %bitcast.10), custom_call_target="tpu_custom_call" | custom-call | tf_op jit(solution)/shard_map/pallas_call | solution.py:833
  2.0 0.0 copy-start
  2.0 0.0 copy-start.1
  2.0 17.8 %all_to_all.20.recv_ref = f32[32,4,512]{2,1,0:T(4,128)S(1)} all-to-all(f32[32,4,512]{2,1,0:T(4,128)S(1)} %shard_map.149), channel_id=1, replica_groups=mesh['ex'=4,'ey'=8] {'ex','ey'}, dimensions={0} | all-to-all | bytes 524288 | tf_op jit(solution)/shard_map/all_to_all | solution.py:908
  19.8 0.0 copy-start.8
  19.8 2.3 %shard_map.150 = (f32[512,128]{1,0:T(8,128)S(1)}, f32[512,128]{1,0:T(8,128)S(1)}, f32[512,128]{1,0:T(8,128)S(1)}, f32[512,128]{1,0:T(8,128)S(1)}, f32[256,128]{1,0:T(8,128)S(1)}, /*index=5*/f32[32,128]{1,0:T(8,128)S(1)}) custom-call(f32[32,4,512]{2,1,0:T(4,128)S(1)} %all_to_all.20.recv_ref, bf16[256,256]{1,0:T(8,128)(2,1)S(1)} %copy-done.1, ...), custom_call_target="tpu_custom_call" | custom-call | tf_op jit(solution)/shard_map/pallas_call | solution.py:833
  22.1 0.0 copy-start.9
  22.1 0.9 %collective-permute-start.1 = (f32[256,128]{1,0:T(8,128)S(1)}, f32[256,128]{1,0:T(8,128)S(1)}, u32[]{:S(2)}, u32[]{:S(2)}) collective-permute-start(f32[256,128]{1,0:T(8,128)S(1)} %get-tuple-element.27), channel_id=1, source_target_pairs={{8,2},{2,8},{10,4},{4,10},{12,6},{6,12},{14,7},{7,14},{15,5},{5,15... | collective-permute-start | bytes 393224 | tf_op jit(solution)/shard_map/ppermute | solution.py:915
  23.1 0.4 collective-permute-start
  23.5 1.3 %shard_map.151 = (f32[32,8,128]{2,1,0:T(8,128)}, f32[8,128]{1,0:T(8,128)S(1)}) custom-call(f32[512,128]{1,0:T(8,128)S(1)} %get-tuple-element.28.g_ref, f32[512,128]{1,0:T(8,128)S(1)} %get-tuple-element.29.x_ref, f32[512,128]{1,0:T(8,128)S(1)} %get-tuple-element.30.dinv_ref, bf16[16,1024]{1,0:T(8,128)(2,1)S(1)} %copy-done.8, bf16[16,128]{1,0:T(8,128)(2,1)S(1)} %copy-done.9), custom_call_target="tpu_custom_call" | custom-call | tf_op jit(solution)/shard_map/pallas_call | solution.py:833
  24.8 2.6 %all-to-all-start.1 = ((f32[32,8,128]{2,1,0:T(8,128)}), f32[32,8,128]{2,1,0:T(8,128)S(1)}, u32[]{:S(2)}, u32[]{:S(2)}) async-start(f32[32,8,128]{2,1,0:T(8,128)} %get-tuple-element.37), calls=%async_computation.1 | async-start | bytes 262144 | tf_op jit(solution)/shard_map/all_to_all | solution.py:919
  27.4 0.0 copy-start.3
  27.4 0.0 copy-start.4
  27.5 0.0 copy-start.5
  27.5 0.0 copy-start.6
  27.5 0.8 %shard_map.152 = (f32[512,128]{1,0:T(8,128)S(1)}, f32[512,128]{1,0:T(8,128)S(1)}, f32[256,128]{1,0:T(8,128)S(1)}, f32[256,128]{1,0:T(8,128)S(1)}) custom-call(f32[256,128]{1,0:T(8,128)S(1)} %collective-permute-done.core_ref, f32[256,128]{1,0:T(8,128)S(1)} %collective-permute-done.1.chip_ref, f32[512,128]{1,0:T(8,128)S(1)} %get-tuple-element.28.g_ref, ...), custom_call_target="tpu_custom_call" | custom-call | tf_op jit(solution)/shard_map/pallas_call | solution.py:833
  28.3 0.3 collective-permute-start.2
  28.6 1.6 %collective-permute-start.3 = (f32[256,128]{1,0:T(8,128)S(1)}, f32[256,128]{1,0:T(8,128)S(1)}, u32[]{:S(2)}, u32[]{:S(2)}) collective-permute-start(f32[256,128]{1,0:T(8,128)S(1)} %get-tuple-element.33), channel_id=1, source_target_pairs={{8,2},{2,8},{10,4},{4,10},{12,6},{6,12},{14,7},{7,14},{15,5},{5,15... | collective-permute-start | bytes 393224 | tf_op jit(solution)/shard_map/ppermute | solution.py:915
  30.3 4.9 %all-to-all-done.1.refs_5_ = f32[32,8,128]{2,1,0:T(8,128)S(1)} async-done(((f32[32,8,128]{2,1,0:T(8,128)}), f32[32,8,128]{2,1,0:T(8,128)S(1)}, u32[]{:S(2)}, u32[]{:S(2)}) %all-to-all-start.1) | async-done | bytes 131104 | tf_op jit(solution)/shard_map/all_to_all | solution.py:919
  35.2 3.3 %shard_map.153 = (f32[512,128]{1,0:T(8,128)S(1)}, f32[512,128]{1,0:T(8,128)S(1)}, f32[256,128]{1,0:T(8,128)S(1)}, f32[256,128]{1,0:T(8,128)S(1)}) custom-call(f32[256,128]{1,0:T(8,128)S(1)} %collective-permute-done.2.core_ref, f32[256,128]{1,0:T(8,128)S(1)} %collective-permute-done.3.chip_ref, f32[512,128]{1,0:T(8,128)S(1)} %get-tuple-element.34.g_ref, ...), custom_call_target="tpu_custom_call" | custom-call | tf_op jit(solution)/shard_map/pallas_call | solution.py:833
  38.6 0.2 collective-permute-start.4
  38.7 1.1 %collective-permute-start.5 = (f32[256,128]{1,0:T(8,128)S(1)}, f32[256,128]{1,0:T(8,128)S(1)}, u32[]{:S(2)}, u32[]{:S(2)}) collective-permute-start(f32[256,128]{1,0:T(8,128)S(1)} %get-tuple-element.39), channel_id=1, source_target_pairs={{8,2},{2,8},{10,4},{4,10},{12,6},{6,12},{14,7},{7,14},{15,5},{5,15... | collective-permute-start | bytes 393224 | tf_op jit(solution)/shard_map/ppermute | solution.py:915
  39.8 2.1 %shard_map.154 = (f32[32,8,128]{2,1,0:T(8,128)}, f32[8,128]{1,0:T(8,128)S(1)}) custom-call(f32[512,128]{1,0:T(8,128)S(1)} %get-tuple-element.40.g_ref, f32[512,128]{1,0:T(8,128)S(1)} %get-tuple-element.30.dinv_ref, f32[512,128]{1,0:T(8,128)S(1)} %get-tuple-element.36.outer_ref, bf16[256,256]{1,0:T(8,128)(2,1)S(1)} %copy-done.1, ...), custom_call_target="tpu_custom_call" | custom-call | tf_op jit(solution)/shard_map/pallas_call | solution.py:833
  41.9 3.3 %all-to-all-start.2 = ((f32[32,8,128]{2,1,0:T(8,128)}), f32[32,8,128]{2,1,0:T(8,128)S(1)}, u32[]{:S(2)}, u32[]{:S(2)}) async-start(f32[32,8,128]{2,1,0:T(8,128)} %get-tuple-element.48), calls=%async_computation.2 | async-start | bytes 262144 | tf_op jit(solution)/shard_map/all_to_all | solution.py:919
  45.3 1.6 %shard_map.155 = (f32[512,128]{1,0:T(8,128)S(1)}, f32[512,128]{1,0:T(8,128)S(1)}, f32[256,128]{1,0:T(8,128)S(1)}, f32[256,128]{1,0:T(8,128)S(1)}, f32[32,128]{1,0:T(8,128)S(1)}) custom-call(f32[256,128]{1,0:T(8,128)S(1)} %collective-permute-done.4.core_ref, f32[256,128]{1,0:T(8,128)S(1)} %collective-permute-done.5.chip_ref, ...), custom_call_target="tpu_custom_call" | custom-call | tf_op jit(solution)/shard_map/pallas_call | solution.py:833
  46.9 0.3 collective-permute-start.6
  47.2 1.6 %collective-permute-start.7 = (f32[256,128]{1,0:T(8,128)S(1)}, f32[256,128]{1,0:T(8,128)S(1)}, u32[]{:S(2)}, u32[]{:S(2)}) collective-permute-start(f32[256,128]{1,0:T(8,128)S(1)} %get-tuple-element.45), channel_id=1, source_target_pairs={{8,2},{2,8},{10,4},{4,10},{12,6},{6,12},{14,7},{7,14},{15,5},{5,15... | collective-permute-start | bytes 393224 | tf_op jit(solution)/shard_map/ppermute | solution.py:915
  48.8 1.5 %shard_map.156 = (f32[1536,128]{1,0:T(8,128)}, f32[8,128]{1,0:T(8,128)S(1)}) custom-call(f32[32,128]{1,0:T(8,128)S(1)} %get-tuple-element.49.points_ref), custom_call_target="tpu_custom_call" | custom-call | tf_op jit(solution)/shard_map/pallas_call | solution.py:833
  50.3 2.7 %all-to-all-done.2.refs_5_ = f32[32,8,128]{2,1,0:T(8,128)S(1)} async-done(((f32[32,8,128]{2,1,0:T(8,128)}), f32[32,8,128]{2,1,0:T(8,128)S(1)}, u32[]{:S(2)}, u32[]{:S(2)}) %all-to-all-start.2) | async-done | bytes 131104 | tf_op jit(solution)/shard_map/all_to_all | solution.py:919
  53.1 2.9 %shard_map.157 = f32[32,4,512]{2,1,0:T(4,128)S(1)} custom-call(f32[256,128]{1,0:T(8,128)S(1)} %collective-permute-done.6.core_ref, f32[256,128]{1,0:T(8,128)S(1)} %collective-permute-done.7.chip_ref, f32[512,128]{1,0:T(8,128)S(1)} %get-tuple-element.46.g_ref, f32[512,128]{1,0:T(8,128)S(1)} %get-tuple-element.47.x_ref, ...), custom_call_target="tpu_custom_call" | custom-call | tf_op jit(solution)/shard_map/pallas_call | solution.py:833
  55.9 14.7 %all_to_all.21.recv_ref = f32[32,4,512]{2,1,0:T(4,128)S(1)} all-to-all(f32[32,4,512]{2,1,0:T(4,128)S(1)} %shard_map.157), channel_id=1, replica_groups=mesh['ex'=4,'ey'=8] {'ex','ey'}, dimensions={0} | all-to-all | bytes 524288 | tf_op jit(solution)/shard_map/all_to_all | solution.py:988
  70.7 0.9 %shard_map.158 = f32[512,128]{1,0:T(8,128)} custom-call(f32[32,4,512]{2,1,0:T(4,128)S(1)} %all_to_all.21.recv_ref), custom_call_target="tpu_custom_call" | custom-call | tf_op jit(solution)/shard_map/pallas_call | solution.py:833
  (20 shorter events, 0.1 us)
Async XLA Ops:
  2.0 17.8 %copy-start = (bf16[256,256]{1,0:T(8,128)(2,1)S(1)}, bf16[256,256]{1,0:T(8,128)(2,1)}, u32[]{:S(2)}) copy-start(bf16[256,256]{1,0:T(8,128)(2,1)} %constant.21.clone.low_ref.refs_1_) | copy-start | bytes 393220
  2.0 17.8 %copy-start.1 = (bf16[256,256]{1,0:T(8,128)(2,1)S(1)}, bf16[256,256]{1,0:T(8,128)(2,1)}, u32[]{:S(2)}) copy-start(bf16[256,256]{1,0:T(8,128)(2,1)} %constant.20.clone.high_ref.refs_0_) | copy-start | bytes 393220
  2.0 17.8 %copy-start.2 = (f32[64,128]{1,0:T(8,128)S(1)}, f32[64,128]{1,0:T(8,128)}, u32[]{:S(2)}) copy-start(f32[64,128]{1,0:T(8,128)} %constant.22.clone.along_ref.refs_2_) | copy-start | bytes 98308
  19.8 3.7 %copy-start.8 = (bf16[16,1024]{1,0:T(8,128)(2,1)S(1)}, bf16[16,1024]{1,0:T(8,128)(2,1)}, u32[]{:S(2)}) copy-start(bf16[16,1024]{1,0:T(8,128)(2,1)} %constant.25.clone.loads_ref) | copy-start | bytes 98308
  22.1 1.4 %copy-start.9 = (bf16[16,128]{1,0:T(8,128)(2,1)S(1)}, bf16[16,128]{1,0:T(8,128)(2,1)}, u32[]{:S(2)}) copy-start(bf16[16,128]{1,0:T(8,128)(2,1)} %constant.26.clone.near_ref) | copy-start | bytes 12292
  22.1 5.3 %collective-permute-start.1 = (f32[256,128]{1,0:T(8,128)S(1)}, f32[256,128]{1,0:T(8,128)S(1)}, u32[]{:S(2)}, u32[]{:S(2)}) collective-permute-start(f32[256,128]{1,0:T(8,128)S(1)} %get-tuple-element.27), channel_id=1, source_target_pairs={{8,2},{2,8},{10,4},{4,10},{12,6},{6,12},{14,7},{7,14},{15,5},{5,15... | collective-permute-start | bytes 393224 | tf_op jit(solution)/shard_map/ppermute | solution.py:915
  23.1 4.4 %collective-permute-start = (f32[256,128]{1,0:T(8,128)S(1)}, f32[256,128]{1,0:T(8,128)S(1)}, u32[]{:S(2)}, u32[]{:S(2)}) collective-permute-start(f32[256,128]{1,0:T(8,128)S(1)} %get-tuple-element.27), channel_id=1, source_target_pairs={{0,8},{8,0},{2,10},{10,2},{4,12},{12,4},{6,14},{14,6},{7,15},{15,7... | collective-permute-start | bytes 393224 | tf_op jit(solution)/shard_map/ppermute | solution.py:914
  24.8 10.4 %all-to-all-start.1 = ((f32[32,8,128]{2,1,0:T(8,128)}), f32[32,8,128]{2,1,0:T(8,128)S(1)}, u32[]{:S(2)}, u32[]{:S(2)}) async-start(f32[32,8,128]{2,1,0:T(8,128)} %get-tuple-element.37), calls=%async_computation.1 | async-start | bytes 262144 | tf_op jit(solution)/shard_map/all_to_all | solution.py:919
  27.4 7.7 %copy-start.3 = (bf16[128,512]{1,0:T(8,128)(2,1)S(1)}, bf16[128,512]{1,0:T(8,128)(2,1)}, u32[]{:S(2)}) copy-start(bf16[128,512]{1,0:T(8,128)(2,1)} %constant.24.clone.refs_4_) | copy-start | bytes 393220
  27.4 7.7 %copy-start.4 = (bf16[128,512]{1,0:T(8,128)(2,1)S(1)}, bf16[128,512]{1,0:T(8,128)(2,1)}, u32[]{:S(2)}) copy-start(bf16[128,512]{1,0:T(8,128)(2,1)} %constant.23.clone.refs_3_) | copy-start | bytes 393220
  27.5 7.7 %copy-start.5 = (bf16[512,32]{1,0:T(8,128)(2,1)S(1)}, bf16[512,32]{1,0:T(8,128)(2,1)}, u32[]{:S(2)}) copy-start(bf16[512,32]{1,0:T(8,128)(2,1)} %constant.28.clone.refs_6_) | copy-start | bytes 98308
  27.5 7.7 %copy-start.6 = (bf16[512,32]{1,0:T(8,128)(2,1)S(1)}, bf16[512,32]{1,0:T(8,128)(2,1)}, u32[]{:S(2)}) copy-start(bf16[512,32]{1,0:T(8,128)(2,1)} %constant.27.clone.refs_8_) | copy-start | bytes 98308
  27.5 7.7 %copy-start.7 = (bf16[128,32]{1,0:T(8,128)(2,1)S(1)}, bf16[128,32]{1,0:T(8,128)(2,1)}, u32[]{:S(2)}) copy-start(bf16[128,32]{1,0:T(8,128)(2,1)} %constant.29.clone.refs_7_) | copy-start | bytes 24580
  28.3 6.9 %collective-permute-start.2 = (f32[256,128]{1,0:T(8,128)S(1)}, f32[256,128]{1,0:T(8,128)S(1)}, u32[]{:S(2)}, u32[]{:S(2)}) collective-permute-start(f32[256,128]{1,0:T(8,128)S(1)} %get-tuple-element.32), channel_id=1, source_target_pairs={{0,8},{8,0},{2,10},{10,2},{4,12},{12,4},{6,14},{14,6},{7,15},{15,7... | collective-permute-start | bytes 393224 | tf_op jit(solution)/shard_map/ppermute | solution.py:914
  28.6 6.5 %collective-permute-start.3 = (f32[256,128]{1,0:T(8,128)S(1)}, f32[256,128]{1,0:T(8,128)S(1)}, u32[]{:S(2)}, u32[]{:S(2)}) collective-permute-start(f32[256,128]{1,0:T(8,128)S(1)} %get-tuple-element.33), channel_id=1, source_target_pairs={{8,2},{2,8},{10,4},{4,10},{12,6},{6,12},{14,7},{7,14},{15,5},{5,15... | collective-permute-start | bytes 393224 | tf_op jit(solution)/shard_map/ppermute | solution.py:915
  38.6 6.7 %collective-permute-start.4 = (f32[256,128]{1,0:T(8,128)S(1)}, f32[256,128]{1,0:T(8,128)S(1)}, u32[]{:S(2)}, u32[]{:S(2)}) collective-permute-start(f32[256,128]{1,0:T(8,128)S(1)} %get-tuple-element.38), channel_id=1, source_target_pairs={{0,8},{8,0},{2,10},{10,2},{4,12},{12,4},{6,14},{14,6},{7,15},{15,7... | collective-permute-start | bytes 393224 | tf_op jit(solution)/shard_map/ppermute | solution.py:914
  38.7 6.5 %collective-permute-start.5 = (f32[256,128]{1,0:T(8,128)S(1)}, f32[256,128]{1,0:T(8,128)S(1)}, u32[]{:S(2)}, u32[]{:S(2)}) collective-permute-start(f32[256,128]{1,0:T(8,128)S(1)} %get-tuple-element.39), channel_id=1, source_target_pairs={{8,2},{2,8},{10,4},{4,10},{12,6},{6,12},{14,7},{7,14},{15,5},{5,15... | collective-permute-start | bytes 393224 | tf_op jit(solution)/shard_map/ppermute | solution.py:915
  41.9 11.1 %all-to-all-start.2 = ((f32[32,8,128]{2,1,0:T(8,128)}), f32[32,8,128]{2,1,0:T(8,128)S(1)}, u32[]{:S(2)}, u32[]{:S(2)}) async-start(f32[32,8,128]{2,1,0:T(8,128)} %get-tuple-element.48), calls=%async_computation.2 | async-start | bytes 262144 | tf_op jit(solution)/shard_map/all_to_all | solution.py:919
  46.9 6.2 %collective-permute-start.6 = (f32[256,128]{1,0:T(8,128)S(1)}, f32[256,128]{1,0:T(8,128)S(1)}, u32[]{:S(2)}, u32[]{:S(2)}) collective-permute-start(f32[256,128]{1,0:T(8,128)S(1)} %get-tuple-element.44), channel_id=1, source_target_pairs={{0,8},{8,0},{2,10},{10,2},{4,12},{12,4},{6,14},{14,6},{7,15},{15,7... | collective-permute-start | bytes 393224 | tf_op jit(solution)/shard_map/ppermute | solution.py:914
  47.2 5.9 %collective-permute-start.7 = (f32[256,128]{1,0:T(8,128)S(1)}, f32[256,128]{1,0:T(8,128)S(1)}, u32[]{:S(2)}, u32[]{:S(2)}) collective-permute-start(f32[256,128]{1,0:T(8,128)S(1)} %get-tuple-element.45), channel_id=1, source_target_pairs={{8,2},{2,8},{10,4},{4,10},{12,6},{6,12},{14,7},{7,14},{15,5},{5,15... | collective-permute-start | bytes 393224 | tf_op jit(solution)/shard_map/ppermute | solution.py:915

commit v10 on v9

--- a/solution.py
+++ b/solution.py
@@ -684,7 +684,23 @@
     return local
 
 
-def prolong_coarse(lay, first_ref, second_ref, interp_ref, image_ref, edge_ref, g_ref, h_ref, x_ref):
+def coarse_kernel(
+    lay,
+    mass,
+    stiff,
+    loads_ref,
+    g_ref,
+    x_ref,
+    interp_ref,
+    image_ref,
+    g_out,
+    x_out,
+    around_ref,
+    rows_ref,
+    first_ref,
+    second_ref,
+):
+    solve_coarse(lay, mass, stiff, loads_ref, rows_ref, first_ref, second_ref)
     mine = lay.slab() + N
     _, _, part_z = lane_parts(lay, (1, lay.width))
     bottom = part_z == 0
@@ -696,21 +712,28 @@
         far.append(jnp.where(bottom, before, after))
     local = stacked(corners(lay, *own))
     dot = functools.partial(jnp.dot, preferred_element_type=F32)
-    x_ref[...] += dot(interp_ref[...], local)
-    g_ref[...] -= dot(image_ref[...], local)
-    h_ref[...] -= dot(image_ref[...], stacked(corners(lay, *outer)))
-    edge = dot(edge_ref[...], stacked(corners(lay, *far)))
+    x_out[...] = x_ref[...] + dot(interp_ref[...], local)
+    g_out[...] = g_ref[...] - dot(image_ref[...], local)
+    around_ref[:N, :] = corners(lay, *outer)
+    around_ref[N:, :] = corners(lay, *far)
+
+
+def correct_layers(lay, around_ref, image_ref, edge_ref, h_ref):
+    dot = functools.partial(jnp.dot, preferred_element_type=F32)
+    h_ref[...] -= dot(image_ref[...], stacked(around_ref[:N, :]))
+    edge = dot(edge_ref[...], stacked(around_ref[N:, :]))
+    _, _, part_z = lane_parts(lay, (FACE, lay.width))
+    bottom = part_z == 0
     low, high = get_rows(h_ref, 0), get_rows(h_ref, N - 1)
     set_rows(h_ref, 0, low - jnp.where(bottom, edge[FACE:], 0.0))
     set_rows(h_ref, N - 1, high - jnp.where(bottom, 0.0, edge[:FACE]))
 
 
-def pair_kernel(lay, one, coarse, kind, core_ref, chip_ref, g_ref, x_ref, dinv_ref, outer_ref, *refs):
+def pair_kernel(lay, one, kind, core_ref, chip_ref, g_ref, x_ref, dinv_ref, outer_ref, *refs):
     refs = list(refs)
     high_ref, low_ref, along_ref, edge_high_ref, edge_low_ref = (refs.pop(0) for _ in range(5))
-    if coarse:
-        loads_ref, image_ref, image_edge_ref = (refs.pop(0) for _ in range(3))
-        interp_ref = refs.pop(0)
+    if kind != "inner":
+        around_ref, image_ref, image_edge_ref = (refs.pop(0) for _ in range(3))
     if kind == "inner":
         token_ref, points_ref = refs.pop(0), refs.pop(0)
     if kind == "last":
@@ -725,17 +748,12 @@
             points_out[...] = points_ref[...]
     s_ref, sh_ref, h_ref, u_ref = (refs.pop(0) for _ in range(4))
     if kind == "last":
-        g_out, x_out = refs.pop(0), refs.pop(0)
+        g_out = refs.pop(0)
 
     g_out[...] = g_ref[...]
-    x_out[...] = x_ref[...]
     receive_layers(lay, core_ref, chip_ref, h_ref)
-    if coarse:
-        rows_ref, first_ref, second_ref = refs
-        solve_coarse(lay, *coarse, loads_ref, rows_ref, first_ref, second_ref)
-        prolong_coarse(
-            lay, first_ref, second_ref, interp_ref, image_ref, image_edge_ref, g_out, h_ref, x_out
-        )
+    if kind != "inner":
+        correct_layers(lay, around_ref, image_ref, image_edge_ref, h_ref)
     assemble_both(lay, g_out, h_ref, s_ref, sh_ref)
     update = (1.0 / THETA) * dinv_ref[...] * s_ref[...]
     u_ref[...] = update
@@ -750,12 +768,12 @@
     update = u_ref[...]
     following = OLD * update + NEW * dinv_ref[...] * s_ref[...]
     if kind == "last":
-        total = (x_out[...] + (update + following)).T
+        total = (x_ref[...] + (update + following)).T
         count, block = out_ref.shape[0], out_ref.shape[1]
         for d in range(count):
             out_ref[d] = total[d * block : (d + 1) * block]
         return
-    x_out[...] += update + following
+    x_out[...] = x_ref[...] + (update + following)
     u_ref[...] = following
     subtract_stiffness(lay, one, u_ref, g_out, high_ref, low_ref, along_ref)
     send_layers(lay, g_out, s_ref, core_out, chip_out)
@@ -953,12 +971,18 @@
         scratch = [fields] * 4
         if last:
             outs = [(lay.mesh_x * lay.mesh_y, block, N**3)]
-            scratch += [fields, fields]
+            scratch += [fields]
+        g, x, around = call(
+            functools.partial(coarse_kernel, lay, *coarse),
+            [fields, fields, (2 * N, width)],
+            [loads, g, x, prolong3, image3],
+            [(lay.slabs * 4, width)] + [(lay.slabs + 2 * N, width)] * 2,
+        )
         outs = call(
-            functools.partial(pair_kernel, lay, one, coarse, "last" if last else "plain"),
+            functools.partial(pair_kernel, lay, one, "last" if last else "plain"),
             outs,
-            [core, chip, g, x, dinv, outer, *stiffness, loads, image3, image_edge, prolong3, *extra],
-            scratch + [(lay.slabs * 4, width)] + [(lay.slabs + 2 * N, width)] * 2,
+            [core, chip, g, x, dinv, outer, *stiffness, around, image3, image_edge, *extra],
+            scratch,
         )
         if last:
             break
@@ -972,7 +996,7 @@
         )
         loads = gather(loads)
         g, x, core, chip, points = call(
-            functools.partial(pair_kernel, lay, one, None, "inner"),
+            functools.partial(pair_kernel, lay, one, "inner"),
             [fields, fields, layer, layer, table],
             [*layers, g, x, dinv, outer, *stiffness, token, points],
             [fields] * 4,

time: 72.1 us -> 69.9 us (0.969)
  blocking collectives: 32.5 us -> 30.9 us
    all_to_all x1, blocking collectives: 14.7 us -> 13.1 us  [shards(): out = lax.all_to_all(out, lay.axis, 0, 0)]
    pallas_call x10 -> x12, Pallas kernels: 18 us -> 18 us  [call(): pl.pallas_call(kernel, out_shape=shapes, in_specs=specs, out_specs=[pl.Bl...]
  transfers between devices with their start and end apart: 10 -> 10, of which waited for: 2 -> 2; matrix products, arithmetic and copies ran while one was open for 0% -> 0% of each run, Pallas kernels for 10% -> 15%
where the time goes in v10:
time: 69.9 us; the launch traced here: 69.5 us
  blocking collectives  30.9 us (44%)
  Pallas kernels  18 us (26%)
  starting transfers between devices  11.9 us (17%)
  waiting for transfers between devices  7.71 us (11%)
  between operations  0.88 us (1%)
    pallas_call x12, Pallas kernels, call(): pl.pallas_call(kernel, out_shape=shapes, in_specs=specs, out_specs=[pl.Bl...  18 us
    all_to_all x1, blocking collectives, shards(): recv = lax.all_to_all(send, lay.axis, 0, 0)  17.8 us
    all_to_all x1, blocking collectives, shards(): out = lax.all_to_all(out, lay.axis, 0, 0)  13.1 us
    all_to_all x2, waiting for transfers between devices, gather(): return lax.all_to_all(loads, lay.axis, 0, 0)  7.69 us
    all_to_all x2, starting transfers between devices, gather(): return lax.all_to_all(loads, lay.axis, 0, 0)  5.61 us
    ppermute x4, starting transfers between devices, swap(): lax.ppermute(chip, lay.axis, lay.swaps(1))  5.28 us
  transfers between devices with their start and end apart: 10, of which 2 were waited for; matrix products, arithmetic and copies ran while one was open for 0% of the time, Pallas kernels for 15%

profile of v10, /device:TPU:0, one launch (start us, length us, event | category | flops | bytes accessed | tf_op | source)
XLA Modules:
  0.0 69.5 jit_solution(11075027682383992750)
XLA Ops:
  0.6 1.4 %shard_map.149 = f32[32,4,512]{2,1,0:T(4,128)S(1)} custom-call(s32[1,3]{1,0:T(1,128)} %bitcast.12, f32[1,3]{1,0:T(1,128)} %bitcast.13, f32[1,3]{1,0:T(1,128)} %bitcast.14, f32[512,128]{1,0:T(8,128)} %bitcast.10), custom_call_target="tpu_custom_call" | custom-call | tf_op jit(solution)/shard_map/pallas_call | solution.py:851
  2.0 0.0 copy-start
  2.0 0.0 copy-start.1
  2.0 17.8 %all_to_all.20.recv_ref = f32[32,4,512]{2,1,0:T(4,128)S(1)} all-to-all(f32[32,4,512]{2,1,0:T(4,128)S(1)} %shard_map.149), channel_id=1, replica_groups=mesh['ex'=4,'ey'=8] {'ex','ey'}, dimensions={0} | all-to-all | bytes 524288 | tf_op jit(solution)/shard_map/all_to_all | solution.py:926
  19.8 0.0 copy-start.8
  19.8 2.3 %shard_map.150 = (f32[512,128]{1,0:T(8,128)S(1)}, f32[512,128]{1,0:T(8,128)S(1)}, f32[512,128]{1,0:T(8,128)S(1)}, f32[512,128]{1,0:T(8,128)S(1)}, f32[256,128]{1,0:T(8,128)S(1)}, /*index=5*/f32[32,128]{1,0:T(8,128)S(1)}) custom-call(f32[32,4,512]{2,1,0:T(4,128)S(1)} %all_to_all.20.recv_ref, bf16[256,256]{1,0:T(8,128)(2,1)S(1)} %copy-done.1, ...), custom_call_target="tpu_custom_call" | custom-call | tf_op jit(solution)/shard_map/pallas_call | solution.py:851
  22.1 0.0 copy-start.9
  22.1 0.9 %collective-permute-start.1 = (f32[256,128]{1,0:T(8,128)S(1)}, f32[256,128]{1,0:T(8,128)S(1)}, u32[]{:S(2)}, u32[]{:S(2)}) collective-permute-start(f32[256,128]{1,0:T(8,128)S(1)} %get-tuple-element.33), channel_id=1, source_target_pairs={{8,2},{2,8},{10,4},{4,10},{12,6},{6,12},{14,7},{7,14},{15,5},{5,15... | collective-permute-start | bytes 393224 | tf_op jit(solution)/shard_map/ppermute | solution.py:933
  23.1 0.2 collective-permute-start
  23.3 1.3 %shard_map.151 = (f32[32,8,128]{2,1,0:T(8,128)}, f32[8,128]{1,0:T(8,128)S(1)}) custom-call(f32[512,128]{1,0:T(8,128)S(1)} %get-tuple-element.34.g_ref, f32[512,128]{1,0:T(8,128)S(1)} %get-tuple-element.35.x_ref, f32[512,128]{1,0:T(8,128)S(1)} %get-tuple-element.36.dinv_ref, bf16[16,1024]{1,0:T(8,128)(2,1)S(1)} %copy-done.8, bf16[16,128]{1,0:T(8,128)(2,1)S(1)} %copy-done.9), custom_call_target="tpu_custom_call" | custom-call | tf_op jit(solution)/shard_map/pallas_call | solution.py:851
  24.5 2.9 %all-to-all-start.1 = ((f32[32,8,128]{2,1,0:T(8,128)}), f32[32,8,128]{2,1,0:T(8,128)S(1)}, u32[]{:S(2)}, u32[]{:S(2)}) async-start(f32[32,8,128]{2,1,0:T(8,128)} %get-tuple-element.40), calls=%async_computation.1 | async-start | bytes 262144 | tf_op jit(solution)/shard_map/all_to_all | solution.py:937
  27.5 0.0 copy-start.2
  27.5 0.8 %shard_map.152 = (f32[512,128]{1,0:T(8,128)S(1)}, f32[512,128]{1,0:T(8,128)S(1)}, f32[256,128]{1,0:T(8,128)S(1)}, f32[256,128]{1,0:T(8,128)S(1)}) custom-call(f32[256,128]{1,0:T(8,128)S(1)} %collective-permute-done.core_ref, f32[256,128]{1,0:T(8,128)S(1)} %collective-permute-done.1.chip_ref, f32[512,128]{1,0:T(8,128)S(1)} %get-tuple-element.34.g_ref, ...), custom_call_target="tpu_custom_call" | custom-call | tf_op jit(solution)/shard_map/pallas_call | solution.py:851
  28.3 0.3 collective-permute-start.2
  28.7 1.6 %collective-permute-start.3 = (f32[256,128]{1,0:T(8,128)S(1)}, f32[256,128]{1,0:T(8,128)S(1)}, u32[]{:S(2)}, u32[]{:S(2)}) collective-permute-start(f32[256,128]{1,0:T(8,128)S(1)} %get-tuple-element.39), channel_id=1, source_target_pairs={{8,2},{2,8},{10,4},{4,10},{12,6},{6,12},{14,7},{7,14},{15,5},{5,15... | collective-permute-start | bytes 393224 | tf_op jit(solution)/shard_map/ppermute | solution.py:933
  30.3 4.9 %all-to-all-done.1.loads_ref = f32[32,8,128]{2,1,0:T(8,128)S(1)} async-done(((f32[32,8,128]{2,1,0:T(8,128)}), f32[32,8,128]{2,1,0:T(8,128)S(1)}, u32[]{:S(2)}, u32[]{:S(2)}) %all-to-all-start.1) | async-done | bytes 131104 | tf_op jit(solution)/shard_map/all_to_all | solution.py:937
  35.3 0.0 copy-start.7
  35.3 1.6 %shard_map.153 = (f32[512,128]{1,0:T(8,128)S(1)}, f32[512,128]{1,0:T(8,128)S(1)}, f32[16,128]{1,0:T(8,128)S(1)}) custom-call(f32[32,8,128]{2,1,0:T(8,128)S(1)} %all-to-all-done.1.loads_ref, f32[512,128]{1,0:T(8,128)S(1)} %get-tuple-element.41.g_ref, f32[512,128]{1,0:T(8,128)S(1)} %get-tuple-element.42.x_ref, bf16[512,32]{1,0:T(8,128)(2,1)S(1)} %copy-done.6, ...), custom_call_target="tpu_custom_call" | custom-call | tf_op jit(solution)/shard_map/pallas_call | solution.py:851
  36.9 1.8 %shard_map.154 = (f32[512,128]{1,0:T(8,128)S(1)}, f32[512,128]{1,0:T(8,128)S(1)}, f32[256,128]{1,0:T(8,128)S(1)}, f32[256,128]{1,0:T(8,128)S(1)}) custom-call(f32[256,128]{1,0:T(8,128)S(1)} %collective-permute-done.2.core_ref, f32[256,128]{1,0:T(8,128)S(1)} %collective-permute-done.3.chip_ref, f32[512,128]{1,0:T(8,128)S(1)} %get-tuple-element.43.g_ref, ...), custom_call_target="tpu_custom_call" | custom-call | tf_op jit(solution)/shard_map/pallas_call | solution.py:851
  38.7 0.2 collective-permute-start.4
  38.9 1.1 %collective-permute-start.5 = (f32[256,128]{1,0:T(8,128)S(1)}, f32[256,128]{1,0:T(8,128)S(1)}, u32[]{:S(2)}, u32[]{:S(2)}) collective-permute-start(f32[256,128]{1,0:T(8,128)S(1)} %get-tuple-element.48), channel_id=1, source_target_pairs={{8,2},{2,8},{10,4},{4,10},{12,6},{6,12},{14,7},{7,14},{15,5},{5,15... | collective-permute-start | bytes 393224 | tf_op jit(solution)/shard_map/ppermute | solution.py:933
  40.0 2.1 %shard_map.155 = (f32[32,8,128]{2,1,0:T(8,128)}, f32[8,128]{1,0:T(8,128)S(1)}) custom-call(f32[512,128]{1,0:T(8,128)S(1)} %get-tuple-element.49.g_ref, f32[512,128]{1,0:T(8,128)S(1)} %get-tuple-element.36.dinv_ref, f32[512,128]{1,0:T(8,128)S(1)} %get-tuple-element.45.outer_ref, bf16[256,256]{1,0:T(8,128)(2,1)S(1)} %copy-done.1, ...), custom_call_target="tpu_custom_call" | custom-call | tf_op jit(solution)/shard_map/pallas_call | solution.py:851
  42.1 2.7 %all-to-all-start.2 = ((f32[32,8,128]{2,1,0:T(8,128)}), f32[32,8,128]{2,1,0:T(8,128)S(1)}, u32[]{:S(2)}, u32[]{:S(2)}) async-start(f32[32,8,128]{2,1,0:T(8,128)} %get-tuple-element.55), calls=%async_computation.2 | async-start | bytes 262144 | tf_op jit(solution)/shard_map/all_to_all | solution.py:937
  44.8 1.6 %shard_map.156 = (f32[512,128]{1,0:T(8,128)S(1)}, f32[512,128]{1,0:T(8,128)S(1)}, f32[256,128]{1,0:T(8,128)S(1)}, f32[256,128]{1,0:T(8,128)S(1)}, f32[32,128]{1,0:T(8,128)S(1)}) custom-call(f32[256,128]{1,0:T(8,128)S(1)} %collective-permute-done.4.core_ref, f32[256,128]{1,0:T(8,128)S(1)} %collective-permute-done.5.chip_ref, ...), custom_call_target="tpu_custom_call" | custom-call | tf_op jit(solution)/shard_map/pallas_call | solution.py:851
  46.4 0.3 collective-permute-start.6
  46.7 1.6 %collective-permute-start.7 = (f32[256,128]{1,0:T(8,128)S(1)}, f32[256,128]{1,0:T(8,128)S(1)}, u32[]{:S(2)}, u32[]{:S(2)}) collective-permute-start(f32[256,128]{1,0:T(8,128)S(1)} %get-tuple-element.54), channel_id=1, source_target_pairs={{8,2},{2,8},{10,4},{4,10},{12,6},{6,12},{14,7},{7,14},{15,5},{5,15... | collective-permute-start | bytes 393224 | tf_op jit(solution)/shard_map/ppermute | solution.py:933
  48.3 1.5 %shard_map.158 = (f32[1536,128]{1,0:T(8,128)}, f32[8,128]{1,0:T(8,128)S(1)}) custom-call(f32[32,128]{1,0:T(8,128)S(1)} %get-tuple-element.61.points_ref), custom_call_target="tpu_custom_call" | custom-call | tf_op jit(solution)/shard_map/pallas_call | solution.py:851
  49.8 2.7 %all-to-all-done.2.loads_ref = f32[32,8,128]{2,1,0:T(8,128)S(1)} async-done(((f32[32,8,128]{2,1,0:T(8,128)}), f32[32,8,128]{2,1,0:T(8,128)S(1)}, u32[]{:S(2)}, u32[]{:S(2)}) %all-to-all-start.2) | async-done | bytes 131104 | tf_op jit(solution)/shard_map/all_to_all | solution.py:937
  52.5 1.6 %shard_map.157 = (f32[512,128]{1,0:T(8,128)S(1)}, f32[512,128]{1,0:T(8,128)S(1)}, f32[16,128]{1,0:T(8,128)S(1)}) custom-call(f32[32,8,128]{2,1,0:T(8,128)S(1)} %all-to-all-done.2.loads_ref, f32[512,128]{1,0:T(8,128)S(1)} %get-tuple-element.56.g_ref, f32[512,128]{1,0:T(8,128)S(1)} %get-tuple-element.57.x_ref, bf16[512,32]{1,0:T(8,128)(2,1)S(1)} %copy-done.6, ...), custom_call_target="tpu_custom_call" | custom-call | tf_op jit(solution)/shard_map/pallas_call | solution.py:851
  54.1 1.3 %shard_map.159 = f32[32,4,512]{2,1,0:T(4,128)S(1)} custom-call(f32[256,128]{1,0:T(8,128)S(1)} %collective-permute-done.6.core_ref, f32[256,128]{1,0:T(8,128)S(1)} %collective-permute-done.7.chip_ref, f32[512,128]{1,0:T(8,128)S(1)} %get-tuple-element.58.g_ref, f32[512,128]{1,0:T(8,128)S(1)} %get-tuple-element.59.x_ref, ...), custom_call_target="tpu_custom_call" | custom-call | tf_op jit(solution)/shard_map/pallas_call | solution.py:851
  55.5 13.1 %all_to_all.21.recv_ref = f32[32,4,512]{2,1,0:T(4,128)S(1)} all-to-all(f32[32,4,512]{2,1,0:T(4,128)S(1)} %shard_map.159), channel_id=1, replica_groups=mesh['ex'=4,'ey'=8] {'ex','ey'}, dimensions={0} | all-to-all | bytes 524288 | tf_op jit(solution)/shard_map/all_to_all | solution.py:1012
  68.6 0.9 %shard_map.160 = f32[512,128]{1,0:T(8,128)} custom-call(f32[32,4,512]{2,1,0:T(4,128)S(1)} %all_to_all.21.recv_ref), custom_call_target="tpu_custom_call" | custom-call | tf_op jit(solution)/shard_map/pallas_call | solution.py:851
  (22 shorter events, 0.1 us)
Async XLA Ops:
  2.0 17.8 %copy-start = (bf16[256,256]{1,0:T(8,128)(2,1)S(1)}, bf16[256,256]{1,0:T(8,128)(2,1)}, u32[]{:S(2)}) copy-start(bf16[256,256]{1,0:T(8,128)(2,1)} %constant.21.clone.low_ref.refs_1_) | copy-start | bytes 393220
  2.0 17.8 %copy-start.1 = (bf16[256,256]{1,0:T(8,128)(2,1)S(1)}, bf16[256,256]{1,0:T(8,128)(2,1)}, u32[]{:S(2)}) copy-start(bf16[256,256]{1,0:T(8,128)(2,1)} %constant.20.clone.high_ref.refs_0_) | copy-start | bytes 393220
  2.0 17.8 %copy-start.3 = (f32[64,128]{1,0:T(8,128)S(1)}, f32[64,128]{1,0:T(8,128)}, u32[]{:S(2)}) copy-start(f32[64,128]{1,0:T(8,128)} %constant.22.clone.along_ref.refs_2_) | copy-start | bytes 98308
  19.8 3.4 %copy-start.8 = (bf16[16,1024]{1,0:T(8,128)(2,1)S(1)}, bf16[16,1024]{1,0:T(8,128)(2,1)}, u32[]{:S(2)}) copy-start(bf16[16,1024]{1,0:T(8,128)(2,1)} %constant.25.clone.loads_ref) | copy-start | bytes 98308
  22.1 1.2 %copy-start.9 = (bf16[16,128]{1,0:T(8,128)(2,1)S(1)}, bf16[16,128]{1,0:T(8,128)(2,1)}, u32[]{:S(2)}) copy-start(bf16[16,128]{1,0:T(8,128)(2,1)} %constant.26.clone.near_ref) | copy-start | bytes 12292
  22.1 5.4 %collective-permute-start.1 = (f32[256,128]{1,0:T(8,128)S(1)}, f32[256,128]{1,0:T(8,128)S(1)}, u32[]{:S(2)}, u32[]{:S(2)}) collective-permute-start(f32[256,128]{1,0:T(8,128)S(1)} %get-tuple-element.33), channel_id=1, source_target_pairs={{8,2},{2,8},{10,4},{4,10},{12,6},{6,12},{14,7},{7,14},{15,5},{5,15... | collective-permute-start | bytes 393224 | tf_op jit(solution)/shard_map/ppermute | solution.py:933
  23.1 4.5 %collective-permute-start = (f32[256,128]{1,0:T(8,128)S(1)}, f32[256,128]{1,0:T(8,128)S(1)}, u32[]{:S(2)}, u32[]{:S(2)}) collective-permute-start(f32[256,128]{1,0:T(8,128)S(1)} %get-tuple-element.33), channel_id=1, source_target_pairs={{0,8},{8,0},{2,10},{10,2},{4,12},{12,4},{6,14},{14,6},{7,15},{15,7... | collective-permute-start | bytes 393224 | tf_op jit(solution)/shard_map/ppermute | solution.py:932
  24.5 10.7 %all-to-all-start.1 = ((f32[32,8,128]{2,1,0:T(8,128)}), f32[32,8,128]{2,1,0:T(8,128)S(1)}, u32[]{:S(2)}, u32[]{:S(2)}) async-start(f32[32,8,128]{2,1,0:T(8,128)} %get-tuple-element.40), calls=%async_computation.1 | async-start | bytes 262144 | tf_op jit(solution)/shard_map/all_to_all | solution.py:937
  27.5 7.7 %copy-start.2 = (bf16[512,32]{1,0:T(8,128)(2,1)S(1)}, bf16[512,32]{1,0:T(8,128)(2,1)}, u32[]{:S(2)}) copy-start(bf16[512,32]{1,0:T(8,128)(2,1)} %constant.28.clone.image_ref.refs_6_) | copy-start | bytes 98308
  27.5 7.7 %copy-start.6 = (bf16[512,32]{1,0:T(8,128)(2,1)S(1)}, bf16[512,32]{1,0:T(8,128)(2,1)}, u32[]{:S(2)}) copy-start(bf16[512,32]{1,0:T(8,128)(2,1)} %constant.27.clone.interp_ref) | copy-start | bytes 98308
  28.3 8.5 %collective-permute-start.2 = (f32[256,128]{1,0:T(8,128)S(1)}, f32[256,128]{1,0:T(8,128)S(1)}, u32[]{:S(2)}, u32[]{:S(2)}) collective-permute-start(f32[256,128]{1,0:T(8,128)S(1)} %get-tuple-element.38), channel_id=1, source_target_pairs={{0,8},{8,0},{2,10},{10,2},{4,12},{12,4},{6,14},{14,6},{7,15},{15,7... | collective-permute-start | bytes 393224 | tf_op jit(solution)/shard_map/ppermute | solution.py:932
  28.7 8.2 %collective-permute-start.3 = (f32[256,128]{1,0:T(8,128)S(1)}, f32[256,128]{1,0:T(8,128)S(1)}, u32[]{:S(2)}, u32[]{:S(2)}) collective-permute-start(f32[256,128]{1,0:T(8,128)S(1)} %get-tuple-element.39), channel_id=1, source_target_pairs={{8,2},{2,8},{10,4},{4,10},{12,6},{6,12},{14,7},{7,14},{15,5},{5,15... | collective-permute-start | bytes 393224 | tf_op jit(solution)/shard_map/ppermute | solution.py:933
  35.2 1.6 %copy-start.4 = (bf16[128,512]{1,0:T(8,128)(2,1)S(1)}, bf16[128,512]{1,0:T(8,128)(2,1)}, u32[]{:S(2)}) copy-start(bf16[128,512]{1,0:T(8,128)(2,1)} %constant.24.clone.refs_4_) | copy-start | bytes 393220
  35.2 1.6 %copy-start.5 = (bf16[128,512]{1,0:T(8,128)(2,1)S(1)}, bf16[128,512]{1,0:T(8,128)(2,1)}, u32[]{:S(2)}) copy-start(bf16[128,512]{1,0:T(8,128)(2,1)} %constant.23.clone.refs_3_) | copy-start | bytes 393220
  35.3 1.6 %copy-start.7 = (bf16[128,32]{1,0:T(8,128)(2,1)S(1)}, bf16[128,32]{1,0:T(8,128)(2,1)}, u32[]{:S(2)}) copy-start(bf16[128,32]{1,0:T(8,128)(2,1)} %constant.29.clone.refs_7_) | copy-start | bytes 24580
  38.7 6.0 %collective-permute-start.4 = (f32[256,128]{1,0:T(8,128)S(1)}, f32[256,128]{1,0:T(8,128)S(1)}, u32[]{:S(2)}, u32[]{:S(2)}) collective-permute-start(f32[256,128]{1,0:T(8,128)S(1)} %get-tuple-element.47), channel_id=1, source_target_pairs={{0,8},{8,0},{2,10},{10,2},{4,12},{12,4},{6,14},{14,6},{7,15},{15,7... | collective-permute-start | bytes 393224 | tf_op jit(solution)/shard_map/ppermute | solution.py:932
  38.9 5.9 %collective-permute-start.5 = (f32[256,128]{1,0:T(8,128)S(1)}, f32[256,128]{1,0:T(8,128)S(1)}, u32[]{:S(2)}, u32[]{:S(2)}) collective-permute-start(f32[256,128]{1,0:T(8,128)S(1)} %get-tuple-element.48), channel_id=1, source_target_pairs={{8,2},{2,8},{10,4},{4,10},{12,6},{6,12},{14,7},{7,14},{15,5},{5,15... | collective-permute-start | bytes 393224 | tf_op jit(solution)/shard_map/ppermute | solution.py:933
  42.1 10.5 %all-to-all-start.2 = ((f32[32,8,128]{2,1,0:T(8,128)}), f32[32,8,128]{2,1,0:T(8,128)S(1)}, u32[]{:S(2)}, u32[]{:S(2)}) async-start(f32[32,8,128]{2,1,0:T(8,128)} %get-tuple-element.55), calls=%async_computation.2 | async-start | bytes 262144 | tf_op jit(solution)/shard_map/all_to_all | solution.py:937
  46.4 7.8 %collective-permute-start.6 = (f32[256,128]{1,0:T(8,128)S(1)}, f32[256,128]{1,0:T(8,128)S(1)}, u32[]{:S(2)}, u32[]{:S(2)}) collective-permute-start(f32[256,128]{1,0:T(8,128)S(1)} %get-tuple-element.53), channel_id=1, source_target_pairs={{0,8},{8,0},{2,10},{10,2},{4,12},{12,4},{6,14},{14,6},{7,15},{15,7... | collective-permute-start | bytes 393224 | tf_op jit(solution)/shard_map/ppermute | solution.py:932
  46.7 7.4 %collective-permute-start.7 = (f32[256,128]{1,0:T(8,128)S(1)}, f32[256,128]{1,0:T(8,128)S(1)}, u32[]{:S(2)}, u32[]{:S(2)}) collective-permute-start(f32[256,128]{1,0:T(8,128)S(1)} %get-tuple-element.54), channel_id=1, source_target_pairs={{8,2},{2,8},{10,4},{4,10},{12,6},{6,12},{14,7},{7,14},{15,5},{5,15... | collective-permute-start | bytes 393224 | tf_op jit(solution)/shard_map/ppermute | solution.py:933

commit v11 on v10

--- a/solution.py
+++ b/solution.py
@@ -348,16 +348,7 @@
     return base, [b + 1.0 + o for b, o in zip(base, offset)], [scale * f for f in force]
 
 
-def for_points(points_ref, local_points, visit):
-    def row_of(row, _):
-        for place in range(local_points):
-            visit(row, place)
-        return 0
-
-    lax.fori_loop(0, points_ref.shape[0], row_of, 0)
-
-
-def right_side(lay, local_points, one, points_ref, g_ref, halo_ref):
+def right_side(lay, local_points, one, points_ref, list_ref, g_ref, halo_ref):
     derivative, weights = one
     shape = (N, lay.width)
     part_x, part_y, part_z = lane_parts(lay, shape)
@@ -375,35 +366,55 @@
             terms = [a + b for a, b in zip(terms[::2], terms[1::2])]
         return plain, terms[0]
 
-    def visit(p, place):
-        base, position, force = point_values(points_ref, p, place, 0.25 * GAUSS_NORM)
-        first = first_z.astype(F32)
-
-        @pl.when((base[2] + 2.0 >= first - 1.0) & (base[2] - 1.0 <= first + lay.depth))
-        def _():
-            x0, x1 = weighted(part_x, base[0], position[0])
-            y0, y1 = weighted(part_y, base[1], position[1])
-            z0, z1 = weighted(elem_z, base[2], position[2])
-            h0, h1 = weighted(elem_halo, base[2], position[2])
-            pick = part_z[0:1] == 0
-            h0 = jnp.where(pick, h0[N - 1 : N], h0[0:1])
-            h1 = jnp.where(pick, h1[N - 1 : N], h1[0:1])
-            x1 = force[0] * x1
-            fz1 = force[2] * z1
-            fz0 = force[1] * z0
+    def place_of(p):
+        return (p, 0) if local_points == 1 else (lax.div(p, local_points), lax.rem(p, local_points))
+
+    first = first_z.astype(F32)
+
+    def collect(p, found):
+        row, place = place_of(p)
+        base = points_ref[row, (place * 9 + 2) * N]
+        list_ref[found] = p
+        reached = (base + 2.0 >= first - 1.0) & (base - 1.0 <= first + lay.depth)
+        return found + jnp.where(reached, 1, 0)
+
+    found = lax.fori_loop(0, points_ref.shape[0] * local_points, collect, jnp.int32(0))
+    pick = part_z[0:1] == 0
+
+    def factors(n):
+        row, place = place_of(list_ref[jnp.minimum(n, found - 1)])
+        base, position, force = point_values(
+            points_ref, row, place, jnp.where(n < found, 0.25 * GAUSS_NORM, 0.0)
+        )
+        x0, x1 = weighted(part_x, base[0], position[0])
+        y0, y1 = weighted(part_y, base[1], position[1])
+        z0, z1 = weighted(elem_z, base[2], position[2])
+        h0, h1 = weighted(elem_halo, base[2], position[2])
+        h0 = jnp.where(pick, h0[N - 1 : N], h0[0:1])
+        h1 = jnp.where(pick, h1[N - 1 : N], h1[0:1])
+        planes = []
+        for j in range(N):
+            row0, row1 = y0[j : j + 1], y1[j : j + 1]
+            planes.append((row0 * z0, row1 * (force[1] * z0) + row0 * (force[2] * z1)))
+        planes.append((y0 * h0, y1 * (force[1] * h0) + y0 * (force[2] * h1)))
+        return force[0] * x1, x0, planes
+
+    def two(t, _):
+        points = [factors(2 * t), factors(2 * t + 1)]
+
+        def term(i, j):
+            parts = [
+                x1[i : i + 1] * planes[j][0] + x0[i : i + 1] * planes[j][1] for x1, x0, planes in points
+            ]
+            return parts[0] + parts[1]
+
+        for i in range(N):
             for j in range(N):
-                first_part = y0[j : j + 1] * z0
-                other_part = y1[j : j + 1] * fz0 + y0[j : j + 1] * fz1
-                for i in range(N):
-                    rows = pl.ds((i * N + j) * N, N)
-                    g_ref[rows, :] += x1[i : i + 1] * first_part + x0[i : i + 1] * other_part
-            first_part = y0 * h0
-            other_part = y1 * (force[1] * h0) + y0 * (force[2] * h1)
-            for i in range(N):
-                rows = pl.ds(i * N, N)
-                halo_ref[rows, :] += x1[i : i + 1] * first_part + x0[i : i + 1] * other_part
-
-    for_points(points_ref, local_points, visit)
+                g_ref[pl.ds((i * N + j) * N, N), :] += term(i, j)
+            halo_ref[pl.ds(i * N, N), :] += term(i, N)
+        return 0
+
+    lax.fori_loop(0, lax.div(found + 1, 2), two, 0)
 
 
 def inverse_diagonal(lay, factor, dinv_ref, outer):
@@ -460,6 +471,7 @@
     halo_ref,
     flat_ref,
     table_ref,
+    list_ref,
     sem,
 ):
     count, block = recv_ref.shape[0], recv_ref.shape[1]
@@ -477,7 +489,7 @@
     inverse_diagonal(lay, factor, dinv_ref, False)
     inverse_diagonal(lay, factor, outer_ref, True)
     copy.wait()
-    right_side(lay, local_points, (derivative, one[1]), table_ref, g_ref, halo_ref)
+    right_side(lay, local_points, (derivative, one[1]), table_ref, list_ref, g_ref, halo_ref)
     assemble(lay, g_ref, s_ref, halo_ref[...])
     x_ref[...] = (1.0 / THETA) * dinv_ref[...] * s_ref[...]
     subtract_stiffness(lay, one, x_ref, g_ref, high_ref, low_ref, along_ref)
@@ -944,7 +956,14 @@
         functools.partial(first_kernel, lay, local_points, derivative, one, factor),
         [fields, fields, fields, fields, (256, width), table],
         [recv, high, low, along],
-        [fields, face_shape, (width, N**3), pltpu.SMEM(table, F32), pltpu.SemaphoreType.DMA],
+        [
+            fields,
+            face_shape,
+            (width, N**3),
+            pltpu.SMEM(table, F32),
+            pltpu.SMEM((devices * local_points,), jnp.int32),
+            pltpu.SemaphoreType.DMA,
+        ],
     )
     faces = swap(face, face)
     loads, token = call(

time: 69.9 us -> 69.6 us (level)
  no operation moved by 1% of the time
where the time goes in v11:
time: 69.6 us; the launch traced here: 69.2 us
  blocking collectives  30.9 us (44%)
  Pallas kernels  17.7 us (25%)
  starting transfers between devices  12 us (17%)
  waiting for transfers between devices  7.71 us (11%)
  between operations  0.88 us (1%)
    all_to_all x1, blocking collectives, shards(): recv = lax.all_to_all(send, lay.axis, 0, 0)  17.8 us
    pallas_call x12, Pallas kernels, call(): pl.pallas_call(kernel, out_shape=shapes, in_specs=specs, out_specs=[pl.Bl...  17.7 us
    all_to_all x1, blocking collectives, shards(): out = lax.all_to_all(out, lay.axis, 0, 0)  13.1 us
    all_to_all x2, waiting for transfers between devices, gather(): return lax.all_to_all(loads, lay.axis, 0, 0)  7.69 us
    all_to_all x2, starting transfers between devices, gather(): return lax.all_to_all(loads, lay.axis, 0, 0)  5.68 us
    ppermute x4, starting transfers between devices, swap(): lax.ppermute(chip, lay.axis, lay.swaps(1))  5.42 us
  transfers between devices with their start and end apart: 10, of which 2 were waited for; matrix products, arithmetic and copies ran while one was open for 0% of the time, Pallas kernels for 15%

profile of v11, /device:TPU:0, one launch (start us, length us, event | category | flops | bytes accessed | tf_op | source)
XLA Modules:
  0.0 69.2 jit_solution(11553548774110773171)
XLA Ops:
  0.6 1.4 %shard_map.149 = f32[32,4,512]{2,1,0:T(4,128)S(1)} custom-call(s32[1,3]{1,0:T(1,128)} %bitcast.12, f32[1,3]{1,0:T(1,128)} %bitcast.13, f32[1,3]{1,0:T(1,128)} %bitcast.14, f32[512,128]{1,0:T(8,128)} %bitcast.10), custom_call_target="tpu_custom_call" | custom-call | tf_op jit(solution)/shard_map/pallas_call | solution.py:863
  2.0 0.0 copy-start
  2.0 0.0 copy-start.1
  2.0 0.0 copy-start.3
  2.0 17.8 %all_to_all.20.recv_ref = f32[32,4,512]{2,1,0:T(4,128)S(1)} all-to-all(f32[32,4,512]{2,1,0:T(4,128)S(1)} %shard_map.149), channel_id=1, replica_groups=mesh['ex'=4,'ey'=8] {'ex','ey'}, dimensions={0} | all-to-all | bytes 524288 | tf_op jit(solution)/shard_map/all_to_all | solution.py:938
  19.8 0.0 copy-start.8
  19.8 1.9 %shard_map.150 = (f32[512,128]{1,0:T(8,128)S(1)}, f32[512,128]{1,0:T(8,128)S(1)}, f32[512,128]{1,0:T(8,128)S(1)}, f32[512,128]{1,0:T(8,128)S(1)}, f32[256,128]{1,0:T(8,128)S(1)}, /*index=5*/f32[32,128]{1,0:T(8,128)S(1)}) custom-call(f32[32,4,512]{2,1,0:T(4,128)S(1)} %all_to_all.20.recv_ref, bf16[256,256]{1,0:T(8,128)(2,1)S(1)} %copy-done.1, ...), custom_call_target="tpu_custom_call" | custom-call | tf_op jit(solution)/shard_map/pallas_call | solution.py:863
  21.8 0.0 copy-start.9
  21.8 1.1 %collective-permute-start.1 = (f32[256,128]{1,0:T(8,128)S(1)}, f32[256,128]{1,0:T(8,128)S(1)}, u32[]{:S(2)}, u32[]{:S(2)}) collective-permute-start(f32[256,128]{1,0:T(8,128)S(1)} %get-tuple-element.33), channel_id=1, source_target_pairs={{8,2},{2,8},{10,4},{4,10},{12,6},{6,12},{14,7},{7,14},{15,5},{5,15... | collective-permute-start | bytes 393224 | tf_op jit(solution)/shard_map/ppermute | solution.py:945
  22.9 0.1 collective-permute-start
  22.9 1.3 %shard_map.151 = (f32[32,8,128]{2,1,0:T(8,128)}, f32[8,128]{1,0:T(8,128)S(1)}) custom-call(f32[512,128]{1,0:T(8,128)S(1)} %get-tuple-element.34.g_ref, f32[512,128]{1,0:T(8,128)S(1)} %get-tuple-element.35.x_ref, f32[512,128]{1,0:T(8,128)S(1)} %get-tuple-element.36.dinv_ref, bf16[16,1024]{1,0:T(8,128)(2,1)S(1)} %copy-done.8, bf16[16,128]{1,0:T(8,128)(2,1)S(1)} %copy-done.9), custom_call_target="tpu_custom_call" | custom-call | tf_op jit(solution)/shard_map/pallas_call | solution.py:863
  24.2 3.0 %all-to-all-start.1 = ((f32[32,8,128]{2,1,0:T(8,128)}), f32[32,8,128]{2,1,0:T(8,128)S(1)}, u32[]{:S(2)}, u32[]{:S(2)}) async-start(f32[32,8,128]{2,1,0:T(8,128)} %get-tuple-element.40), calls=%async_computation.1 | async-start | bytes 262144 | tf_op jit(solution)/shard_map/all_to_all | solution.py:949
  27.3 0.0 copy-start.6
  27.3 0.8 %shard_map.152 = (f32[512,128]{1,0:T(8,128)S(1)}, f32[512,128]{1,0:T(8,128)S(1)}, f32[256,128]{1,0:T(8,128)S(1)}, f32[256,128]{1,0:T(8,128)S(1)}) custom-call(f32[256,128]{1,0:T(8,128)S(1)} %collective-permute-done.core_ref, f32[256,128]{1,0:T(8,128)S(1)} %collective-permute-done.1.chip_ref, f32[512,128]{1,0:T(8,128)S(1)} %get-tuple-element.34.g_ref, ...), custom_call_target="tpu_custom_call" | custom-call | tf_op jit(solution)/shard_map/pallas_call | solution.py:863
  28.1 0.3 collective-permute-start.2
  28.4 1.6 %collective-permute-start.3 = (f32[256,128]{1,0:T(8,128)S(1)}, f32[256,128]{1,0:T(8,128)S(1)}, u32[]{:S(2)}, u32[]{:S(2)}) collective-permute-start(f32[256,128]{1,0:T(8,128)S(1)} %get-tuple-element.39), channel_id=1, source_target_pairs={{8,2},{2,8},{10,4},{4,10},{12,6},{6,12},{14,7},{7,14},{15,5},{5,15... | collective-permute-start | bytes 393224 | tf_op jit(solution)/shard_map/ppermute | solution.py:945
  30.0 4.9 %all-to-all-done.1.loads_ref = f32[32,8,128]{2,1,0:T(8,128)S(1)} async-done(((f32[32,8,128]{2,1,0:T(8,128)}), f32[32,8,128]{2,1,0:T(8,128)S(1)}, u32[]{:S(2)}, u32[]{:S(2)}) %all-to-all-start.1) | async-done | bytes 131104 | tf_op jit(solution)/shard_map/all_to_all | solution.py:949
  35.0 1.6 %shard_map.153 = (f32[512,128]{1,0:T(8,128)S(1)}, f32[512,128]{1,0:T(8,128)S(1)}, f32[16,128]{1,0:T(8,128)S(1)}) custom-call(f32[32,8,128]{2,1,0:T(8,128)S(1)} %all-to-all-done.1.loads_ref, f32[512,128]{1,0:T(8,128)S(1)} %get-tuple-element.41.g_ref, f32[512,128]{1,0:T(8,128)S(1)} %get-tuple-element.42.x_ref, bf16[512,32]{1,0:T(8,128)(2,1)S(1)} %copy-done.6, ...), custom_call_target="tpu_custom_call" | custom-call | tf_op jit(solution)/shard_map/pallas_call | solution.py:863
  36.6 1.8 %shard_map.154 = (f32[512,128]{1,0:T(8,128)S(1)}, f32[512,128]{1,0:T(8,128)S(1)}, f32[256,128]{1,0:T(8,128)S(1)}, f32[256,128]{1,0:T(8,128)S(1)}) custom-call(f32[256,128]{1,0:T(8,128)S(1)} %collective-permute-done.2.core_ref, f32[256,128]{1,0:T(8,128)S(1)} %collective-permute-done.3.chip_ref, f32[512,128]{1,0:T(8,128)S(1)} %get-tuple-element.43.g_ref, ...), custom_call_target="tpu_custom_call" | custom-call | tf_op jit(solution)/shard_map/pallas_call | solution.py:863
  38.5 0.2 collective-permute-start.4
  38.6 1.1 %collective-permute-start.5 = (f32[256,128]{1,0:T(8,128)S(1)}, f32[256,128]{1,0:T(8,128)S(1)}, u32[]{:S(2)}, u32[]{:S(2)}) collective-permute-start(f32[256,128]{1,0:T(8,128)S(1)} %get-tuple-element.48), channel_id=1, source_target_pairs={{8,2},{2,8},{10,4},{4,10},{12,6},{6,12},{14,7},{7,14},{15,5},{5,15... | collective-permute-start | bytes 393224 | tf_op jit(solution)/shard_map/ppermute | solution.py:945
  39.7 2.1 %shard_map.155 = (f32[32,8,128]{2,1,0:T(8,128)}, f32[8,128]{1,0:T(8,128)S(1)}) custom-call(f32[512,128]{1,0:T(8,128)S(1)} %get-tuple-element.49.g_ref, f32[512,128]{1,0:T(8,128)S(1)} %get-tuple-element.36.dinv_ref, f32[512,128]{1,0:T(8,128)S(1)} %get-tuple-element.45.outer_ref, bf16[256,256]{1,0:T(8,128)(2,1)S(1)} %copy-done.1, ...), custom_call_target="tpu_custom_call" | custom-call | tf_op jit(solution)/shard_map/pallas_call | solution.py:863
  41.8 2.7 %all-to-all-start.2 = ((f32[32,8,128]{2,1,0:T(8,128)}), f32[32,8,128]{2,1,0:T(8,128)S(1)}, u32[]{:S(2)}, u32[]{:S(2)}) async-start(f32[32,8,128]{2,1,0:T(8,128)} %get-tuple-element.55), calls=%async_computation.2 | async-start | bytes 262144 | tf_op jit(solution)/shard_map/all_to_all | solution.py:949
  44.5 1.6 %shard_map.156 = (f32[512,128]{1,0:T(8,128)S(1)}, f32[512,128]{1,0:T(8,128)S(1)}, f32[256,128]{1,0:T(8,128)S(1)}, f32[256,128]{1,0:T(8,128)S(1)}, f32[32,128]{1,0:T(8,128)S(1)}) custom-call(f32[256,128]{1,0:T(8,128)S(1)} %collective-permute-done.4.core_ref, f32[256,128]{1,0:T(8,128)S(1)} %collective-permute-done.5.chip_ref, ...), custom_call_target="tpu_custom_call" | custom-call | tf_op jit(solution)/shard_map/pallas_call | solution.py:863
  46.1 0.3 collective-permute-start.6
  46.4 1.6 %collective-permute-start.7 = (f32[256,128]{1,0:T(8,128)S(1)}, f32[256,128]{1,0:T(8,128)S(1)}, u32[]{:S(2)}, u32[]{:S(2)}) collective-permute-start(f32[256,128]{1,0:T(8,128)S(1)} %get-tuple-element.54), channel_id=1, source_target_pairs={{8,2},{2,8},{10,4},{4,10},{12,6},{6,12},{14,7},{7,14},{15,5},{5,15... | collective-permute-start | bytes 393224 | tf_op jit(solution)/shard_map/ppermute | solution.py:945
  48.0 1.5 %shard_map.158 = (f32[1536,128]{1,0:T(8,128)}, f32[8,128]{1,0:T(8,128)S(1)}) custom-call(f32[32,128]{1,0:T(8,128)S(1)} %get-tuple-element.61.points_ref), custom_call_target="tpu_custom_call" | custom-call | tf_op jit(solution)/shard_map/pallas_call | solution.py:863
  49.5 2.7 %all-to-all-done.2.loads_ref = f32[32,8,128]{2,1,0:T(8,128)S(1)} async-done(((f32[32,8,128]{2,1,0:T(8,128)}), f32[32,8,128]{2,1,0:T(8,128)S(1)}, u32[]{:S(2)}, u32[]{:S(2)}) %all-to-all-start.2) | async-done | bytes 131104 | tf_op jit(solution)/shard_map/all_to_all | solution.py:949
  52.3 1.6 %shard_map.157 = (f32[512,128]{1,0:T(8,128)S(1)}, f32[512,128]{1,0:T(8,128)S(1)}, f32[16,128]{1,0:T(8,128)S(1)}) custom-call(f32[32,8,128]{2,1,0:T(8,128)S(1)} %all-to-all-done.2.loads_ref, f32[512,128]{1,0:T(8,128)S(1)} %get-tuple-element.56.g_ref, f32[512,128]{1,0:T(8,128)S(1)} %get-tuple-element.57.x_ref, bf16[512,32]{1,0:T(8,128)(2,1)S(1)} %copy-done.6, ...), custom_call_target="tpu_custom_call" | custom-call | tf_op jit(solution)/shard_map/pallas_call | solution.py:863
  53.9 1.3 %shard_map.159 = f32[32,4,512]{2,1,0:T(4,128)S(1)} custom-call(f32[256,128]{1,0:T(8,128)S(1)} %collective-permute-done.6.core_ref, f32[256,128]{1,0:T(8,128)S(1)} %collective-permute-done.7.chip_ref, f32[512,128]{1,0:T(8,128)S(1)} %get-tuple-element.58.g_ref, f32[512,128]{1,0:T(8,128)S(1)} %get-tuple-element.59.x_ref, ...), custom_call_target="tpu_custom_call" | custom-call | tf_op jit(solution)/shard_map/pallas_call | solution.py:863
  55.2 13.1 %all_to_all.21.recv_ref = f32[32,4,512]{2,1,0:T(4,128)S(1)} all-to-all(f32[32,4,512]{2,1,0:T(4,128)S(1)} %shard_map.159), channel_id=1, replica_groups=mesh['ex'=4,'ey'=8] {'ex','ey'}, dimensions={0} | all-to-all | bytes 524288 | tf_op jit(solution)/shard_map/all_to_all | solution.py:1031
  68.3 0.9 %shard_map.160 = f32[512,128]{1,0:T(8,128)} custom-call(f32[32,4,512]{2,1,0:T(4,128)S(1)} %all_to_all.21.recv_ref), custom_call_target="tpu_custom_call" | custom-call | tf_op jit(solution)/shard_map/pallas_call | solution.py:863
  (22 shorter events, 0.1 us)
Async XLA Ops:
  2.0 17.8 %copy-start = (bf16[256,256]{1,0:T(8,128)(2,1)S(1)}, bf16[256,256]{1,0:T(8,128)(2,1)}, u32[]{:S(2)}) copy-start(bf16[256,256]{1,0:T(8,128)(2,1)} %constant.21.clone.low_ref.refs_1_) | copy-start | bytes 393220
  2.0 17.8 %copy-start.1 = (bf16[256,256]{1,0:T(8,128)(2,1)S(1)}, bf16[256,256]{1,0:T(8,128)(2,1)}, u32[]{:S(2)}) copy-start(bf16[256,256]{1,0:T(8,128)(2,1)} %constant.20.clone.high_ref.refs_0_) | copy-start | bytes 393220
  2.0 17.8 %copy-start.3 = (f32[64,128]{1,0:T(8,128)S(1)}, f32[64,128]{1,0:T(8,128)}, u32[]{:S(2)}) copy-start(f32[64,128]{1,0:T(8,128)} %constant.22.clone.along_ref.refs_2_) | copy-start | bytes 98308
  19.8 3.1 %copy-start.8 = (bf16[16,1024]{1,0:T(8,128)(2,1)S(1)}, bf16[16,1024]{1,0:T(8,128)(2,1)}, u32[]{:S(2)}) copy-start(bf16[16,1024]{1,0:T(8,128)(2,1)} %constant.25.clone.loads_ref) | copy-start | bytes 98308
  21.8 1.2 %copy-start.9 = (bf16[16,128]{1,0:T(8,128)(2,1)S(1)}, bf16[16,128]{1,0:T(8,128)(2,1)}, u32[]{:S(2)}) copy-start(bf16[16,128]{1,0:T(8,128)(2,1)} %constant.26.clone.near_ref) | copy-start | bytes 12292
  21.8 5.5 %collective-permute-start.1 = (f32[256,128]{1,0:T(8,128)S(1)}, f32[256,128]{1,0:T(8,128)S(1)}, u32[]{:S(2)}, u32[]{:S(2)}) collective-permute-start(f32[256,128]{1,0:T(8,128)S(1)} %get-tuple-element.33), channel_id=1, source_target_pairs={{8,2},{2,8},{10,4},{4,10},{12,6},{6,12},{14,7},{7,14},{15,5},{5,15... | collective-permute-start | bytes 393224 | tf_op jit(solution)/shard_map/ppermute | solution.py:945
  22.9 4.4 %collective-permute-start = (f32[256,128]{1,0:T(8,128)S(1)}, f32[256,128]{1,0:T(8,128)S(1)}, u32[]{:S(2)}, u32[]{:S(2)}) collective-permute-start(f32[256,128]{1,0:T(8,128)S(1)} %get-tuple-element.33), channel_id=1, source_target_pairs={{0,8},{8,0},{2,10},{10,2},{4,12},{12,4},{6,14},{14,6},{7,15},{15,7... | collective-permute-start | bytes 393224 | tf_op jit(solution)/shard_map/ppermute | solution.py:944
  24.2 10.8 %all-to-all-start.1 = ((f32[32,8,128]{2,1,0:T(8,128)}), f32[32,8,128]{2,1,0:T(8,128)S(1)}, u32[]{:S(2)}, u32[]{:S(2)}) async-start(f32[32,8,128]{2,1,0:T(8,128)} %get-tuple-element.40), calls=%async_computation.1 | async-start | bytes 262144 | tf_op jit(solution)/shard_map/all_to_all | solution.py:949
  27.2 7.7 %copy-start.2 = (bf16[512,32]{1,0:T(8,128)(2,1)S(1)}, bf16[512,32]{1,0:T(8,128)(2,1)}, u32[]{:S(2)}) copy-start(bf16[512,32]{1,0:T(8,128)(2,1)} %constant.28.clone.image_ref.refs_6_) | copy-start | bytes 98308
  27.3 7.7 %copy-start.6 = (bf16[512,32]{1,0:T(8,128)(2,1)S(1)}, bf16[512,32]{1,0:T(8,128)(2,1)}, u32[]{:S(2)}) copy-start(bf16[512,32]{1,0:T(8,128)(2,1)} %constant.27.clone.interp_ref) | copy-start | bytes 98308
  28.1 8.5 %collective-permute-start.2 = (f32[256,128]{1,0:T(8,128)S(1)}, f32[256,128]{1,0:T(8,128)S(1)}, u32[]{:S(2)}, u32[]{:S(2)}) collective-permute-start(f32[256,128]{1,0:T(8,128)S(1)} %get-tuple-element.38), channel_id=1, source_target_pairs={{0,8},{8,0},{2,10},{10,2},{4,12},{12,4},{6,14},{14,6},{7,15},{15,7... | collective-permute-start | bytes 393224 | tf_op jit(solution)/shard_map/ppermute | solution.py:944
  28.4 8.2 %collective-permute-start.3 = (f32[256,128]{1,0:T(8,128)S(1)}, f32[256,128]{1,0:T(8,128)S(1)}, u32[]{:S(2)}, u32[]{:S(2)}) collective-permute-start(f32[256,128]{1,0:T(8,128)S(1)} %get-tuple-element.39), channel_id=1, source_target_pairs={{8,2},{2,8},{10,4},{4,10},{12,6},{6,12},{14,7},{7,14},{15,5},{5,15... | collective-permute-start | bytes 393224 | tf_op jit(solution)/shard_map/ppermute | solution.py:945
  35.0 1.6 %copy-start.4 = (bf16[128,512]{1,0:T(8,128)(2,1)S(1)}, bf16[128,512]{1,0:T(8,128)(2,1)}, u32[]{:S(2)}) copy-start(bf16[128,512]{1,0:T(8,128)(2,1)} %constant.24.clone.refs_4_) | copy-start | bytes 393220
  35.0 1.6 %copy-start.5 = (bf16[128,512]{1,0:T(8,128)(2,1)S(1)}, bf16[128,512]{1,0:T(8,128)(2,1)}, u32[]{:S(2)}) copy-start(bf16[128,512]{1,0:T(8,128)(2,1)} %constant.23.clone.refs_3_) | copy-start | bytes 393220
  35.0 1.6 %copy-start.7 = (bf16[128,32]{1,0:T(8,128)(2,1)S(1)}, bf16[128,32]{1,0:T(8,128)(2,1)}, u32[]{:S(2)}) copy-start(bf16[128,32]{1,0:T(8,128)(2,1)} %constant.29.clone.refs_7_) | copy-start | bytes 24580
  38.5 6.0 %collective-permute-start.4 = (f32[256,128]{1,0:T(8,128)S(1)}, f32[256,128]{1,0:T(8,128)S(1)}, u32[]{:S(2)}, u32[]{:S(2)}) collective-permute-start(f32[256,128]{1,0:T(8,128)S(1)} %get-tuple-element.47), channel_id=1, source_target_pairs={{0,8},{8,0},{2,10},{10,2},{4,12},{12,4},{6,14},{14,6},{7,15},{15,7... | collective-permute-start | bytes 393224 | tf_op jit(solution)/shard_map/ppermute | solution.py:944
  38.6 5.9 %collective-permute-start.5 = (f32[256,128]{1,0:T(8,128)S(1)}, f32[256,128]{1,0:T(8,128)S(1)}, u32[]{:S(2)}, u32[]{:S(2)}) collective-permute-start(f32[256,128]{1,0:T(8,128)S(1)} %get-tuple-element.48), channel_id=1, source_target_pairs={{8,2},{2,8},{10,4},{4,10},{12,6},{6,12},{14,7},{7,14},{15,5},{5,15... | collective-permute-start | bytes 393224 | tf_op jit(solution)/shard_map/ppermute | solution.py:945
  41.8 10.5 %all-to-all-start.2 = ((f32[32,8,128]{2,1,0:T(8,128)}), f32[32,8,128]{2,1,0:T(8,128)S(1)}, u32[]{:S(2)}, u32[]{:S(2)}) async-start(f32[32,8,128]{2,1,0:T(8,128)} %get-tuple-element.55), calls=%async_computation.2 | async-start | bytes 262144 | tf_op jit(solution)/shard_map/all_to_all | solution.py:949
  46.1 7.8 %collective-permute-start.6 = (f32[256,128]{1,0:T(8,128)S(1)}, f32[256,128]{1,0:T(8,128)S(1)}, u32[]{:S(2)}, u32[]{:S(2)}) collective-permute-start(f32[256,128]{1,0:T(8,128)S(1)} %get-tuple-element.53), channel_id=1, source_target_pairs={{0,8},{8,0},{2,10},{10,2},{4,12},{12,4},{6,14},{14,6},{7,15},{15,7... | collective-permute-start | bytes 393224 | tf_op jit(solution)/shard_map/ppermute | solution.py:944
  46.4 7.4 %collective-permute-start.7 = (f32[256,128]{1,0:T(8,128)S(1)}, f32[256,128]{1,0:T(8,128)S(1)}, u32[]{:S(2)}, u32[]{:S(2)}) collective-permute-start(f32[256,128]{1,0:T(8,128)S(1)} %get-tuple-element.54), channel_id=1, source_target_pairs={{8,2},{2,8},{10,4},{4,10},{12,6},{6,12},{14,7},{7,14},{15,5},{5,15... | collective-permute-start | bytes 393224 | tf_op jit(solution)/shard_map/ppermute | solution.py:945

commit v12 on v11

--- a/solution.py
+++ b/solution.py
@@ -596,13 +596,16 @@
     low_ref,
     along_ref,
     token_ref,
+    points_ref,
     g_out,
     x_out,
     core_out,
     chip_out,
+    points_out,
     s_ref,
     u_ref,
 ):
+    points_out[...] = points_ref[...]
     assemble(lay, g_ref, s_ref, halo_of(lay, core_ref, chip_ref))
     update = OLD * x_ref[...] + NEW * dinv_ref[...] * s_ref[...]
     u_ref[...] = update
@@ -705,6 +708,7 @@
     x_ref,
     interp_ref,
     image_ref,
+    done_ref,
     g_out,
     x_out,
     around_ref,
@@ -747,17 +751,12 @@
     if kind != "inner":
         around_ref, image_ref, image_edge_ref = (refs.pop(0) for _ in range(3))
     if kind == "inner":
-        token_ref, points_ref = refs.pop(0), refs.pop(0)
-    if kind == "last":
         token_ref = refs.pop(0)
     if kind == "last":
         out_ref = refs.pop(0)
     else:
         g_out, x_out = refs.pop(0), refs.pop(0)
         core_out, chip_out = refs.pop(0), refs.pop(0)
-        if kind == "inner":
-            points_out = refs.pop(0)
-            points_out[...] = points_ref[...]
     s_ref, sh_ref, h_ref, u_ref = (refs.pop(0) for _ in range(4))
     if kind == "last":
         g_out = refs.pop(0)
@@ -973,11 +972,16 @@
         [fields],
     )
     loads = gather(loads)
-    g, x, core, chip = call(
+    g, x, core, chip, points = call(
         functools.partial(second_kernel, lay, one),
-        [fields, fields, layer, layer],
-        [*faces, g, x, dinv, high, low, along, token],
+        [fields, fields, layer, layer, table],
+        [*faces, g, x, dinv, high, low, along, token, points],
         [fields, fields],
+    )
+    forces, done = call(
+        functools.partial(forces_kernel, tiles_y, local_points),
+        [(3 * N**3, tiles_y * EZ), (N, 128)],
+        [points],
     )
     coarse = ((mass[0, 0], mass[0, 1]), (stiff[0, 0], stiff[0, 1]))
     stiffness = [high, low, along, edge_high, edge_low]
@@ -986,7 +990,6 @@
         core, chip = swap(core, chip)
         last = cycle + 1 == CYCLES
         outs = [fields, fields, layer, layer]
-        extra = [done] if last else []
         scratch = [fields] * 4
         if last:
             outs = [(lay.mesh_x * lay.mesh_y, block, N**3)]
@@ -994,13 +997,13 @@
         g, x, around = call(
             functools.partial(coarse_kernel, lay, *coarse),
             [fields, fields, (2 * N, width)],
-            [loads, g, x, prolong3, image3],
+            [loads, g, x, prolong3, image3, done],
             [(lay.slabs * 4, width)] + [(lay.slabs + 2 * N, width)] * 2,
         )
         outs = call(
             functools.partial(pair_kernel, lay, one, "last" if last else "plain"),
             outs,
-            [core, chip, g, x, dinv, outer, *stiffness, around, image3, image_edge, *extra],
+            [core, chip, g, x, dinv, outer, *stiffness, around, image3, image_edge],
             scratch,
         )
         if last:
@@ -1014,16 +1017,11 @@
             [fields] * 6,
         )
         loads = gather(loads)
-        g, x, core, chip, points = call(
+        g, x, core, chip = call(
             functools.partial(pair_kernel, lay, one, "inner"),
-            [fields, fields, layer, layer, table],
-            [*layers, g, x, dinv, outer, *stiffness, token, points],
+            [fields, fields, layer, layer],
+            [*layers, g, x, dinv, outer, *stiffness, token],
             [fields] * 4,
-        )
-        forces, done = call(
-            functools.partial(forces_kernel, tiles_y, local_points),
-            [(3 * N**3, tiles_y * EZ), (N, 128)],
-            [points],
         )
     (out,) = outs
     if not lay.joint:

time: 69.6 us -> 69.5 us (level)
  no operation moved by 1% of the time
where the time goes in v12:
time: 69.5 us; the launch traced here: 69 us
  blocking collectives  30.9 us (44%)
  Pallas kernels  17.7 us (25%)
  starting transfers between devices  11.8 us (17%)
  waiting for transfers between devices  7.72 us (11%)
  between operations  0.88 us (1%)
    all_to_all x1, blocking collectives, shards(): recv = lax.all_to_all(send, lay.axis, 0, 0)  17.8 us
    pallas_call x12, Pallas kernels, call(): pl.pallas_call(kernel, out_shape=shapes, in_specs=specs, out_specs=[pl.Bl...  17.7 us
    all_to_all x1, blocking collectives, shards(): out = lax.all_to_all(out, lay.axis, 0, 0)  13.1 us
    all_to_all x2, waiting for transfers between devices, gather(): return lax.all_to_all(loads, lay.axis, 0, 0)  7.7 us
    all_to_all x2, starting transfers between devices, gather(): return lax.all_to_all(loads, lay.axis, 0, 0)  5.51 us
    ppermute x4, starting transfers between devices, swap(): lax.ppermute(chip, lay.axis, lay.swaps(1))  5.43 us
  transfers between devices with their start and end apart: 10, of which 2 were waited for; matrix products, arithmetic and copies ran while one was open for 0% of the time, Pallas kernels for 15%

profile of v12, /device:TPU:0, one launch (start us, length us, event | category | flops | bytes accessed | tf_op | source)
XLA Modules:
  0.0 69.0 jit_solution(4387825303984786485)
XLA Ops:
  0.6 1.4 %shard_map.149 = f32[32,4,512]{2,1,0:T(4,128)S(1)} custom-call(s32[1,3]{1,0:T(1,128)} %bitcast.12, f32[1,3]{1,0:T(1,128)} %bitcast.13, f32[1,3]{1,0:T(1,128)} %bitcast.14, f32[512,128]{1,0:T(8,128)} %bitcast.10), custom_call_target="tpu_custom_call" | custom-call | tf_op jit(solution)/shard_map/pallas_call | solution.py:862
  2.0 0.0 copy-start
  2.0 0.0 copy-start.1
  2.0 17.8 %all_to_all.20.recv_ref = f32[32,4,512]{2,1,0:T(4,128)S(1)} all-to-all(f32[32,4,512]{2,1,0:T(4,128)S(1)} %shard_map.149), channel_id=1, replica_groups=mesh['ex'=4,'ey'=8] {'ex','ey'}, dimensions={0} | all-to-all | bytes 524288 | tf_op jit(solution)/shard_map/all_to_all | solution.py:937
  19.8 0.0 copy-start.8
  19.8 1.9 %shard_map.150 = (f32[512,128]{1,0:T(8,128)S(1)}, f32[512,128]{1,0:T(8,128)S(1)}, f32[512,128]{1,0:T(8,128)S(1)}, f32[512,128]{1,0:T(8,128)S(1)}, f32[256,128]{1,0:T(8,128)S(1)}, /*index=5*/f32[32,128]{1,0:T(8,128)S(1)}) custom-call(f32[32,4,512]{2,1,0:T(4,128)S(1)} %all_to_all.20.recv_ref, bf16[256,256]{1,0:T(8,128)(2,1)S(1)} %copy-done.1, ...), custom_call_target="tpu_custom_call" | custom-call | tf_op jit(solution)/shard_map/pallas_call | solution.py:862
  21.8 1.1 %collective-permute-start.1 = (f32[256,128]{1,0:T(8,128)S(1)}, f32[256,128]{1,0:T(8,128)S(1)}, u32[]{:S(2)}, u32[]{:S(2)}) collective-permute-start(f32[256,128]{1,0:T(8,128)S(1)} %get-tuple-element.33), channel_id=1, source_target_pairs={{8,2},{2,8},{10,4},{4,10},{12,6},{6,12},{14,7},{7,14},{15,5},{5,15... | collective-permute-start | bytes 393224 | tf_op jit(solution)/shard_map/ppermute | solution.py:944
  22.9 0.1 collective-permute-start
  22.9 1.3 %shard_map.151 = (f32[32,8,128]{2,1,0:T(8,128)}, f32[8,128]{1,0:T(8,128)S(1)}) custom-call(f32[512,128]{1,0:T(8,128)S(1)} %get-tuple-element.34.g_ref, f32[512,128]{1,0:T(8,128)S(1)} %get-tuple-element.35.x_ref, f32[512,128]{1,0:T(8,128)S(1)} %get-tuple-element.36.dinv_ref, bf16[16,1024]{1,0:T(8,128)(2,1)S(1)} %copy-done.8, bf16[16,128]{1,0:T(8,128)(2,1)S(1)} %copy-done.9), custom_call_target="tpu_custom_call" | custom-call | tf_op jit(solution)/shard_map/pallas_call | solution.py:862
  24.2 2.9 %all-to-all-start.1 = ((f32[32,8,128]{2,1,0:T(8,128)}), f32[32,8,128]{2,1,0:T(8,128)S(1)}, u32[]{:S(2)}, u32[]{:S(2)}) async-start(f32[32,8,128]{2,1,0:T(8,128)} %get-tuple-element.41), calls=%async_computation.1 | async-start | bytes 262144 | tf_op jit(solution)/shard_map/all_to_all | solution.py:948
  27.1 0.0 copy-start.2
  27.1 0.0 copy-start.6
  27.1 0.8 %shard_map.152 = (f32[512,128]{1,0:T(8,128)S(1)}, f32[512,128]{1,0:T(8,128)S(1)}, f32[256,128]{1,0:T(8,128)S(1)}, f32[256,128]{1,0:T(8,128)S(1)}, f32[32,128]{1,0:T(8,128)S(1)}) custom-call(f32[256,128]{1,0:T(8,128)S(1)} %collective-permute-done.core_ref, f32[256,128]{1,0:T(8,128)S(1)} %collective-permute-done.1.chip_ref, ...), custom_call_target="tpu_custom_call" | custom-call | tf_op jit(solution)/shard_map/pallas_call | solution.py:862
  27.9 0.3 collective-permute-start.2
  28.2 1.6 %collective-permute-start.3 = (f32[256,128]{1,0:T(8,128)S(1)}, f32[256,128]{1,0:T(8,128)S(1)}, u32[]{:S(2)}, u32[]{:S(2)}) collective-permute-start(f32[256,128]{1,0:T(8,128)S(1)} %get-tuple-element.40), channel_id=1, source_target_pairs={{8,2},{2,8},{10,4},{4,10},{12,6},{6,12},{14,7},{7,14},{15,5},{5,15... | collective-permute-start | bytes 393224 | tf_op jit(solution)/shard_map/ppermute | solution.py:944
  29.9 1.5 %shard_map.153 = (f32[1536,128]{1,0:T(8,128)}, f32[8,128]{1,0:T(8,128)S(1)}) custom-call(f32[32,128]{1,0:T(8,128)S(1)} %get-tuple-element.44.points_ref), custom_call_target="tpu_custom_call" | custom-call | tf_op jit(solution)/shard_map/pallas_call | solution.py:862
  31.4 3.5 %all-to-all-done.1.loads_ref = f32[32,8,128]{2,1,0:T(8,128)S(1)} async-done(((f32[32,8,128]{2,1,0:T(8,128)}), f32[32,8,128]{2,1,0:T(8,128)S(1)}, u32[]{:S(2)}, u32[]{:S(2)}) %all-to-all-start.1) | async-done | bytes 131104 | tf_op jit(solution)/shard_map/all_to_all | solution.py:948
  34.8 0.0 copy-start.7
  34.8 1.6 %shard_map.154 = (f32[512,128]{1,0:T(8,128)S(1)}, f32[512,128]{1,0:T(8,128)S(1)}, f32[16,128]{1,0:T(8,128)S(1)}) custom-call(f32[32,8,128]{2,1,0:T(8,128)S(1)} %all-to-all-done.1.loads_ref, f32[512,128]{1,0:T(8,128)S(1)} %get-tuple-element.42.g_ref, f32[512,128]{1,0:T(8,128)S(1)} %get-tuple-element.43.x_ref, bf16[512,32]{1,0:T(8,128)(2,1)S(1)} %copy-done.6, ...), custom_call_target="tpu_custom_call" | custom-call | tf_op jit(solution)/shard_map/pallas_call | solution.py:862
  36.5 1.8 %shard_map.155 = (f32[512,128]{1,0:T(8,128)S(1)}, f32[512,128]{1,0:T(8,128)S(1)}, f32[256,128]{1,0:T(8,128)S(1)}, f32[256,128]{1,0:T(8,128)S(1)}) custom-call(f32[256,128]{1,0:T(8,128)S(1)} %collective-permute-done.2.core_ref, f32[256,128]{1,0:T(8,128)S(1)} %collective-permute-done.3.chip_ref, f32[512,128]{1,0:T(8,128)S(1)} %get-tuple-element.46.g_ref, ...), custom_call_target="tpu_custom_call" | custom-call | tf_op jit(solution)/shard_map/pallas_call | solution.py:862
  38.3 0.2 collective-permute-start.4
  38.5 1.1 %collective-permute-start.5 = (f32[256,128]{1,0:T(8,128)S(1)}, f32[256,128]{1,0:T(8,128)S(1)}, u32[]{:S(2)}, u32[]{:S(2)}) collective-permute-start(f32[256,128]{1,0:T(8,128)S(1)} %get-tuple-element.51), channel_id=1, source_target_pairs={{8,2},{2,8},{10,4},{4,10},{12,6},{6,12},{14,7},{7,14},{15,5},{5,15... | collective-permute-start | bytes 393224 | tf_op jit(solution)/shard_map/ppermute | solution.py:944
  39.6 2.1 %shard_map.156 = (f32[32,8,128]{2,1,0:T(8,128)}, f32[8,128]{1,0:T(8,128)S(1)}) custom-call(f32[512,128]{1,0:T(8,128)S(1)} %get-tuple-element.52.g_ref, f32[512,128]{1,0:T(8,128)S(1)} %get-tuple-element.36.dinv_ref, f32[512,128]{1,0:T(8,128)S(1)} %get-tuple-element.48.outer_ref, bf16[256,256]{1,0:T(8,128)(2,1)S(1)} %copy-done.1, ...), custom_call_target="tpu_custom_call" | custom-call | tf_op jit(solution)/shard_map/pallas_call | solution.py:862
  41.7 2.6 %all-to-all-start.2 = ((f32[32,8,128]{2,1,0:T(8,128)}), f32[32,8,128]{2,1,0:T(8,128)S(1)}, u32[]{:S(2)}, u32[]{:S(2)}) async-start(f32[32,8,128]{2,1,0:T(8,128)} %get-tuple-element.57), calls=%async_computation.2 | async-start | bytes 262144 | tf_op jit(solution)/shard_map/all_to_all | solution.py:948
  44.3 1.6 %shard_map.157 = (f32[512,128]{1,0:T(8,128)S(1)}, f32[512,128]{1,0:T(8,128)S(1)}, f32[256,128]{1,0:T(8,128)S(1)}, f32[256,128]{1,0:T(8,128)S(1)}) custom-call(f32[256,128]{1,0:T(8,128)S(1)} %collective-permute-done.4.core_ref, f32[256,128]{1,0:T(8,128)S(1)} %collective-permute-done.5.chip_ref, f32[512,128]{1,0:T(8,128)S(1)} %get-tuple-element.52.g_ref, ...), custom_call_target="tpu_custom_call" | custom-call | tf_op jit(solution)/shard_map/pallas_call | solution.py:862
  45.9 0.3 collective-permute-start.6
  46.3 1.6 %collective-permute-start.7 = (f32[256,128]{1,0:T(8,128)S(1)}, f32[256,128]{1,0:T(8,128)S(1)}, u32[]{:S(2)}, u32[]{:S(2)}) collective-permute-start(f32[256,128]{1,0:T(8,128)S(1)} %get-tuple-element.56), channel_id=1, source_target_pairs={{8,2},{2,8},{10,4},{4,10},{12,6},{6,12},{14,7},{7,14},{15,5},{5,15... | collective-permute-start | bytes 393224 | tf_op jit(solution)/shard_map/ppermute | solution.py:944
  47.9 4.2 %all-to-all-done.2.loads_ref = f32[32,8,128]{2,1,0:T(8,128)S(1)} async-done(((f32[32,8,128]{2,1,0:T(8,128)}), f32[32,8,128]{2,1,0:T(8,128)S(1)}, u32[]{:S(2)}, u32[]{:S(2)}) %all-to-all-start.2) | async-done | bytes 131104 | tf_op jit(solution)/shard_map/all_to_all | solution.py:948
  52.1 1.6 %shard_map.158 = (f32[512,128]{1,0:T(8,128)S(1)}, f32[512,128]{1,0:T(8,128)S(1)}, f32[16,128]{1,0:T(8,128)S(1)}) custom-call(f32[32,8,128]{2,1,0:T(8,128)S(1)} %all-to-all-done.2.loads_ref, f32[512,128]{1,0:T(8,128)S(1)} %get-tuple-element.58.g_ref, f32[512,128]{1,0:T(8,128)S(1)} %get-tuple-element.59.x_ref, bf16[512,32]{1,0:T(8,128)(2,1)S(1)} %copy-done.6, ...), custom_call_target="tpu_custom_call" | custom-call | tf_op jit(solution)/shard_map/pallas_call | solution.py:862
  53.7 1.3 %shard_map.159 = f32[32,4,512]{2,1,0:T(4,128)S(1)} custom-call(f32[256,128]{1,0:T(8,128)S(1)} %collective-permute-done.6.core_ref, f32[256,128]{1,0:T(8,128)S(1)} %collective-permute-done.7.chip_ref, f32[512,128]{1,0:T(8,128)S(1)} %get-tuple-element.60.g_ref, f32[512,128]{1,0:T(8,128)S(1)} %get-tuple-element.61.x_ref, ...), custom_call_target="tpu_custom_call" | custom-call | tf_op jit(solution)/shard_map/pallas_call | solution.py:862
  55.0 13.1 %all_to_all.21.recv_ref = f32[32,4,512]{2,1,0:T(4,128)S(1)} all-to-all(f32[32,4,512]{2,1,0:T(4,128)S(1)} %shard_map.159), channel_id=1, replica_groups=mesh['ex'=4,'ey'=8] {'ex','ey'}, dimensions={0} | all-to-all | bytes 524288 | tf_op jit(solution)/shard_map/all_to_all | solution.py:1029
  68.2 0.9 %shard_map.160 = f32[512,128]{1,0:T(8,128)} custom-call(f32[32,4,512]{2,1,0:T(4,128)S(1)} %all_to_all.21.recv_ref), custom_call_target="tpu_custom_call" | custom-call | tf_op jit(solution)/shard_map/pallas_call | solution.py:862
  (22 shorter events, 0.1 us)
Async XLA Ops:
  2.0 17.8 %copy-start = (bf16[256,256]{1,0:T(8,128)(2,1)S(1)}, bf16[256,256]{1,0:T(8,128)(2,1)}, u32[]{:S(2)}) copy-start(bf16[256,256]{1,0:T(8,128)(2,1)} %constant.21.clone.low_ref.refs_1_) | copy-start | bytes 393220
  2.0 17.8 %copy-start.1 = (bf16[256,256]{1,0:T(8,128)(2,1)S(1)}, bf16[256,256]{1,0:T(8,128)(2,1)}, u32[]{:S(2)}) copy-start(bf16[256,256]{1,0:T(8,128)(2,1)} %constant.20.clone.high_ref.refs_0_) | copy-start | bytes 393220
  2.0 17.8 %copy-start.3 = (f32[64,128]{1,0:T(8,128)S(1)}, f32[64,128]{1,0:T(8,128)}, u32[]{:S(2)}) copy-start(f32[64,128]{1,0:T(8,128)} %constant.22.clone.along_ref.refs_2_) | copy-start | bytes 98308
  19.8 3.1 %copy-start.8 = (bf16[16,1024]{1,0:T(8,128)(2,1)S(1)}, bf16[16,1024]{1,0:T(8,128)(2,1)}, u32[]{:S(2)}) copy-start(bf16[16,1024]{1,0:T(8,128)(2,1)} %constant.25.clone.loads_ref) | copy-start | bytes 98308
  21.8 1.2 %copy-start.9 = (bf16[16,128]{1,0:T(8,128)(2,1)S(1)}, bf16[16,128]{1,0:T(8,128)(2,1)}, u32[]{:S(2)}) copy-start(bf16[16,128]{1,0:T(8,128)(2,1)} %constant.26.clone.near_ref) | copy-start | bytes 12292
  21.8 5.3 %collective-permute-start.1 = (f32[256,128]{1,0:T(8,128)S(1)}, f32[256,128]{1,0:T(8,128)S(1)}, u32[]{:S(2)}, u32[]{:S(2)}) collective-permute-start(f32[256,128]{1,0:T(8,128)S(1)} %get-tuple-element.33), channel_id=1, source_target_pairs={{8,2},{2,8},{10,4},{4,10},{12,6},{6,12},{14,7},{7,14},{15,5},{5,15... | collective-permute-start | bytes 393224 | tf_op jit(solution)/shard_map/ppermute | solution.py:944
  22.9 4.2 %collective-permute-start = (f32[256,128]{1,0:T(8,128)S(1)}, f32[256,128]{1,0:T(8,128)S(1)}, u32[]{:S(2)}, u32[]{:S(2)}) collective-permute-start(f32[256,128]{1,0:T(8,128)S(1)} %get-tuple-element.33), channel_id=1, source_target_pairs={{0,8},{8,0},{2,10},{10,2},{4,12},{12,4},{6,14},{14,6},{7,15},{15,7... | collective-permute-start | bytes 393224 | tf_op jit(solution)/shard_map/ppermute | solution.py:943
  24.2 10.6 %all-to-all-start.1 = ((f32[32,8,128]{2,1,0:T(8,128)}), f32[32,8,128]{2,1,0:T(8,128)S(1)}, u32[]{:S(2)}, u32[]{:S(2)}) async-start(f32[32,8,128]{2,1,0:T(8,128)} %get-tuple-element.41), calls=%async_computation.1 | async-start | bytes 262144 | tf_op jit(solution)/shard_map/all_to_all | solution.py:948
  27.1 7.7 %copy-start.2 = (bf16[512,32]{1,0:T(8,128)(2,1)S(1)}, bf16[512,32]{1,0:T(8,128)(2,1)}, u32[]{:S(2)}) copy-start(bf16[512,32]{1,0:T(8,128)(2,1)} %constant.28.clone.image_ref.refs_6_) | copy-start | bytes 98308
  27.1 7.7 %copy-start.6 = (bf16[512,32]{1,0:T(8,128)(2,1)S(1)}, bf16[512,32]{1,0:T(8,128)(2,1)}, u32[]{:S(2)}) copy-start(bf16[512,32]{1,0:T(8,128)(2,1)} %constant.27.clone.interp_ref) | copy-start | bytes 98308
  27.9 8.5 %collective-permute-start.2 = (f32[256,128]{1,0:T(8,128)S(1)}, f32[256,128]{1,0:T(8,128)S(1)}, u32[]{:S(2)}, u32[]{:S(2)}) collective-permute-start(f32[256,128]{1,0:T(8,128)S(1)} %get-tuple-element.39), channel_id=1, source_target_pairs={{0,8},{8,0},{2,10},{10,2},{4,12},{12,4},{6,14},{14,6},{7,15},{15,7... | collective-permute-start | bytes 393224 | tf_op jit(solution)/shard_map/ppermute | solution.py:943
  28.2 8.2 %collective-permute-start.3 = (f32[256,128]{1,0:T(8,128)S(1)}, f32[256,128]{1,0:T(8,128)S(1)}, u32[]{:S(2)}, u32[]{:S(2)}) collective-permute-start(f32[256,128]{1,0:T(8,128)S(1)} %get-tuple-element.40), channel_id=1, source_target_pairs={{8,2},{2,8},{10,4},{4,10},{12,6},{6,12},{14,7},{7,14},{15,5},{5,15... | collective-permute-start | bytes 393224 | tf_op jit(solution)/shard_map/ppermute | solution.py:944
  34.8 1.6 %copy-start.4 = (bf16[128,512]{1,0:T(8,128)(2,1)S(1)}, bf16[128,512]{1,0:T(8,128)(2,1)}, u32[]{:S(2)}) copy-start(bf16[128,512]{1,0:T(8,128)(2,1)} %constant.24.clone.refs_4_) | copy-start | bytes 393220
  34.8 1.6 %copy-start.5 = (bf16[128,512]{1,0:T(8,128)(2,1)S(1)}, bf16[128,512]{1,0:T(8,128)(2,1)}, u32[]{:S(2)}) copy-start(bf16[128,512]{1,0:T(8,128)(2,1)} %constant.23.clone.refs_3_) | copy-start | bytes 393220
  34.8 1.6 %copy-start.7 = (bf16[128,32]{1,0:T(8,128)(2,1)S(1)}, bf16[128,32]{1,0:T(8,128)(2,1)}, u32[]{:S(2)}) copy-start(bf16[128,32]{1,0:T(8,128)(2,1)} %constant.29.clone.refs_7_) | copy-start | bytes 24580
  38.3 6.0 %collective-permute-start.4 = (f32[256,128]{1,0:T(8,128)S(1)}, f32[256,128]{1,0:T(8,128)S(1)}, u32[]{:S(2)}, u32[]{:S(2)}) collective-permute-start(f32[256,128]{1,0:T(8,128)S(1)} %get-tuple-element.50), channel_id=1, source_target_pairs={{0,8},{8,0},{2,10},{10,2},{4,12},{12,4},{6,14},{14,6},{7,15},{15,7... | collective-permute-start | bytes 393224 | tf_op jit(solution)/shard_map/ppermute | solution.py:943
  38.5 5.8 %collective-permute-start.5 = (f32[256,128]{1,0:T(8,128)S(1)}, f32[256,128]{1,0:T(8,128)S(1)}, u32[]{:S(2)}, u32[]{:S(2)}) collective-permute-start(f32[256,128]{1,0:T(8,128)S(1)} %get-tuple-element.51), channel_id=1, source_target_pairs={{8,2},{2,8},{10,4},{4,10},{12,6},{6,12},{14,7},{7,14},{15,5},{5,15... | collective-permute-start | bytes 393224 | tf_op jit(solution)/shard_map/ppermute | solution.py:944
  41.7 10.5 %all-to-all-start.2 = ((f32[32,8,128]{2,1,0:T(8,128)}), f32[32,8,128]{2,1,0:T(8,128)S(1)}, u32[]{:S(2)}, u32[]{:S(2)}) async-start(f32[32,8,128]{2,1,0:T(8,128)} %get-tuple-element.57), calls=%async_computation.2 | async-start | bytes 262144 | tf_op jit(solution)/shard_map/all_to_all | solution.py:948
  45.9 7.8 %collective-permute-start.6 = (f32[256,128]{1,0:T(8,128)S(1)}, f32[256,128]{1,0:T(8,128)S(1)}, u32[]{:S(2)}, u32[]{:S(2)}) collective-permute-start(f32[256,128]{1,0:T(8,128)S(1)} %get-tuple-element.55), channel_id=1, source_target_pairs={{0,8},{8,0},{2,10},{10,2},{4,12},{12,4},{6,14},{14,6},{7,15},{15,7... | collective-permute-start | bytes 393224 | tf_op jit(solution)/shard_map/ppermute | solution.py:943
  46.3 7.4 %collective-permute-start.7 = (f32[256,128]{1,0:T(8,128)S(1)}, f32[256,128]{1,0:T(8,128)S(1)}, u32[]{:S(2)}, u32[]{:S(2)}) collective-permute-start(f32[256,128]{1,0:T(8,128)S(1)} %get-tuple-element.56), channel_id=1, source_target_pairs={{8,2},{2,8},{10,4},{4,10},{12,6},{6,12},{14,7},{7,14},{15,5},{5,15... | collective-permute-start | bytes 393224 | tf_op jit(solution)/shard_map/ppermute | solution.py:944

commit v13 on v12

--- a/solution.py
+++ b/solution.py
@@ -118,7 +118,9 @@
 def times3(high, low, x):
     xh, xl = split(x)
     dot = functools.partial(jnp.dot, preferred_element_type=F32)
-    return dot(high, xh) + dot(high, xl) + dot(low, xh)
+    width = x.shape[1]
+    both = dot(high, jnp.concatenate([xh, xl], 1))
+    return both[:, :width] + both[:, width:] + dot(low, xh)
 
 
 def split_table(x):

time: 69.5 us -> 69.4 us (level)
  no operation moved by 1% of the time
where the time goes in v13:
time: 69.4 us; the launch traced here: 69.1 us
  blocking collectives  30.9 us (45%)
  Pallas kernels  17.6 us (25%)
  starting transfers between devices  11.9 us (17%)
  waiting for transfers between devices  7.67 us (11%)
  between operations  0.88 us (1%)
    all_to_all x1, blocking collectives, shards(): recv = lax.all_to_all(send, lay.axis, 0, 0)  17.8 us
    pallas_call x12, Pallas kernels, call(): pl.pallas_call(kernel, out_shape=shapes, in_specs=specs, out_specs=[pl.Bl...  17.6 us
    all_to_all x1, blocking collectives, shards(): out = lax.all_to_all(out, lay.axis, 0, 0)  13.2 us
    all_to_all x2, waiting for transfers between devices, gather(): return lax.all_to_all(loads, lay.axis, 0, 0)  7.65 us
    ppermute x4, starting transfers between devices, swap(): lax.ppermute(chip, lay.axis, lay.swaps(1))  5.43 us
    all_to_all x2, starting transfers between devices, gather(): return lax.all_to_all(loads, lay.axis, 0, 0)  5.36 us
  transfers between devices with their start and end apart: 10, of which 2 were waited for; matrix products, arithmetic and copies ran while one was open for 0% of the time, Pallas kernels for 15%

profile of v13, /device:TPU:0, one launch (start us, length us, event | category | flops | bytes accessed | tf_op | source)
XLA Modules:
  0.0 69.1 jit_solution(3059934435849381857)
XLA Ops:
  0.6 1.4 %shard_map.149 = f32[32,4,512]{2,1,0:T(4,128)S(1)} custom-call(s32[1,3]{1,0:T(1,128)} %bitcast.12, f32[1,3]{1,0:T(1,128)} %bitcast.13, f32[1,3]{1,0:T(1,128)} %bitcast.14, f32[512,128]{1,0:T(8,128)} %bitcast.10), custom_call_target="tpu_custom_call" | custom-call | tf_op jit(solution)/shard_map/pallas_call | solution.py:864
  2.0 0.0 copy-start
  2.0 0.0 copy-start.1
  2.0 0.0 copy-start.3
  2.0 17.8 %all_to_all.20.recv_ref = f32[32,4,512]{2,1,0:T(4,128)S(1)} all-to-all(f32[32,4,512]{2,1,0:T(4,128)S(1)} %shard_map.149), channel_id=1, replica_groups=mesh['ex'=4,'ey'=8] {'ex','ey'}, dimensions={0} | all-to-all | bytes 524288 | tf_op jit(solution)/shard_map/all_to_all | solution.py:939
  19.8 0.0 copy-start.8
  19.8 1.9 %shard_map.150 = (f32[512,128]{1,0:T(8,128)S(1)}, f32[512,128]{1,0:T(8,128)S(1)}, f32[512,128]{1,0:T(8,128)S(1)}, f32[512,128]{1,0:T(8,128)S(1)}, f32[256,128]{1,0:T(8,128)S(1)}, /*index=5*/f32[32,128]{1,0:T(8,128)S(1)}) custom-call(f32[32,4,512]{2,1,0:T(4,128)S(1)} %all_to_all.20.recv_ref, bf16[256,256]{1,0:T(8,128)(2,1)S(1)} %copy-done.1, ...), custom_call_target="tpu_custom_call" | custom-call | tf_op jit(solution)/shard_map/pallas_call | solution.py:864
  21.8 1.1 %collective-permute-start.1 = (f32[256,128]{1,0:T(8,128)S(1)}, f32[256,128]{1,0:T(8,128)S(1)}, u32[]{:S(2)}, u32[]{:S(2)}) collective-permute-start(f32[256,128]{1,0:T(8,128)S(1)} %get-tuple-element.33), channel_id=1, source_target_pairs={{8,2},{2,8},{10,4},{4,10},{12,6},{6,12},{14,7},{7,14},{15,5},{5,15... | collective-permute-start | bytes 393224 | tf_op jit(solution)/shard_map/ppermute | solution.py:946
  22.9 0.4 collective-permute-start
  23.2 1.3 %shard_map.151 = (f32[32,8,128]{2,1,0:T(8,128)}, f32[8,128]{1,0:T(8,128)S(1)}) custom-call(f32[512,128]{1,0:T(8,128)S(1)} %get-tuple-element.34.g_ref, f32[512,128]{1,0:T(8,128)S(1)} %get-tuple-element.35.x_ref, f32[512,128]{1,0:T(8,128)S(1)} %get-tuple-element.36.dinv_ref, bf16[16,1024]{1,0:T(8,128)(2,1)S(1)} %copy-done.8, bf16[16,128]{1,0:T(8,128)(2,1)S(1)} %copy-done.9), custom_call_target="tpu_custom_call" | custom-call | tf_op jit(solution)/shard_map/pallas_call | solution.py:864
  24.5 2.7 %all-to-all-start.1 = ((f32[32,8,128]{2,1,0:T(8,128)}), f32[32,8,128]{2,1,0:T(8,128)S(1)}, u32[]{:S(2)}, u32[]{:S(2)}) async-start(f32[32,8,128]{2,1,0:T(8,128)} %get-tuple-element.41), calls=%async_computation.1 | async-start | bytes 262144 | tf_op jit(solution)/shard_map/all_to_all | solution.py:950
  27.3 0.0 copy-start.6
  27.3 0.8 %shard_map.152 = (f32[512,128]{1,0:T(8,128)S(1)}, f32[512,128]{1,0:T(8,128)S(1)}, f32[256,128]{1,0:T(8,128)S(1)}, f32[256,128]{1,0:T(8,128)S(1)}, f32[32,128]{1,0:T(8,128)S(1)}) custom-call(f32[256,128]{1,0:T(8,128)S(1)} %collective-permute-done.core_ref, f32[256,128]{1,0:T(8,128)S(1)} %collective-permute-done.1.chip_ref, ...), custom_call_target="tpu_custom_call" | custom-call | tf_op jit(solution)/shard_map/pallas_call | solution.py:864
  28.1 0.3 collective-permute-start.2
  28.4 1.6 %collective-permute-start.3 = (f32[256,128]{1,0:T(8,128)S(1)}, f32[256,128]{1,0:T(8,128)S(1)}, u32[]{:S(2)}, u32[]{:S(2)}) collective-permute-start(f32[256,128]{1,0:T(8,128)S(1)} %get-tuple-element.40), channel_id=1, source_target_pairs={{8,2},{2,8},{10,4},{4,10},{12,6},{6,12},{14,7},{7,14},{15,5},{5,15... | collective-permute-start | bytes 393224 | tf_op jit(solution)/shard_map/ppermute | solution.py:946
  30.0 1.5 %shard_map.153 = (f32[1536,128]{1,0:T(8,128)}, f32[8,128]{1,0:T(8,128)S(1)}) custom-call(f32[32,128]{1,0:T(8,128)S(1)} %get-tuple-element.44.points_ref), custom_call_target="tpu_custom_call" | custom-call | tf_op jit(solution)/shard_map/pallas_call | solution.py:864
  31.5 3.5 %all-to-all-done.1.loads_ref = f32[32,8,128]{2,1,0:T(8,128)S(1)} async-done(((f32[32,8,128]{2,1,0:T(8,128)}), f32[32,8,128]{2,1,0:T(8,128)S(1)}, u32[]{:S(2)}, u32[]{:S(2)}) %all-to-all-start.1) | async-done | bytes 131104 | tf_op jit(solution)/shard_map/all_to_all | solution.py:950
  35.0 0.0 copy-start.7
  35.0 1.6 %shard_map.154 = (f32[512,128]{1,0:T(8,128)S(1)}, f32[512,128]{1,0:T(8,128)S(1)}, f32[16,128]{1,0:T(8,128)S(1)}) custom-call(f32[32,8,128]{2,1,0:T(8,128)S(1)} %all-to-all-done.1.loads_ref, f32[512,128]{1,0:T(8,128)S(1)} %get-tuple-element.42.g_ref, f32[512,128]{1,0:T(8,128)S(1)} %get-tuple-element.43.x_ref, bf16[512,32]{1,0:T(8,128)(2,1)S(1)} %copy-done.6, ...), custom_call_target="tpu_custom_call" | custom-call | tf_op jit(solution)/shard_map/pallas_call | solution.py:864
  36.6 1.7 %shard_map.155 = (f32[512,128]{1,0:T(8,128)S(1)}, f32[512,128]{1,0:T(8,128)S(1)}, f32[256,128]{1,0:T(8,128)S(1)}, f32[256,128]{1,0:T(8,128)S(1)}) custom-call(f32[256,128]{1,0:T(8,128)S(1)} %collective-permute-done.2.core_ref, f32[256,128]{1,0:T(8,128)S(1)} %collective-permute-done.3.chip_ref, f32[512,128]{1,0:T(8,128)S(1)} %get-tuple-element.46.g_ref, ...), custom_call_target="tpu_custom_call" | custom-call | tf_op jit(solution)/shard_map/pallas_call | solution.py:864
  38.4 0.2 collective-permute-start.4
  38.5 1.1 %collective-permute-start.5 = (f32[256,128]{1,0:T(8,128)S(1)}, f32[256,128]{1,0:T(8,128)S(1)}, u32[]{:S(2)}, u32[]{:S(2)}) collective-permute-start(f32[256,128]{1,0:T(8,128)S(1)} %get-tuple-element.51), channel_id=1, source_target_pairs={{8,2},{2,8},{10,4},{4,10},{12,6},{6,12},{14,7},{7,14},{15,5},{5,15... | collective-permute-start | bytes 393224 | tf_op jit(solution)/shard_map/ppermute | solution.py:946
  39.6 2.1 %shard_map.156 = (f32[32,8,128]{2,1,0:T(8,128)}, f32[8,128]{1,0:T(8,128)S(1)}) custom-call(f32[512,128]{1,0:T(8,128)S(1)} %get-tuple-element.52.g_ref, f32[512,128]{1,0:T(8,128)S(1)} %get-tuple-element.36.dinv_ref, f32[512,128]{1,0:T(8,128)S(1)} %get-tuple-element.48.outer_ref, bf16[256,256]{1,0:T(8,128)(2,1)S(1)} %copy-done.1, ...), custom_call_target="tpu_custom_call" | custom-call | tf_op jit(solution)/shard_map/pallas_call | solution.py:864
  41.7 2.6 %all-to-all-start.2 = ((f32[32,8,128]{2,1,0:T(8,128)}), f32[32,8,128]{2,1,0:T(8,128)S(1)}, u32[]{:S(2)}, u32[]{:S(2)}) async-start(f32[32,8,128]{2,1,0:T(8,128)} %get-tuple-element.57), calls=%async_computation.2 | async-start | bytes 262144 | tf_op jit(solution)/shard_map/all_to_all | solution.py:950
  44.4 1.7 %shard_map.157 = (f32[512,128]{1,0:T(8,128)S(1)}, f32[512,128]{1,0:T(8,128)S(1)}, f32[256,128]{1,0:T(8,128)S(1)}, f32[256,128]{1,0:T(8,128)S(1)}) custom-call(f32[256,128]{1,0:T(8,128)S(1)} %collective-permute-done.4.core_ref, f32[256,128]{1,0:T(8,128)S(1)} %collective-permute-done.5.chip_ref, f32[512,128]{1,0:T(8,128)S(1)} %get-tuple-element.52.g_ref, ...), custom_call_target="tpu_custom_call" | custom-call | tf_op jit(solution)/shard_map/pallas_call | solution.py:864
  46.0 0.3 collective-permute-start.6
  46.4 1.6 %collective-permute-start.7 = (f32[256,128]{1,0:T(8,128)S(1)}, f32[256,128]{1,0:T(8,128)S(1)}, u32[]{:S(2)}, u32[]{:S(2)}) collective-permute-start(f32[256,128]{1,0:T(8,128)S(1)} %get-tuple-element.56), channel_id=1, source_target_pairs={{8,2},{2,8},{10,4},{4,10},{12,6},{6,12},{14,7},{7,14},{15,5},{5,15... | collective-permute-start | bytes 393224 | tf_op jit(solution)/shard_map/ppermute | solution.py:946
  48.0 4.2 %all-to-all-done.2.loads_ref = f32[32,8,128]{2,1,0:T(8,128)S(1)} async-done(((f32[32,8,128]{2,1,0:T(8,128)}), f32[32,8,128]{2,1,0:T(8,128)S(1)}, u32[]{:S(2)}, u32[]{:S(2)}) %all-to-all-start.2) | async-done | bytes 131104 | tf_op jit(solution)/shard_map/all_to_all | solution.py:950
  52.2 1.6 %shard_map.158 = (f32[512,128]{1,0:T(8,128)S(1)}, f32[512,128]{1,0:T(8,128)S(1)}, f32[16,128]{1,0:T(8,128)S(1)}) custom-call(f32[32,8,128]{2,1,0:T(8,128)S(1)} %all-to-all-done.2.loads_ref, f32[512,128]{1,0:T(8,128)S(1)} %get-tuple-element.58.g_ref, f32[512,128]{1,0:T(8,128)S(1)} %get-tuple-element.59.x_ref, bf16[512,32]{1,0:T(8,128)(2,1)S(1)} %copy-done.6, ...), custom_call_target="tpu_custom_call" | custom-call | tf_op jit(solution)/shard_map/pallas_call | solution.py:864
  53.8 1.3 %shard_map.159 = f32[32,4,512]{2,1,0:T(4,128)S(1)} custom-call(f32[256,128]{1,0:T(8,128)S(1)} %collective-permute-done.6.core_ref, f32[256,128]{1,0:T(8,128)S(1)} %collective-permute-done.7.chip_ref, f32[512,128]{1,0:T(8,128)S(1)} %get-tuple-element.60.g_ref, f32[512,128]{1,0:T(8,128)S(1)} %get-tuple-element.61.x_ref, ...), custom_call_target="tpu_custom_call" | custom-call | tf_op jit(solution)/shard_map/pallas_call | solution.py:864
  55.0 13.2 %all_to_all.21.recv_ref = f32[32,4,512]{2,1,0:T(4,128)S(1)} all-to-all(f32[32,4,512]{2,1,0:T(4,128)S(1)} %shard_map.159), channel_id=1, replica_groups=mesh['ex'=4,'ey'=8] {'ex','ey'}, dimensions={0} | all-to-all | bytes 524288 | tf_op jit(solution)/shard_map/all_to_all | solution.py:1031
  68.2 0.9 %shard_map.160 = f32[512,128]{1,0:T(8,128)} custom-call(f32[32,4,512]{2,1,0:T(4,128)S(1)} %all_to_all.21.recv_ref), custom_call_target="tpu_custom_call" | custom-call | tf_op jit(solution)/shard_map/pallas_call | solution.py:864
  (22 shorter events, 0.1 us)
Async XLA Ops:
  2.0 17.8 %copy-start = (bf16[256,256]{1,0:T(8,128)(2,1)S(1)}, bf16[256,256]{1,0:T(8,128)(2,1)}, u32[]{:S(2)}) copy-start(bf16[256,256]{1,0:T(8,128)(2,1)} %constant.21.clone.low_ref.refs_1_) | copy-start | bytes 393220
  2.0 17.8 %copy-start.1 = (bf16[256,256]{1,0:T(8,128)(2,1)S(1)}, bf16[256,256]{1,0:T(8,128)(2,1)}, u32[]{:S(2)}) copy-start(bf16[256,256]{1,0:T(8,128)(2,1)} %constant.20.clone.high_ref.refs_0_) | copy-start | bytes 393220
  2.0 17.8 %copy-start.3 = (f32[64,128]{1,0:T(8,128)S(1)}, f32[64,128]{1,0:T(8,128)}, u32[]{:S(2)}) copy-start(f32[64,128]{1,0:T(8,128)} %constant.22.clone.along_ref.refs_2_) | copy-start | bytes 98308
  19.8 3.4 %copy-start.8 = (bf16[16,1024]{1,0:T(8,128)(2,1)S(1)}, bf16[16,1024]{1,0:T(8,128)(2,1)}, u32[]{:S(2)}) copy-start(bf16[16,1024]{1,0:T(8,128)(2,1)} %constant.25.clone.loads_ref) | copy-start | bytes 98308
  21.8 1.5 %copy-start.9 = (bf16[16,128]{1,0:T(8,128)(2,1)S(1)}, bf16[16,128]{1,0:T(8,128)(2,1)}, u32[]{:S(2)}) copy-start(bf16[16,128]{1,0:T(8,128)(2,1)} %constant.26.clone.near_ref) | copy-start | bytes 12292
  21.8 5.5 %collective-permute-start.1 = (f32[256,128]{1,0:T(8,128)S(1)}, f32[256,128]{1,0:T(8,128)S(1)}, u32[]{:S(2)}, u32[]{:S(2)}) collective-permute-start(f32[256,128]{1,0:T(8,128)S(1)} %get-tuple-element.33), channel_id=1, source_target_pairs={{8,2},{2,8},{10,4},{4,10},{12,6},{6,12},{14,7},{7,14},{15,5},{5,15... | collective-permute-start | bytes 393224 | tf_op jit(solution)/shard_map/ppermute | solution.py:946
  22.9 4.4 %collective-permute-start = (f32[256,128]{1,0:T(8,128)S(1)}, f32[256,128]{1,0:T(8,128)S(1)}, u32[]{:S(2)}, u32[]{:S(2)}) collective-permute-start(f32[256,128]{1,0:T(8,128)S(1)} %get-tuple-element.33), channel_id=1, source_target_pairs={{0,8},{8,0},{2,10},{10,2},{4,12},{12,4},{6,14},{14,6},{7,15},{15,7... | collective-permute-start | bytes 393224 | tf_op jit(solution)/shard_map/ppermute | solution.py:945
  24.5 10.5 %all-to-all-start.1 = ((f32[32,8,128]{2,1,0:T(8,128)}), f32[32,8,128]{2,1,0:T(8,128)S(1)}, u32[]{:S(2)}, u32[]{:S(2)}) async-start(f32[32,8,128]{2,1,0:T(8,128)} %get-tuple-element.41), calls=%async_computation.1 | async-start | bytes 262144 | tf_op jit(solution)/shard_map/all_to_all | solution.py:950
  27.2 7.7 %copy-start.2 = (bf16[512,32]{1,0:T(8,128)(2,1)S(1)}, bf16[512,32]{1,0:T(8,128)(2,1)}, u32[]{:S(2)}) copy-start(bf16[512,32]{1,0:T(8,128)(2,1)} %constant.28.clone.image_ref.refs_6_) | copy-start | bytes 98308
  27.3 7.7 %copy-start.6 = (bf16[512,32]{1,0:T(8,128)(2,1)S(1)}, bf16[512,32]{1,0:T(8,128)(2,1)}, u32[]{:S(2)}) copy-start(bf16[512,32]{1,0:T(8,128)(2,1)} %constant.27.clone.interp_ref) | copy-start | bytes 98308
  28.1 8.5 %collective-permute-start.2 = (f32[256,128]{1,0:T(8,128)S(1)}, f32[256,128]{1,0:T(8,128)S(1)}, u32[]{:S(2)}, u32[]{:S(2)}) collective-permute-start(f32[256,128]{1,0:T(8,128)S(1)} %get-tuple-element.39), channel_id=1, source_target_pairs={{0,8},{8,0},{2,10},{10,2},{4,12},{12,4},{6,14},{14,6},{7,15},{15,7... | collective-permute-start | bytes 393224 | tf_op jit(solution)/shard_map/ppermute | solution.py:945
  28.4 8.2 %collective-permute-start.3 = (f32[256,128]{1,0:T(8,128)S(1)}, f32[256,128]{1,0:T(8,128)S(1)}, u32[]{:S(2)}, u32[]{:S(2)}) collective-permute-start(f32[256,128]{1,0:T(8,128)S(1)} %get-tuple-element.40), channel_id=1, source_target_pairs={{8,2},{2,8},{10,4},{4,10},{12,6},{6,12},{14,7},{7,14},{15,5},{5,15... | collective-permute-start | bytes 393224 | tf_op jit(solution)/shard_map/ppermute | solution.py:946
  35.0 1.6 %copy-start.4 = (bf16[128,512]{1,0:T(8,128)(2,1)S(1)}, bf16[128,512]{1,0:T(8,128)(2,1)}, u32[]{:S(2)}) copy-start(bf16[128,512]{1,0:T(8,128)(2,1)} %constant.24.clone.refs_4_) | copy-start | bytes 393220
  35.0 1.6 %copy-start.5 = (bf16[128,512]{1,0:T(8,128)(2,1)S(1)}, bf16[128,512]{1,0:T(8,128)(2,1)}, u32[]{:S(2)}) copy-start(bf16[128,512]{1,0:T(8,128)(2,1)} %constant.23.clone.refs_3_) | copy-start | bytes 393220
  35.0 1.6 %copy-start.7 = (bf16[128,32]{1,0:T(8,128)(2,1)S(1)}, bf16[128,32]{1,0:T(8,128)(2,1)}, u32[]{:S(2)}) copy-start(bf16[128,32]{1,0:T(8,128)(2,1)} %constant.29.clone.refs_7_) | copy-start | bytes 24580
  38.4 6.0 %collective-permute-start.4 = (f32[256,128]{1,0:T(8,128)S(1)}, f32[256,128]{1,0:T(8,128)S(1)}, u32[]{:S(2)}, u32[]{:S(2)}) collective-permute-start(f32[256,128]{1,0:T(8,128)S(1)} %get-tuple-element.50), channel_id=1, source_target_pairs={{0,8},{8,0},{2,10},{10,2},{4,12},{12,4},{6,14},{14,6},{7,15},{15,7... | collective-permute-start | bytes 393224 | tf_op jit(solution)/shard_map/ppermute | solution.py:945
  38.5 5.8 %collective-permute-start.5 = (f32[256,128]{1,0:T(8,128)S(1)}, f32[256,128]{1,0:T(8,128)S(1)}, u32[]{:S(2)}, u32[]{:S(2)}) collective-permute-start(f32[256,128]{1,0:T(8,128)S(1)} %get-tuple-element.51), channel_id=1, source_target_pairs={{8,2},{2,8},{10,4},{4,10},{12,6},{6,12},{14,7},{7,14},{15,5},{5,15... | collective-permute-start | bytes 393224 | tf_op jit(solution)/shard_map/ppermute | solution.py:946
  41.7 10.5 %all-to-all-start.2 = ((f32[32,8,128]{2,1,0:T(8,128)}), f32[32,8,128]{2,1,0:T(8,128)S(1)}, u32[]{:S(2)}, u32[]{:S(2)}) async-start(f32[32,8,128]{2,1,0:T(8,128)} %get-tuple-element.57), calls=%async_computation.2 | async-start | bytes 262144 | tf_op jit(solution)/shard_map/all_to_all | solution.py:950
  46.0 7.7 %collective-permute-start.6 = (f32[256,128]{1,0:T(8,128)S(1)}, f32[256,128]{1,0:T(8,128)S(1)}, u32[]{:S(2)}, u32[]{:S(2)}) collective-permute-start(f32[256,128]{1,0:T(8,128)S(1)} %get-tuple-element.55), channel_id=1, source_target_pairs={{0,8},{8,0},{2,10},{10,2},{4,12},{12,4},{6,14},{14,6},{7,15},{15,7... | collective-permute-start | bytes 393224 | tf_op jit(solution)/shard_map/ppermute | solution.py:945
  46.4 7.4 %collective-permute-start.7 = (f32[256,128]{1,0:T(8,128)S(1)}, f32[256,128]{1,0:T(8,128)S(1)}, u32[]{:S(2)}, u32[]{:S(2)}) collective-permute-start(f32[256,128]{1,0:T(8,128)S(1)} %get-tuple-element.56), channel_id=1, source_target_pairs={{8,2},{2,8},{10,4},{4,10},{12,6},{6,12},{14,7},{7,14},{15,5},{5,15... | collective-permute-start | bytes 393224 | tf_op jit(solution)/shard_map/ppermute | solution.py:946
